TPU v7x, 32 devices: a whole 2x2x4 slice. The times are simulated.
32 devices in a mesh: seq: 8 (over z, x), tp: 4 (over y, core).
Axes of the slice: x: 2, y: 2, z: 4, core: 2. Of those that a mesh axis runs over, the one named last changes fastest.
Arguments:
- tiles: bfloat16 [6144, 1536], P('seq', 'tp'), may hold values from -6 to 6
- tile_target: int32 [6144], P('seq'), may hold values from 0 to 6143, as said below
- slide_id: int32 [6144], P('seq'), may hold values from 0 to 15, never falling along the last dimension, each value on 1 to 1536 neighbouring positions
- proj_weight: bfloat16 [1536, 768], P('tp'), may hold values from -0.15625 to 0.15625
- norm_gain: float32 [768], replicated, may hold values from 0.1 to 1.9
- query_weight: bfloat16 [768, 768], P(None, 'tp'), may hold values from -2 to 2
- key_weight: bfloat16 [768, 768], P(None, 'tp'), may hold values from -2 to 2
- value_weight: bfloat16 [768, 768], P(None, 'tp'), may hold values from -0.21875 to 0.21875
- sub_gain: float32 [768], P('tp'), may hold values from 0.1 to 1.9
- out_weight: bfloat16 [768, 768], P('tp'), may hold values from -0.21875 to 0.21875
Outputs:
- layer_out: bfloat16 [6144, 768], P(('seq', 'tp'))
Inputs may be any that keep to these rules, and one draw needn't show every extreme that they name: `tile_target`: A permutation of the positions. The 768 tiles of each seq index send exactly 96 tiles into the block of 768 positions of every seq index.
All inputs are finite; a program needn't handle non-finite values.
Results may differ from a plain program's by a relative error of at most 0.012.
Values may be sent and summed in bfloat16 or wider, within the bound.
No kernel may reach another device: no remote copies, remote signals or barrier semaphores. Data moves between devices by JAX's collectives and lax.ppermute only.
A program may use at most 128 MiB of HBM per device.

v0:
```python
import functools

import jax
import jax.numpy as jnp
from jax import lax
from jax.experimental import pallas as pl
from jax.experimental.pallas import tpu as pltpu
from jax.sharding import PartitionSpec as P

BRANCHES = 5
HEAD_DIM = 48
SLOT = 64
LANES = 128
IDS = 16
CLASSES = 2 ** (BRANCHES - 1)
NEG = -1e30
EPS = 1e-05
BF16 = jnp.bfloat16
F32 = jnp.float32
VMEM_BYTES = 40 * 1024 * 1024


def up_to(count, step):
    return (count + step - 1) // step * step


def iota(shape, dim):
    return lax.broadcasted_iota(jnp.int32, shape, dim)


def dot(left, right):
    return jnp.dot(left, right, preferred_element_type=F32)


def dot_nt(left, right):
    return lax.dot_general(left, right, (((1,), (1,)), ((), ())), preferred_element_type=F32)


def dot_tn(left, right):
    return lax.dot_general(left, right, (((0,), (0,)), ((), ())), preferred_element_type=F32)


def one_hot(mask):
    return jnp.where(mask, 1.0, 0.0).astype(BF16)


def stored_at(position, rows):
    residue = position & (CLASSES - 1)
    flipped = jnp.zeros_like(residue)
    for bit in range(BRANCHES - 1):
        flipped = flipped + (((residue >> bit) & 1) << (BRANCHES - 2 - bit))
    return flipped * (rows // CLASSES) + (position >> (BRANCHES - 1))


def head_start(level, head, column, rows):
    start = 0
    for bit in range(level):
        value = (head >> bit) & 1 if bit < 2 else (column >> (bit - 2)) & 1
        start = start + value * (rows >> (bit + 1))
    return start


def levels_of(index, head, column, rows):
    total = jnp.zeros(index.shape, jnp.int32)
    for level in range(1, BRANCHES):
        start = head_start(level, head, column, rows)
        inside = (index >= start) & (index < start + (rows >> level))
        total = total + jnp.where(inside, 1, 0)
    return total


def call(kernel, name, outs, args, scratch=(), flops=0, moved=0):
    vmem = pl.BlockSpec(memory_space=pltpu.VMEM)
    return pl.pallas_call(
        kernel,
        name=name,
        out_shape=[jax.ShapeDtypeStruct(shape, dtype) for shape, dtype in outs],
        in_specs=[vmem] * len(args),
        out_specs=[vmem] * len(outs),
        scratch_shapes=list(scratch),
        compiler_params=pltpu.CompilerParams(vmem_limit_bytes=VMEM_BYTES),
        cost_estimate=pl.CostEstimate(flops=flops, bytes_accessed=moved, transcendentals=0),
    )(*args)


def route_kernel(n_seq, n_tp, peer, target_ref, slide_ref, tiles_ref, out_ref):
    rows = tiles_ref.shape[0]
    chunks = tiles_ref.shape[1] // LANES
    sub = peer // n_tp
    sub_pad = up_to(sub, 8)
    blocks = n_seq * n_tp
    place, column = lax.axis_index("seq"), lax.axis_index("tp")
    target = target_ref[...]
    owner = jnp.floor((target.astype(F32) + 0.5) * (1.0 / rows)).astype(jnp.int32)
    flags = jnp.where(iota((n_seq, rows), 0) == owner, 1.0, 0.0)
    before = one_hot(iota((rows, rows), 0) <= iota((rows, rows), 1))
    counts = dot(flags.astype(BF16), before)
    slot = jnp.sum(flags * counts, axis=0, keepdims=True).astype(jnp.int32) - 1
    lane_of = jnp.zeros_like(slot)
    for turn in range(1, n_tp):
        lane_of = lane_of + jnp.where(slot >= turn * sub, 1, 0)
    low = slot - lane_of * sub
    target_row = (owner * n_tp + lane_of) * sub_pad + low
    picked = dot(one_hot(iota((blocks * sub_pad, rows), 0) == target_row), tiles_ref[...])

    spot = stored_at(target - owner * rows, rows)
    high = spot >> 7
    code = ((spot & 127) + 128).astype(F32)
    for bit in range(3):
        code = code * jnp.where((high >> bit) & 1 == 1, 256.0 ** (2**bit), 1.0)
    arrival = place * sub_pad + low
    extra = n_seq * 8
    code_rows = up_to(n_seq * sub_pad, LANES) // LANES
    line = iota((extra, rows), 0)
    mine = (owner == (line >> 3)) & (lane_of == column) & ((arrival >> 7) == (line & 7))
    coded = dot_nt(
        jnp.where(mine, code, 0.0).astype(BF16),
        one_hot(iota((LANES, rows), 0) == (arrival & 127)),
    )
    share = rows // n_tp
    kept = stored_at(iota((1, rows), 1), rows) - column * share
    held = (kept >= 0) & (kept < share) & ((kept >> 7) + code_rows == (line & 7))
    ids = dot_nt(
        jnp.where(held, slide_ref[...].astype(F32), 0.0).astype(BF16),
        one_hot(iota((LANES, rows), 0) == (kept & 127)),
    )
    notes = coded + ids
    pad = out_ref.shape[1] - chunks * sub_pad - 8
    for block in range(blocks):
        base = block * sub_pad
        pieces = [
            picked[base : base + sub_pad, part * LANES : (part + 1) * LANES] for part in range(chunks)
        ]
        start = block // n_tp * 8
        pieces.append(notes[start : start + 8])
        if pad:
            pieces.append(jnp.zeros((pad, LANES), F32))
        out_ref[block] = jnp.concatenate(pieces, axis=0).astype(BF16)


def weights_kernel(query_ref, key_ref, value_ref, gain_ref, out_weight_ref, all_ref, scaled_ref):
    width = query_ref.shape[1]
    heads = width // HEAD_DIM
    wide = heads * SLOT
    spread = one_hot(spread_mask(width, wide, 0))
    for place, ref in enumerate((query_ref, key_ref, value_ref)):
        all_ref[:, place * wide : (place + 1) * wide] = dot(ref[...], spread).astype(BF16)
    total = all_ref.shape[1] - 3 * wide
    at = iota((width, total), 0)
    lane = iota((width, total), 1)
    packed = dot(key_ref[...], one_hot(lane == at)) + dot(value_ref[...], one_hot(lane == at + width))
    all_ref[:, 3 * wide :] = packed.astype(BF16)
    same = iota((width, width), 0) == iota((width, width), 1)
    gain = jnp.sum(jnp.where(same, gain_ref[...], 0.0), axis=1, keepdims=True)
    scaled_ref[...] = (out_weight_ref[...].astype(F32) * gain).astype(BF16)


def spread_mask(width, wide, shift):
    row = iota((width, wide), 0) - shift
    lane = iota((width, wide), 1)
    inner = lane & (SLOT - 1)
    return (inner < HEAD_DIM) & (row == (lane >> 6) * HEAD_DIM + inner)


def project_kernel(n_seq, n_tp, peer, recv_ref, *refs):
    weight_refs = refs[:n_tp]
    stream_ref, codes_ref, ids_ref, work = refs[n_tp:]
    sub_pad = up_to(peer // n_tp, 8)
    chunks = work.shape[1] // LANES
    column = lax.axis_index("tp")
    code_rows = codes_ref.shape[2] // LANES
    share = ids_ref.shape[2]
    total = None
    for turn in range(n_tp):
        other = column ^ turn
        codes = jnp.zeros((8, LANES), F32)
        for source in range(n_seq):
            block = recv_ref[source * n_tp + other].astype(F32)
            for part in range(chunks):
                work[source * sub_pad : (source + 1) * sub_pad, part * LANES : (part + 1) * LANES] = block[
                    part * sub_pad : (part + 1) * sub_pad
                ]
            note = block[chunks * sub_pad : chunks * sub_pad + 8]
            codes = codes + note
            for piece in range(up_to(share, LANES) // LANES):
                length = min(LANES, share - piece * LANES)
                ids_ref[other, source : source + 1, piece * LANES : piece * LANES + length] = note[
                    code_rows + piece : code_rows + piece + 1, :length
                ]
        power = jnp.zeros((8, LANES), F32)
        scale = jnp.ones((8, LANES), F32)
        for step in range(1, 8):
            above = codes >= 128.0 * 256.0**step
            power = power + jnp.where(above, 128.0, 0.0)
            scale = scale * jnp.where(above, 1.0 / 256.0, 1.0)
        spots = jnp.where(codes > 0.0, codes * scale - 128.0 + power, -1.0)
        for piece in range(code_rows):
            codes_ref[turn, :, piece * LANES : (piece + 1) * LANES] = spots[piece : piece + 1].astype(jnp.int32)
        part_sum = dot(work[...].astype(BF16), weight_refs[turn][...])
        total = part_sum if total is None else total + part_sum
    stream_ref[...] = total.astype(BF16)


def heads_kernel(n_tp, levels, codes_ref, gain_ref, weights_ref, *refs):
    shards = refs[:n_tp]
    query_ref, key_ref, value_ref = refs[n_tp : n_tp + 3]
    sets = refs[n_tp + 3 : n_tp + 3 + len(levels)]
    packed = refs[-1]
    rows = query_ref.shape[0]
    wide = query_ref.shape[1]
    heads = wide // SLOT
    column = lax.axis_index("tp")
    ordered = None
    for turn in range(n_tp):
        count = shards[turn].shape[0]
        spots = codes_ref[turn]
        place = one_hot(iota((rows, spots.shape[1]), 0) == spots)[:, :count]
        moved = dot(place, shards[turn][...])
        ordered = moved if ordered is None else ordered + moved
    mean = jnp.mean(ordered, axis=-1, keepdims=True)
    second = jnp.mean(ordered * ordered, axis=-1, keepdims=True)
    normed = (ordered - mean) * lax.rsqrt(second - mean * mean + EPS) * gain_ref[...]
    result = dot(normed.astype(BF16), weights_ref[...])
    query_ref[...] = (result[:, :wide] * HEAD_DIM ** (-0.5)).astype(BF16)
    key_ref[...] = result[:, wide : 2 * wide].astype(BF16)
    value_ref[...] = result[:, 2 * wide : 3 * wide].astype(BF16)
    packed[...] = result[:, 3 * wide :].astype(BF16)
    width = heads * HEAD_DIM
    for ref, level in zip(sets, levels):
        count = rows >> level
        lane = iota((count, 2 * width), 1)
        lane = jnp.where(lane >= width, lane - width, lane)
        chosen = None
        for head in range(heads):
            part = packed[pl.ds(head_start(level, head, column, rows), count), :]
            if chosen is None:
                chosen = part
            else:
                chosen = jnp.where(lane >= head * HEAD_DIM, part, chosen)
        ref[...] = chosen


def id_lanes(ids, wide, apart):
    count = ids.shape[1]
    lane = iota((IDS, wide), 1) & (SLOT - 1)
    group = iota((IDS, wide), 0)
    same = lane - HEAD_DIM == group
    if apart is None:
        table = jnp.where(same, 1.0, 0.0)
    else:
        table = jnp.where((lane >= HEAD_DIM) & ~same, apart, 0.0)
    return dot_tn(one_hot(iota((IDS, count), 0) == ids), table.astype(BF16))


def own_kernel(n_tp, groups, codes_ref, ids_ref, query_ref, key_ref, value_ref, *refs):
    shards = refs[:n_tp]
    acc_ref, masked_ref, base_ref = refs[n_tp : n_tp + 3]
    apart_refs = refs[n_tp + 3 : n_tp + 3 + len(groups)]
    keys_ref, values_ref, apart_all = refs[-3:]
    rows, wide = query_ref.shape
    heads = wide // SLOT
    place, column = lax.axis_index("seq"), lax.axis_index("tp")
    ids = ids_ref[pl.ds(place, 1), :].astype(jnp.int32)
    masked_ref[...] = (query_ref[...].astype(F32) + id_lanes(ids, wide, None)).astype(BF16)
    keys_ref[...] = (key_ref[...].astype(F32) + id_lanes(ids, wide, NEG)).astype(BF16)
    ones = jnp.where((iota((rows, wide), 1) & (SLOT - 1)) >= HEAD_DIM, 1.0, 0.0)
    values_ref[...] = (value_ref[...].astype(F32) + ones).astype(BF16)
    half = rows // 2
    for part in range(2):
        start = part * half
        query = masked_ref[start : start + half, :]
        slot_of = iota((half, wide), 1) >> 6
        spare = (iota((half, wide), 1) & (SLOT - 1)) >= HEAD_DIM + 8
        acc = None
        for head in range(heads):
            one = jnp.where(slot_of == head, query, jnp.zeros((), BF16))
            scores = dot_nt(one, keys_ref[...])
            top = jnp.max(scores, axis=1, keepdims=True)
            weights = jnp.exp(scores - top)
            if part == (head & 1):
                level_q = levels_of(start + iota((half, 1), 0), head, column, rows)
                level_k = levels_of(start + iota((1, half), 1), head, column, rows)
                times = (jnp.minimum(level_q, level_k) + 1).astype(F32)
                scaled = weights[:, start : start + half] * times
                others = weights[:, half - start : rows - start]
                weights = jnp.concatenate([scaled, others] if part == 0 else [others, scaled], axis=1)
            got = dot(weights.astype(BF16), values_ref[...])
            got = jnp.where(spare, top, got)
            acc = got if acc is None else jnp.where(slot_of == head, got, acc)
        acc_ref[start : start + half, :] = acc

    share = base_ref.shape[0]
    wanted = stored_at(column * share + iota((share, 1), 0), rows)
    base = None
    for turn in range(n_tp):
        spots = codes_ref[turn]
        moved = dot(one_hot(wanted == spots)[:, : shards[turn].shape[0]], shards[turn][...])
        base = moved if base is None else base + moved
    base_ref[...] = base.astype(BF16)

    for ref, (level, masks) in zip(apart_refs, groups):
        count = rows >> level
        slots = iota((count, wide), 1) >> 6
        for index, mask in enumerate(masks):
            far = ids_ref[pl.ds(place ^ mask, 1), :].astype(jnp.int32)
            apart_all[...] = id_lanes(far, wide, NEG).astype(BF16)
            chosen = None
            for head in range(heads):
                part = apart_all[pl.ds(head_start(level, head, column, rows), count), :]
                chosen = part if chosen is None else jnp.where(slots >= head, part, chosen)
            ref[index * count : (index + 1) * count, :] = chosen


def far_kernel(n_tp, groups, acc_ref, query_ref, *refs):
    n_groups = len(groups)
    apart_refs = refs[:n_groups]
    refs = refs[n_groups:]
    set_refs = []
    for _, masks in groups:
        set_refs.append(refs[: len(masks)])
        refs = refs[len(masks) :]
    out_refs, acc = refs[:n_tp], refs[n_tp]
    rows, wide = acc_ref.shape
    heads = wide // SLOT
    width = heads * HEAD_DIM
    column = lax.axis_index("tp")
    acc[...] = acc_ref[...]
    spread_key = one_hot(spread_mask(2 * width, wide, 0))
    spread_value = one_hot(spread_mask(2 * width, wide, width))
    for apart_ref, sets, (level, masks) in zip(apart_refs, set_refs, groups):
        count = rows >> level
        total = count * len(masks)
        pairs = jnp.concatenate([ref[...] for ref in sets], axis=0)
        keys = (dot(pairs, spread_key) + apart_ref[...].astype(F32)).astype(BF16)
        ones = jnp.where((iota((total, wide), 1) & (SLOT - 1)) >= HEAD_DIM, 1.0, 0.0)
        values = (dot(pairs, spread_value) + ones).astype(BF16)
        slot_of = iota((count, wide), 1) >> 6
        spare = (iota((count, wide), 1) & (SLOT - 1)) >= HEAD_DIM + 8
        for head in range(heads):
            first = head_start(level, head, column, rows)
            here = pl.ds(first, count)
            one = jnp.where(slot_of == head, query_ref[here, :], jnp.zeros((), BF16))
            scores = dot_nt(one, keys)
            before = acc[here, :]
            at = head * SLOT + HEAD_DIM + 8
            top_before = before[:, at : at + 1]
            top = jnp.maximum(top_before, jnp.max(scores, axis=1, keepdims=True))
            weights = jnp.exp(scores - top)
            level_q = levels_of(first + iota((count, 1), 0), head, column, rows)
            key_row = iota((1, total), 1)
            for index in range(1, len(masks)):
                key_row = key_row - jnp.where(iota((1, total), 1) >= index * count, count, 0)
            level_k = levels_of(first + key_row, head, column, rows)
            times = (jnp.minimum(level_q, level_k) - (level - 1)).astype(F32)
            got = dot((weights * times).astype(BF16), values)
            now = jnp.where(spare, top, before * jnp.exp(top_before - top) + got)
            acc[here, :] = jnp.where(slot_of == head, now, before)

    every = acc[...]
    lane = iota((rows, wide), 1)
    slot_of, inner = lane >> 6, lane & (SLOT - 1)
    share_of = None
    for head in range(heads):
        at = head * SLOT + HEAD_DIM
        part = 1.0 / every[:, at : at + 1]
        share_of = part + jnp.zeros_like(every) if share_of is None else jnp.where(slot_of == head, part, share_of)
    inside = inner < HEAD_DIM
    attn = jnp.where(inside, every * share_of, 0.0)
    mean = jnp.sum(attn, axis=1, keepdims=True) * (1.0 / width)
    high = mean.astype(BF16).astype(F32)
    rest = mean - high
    message = jnp.where(inside, attn - mean, jnp.where(inner == HEAD_DIM, high, rest)).astype(BF16)
    share = out_refs[0].shape[0]
    for turn in range(n_tp):
        wanted = stored_at((column ^ turn) * share + iota((share, 1), 0), rows)
        out_refs[turn][...] = dot(one_hot(wanted == iota((share, rows), 1)), message).astype(BF16)


def mix_kernel(n_tp, base_ref, *refs):
    message_refs = refs[:n_tp]
    weight_refs = refs[n_tp : 2 * n_tp]
    out_ref = refs[-1]
    share, wide = message_refs[0].shape
    heads = wide // SLOT
    features = n_tp * heads * HEAD_DIM
    inside = (iota((share, wide), 1) & (SLOT - 1)) < HEAD_DIM
    parts = []
    means = []
    for ref in message_refs:
        message = ref[...].astype(F32)
        parts.append(message)
        means.append(message[:, HEAD_DIM : HEAD_DIM + 1] + message[:, HEAD_DIM + 1 : HEAD_DIM + 2])
    mean = sum(means) * (1.0 / n_tp)
    parts = [jnp.where(inside, part + (own - mean), 0.0) for part, own in zip(parts, means)]
    spread = sum(jnp.sum(part * part, axis=1, keepdims=True) for part in parts) * (1.0 / features)
    factor = lax.rsqrt(spread + EPS)
    total = base_ref[...].astype(F32)
    gap = jnp.zeros((SLOT - HEAD_DIM, out_ref.shape[1]), BF16)
    for part, ref in zip(parts, weight_refs):
        pieces = []
        for head in range(heads):
            pieces += [ref[head * HEAD_DIM : (head + 1) * HEAD_DIM, :], gap]
        total = total + dot((part * factor).astype(BF16), jnp.concatenate(pieces, axis=0))
    out_ref[...] = total.astype(BF16)


def swap(block, axis, mask):
    count = lax.axis_size(axis)
    return lax.ppermute(block, axis, [(index, index ^ mask) for index in range(count)])


def gather_tp(block):
    across = swap(block, "tp", 2)
    return [block, swap(block, "tp", 1), across, swap(across, "tp", 1)]


def body(
    tiles,
    tile_target,
    slide_id,
    proj_weight,
    norm_gain,
    query_weight,
    key_weight,
    value_weight,
    sub_gain,
    out_weight,
):
    n_seq = lax.axis_size("seq")
    n_tp = lax.axis_size("tp")
    rows, tile_width = tiles.shape
    features = proj_weight.shape[1]
    width = query_weight.shape[1]
    heads = width // HEAD_DIM
    wide = heads * SLOT
    share = rows // n_tp
    peer = rows // n_seq
    sub_pad = up_to(peer // n_tp, 8)
    arriving = n_seq * sub_pad
    chunks = tile_width // LANES
    block_rows = up_to(chunks * sub_pad + 8, 16)

    first_group = max(1, n_seq // 16)
    sizes = [min(first_group * 2**branch, n_seq) for branch in range(BRANCHES)]
    groups = []
    for level in range(BRANCHES):
        masks = tuple(range(1 if level == 0 else sizes[level - 1], sizes[level]))
        if masks:
            groups.append((level, masks))

    (blocks,) = call(
        functools.partial(route_kernel, n_seq, n_tp, peer),
        "route",
        [((n_seq * n_tp, block_rows, LANES), BF16)],
        [tile_target.reshape(1, rows), slide_id.reshape(1, rows), tiles],
    )
    received = lax.all_to_all(blocks, ("seq", "tp"), split_axis=0, concat_axis=0, tiled=True)
    all_weights, scaled_weight = call(
        weights_kernel,
        "weights",
        [((features, 3 * wide + 2 * width), BF16), ((width, features), BF16)],
        [query_weight, key_weight, value_weight, sub_gain.reshape(1, width), out_weight],
    )
    proj_parts = gather_tp(proj_weight)
    out_parts = gather_tp(scaled_weight)

    stream, codes, ids = call(
        functools.partial(project_kernel, n_seq, n_tp, peer),
        "project",
        [
            ((arriving, features), BF16),
            ((n_tp, 1, up_to(arriving, LANES)), jnp.int32),
            ((n_tp, n_seq, share), F32),
        ],
        [received] + proj_parts,
        scratch=[pltpu.VMEM((arriving, tile_width), F32)],
    )
    ids = ids.transpose(1, 0, 2).reshape(n_seq, rows)
    shards = gather_tp(stream)

    results = call(
        functools.partial(heads_kernel, n_tp, [level for level, _ in groups]),
        "heads",
        [((rows, wide), BF16)] * 3 + [((rows >> level, 2 * width), BF16) for level, _ in groups],
        [codes, norm_gain.reshape(1, features), all_weights] + shards,
        scratch=[pltpu.VMEM((rows, 2 * width), BF16)],
    )
    query, key, value = results[:3]
    far_sets = [None] * len(groups)
    for index in reversed(range(len(groups))):
        far_sets[index] = [swap(results[3 + index], "seq", mask) for mask in groups[index][1]]

    own = call(
        functools.partial(own_kernel, n_tp, groups),
        "own",
        [((rows, wide), F32), ((rows, wide), BF16), ((share, features), BF16)]
        + [(((rows >> level) * len(masks), wide), BF16) for level, masks in groups],
        [codes, ids, query, key, value] + shards,
        scratch=[pltpu.VMEM((rows, wide), BF16)] * 3,
    )
    messages = call(
        functools.partial(far_kernel, n_tp, groups),
        "far",
        [((share, wide), BF16)] * n_tp,
        [own[0], own[1]] + list(own[3:]) + [one for sets in far_sets for one in sets],
        scratch=[pltpu.VMEM((rows, wide), F32)],
    )
    arrived = [messages[0]] + [swap(messages[turn], "tp", turn) for turn in range(1, n_tp)]
    (result,) = call(
        functools.partial(mix_kernel, n_tp),
        "mix",
        [((share, features), BF16)],
        [own[2]] + arrived + out_parts,
    )
    return result


def solution(mesh):
    return jax.shard_map(
        body,
        mesh=mesh,
        in_specs=(
            P("seq", "tp"),
            P("seq"),
            P("seq"),
            P("tp", None),
            P(),
            P(None, "tp"),
            P(None, "tp"),
            P(None, "tp"),
            P("tp"),
            P("tp", None),
        ),
        out_specs=P(("seq", "tp"), None),
        check_vma=False,
    )
```

profile of v0, /device:TPU:0, one launch (start us, length us, event | category | flops | bytes accessed | tf_op | source)
XLA Modules:
  0.0 102.7 jit_solution(11247479310215405305)
XLA Ops:
  2.4 2.0 %route.1 = bf16[32,80,128]{2,1,0:T(8,128)(2,1)} custom-call(s32[1,768]{1,0:T(1,128)S(1)} %reshape.15.target_ref, s32[1,768]{1,0:T(1,128)S(1)} %reshape.16.slide_ref, bf16[768,384]{1,0:T(8,128)(2,1)S(1)} %copy-done), custom_call_target="tpu_custom_call" | custom-call | tf_op jit(solution)/shard_map/route/pallas_call | solution.py:74
  4.5 7.3 %all-to-all-start = ((bf16[32,80,128]{2,1,0:T(8,128)(2,1)}), bf16[32,80,128]{2,1,0:T(8,128)(2,1)S(1)}, u32[]{:S(2)}, u32[]{:S(2)}) async-start(bf16[32,80,128]{2,1,0:T(8,128)(2,1)} %route.1), calls=%async_computation | async-start | bytes 1310720 | tf_op jit(solution)/shard_map/all_to_all | solution.py:457
  11.8 1.8 %collective-permute-start.1 = (bf16[384,768]{1,0:T(8,128)(2,1)S(1)}, bf16[384,768]{1,0:T(8,128)(2,1)S(1)}, u32[]{:S(2)}, u32[]{:S(2)}) collective-permute-start(bf16[384,768]{1,0:T(8,128)(2,1)S(1)} %copy-done.1), channel_id=1, source_target_pairs={{0,2},{1,3},{2,0},{3,1},{4,6},{5,7},{6,4},{7,5},{8,10},{9,11},{10,... | collective-permute-start | bytes 1769480 | tf_op jit(solution)/shard_map/ppermute | solution.py:409
  13.6 20.7 %collective-permute-done.1.refs_2_ = bf16[384,768]{1,0:T(8,128)(2,1)S(1)} collective-permute-done((bf16[384,768]{1,0:T(8,128)(2,1)S(1)}, bf16[384,768]{1,0:T(8,128)(2,1)S(1)}, u32[]{:S(2)}, u32[]{:S(2)}) %collective-permute-start.1) | collective-permute-done | bytes 589856 | tf_op jit(solution)/shard_map/ppermute | solution.py:409
  34.3 2.0 %collective-permute-done.2.refs_3_ = bf16[384,768]{1,0:T(8,128)(2,1)S(1)} collective-permute-done((bf16[384,768]{1,0:T(8,128)(2,1)S(1)}, bf16[384,768]{1,0:T(8,128)(2,1)S(1)}, u32[]{:S(2)}, u32[]{:S(2)}) %collective-permute-start.2) | collective-permute-done | bytes 589856 | tf_op jit(solution)/shard_map/ppermute | solution.py:409
  37.1 1.1 %copy-done.3 = bf16[384,768]{1,0:T(8,128)(2,1)S(1)} copy-done((bf16[384,768]{1,0:T(8,128)(2,1)S(1)}, bf16[384,768]{1,0:T(8,128)(2,1)}, u32[]{:S(2)}) %copy-start.3) | copy-done | bytes 589848
  40.2 8.4 %collective-permute-done.4.refs_2_ = bf16[192,768]{1,0:T(8,128)(2,1)S(1)} collective-permute-done((bf16[192,768]{1,0:T(8,128)(2,1)S(1)}, bf16[192,768]{1,0:T(8,128)(2,1)S(1)}, u32[]{:S(2)}, u32[]{:S(2)}) %collective-permute-start.4) | collective-permute-done | bytes 294944 | tf_op jit(solution)/shard_map/ppermute | solution.py:409
  48.8 1.1 %copy.13.key_ref = bf16[768,192]{1,0:T(8,128)(2,1)S(1)} copy(bf16[768,192]{0,1:T(8,128)(2,1)} %param.16) | data formatting | bytes 589824 | tf_op args[6]
  49.9 1.1 %copy.14.value_ref = bf16[768,192]{1,0:T(8,128)(2,1)S(1)} copy(bf16[768,192]{0,1:T(8,128)(2,1)} %param.17) | data formatting | bytes 589824 | tf_op args[7]
  52.7 4.5 %heads.1 = (bf16[768,256]{1,0:T(8,128)(2,1)S(1)}, bf16[768,256]{1,0:T(8,128)(2,1)S(1)}, bf16[768,256]{1,0:T(8,128)(2,1)S(1)}, bf16[384,384]{1,0:T(8,128)(2,1)}, ...) custom-call(s32[4,1,256]{2,1,0:T(1,128)S(1)} %get-tuple-element.26.codes_ref, f32[1,768]{1,0:T(1,128)S(1)} %reshape.18.gain_ref, ...), custom_call_target="tpu_custom_call" | custom-call | tf_op jit(solution)/shard_map/heads/pallas_call | solution.py:74
  57.2 1.2 %collective-permute-start.6 = (bf16[384,384]{1,0:T(8,128)(2,1)}, bf16[384,384]{1,0:T(8,128)(2,1)}, u32[]{:S(2)}, u32[]{:S(2)}) collective-permute-start(bf16[384,384]{1,0:T(8,128)(2,1)} %get-tuple-element.39), channel_id=1, source_target_pairs={{0,4},{4,0},{8,12},{12,8},{16,20},{20,16},{24,28},{28,24},{1,5},{5... | collective-permute-start | bytes 884744 | tf_op jit(solution)/shard_map/ppermute | solution.py:409
  58.4 3.6 %collective-permute-start.12 = (bf16[96,384]{1,0:T(8,128)(2,1)S(1)}, bf16[96,384]{1,0:T(8,128)(2,1)S(1)}, u32[]{:S(2)}, u32[]{:S(2)}) collective-permute-start(bf16[96,384]{1,0:T(8,128)(2,1)S(1)} %get-tuple-element.41), channel_id=1, source_target_pairs={{0,28},{4,24},{8,20},{12,16},{16,12},{20,8},{24,4},{28,0},{1,29},{... | collective-permute-start | bytes 221192 | tf_op jit(solution)/shard_map/ppermute | solution.py:409
  62.5 1.4 %collective-permute-start.10 = (bf16[96,384]{1,0:T(8,128)(2,1)S(1)}, bf16[96,384]{1,0:T(8,128)(2,1)S(1)}, u32[]{:S(2)}, u32[]{:S(2)}) collective-permute-start(bf16[96,384]{1,0:T(8,128)(2,1)S(1)} %get-tuple-element.41), channel_id=1, source_target_pairs={{0,20},{4,16},{8,28},{12,24},{16,4},{20,0},{24,12},{28,8},{1,21},{... | collective-permute-start | bytes 221192 | tf_op jit(solution)/shard_map/ppermute | solution.py:409
  63.9 2.1 %collective-permute-start.9 = (bf16[96,384]{1,0:T(8,128)(2,1)S(1)}, bf16[96,384]{1,0:T(8,128)(2,1)S(1)}, u32[]{:S(2)}, u32[]{:S(2)}) collective-permute-start(bf16[96,384]{1,0:T(8,128)(2,1)S(1)} %get-tuple-element.41), channel_id=1, source_target_pairs={{0,16},{4,20},{8,24},{12,28},{16,0},{20,4},{24,8},{28,12},{1,17},{... | collective-permute-start | bytes 221192 | tf_op jit(solution)/shard_map/ppermute | solution.py:409
  66.7 1.9 %collective-permute-done.11.refs_8_ = bf16[96,384]{1,0:T(8,128)(2,1)S(1)} collective-permute-done((bf16[96,384]{1,0:T(8,128)(2,1)S(1)}, bf16[96,384]{1,0:T(8,128)(2,1)S(1)}, u32[]{:S(2)}, u32[]{:S(2)}) %collective-permute-start.11) | collective-permute-done | bytes 73760 | tf_op jit(solution)/shard_map/ppermute | solution.py:409
  69.2 5.6 %collective-permute-done.10.refs_7_ = bf16[96,384]{1,0:T(8,128)(2,1)S(1)} collective-permute-done((bf16[96,384]{1,0:T(8,128)(2,1)S(1)}, bf16[96,384]{1,0:T(8,128)(2,1)S(1)}, u32[]{:S(2)}, u32[]{:S(2)}) %collective-permute-start.10) | collective-permute-done | bytes 73760 | tf_op jit(solution)/shard_map/ppermute | solution.py:409
  76.1 2.2 %collective-permute-start.7 = (bf16[192,384]{1,0:T(8,128)(2,1)}, bf16[192,384]{1,0:T(8,128)(2,1)}, u32[]{:S(2)}, u32[]{:S(2)}) collective-permute-start(bf16[192,384]{1,0:T(8,128)(2,1)} %get-tuple-element.40), channel_id=1, source_target_pairs={{0,8},{4,12},{8,0},{12,4},{16,24},{20,28},{24,16},{28,20},{1,9},{5... | collective-permute-start | bytes 442376 | tf_op jit(solution)/shard_map/ppermute | solution.py:409
  78.9 1.4 %reshape.17.ids_ref = f32[8,768]{1,0:T(8,128)} reshape(f32[8,4,192]{2,1,0:T(4,128)} %copy.11) | data formatting | bytes 49152 | tf_op jit(solution)/shard_map/reshape | solution.py:478
  81.1 4.8 %own.1 = (f32[768,256]{1,0:T(8,128)S(1)}, bf16[768,256]{1,0:T(8,128)(2,1)S(1)}, bf16[192,768]{1,0:T(8,128)(2,1)S(1)}, bf16[384,256]{1,0:T(8,128)(2,1)S(1)}, bf16...) custom-call(s32[4,1,256]{2,1,0:T(1,128)S(1)} %get-tuple-element.26.codes_ref, f32[8,768]{1,0:T(8,128)S(1)} %copy-done.5, ...), custom_call_target="tpu_custom_call" | custom-call | tf_op jit(solution)/shard_map/own/pallas_call | solution.py:74
  86.0 8.2 %far.1 = (bf16[192,256]{1,0:T(8,128)(2,1)S(1)}, bf16[192,256]{1,0:T(8,128)(2,1)S(1)}, bf16[192,256]{1,0:T(8,128)(2,1)S(1)}, bf16[192,256]{1,0:T(8,128)(2,1)S(1)}) custom-call(f32[768,256]{1,0:T(8,128)S(1)} %get-tuple-element.34.acc_ref, bf16[768,256]{1,0:T(8,128)(2,1)S(1)} %get-tuple-element.35.query_ref, bf16[384,256]{1,0:T(8,128)(2,1)S(1)} %get-tuple-element.36.refs_0_, ...), custom_call_target="tpu_custom_call" | custom-call | tf_op jit(solution)/shard_map/far/pallas_call | solution.py:74
  94.2 1.4 %collective-permute-start.14 = (bf16[192,256]{1,0:T(8,128)(2,1)S(1)}, bf16[192,256]{1,0:T(8,128)(2,1)S(1)}, u32[]{:S(2)}, u32[]{:S(2)}) collective-permute-start(bf16[192,256]{1,0:T(8,128)(2,1)S(1)} %get-tuple-element.44), channel_id=1, source_target_pairs={{0,2},{1,3},{2,0},{3,1},{4,6},{5,7},{6,4},{7,5},{8,10},{9,11},{10,... | collective-permute-start | bytes 294920 | tf_op jit(solution)/shard_map/ppermute | solution.py:409
  96.1 3.8 %collective-permute-done.14.refs_2_ = bf16[192,256]{1,0:T(8,128)(2,1)S(1)} collective-permute-done((bf16[192,256]{1,0:T(8,128)(2,1)S(1)}, bf16[192,256]{1,0:T(8,128)(2,1)S(1)}, u32[]{:S(2)}, u32[]{:S(2)}) %collective-permute-start.14) | collective-permute-done | bytes 98336 | tf_op jit(solution)/shard_map/ppermute | solution.py:409
  99.9 1.2 %collective-permute-done.15.refs_3_ = bf16[192,256]{1,0:T(8,128)(2,1)S(1)} collective-permute-done((bf16[192,256]{1,0:T(8,128)(2,1)S(1)}, bf16[192,256]{1,0:T(8,128)(2,1)S(1)}, u32[]{:S(2)}, u32[]{:S(2)}) %collective-permute-start.15) | collective-permute-done | bytes 98336 | tf_op jit(solution)/shard_map/ppermute | solution.py:409
  101.1 1.6 %mix.1 = bf16[192,768]{1,0:T(8,128)(2,1)} custom-call(bf16[192,768]{1,0:T(8,128)(2,1)S(1)} %get-tuple-element.33.base_ref, bf16[192,256]{1,0:T(8,128)(2,1)S(1)} %get-tuple-element.42.refs_0_, bf16[192,256]{1,0:T(8,128)(2,1)S(1)} %collective-permute-done.13.refs_1_, bf16[192,256]{1,0:T(8,128)(2,1)S(1)} %collective-permute-done.14.refs_2_, ...), custom_call_target="tpu_custom_call" | custom-call | tf_op jit(solution)/shard_map/mix/pallas_call | solution.py:74
  (69 shorter events, 12.0 us)
Async XLA Ops:
  4.5 44.2 %copy-start.17 = (bf16[768,192]{0,1:T(8,128)(2,1)S(1)}, bf16[768,192]{0,1:T(8,128)(2,1)}, u32[]{:S(2)}) copy-start(bf16[768,192]{0,1:T(8,128)(2,1)} %param.15) | copy-start | bytes 884740
  4.5 32.7 %all-to-all-start = ((bf16[32,80,128]{2,1,0:T(8,128)(2,1)}), bf16[32,80,128]{2,1,0:T(8,128)(2,1)S(1)}, u32[]{:S(2)}, u32[]{:S(2)}) async-start(bf16[32,80,128]{2,1,0:T(8,128)(2,1)} %route.1), calls=%async_computation | async-start | bytes 1310720 | tf_op jit(solution)/shard_map/all_to_all | solution.py:457
  11.8 22.5 %collective-permute-start.1 = (bf16[384,768]{1,0:T(8,128)(2,1)S(1)}, bf16[384,768]{1,0:T(8,128)(2,1)S(1)}, u32[]{:S(2)}, u32[]{:S(2)}) collective-permute-start(bf16[384,768]{1,0:T(8,128)(2,1)S(1)} %copy-done.1), channel_id=1, source_target_pairs={{0,2},{1,3},{2,0},{3,1},{4,6},{5,7},{6,4},{7,5},{8,10},{9,11},{10,... | collective-permute-start | bytes 1769480 | tf_op jit(solution)/shard_map/ppermute | solution.py:409
  13.6 20.7 %collective-permute-start = (bf16[384,768]{1,0:T(8,128)(2,1)S(1)}, bf16[384,768]{1,0:T(8,128)(2,1)S(1)}, u32[]{:S(2)}, u32[]{:S(2)}) collective-permute-start(bf16[384,768]{1,0:T(8,128)(2,1)S(1)} %copy-done.1), channel_id=1, source_target_pairs={{0,1},{1,0},{2,3},{3,2},{4,5},{5,4},{6,7},{7,6},{8,9},{9,8},{10,11... | collective-permute-start | bytes 1769480 | tf_op jit(solution)/shard_map/ppermute | solution.py:409
  34.3 2.0 %collective-permute-start.2 = (bf16[384,768]{1,0:T(8,128)(2,1)S(1)}, bf16[384,768]{1,0:T(8,128)(2,1)S(1)}, u32[]{:S(2)}, u32[]{:S(2)}) collective-permute-start(bf16[384,768]{1,0:T(8,128)(2,1)S(1)} %collective-permute-done.1.refs_2_), channel_id=1, source_target_pairs={{0,1},{1,0},{2,3},{3,2},{4,5},{5,4},{6,7},{7,6},{8,9},{9,8},{10,11... | collective-permute-start | bytes 1769480 | tf_op jit(solution)/shard_map/ppermute | solution.py:409
  39.6 11.5 %copy-start.16 = (f32[192]{0:T(256)S(1)}, f32[192]{0:T(256)}, u32[]{:S(2)}) copy-start(f32[192]{0:T(256)} %param.18) | copy-start | bytes 2308
  39.6 13.1 %copy-start.18 = (f32[768]{0:T(1024)S(1)}, f32[768]{0:T(1024)}, u32[]{:S(2)}) copy-start(f32[768]{0:T(1024)} %param.14) | copy-start | bytes 9220
  39.6 9.0 %collective-permute-start.4 = (bf16[192,768]{1,0:T(8,128)(2,1)S(1)}, bf16[192,768]{1,0:T(8,128)(2,1)S(1)}, u32[]{:S(2)}, u32[]{:S(2)}) collective-permute-start(bf16[192,768]{1,0:T(8,128)(2,1)S(1)} %get-tuple-element.29.refs_0_), channel_id=1, source_target_pairs={{0,2},{1,3},{2,0},{3,1},{4,6},{5,7},{6,4},{7,5},{8,10},{9,11},{10,... | collective-permute-start | bytes 884744 | tf_op jit(solution)/shard_map/ppermute | solution.py:409
  40.2 12.5 %collective-permute-start.3 = (bf16[192,768]{1,0:T(8,128)(2,1)S(1)}, bf16[192,768]{1,0:T(8,128)(2,1)S(1)}, u32[]{:S(2)}, u32[]{:S(2)}) collective-permute-start(bf16[192,768]{1,0:T(8,128)(2,1)S(1)} %get-tuple-element.29.refs_0_), channel_id=1, source_target_pairs={{0,1},{1,0},{2,3},{3,2},{4,5},{5,4},{6,7},{7,6},{8,9},{9,8},{10,11... | collective-permute-start | bytes 884744 | tf_op jit(solution)/shard_map/ppermute | solution.py:409
  48.6 4.1 %collective-permute-start.5 = (bf16[192,768]{1,0:T(8,128)(2,1)S(1)}, bf16[192,768]{1,0:T(8,128)(2,1)S(1)}, u32[]{:S(2)}, u32[]{:S(2)}) collective-permute-start(bf16[192,768]{1,0:T(8,128)(2,1)S(1)} %collective-permute-done.4.refs_2_), channel_id=1, source_target_pairs={{0,1},{1,0},{2,3},{3,2},{4,5},{5,4},{6,7},{7,6},{8,9},{9,8},{10,11... | collective-permute-start | bytes 884744 | tf_op jit(solution)/shard_map/ppermute | solution.py:409
  52.0 26.3 %copy-start.15 = (f32[4,8,192]{2,1,0:T(8,128)S(1)}, f32[4,8,192]{2,1,0:T(8,128)}, u32[]{:S(2)}) copy-start(f32[4,8,192]{2,1,0:T(8,128)} %copy-done.14) | copy-start | bytes 73732
  52.0 11.9 %collective-permute-start.17 = (bf16[192,768]{1,0:T(8,128)(2,1)S(1)}, bf16[192,768]{1,0:T(8,128)(2,1)S(1)}, u32[]{:S(2)}, u32[]{:S(2)}) collective-permute-start(bf16[192,768]{1,0:T(8,128)(2,1)S(1)} %get-tuple-element.46.refs_4_), channel_id=1, source_target_pairs={{0,2},{1,3},{2,0},{3,1},{4,6},{5,7},{6,4},{7,5},{8,10},{9,11},{10,... | collective-permute-start | bytes 884744 | tf_op jit(solution)/shard_map/ppermute | solution.py:409
  57.2 28.7 %collective-permute-start.6 = (bf16[384,384]{1,0:T(8,128)(2,1)}, bf16[384,384]{1,0:T(8,128)(2,1)}, u32[]{:S(2)}, u32[]{:S(2)}) collective-permute-start(bf16[384,384]{1,0:T(8,128)(2,1)} %get-tuple-element.39), channel_id=1, source_target_pairs={{0,4},{4,0},{8,12},{12,8},{16,20},{20,16},{24,28},{28,24},{1,5},{5... | collective-permute-start | bytes 884744 | tf_op jit(solution)/shard_map/ppermute | solution.py:409
  58.4 7.7 %collective-permute-start.12 = (bf16[96,384]{1,0:T(8,128)(2,1)S(1)}, bf16[96,384]{1,0:T(8,128)(2,1)S(1)}, u32[]{:S(2)}, u32[]{:S(2)}) collective-permute-start(bf16[96,384]{1,0:T(8,128)(2,1)S(1)} %get-tuple-element.41), channel_id=1, source_target_pairs={{0,28},{4,24},{8,20},{12,16},{16,12},{20,8},{24,4},{28,0},{1,29},{... | collective-permute-start | bytes 221192 | tf_op jit(solution)/shard_map/ppermute | solution.py:409
  62.1 6.5 %collective-permute-start.11 = (bf16[96,384]{1,0:T(8,128)(2,1)S(1)}, bf16[96,384]{1,0:T(8,128)(2,1)S(1)}, u32[]{:S(2)}, u32[]{:S(2)}) collective-permute-start(bf16[96,384]{1,0:T(8,128)(2,1)S(1)} %get-tuple-element.41), channel_id=1, source_target_pairs={{0,24},{4,28},{8,16},{12,20},{16,8},{20,12},{24,0},{28,4},{1,25},{... | collective-permute-start | bytes 221192 | tf_op jit(solution)/shard_map/ppermute | solution.py:409
  62.5 12.3 %collective-permute-start.10 = (bf16[96,384]{1,0:T(8,128)(2,1)S(1)}, bf16[96,384]{1,0:T(8,128)(2,1)S(1)}, u32[]{:S(2)}, u32[]{:S(2)}) collective-permute-start(bf16[96,384]{1,0:T(8,128)(2,1)S(1)} %get-tuple-element.41), channel_id=1, source_target_pairs={{0,20},{4,16},{8,28},{12,24},{16,4},{20,0},{24,12},{28,8},{1,21},{... | collective-permute-start | bytes 221192 | tf_op jit(solution)/shard_map/ppermute | solution.py:409
  63.9 11.5 %collective-permute-start.9 = (bf16[96,384]{1,0:T(8,128)(2,1)S(1)}, bf16[96,384]{1,0:T(8,128)(2,1)S(1)}, u32[]{:S(2)}, u32[]{:S(2)}) collective-permute-start(bf16[96,384]{1,0:T(8,128)(2,1)S(1)} %get-tuple-element.41), channel_id=1, source_target_pairs={{0,16},{4,20},{8,24},{12,28},{16,0},{20,4},{24,8},{28,12},{1,17},{... | collective-permute-start | bytes 221192 | tf_op jit(solution)/shard_map/ppermute | solution.py:409
  66.7 29.4 %collective-permute-start.16 = (bf16[192,768]{1,0:T(8,128)(2,1)S(1)}, bf16[192,768]{1,0:T(8,128)(2,1)S(1)}, u32[]{:S(2)}, u32[]{:S(2)}) collective-permute-start(bf16[192,768]{1,0:T(8,128)(2,1)S(1)} %get-tuple-element.46.refs_4_), channel_id=1, source_target_pairs={{0,1},{1,0},{2,3},{3,2},{4,5},{5,4},{6,7},{7,6},{8,9},{9,8},{10,11... | collective-permute-start | bytes 884744 | tf_op jit(solution)/shard_map/ppermute | solution.py:409
  69.2 26.9 %collective-permute-start.18 = (bf16[192,768]{1,0:T(8,128)(2,1)S(1)}, bf16[192,768]{1,0:T(8,128)(2,1)S(1)}, u32[]{:S(2)}, u32[]{:S(2)}) collective-permute-start(bf16[192,768]{1,0:T(8,128)(2,1)S(1)} %collective-permute-done.17.refs_6_), channel_id=1, source_target_pairs={{0,1},{1,0},{2,3},{3,2},{4,5},{5,4},{6,7},{7,6},{8,9},{9,8},{10,11... | collective-permute-start | bytes 884744 | tf_op jit(solution)/shard_map/ppermute | solution.py:409
  75.5 10.5 %collective-permute-start.8 = (bf16[192,384]{1,0:T(8,128)(2,1)}, bf16[192,384]{1,0:T(8,128)(2,1)}, u32[]{:S(2)}, u32[]{:S(2)}) collective-permute-start(bf16[192,384]{1,0:T(8,128)(2,1)} %get-tuple-element.40), channel_id=1, source_target_pairs={{0,12},{4,8},{8,4},{12,0},{16,28},{20,24},{24,20},{28,16},{1,13},{... | collective-permute-start | bytes 442376 | tf_op jit(solution)/shard_map/ppermute | solution.py:409
  76.1 9.8 %collective-permute-start.7 = (bf16[192,384]{1,0:T(8,128)(2,1)}, bf16[192,384]{1,0:T(8,128)(2,1)}, u32[]{:S(2)}, u32[]{:S(2)}) collective-permute-start(bf16[192,384]{1,0:T(8,128)(2,1)} %get-tuple-element.40), channel_id=1, source_target_pairs={{0,8},{4,12},{8,0},{12,4},{16,24},{20,28},{24,16},{28,20},{1,9},{5... | collective-permute-start | bytes 442376 | tf_op jit(solution)/shard_map/ppermute | solution.py:409
  94.1 2.0 %collective-permute-start.13 = (bf16[192,256]{1,0:T(8,128)(2,1)S(1)}, bf16[192,256]{1,0:T(8,128)(2,1)S(1)}, u32[]{:S(2)}, u32[]{:S(2)}) collective-permute-start(bf16[192,256]{1,0:T(8,128)(2,1)S(1)} %get-tuple-element.43), channel_id=1, source_target_pairs={{0,1},{1,0},{2,3},{3,2},{4,5},{5,4},{6,7},{7,6},{8,9},{9,8},{10,11... | collective-permute-start | bytes 294920 | tf_op jit(solution)/shard_map/ppermute | solution.py:409
  94.2 5.7 %collective-permute-start.14 = (bf16[192,256]{1,0:T(8,128)(2,1)S(1)}, bf16[192,256]{1,0:T(8,128)(2,1)S(1)}, u32[]{:S(2)}, u32[]{:S(2)}) collective-permute-start(bf16[192,256]{1,0:T(8,128)(2,1)S(1)} %get-tuple-element.44), channel_id=1, source_target_pairs={{0,2},{1,3},{2,0},{3,1},{4,6},{5,7},{6,4},{7,5},{8,10},{9,11},{10,... | collective-permute-start | bytes 294920 | tf_op jit(solution)/shard_map/ppermute | solution.py:409
  95.6 5.5 %collective-permute-start.15 = (bf16[192,256]{1,0:T(8,128)(2,1)S(1)}, bf16[192,256]{1,0:T(8,128)(2,1)S(1)}, u32[]{:S(2)}, u32[]{:S(2)}) collective-permute-start(bf16[192,256]{1,0:T(8,128)(2,1)S(1)} %get-tuple-element.45), channel_id=1, source_target_pairs={{0,3},{1,2},{2,1},{3,0},{4,7},{5,6},{6,5},{7,4},{8,11},{9,10},{10,... | collective-permute-start | bytes 294920 | tf_op jit(solution)/shard_map/ppermute | solution.py:409
  (15 other events, 47.2 us)
where the time goes:
time: 103 us
  waiting for transfers between devices  43.6 us (42%)
  starting transfers between devices  23.5 us (23%)
  Pallas kernels  22.7 us (22%)
  local copies, waits for them, and re-layouts  12.7 us (12%)
    ppermute x19, waiting for transfers between devices, swap(): lax.ppermute(block, axis, [(index, index ^ mask) for index in range(count)])  43.6 us
    pallas_call x7, Pallas kernels, call(): pl.pallas_call(kernel, name=name, out_shape=[jax.ShapeDtypeStruct(shape,...  22.7 us
    ppermute x19, starting transfers between devices, swap(): lax.ppermute(block, axis, [(index, index ^ mask) for index in range(count)])  16.2 us
    unnamed x41, local copies, waits for them, and re-layouts  9.26 us
    all_to_all x1, starting transfers between devices, body(): lax.all_to_all(blocks, ('seq', 'tp'), split_axis=0, concat_axis=0, tiled=...  7.3 us
  transfers between devices with their start and end apart: 20, of which 7 were waited for; matrix products, arithmetic and copies ran while one was open for 4% of the time, Pallas kernels for 18%

commit v1 on v0

v1 whole, which is shorter than its diff:
```python
import functools

import jax
import jax.numpy as jnp
from jax import lax
from jax.experimental import pallas as pl
from jax.experimental.pallas import tpu as pltpu
from jax.sharding import PartitionSpec as P

BRANCHES = 5
HEAD_DIM = 48
SLOT = 64
LANES = 128
IDS = 16
CLASSES = 2 ** (BRANCHES - 1)
NEG = -1e30
EPS = 1e-05
BF16 = jnp.bfloat16
F32 = jnp.float32
VMEM_BYTES = 16 * 1024 * 1024
LARGE_VMEM_BYTES = 48 * 1024 * 1024
ALL_VMEM_BYTES = 56 * 1024 * 1024


def up_to(count, step):
    return (count + step - 1) // step * step


def iota(shape, dim):
    return lax.broadcasted_iota(jnp.int32, shape, dim)


def dot(left, right):
    return jnp.dot(left, right, preferred_element_type=F32)


def dot_nt(left, right):
    return lax.dot_general(left, right, (((1,), (1,)), ((), ())), preferred_element_type=F32)


def dot_tn(left, right):
    return lax.dot_general(left, right, (((0,), (0,)), ((), ())), preferred_element_type=F32)


def one_hot(mask):
    return jnp.where(mask, 1.0, 0.0).astype(BF16)


def stored_at(position, rows):
    residue = position & (CLASSES - 1)
    flipped = jnp.zeros_like(residue)
    for bit in range(BRANCHES - 1):
        flipped = flipped + (((residue >> bit) & 1) << (BRANCHES - 2 - bit))
    return flipped * (rows // CLASSES) + (position >> (BRANCHES - 1))


def head_start(level, head, column, rows):
    start = 0
    for bit in range(level):
        value = (head >> bit) & 1 if bit < 2 else (column >> (bit - 2)) & 1
        start = start + value * (rows >> (bit + 1))
    return start


def call(kernel, name, outs, args, scratch=(), cost=1, vmem_bytes=VMEM_BYTES, apart=(), out_apart=()):
    vmem = pl.BlockSpec(memory_space=pltpu.VMEM)
    anywhere = pl.BlockSpec(memory_space=pltpu.HBM)
    return pl.pallas_call(
        kernel,
        name=name,
        out_shape=[jax.ShapeDtypeStruct(shape, dtype) for shape, dtype in outs],
        in_specs=[anywhere if index in apart else vmem for index in range(len(args))],
        out_specs=[anywhere if index in out_apart else vmem for index in range(len(outs))],
        scratch_shapes=list(scratch),
        compiler_params=pltpu.CompilerParams(vmem_limit_bytes=vmem_bytes),
        cost_estimate=pl.CostEstimate(flops=int(cost * 1e9), bytes_accessed=0, transcendentals=0),
    )(*args)


def one_row(ref):
    return jnp.concatenate([ref[index : index + 1, :] for index in range(ref.shape[0])], axis=1)


def route_kernel(
    n_seq,
    n_tp,
    peer,
    target_hbm,
    slide_hbm,
    tiles_hbm,
    proj_hbm,
    out_weight_hbm,
    out_hbm,
    bundle_hbm,
    rest_hbm,
    target_ref,
    slide_ref,
    tiles_ref,
    out_ref,
    bundle_ref,
    rest_ref,
    sems,
    out_sems,
):
    depth = proj_hbm.shape[0]
    along = bundle_hbm.shape[0] - depth
    fetches = [
        pltpu.make_async_copy(target_hbm, target_ref, sems.at[0]),
        pltpu.make_async_copy(slide_hbm, slide_ref, sems.at[1]),
        pltpu.make_async_copy(tiles_hbm, tiles_ref, sems.at[2]),
        pltpu.make_async_copy(proj_hbm, bundle_ref.at[pl.ds(0, depth)], sems.at[3]),
        pltpu.make_async_copy(out_weight_hbm.at[pl.ds(0, along)], bundle_ref.at[pl.ds(depth, along)], sems.at[4]),
        pltpu.make_async_copy(out_weight_hbm.at[pl.ds(along, rest_hbm.shape[0])], rest_ref, sems.at[5]),
    ]
    for fetch in fetches:
        fetch.start()
    fetches[0].wait()
    rows = tiles_ref.shape[0]
    chunks = tiles_ref.shape[1] // LANES
    sub = peer // n_tp
    sub_pad = up_to(sub, 8)
    blocks = n_seq * n_tp
    place, column = lax.axis_index("seq"), lax.axis_index("tp")
    target = one_row(target_ref)
    owner = jnp.floor((target.astype(F32) + 0.5) * (1.0 / rows)).astype(jnp.int32)
    flags = jnp.where(iota((n_seq, rows), 0) == owner, 1.0, 0.0)
    before = one_hot(iota((rows, rows), 0) <= iota((rows, rows), 1))
    counts = dot(flags.astype(BF16), before)
    slot = jnp.sum(flags * counts, axis=0, keepdims=True).astype(jnp.int32) - 1
    lane_of = jnp.zeros_like(slot)
    for turn in range(1, n_tp):
        lane_of = lane_of + jnp.where(slot >= turn * sub, 1, 0)
    low = slot - lane_of * sub
    target_row = (owner * n_tp + lane_of) * sub_pad + low
    chooser = one_hot(iota((blocks * sub_pad, rows), 0) == target_row)

    spot = stored_at(target - owner * rows, rows)
    high = spot >> 7
    code = ((spot & 127) + 128).astype(F32)
    for bit in range(3):
        code = code * jnp.where((high >> bit) & 1 == 1, 256.0 ** (2**bit), 1.0)
    arrival = place * sub_pad + low
    extra = n_seq * 8
    code_rows = up_to(n_seq * sub_pad, LANES) // LANES
    line = iota((extra, rows), 0)
    mine = (owner == (line >> 3)) & (lane_of == column) & ((arrival >> 7) == (line & 7))
    coded = dot_nt(
        jnp.where(mine, code, 0.0).astype(BF16),
        one_hot(iota((LANES, rows), 0) == (arrival & 127)),
    )
    share = rows // n_tp
    fetches[1].wait()
    kept = stored_at(iota((1, rows), 1), rows) - column * share
    held = (kept >= 0) & (kept < share) & ((kept >> 7) + code_rows == (line & 7))
    ids = dot_nt(
        jnp.where(held, one_row(slide_ref).astype(F32), 0.0).astype(BF16),
        one_hot(iota((LANES, rows), 0) == (kept & 127)),
    )
    notes = coded + ids
    for fetch in fetches[3:]:
        fetch.wait()
    stores = [
        pltpu.make_async_copy(bundle_ref, bundle_hbm, sems.at[6]),
        pltpu.make_async_copy(rest_ref, rest_hbm, sems.at[7]),
    ]
    for store in stores:
        store.start()
    fetches[2].wait()
    picked = dot(chooser, tiles_ref[...])
    pad = out_hbm.shape[1] - chunks * sub_pad - 8
    for block in range(blocks):
        base = block * sub_pad
        pieces = [
            picked[base : base + sub_pad, part * LANES : (part + 1) * LANES] for part in range(chunks)
        ]
        start = block // n_tp * 8
        pieces.append(notes[start : start + 8])
        if pad:
            pieces.append(jnp.zeros((pad, LANES), F32))
        out_ref[block] = jnp.concatenate(pieces, axis=0).astype(BF16)
        if block % n_tp == n_tp - 1:
            some = pl.ds(block - n_tp + 1, n_tp)
            stores.append(pltpu.make_async_copy(out_ref.at[some], out_hbm.at[some], out_sems.at[block // n_tp]))
            stores[-1].start()
    for store in stores:
        store.wait()


def spread_mask(width, wide, shift):
    row = iota((width, wide), 0) - shift
    lane = iota((width, wide), 1)
    inner = lane & (SLOT - 1)
    return (inner < HEAD_DIM) & (row == (lane >> 6) * HEAD_DIM + inner)


def project_kernel(n_seq, n_tp, peer, recv_hbm, *refs):
    weight_refs = refs[: n_tp - 1]
    total_ref, last_ref, codes_ref, ids_ref, recv_ref, work, sems = refs[n_tp - 1 :]
    fetches = []
    for source in range(n_seq):
        some = pl.ds(source * n_tp, n_tp)
        fetches.append(pltpu.make_async_copy(recv_hbm.at[some], recv_ref.at[some], sems.at[source]))
        fetches[-1].start()
    sub_pad = up_to(peer // n_tp, 8)
    chunks = work.shape[2] // LANES
    column = lax.axis_index("tp")
    code_rows = codes_ref.shape[2] // LANES
    share = ids_ref.shape[1] // n_tp
    at = chunks * sub_pad
    even = at // 16 * 16
    notes = [jnp.zeros((8, LANES), F32)] * n_tp
    for source in range(n_seq):
        fetches[source].wait()
        for turn in range(n_tp):
            block = recv_ref[source * n_tp + (column ^ turn)].astype(F32)
            for part in range(chunks):
                work[turn, source * sub_pad : (source + 1) * sub_pad, part * LANES : (part + 1) * LANES] = block[
                    part * sub_pad : (part + 1) * sub_pad
                ]
            notes[turn] = notes[turn] + block[at : at + 8]
        pieces = []
        for other in range(n_tp):
            note = recv_ref[source * n_tp + other, even : even + 16, :].astype(F32)[at - even :]
            for piece in range(up_to(share, LANES) // LANES):
                length = min(LANES, share - piece * LANES)
                pieces.append(note[code_rows + piece : code_rows + piece + 1, :length])
        ids_ref[source : source + 1, :] = jnp.concatenate(pieces, axis=1)
    total = None
    for turn in range(n_tp - 1):
        part_sum = dot(work[turn].astype(BF16), weight_refs[turn][: work.shape[2]])
        total = part_sum if total is None else total + part_sum
    total_ref[...] = total
    last_ref[...] = work[n_tp - 1].astype(BF16)
    for turn in range(n_tp):
        codes = notes[turn]
        power = jnp.zeros((8, LANES), F32)
        scale = jnp.ones((8, LANES), F32)
        for step in range(1, 8):
            above = codes >= 128.0 * 256.0**step
            power = power + jnp.where(above, 128.0, 0.0)
            scale = scale * jnp.where(above, 1.0 / 256.0, 1.0)
        spots = jnp.where(codes > 0.0, codes * scale - 128.0 + power, -1.0)
        for piece in range(code_rows):
            codes_ref[turn, :, piece * LANES : (piece + 1) * LANES] = spots[piece : piece + 1].astype(jnp.int32)


def stream_kernel(total_ref, last_ref, weight_ref, stream_ref):
    part_sum = dot(last_ref[...], weight_ref[: last_ref.shape[1]])
    stream_ref[...] = (total_ref[...] + part_sum).astype(BF16)


def key_value_query(stream, gain, weights):
    rows = stream.astype(F32)
    mean = jnp.mean(rows, axis=-1, keepdims=True)
    second = jnp.mean(rows * rows, axis=-1, keepdims=True)
    normed = ((rows - mean) * lax.rsqrt(second - mean * mean + EPS) * gain).astype(BF16)
    result = dot_nt(normed, weights)
    third = weights.shape[0] // 3
    scale = jnp.where(iota((1, 3 * third), 1) >= 2 * third, HEAD_DIM ** (-0.5), 1.0)
    return (result * scale).astype(BF16)


def place_heads(turn, codes_ref, gain_ref, key_ref, value_ref, query_ref, stream_ref, rows):
    weights = jnp.concatenate([key_ref[...], value_ref[...], query_ref[...]], axis=0)
    result = key_value_query(stream_ref[...], one_row(gain_ref), weights)
    spots = codes_ref[turn]
    place = one_hot(iota((rows, spots.shape[1]), 0) == spots)[:, : result.shape[0]]
    return dot(place, result)


def first_heads_kernel(
    groups,
    codes_ref,
    gain_ref,
    key_ref,
    value_ref,
    query_ref,
    stream_ref,
    ids_ref,
    sub_gain_ref,
    out_ref,
    same_ref,
    apart_ref,
    back_ref,
    gains_ref,
    *refs,
):
    rows, wide = same_ref.shape
    heads = wide // SLOT
    width = heads * HEAD_DIM
    place, column = lax.axis_index("seq"), lax.axis_index("tp")
    first = place_heads(0, codes_ref, gain_ref, key_ref, value_ref, query_ref, stream_ref, rows)
    out_ref[...] = first.astype(BF16)

    ids = ids_ref[pl.ds(place, 1), :].astype(jnp.int32)
    same_ref[...] = id_lanes(ids, wide, None).astype(BF16)
    apart_ref[...] = id_lanes(ids, wide, NEG).astype(BF16)
    share = back_ref.shape[1]
    for turn in range(back_ref.shape[0]):
        wanted = stored_at((column ^ turn) * share + iota((share, 1), 0), rows)
        back_ref[turn] = one_hot(wanted == iota((share, rows), 1))
    gain = sub_gain_ref[...]
    high = gain.astype(BF16).astype(F32)
    mid = (gain - high).astype(BF16).astype(F32)
    low = (gain - high) - mid
    line = iota((16, width), 0)
    parts = jnp.where(line == 0, high, jnp.where(line == 1, mid, jnp.where(line == 2, low, 0.0)))
    gains_ref[...] = dot(parts.astype(BF16), one_hot(spread_mask(width, wide, 0))).astype(BF16)
    apart_refs, apart_all = refs[:-1], refs[-1]
    for ref, (level, masks) in zip(apart_refs, groups):
        count = rows >> level
        slots = iota((count, wide), 1) >> 6
        for index, mask in enumerate(masks):
            far = ids_ref[pl.ds(place ^ mask, 1), :].astype(jnp.int32)
            apart_all[...] = id_lanes(far, wide, NEG).astype(BF16)
            chosen = None
            for head in range(heads):
                part = apart_all[pl.ds(head_start(level, head, column, rows), count), :]
                chosen = part if chosen is None else jnp.where(slots >= head, part, chosen)
            ref[index * count : (index + 1) * count, :] = chosen


def more_heads_kernel(
    turn, codes_ref, gain_ref, key_ref, value_ref, query_ref, stream_ref, before_ref, out_ref
):
    more = place_heads(turn, codes_ref, gain_ref, key_ref, value_ref, query_ref, stream_ref, out_ref.shape[0])
    out_ref[...] = (before_ref[...].astype(F32) + more).astype(BF16)


def last_heads_kernel(
    turn, levels, codes_ref, gain_ref, key_ref, value_ref, query_ref, stream_ref, before_ref, packed, *sets
):
    rows = packed.shape[0]
    width = key_ref.shape[0]
    heads = width // HEAD_DIM
    column = lax.axis_index("tp")
    more_heads_kernel(
        turn, codes_ref, gain_ref, key_ref, value_ref, query_ref, stream_ref, before_ref, packed
    )
    for ref, level in zip(sets, levels):
        count = rows >> level
        lane = iota((count, 2 * width), 1)
        lane = jnp.where(lane >= width, lane - width, lane)
        chosen = None
        for head in range(heads):
            part = packed[pl.ds(head_start(level, head, column, rows), count), : 2 * width]
            chosen = part if chosen is None else jnp.where(lane >= head * HEAD_DIM, part, chosen)
        ref[...] = chosen


def id_lanes(ids, wide, apart):
    count = ids.shape[1]
    lane = iota((IDS, wide), 1) & (SLOT - 1)
    group = iota((IDS, wide), 0)
    same = lane - HEAD_DIM == group
    if apart is None:
        table = jnp.where(same, 1.0, 0.0)
    else:
        table = jnp.where((lane >= HEAD_DIM) & ~same, apart, 0.0)
    return dot_tn(one_hot(iota((IDS, count), 0) == ids), table.astype(BF16))


def agreement(level, firsts, column, rows, total, count):
    q_on, k_on = [], []
    for index, (head, first) in enumerate(firsts):
        for size, lines in ((count, q_on), (total, k_on)):
            line, at = iota((8, size), 0), iota((8, size), 1)
            if size > count:
                for step in range(1, size // count):
                    at = at - jnp.where(iota((8, size), 1) >= step * count, count, 0)
            start = jnp.zeros((8, size), jnp.int32)
            length = jnp.zeros((8, size), jnp.int32)
            for branch in range(level, BRANCHES):
                start = jnp.where(line == branch, head_start(branch, head, column, rows) - first, start)
                length = jnp.where(line == branch, rows >> branch, length)
            lines.append(jnp.where((at >= start) & (at < start + length), 1.0, 0.0))
        blank = jnp.zeros((8, count), F32)
        q_on[index] = jnp.concatenate(
            [q_on[index] if place == index else blank for place in range(len(firsts))], axis=1
        )
    return jnp.concatenate(q_on, axis=0).astype(BF16), jnp.concatenate(k_on, axis=0).astype(BF16)


def repeat(block, times):
    return jnp.concatenate([block] * times, axis=1)


def own_kernel(packed_ref, same_ref, apart_ref, acc_ref, tops_ref, masked_ref, keys_ref, values_ref):
    rows, wide = masked_ref.shape
    heads = wide // SLOT
    width = heads * HEAD_DIM
    column = lax.axis_index("tp")
    spread = one_hot(spread_mask(width, wide, 0))
    pairs = packed_ref[:, : 2 * width]
    query = dot(packed_ref[:, 2 * width :], spread)
    masked_ref[...] = (query + same_ref[...].astype(F32)).astype(BF16)
    key = dot(pairs, one_hot(spread_mask(2 * width, wide, 0)))
    keys_ref[...] = (key + apart_ref[...].astype(F32)).astype(BF16)
    ones = jnp.where((iota((rows, wide), 1) & (SLOT - 1)) >= HEAD_DIM, 1.0, 0.0)
    value = dot(pairs, one_hot(spread_mask(2 * width, wide, width)))
    values_ref[...] = (value + ones).astype(BF16)
    half = rows // 2
    slot_of = iota((half, wide), 1) >> 6
    for part in range(2):
        start = part * half
        query = masked_ref[start : start + half, :]
        acc = None
        for head in range(heads):
            one = jnp.where(slot_of == head, query, jnp.zeros((), BF16))
            scores = dot_nt(one, keys_ref[...])
            top = jnp.max(scores, axis=1, keepdims=True)
            tops_ref[head, start : start + half, :] = jnp.broadcast_to(top, (half, LANES))
            weights = jnp.exp(scores - top)
            if part == (head & 1):
                times = dot_tn(*agreement(0, [(head, start)], column, rows, half, half))
                scaled = weights[:, start : start + half] * times
                others = weights[:, half - start : rows - start]
                weights = jnp.concatenate([scaled, others] if part == 0 else [others, scaled], axis=1)
            got = dot(weights.astype(BF16), values_ref[...])
            acc = got if acc is None else jnp.where(slot_of == head, got, acc)
        acc_ref[start : start + half, :] = acc


def merge_sets(level, masks, sets, acc_ref, tops_ref, query_ref, apart_ref, finish):
    rows, wide = query_ref.shape
    heads = wide // SLOT
    width = heads * HEAD_DIM
    column = lax.axis_index("tp")
    count = rows >> level
    some = min(max(1, rows // count), len(masks))
    total = some * count
    spread_key = one_hot(spread_mask(2 * width, wide, 0))
    spread_value = one_hot(spread_mask(2 * width, wide, width))
    slot_of = iota((count, wide), 1) >> 6
    together = heads if heads * count * total <= 2**20 else 1
    for low in range(0, heads, together):
        firsts = [(head, head_start(level, head, column, rows)) for head in range(low, low + together)]
        q_on, k_on = agreement(level, firsts, column, rows, total, count)
        times = dot_tn(q_on, k_on)
        query = jnp.concatenate(
            [
                jnp.where(slot_of == head, query_ref[pl.ds(first, count), :], jnp.zeros((), BF16))
                for head, first in firsts
            ],
            axis=0,
        )
        sums = jnp.concatenate([acc_ref[pl.ds(first, count), :] for _, first in firsts], axis=0)
        tops = jnp.concatenate([tops_ref[head, pl.ds(first, count), :] for head, first in firsts], axis=0)
        for begin in range(0, len(masks), some):
            pairs = jnp.concatenate([ref[...] for ref in sets[begin : begin + some]], axis=0)
            keys = dot(pairs, spread_key) + apart_ref[begin * count : begin * count + total, :].astype(F32)
            ones = jnp.where((iota((total, wide), 1) & (SLOT - 1)) >= HEAD_DIM, 1.0, 0.0)
            values = (dot(pairs, spread_value) + ones).astype(BF16)
            scores = dot_nt(query, keys.astype(BF16))
            top = jnp.maximum(tops, jnp.max(scores, axis=1, keepdims=True))
            weights = jnp.exp(scores - repeat(top, total // LANES)) * times
            got = dot(weights.astype(BF16), values)
            sums = sums * repeat(jnp.exp(tops - top), wide // LANES) + got
            tops = top
        finish(firsts, sums, tops)


def slot_lane(values, inner):
    wide = values.shape[1]
    row, lane = iota((wide, wide), 0), iota((wide, wide), 1)
    pick = one_hot(row == (lane >> 6) * SLOT + inner)
    high = values.astype(BF16)
    low = (values - high.astype(F32)).astype(BF16)
    return dot(high, pick) + dot(low, pick)


def near_kernel(groups, acc_ref, tops_ref, query_ref, *refs):
    apart_refs, refs = refs[: len(groups)], refs[len(groups) :]
    sums_ref, new_tops_ref = refs[-2:]
    wide = query_ref.shape[1]
    sums_ref[...] = acc_ref[...]
    new_tops_ref[...] = tops_ref[...]

    def finish(firsts, sums, tops):
        count = sums.shape[0] // len(firsts)
        slot_of = iota((count, wide), 1) >> 6
        for index, (head, first) in enumerate(firsts):
            here, part = pl.ds(first, count), slice(index * count, (index + 1) * count)
            sums_ref[here, :] = jnp.where(slot_of == head, sums[part], sums_ref[here, :])
            new_tops_ref[head, here, :] = tops[part]

    for apart_ref, (level, masks) in zip(apart_refs, groups):
        merge_sets(level, masks, refs[: len(masks)], sums_ref, new_tops_ref, query_ref, apart_ref, finish)
        refs = refs[len(masks) :]


def mid_kernel(groups, acc_ref, tops_ref, query_ref, *refs):
    sums_ref, _, early_ref, centre_ref = refs[-4:]
    near_kernel(groups, acc_ref, tops_ref, query_ref, *refs[:-2])
    rows, wide = query_ref.shape
    heads = wide // SLOT
    every = sums_ref[...]
    inner = iota((rows, wide), 1) & (SLOT - 1)
    attn = jnp.where(inner < HEAD_DIM, every / slot_lane(every, HEAD_DIM), 0.0)
    average = jnp.full((wide, wide), 1.0, BF16)
    centre = (dot(attn.astype(BF16), average) * (1.0 / (heads * HEAD_DIM))).astype(BF16).astype(F32)
    centre_ref[...] = centre
    early_ref[...] = jnp.where(inner < HEAD_DIM, attn - centre, centre).astype(BF16)


def far_kernel(n_tp, level, masks, acc_ref, tops_ref, query_ref, early_ref, centre_ref, back_ref, gains_ref, *refs):
    apart_ref, refs = refs[0], refs[1:]
    sets, refs = refs[: len(masks)], refs[len(masks) :]
    out_refs, message = refs[:n_tp], refs[-1]
    message[...] = early_ref[...]

    def finish(firsts, sums, tops):
        count = sums.shape[0] // len(firsts)
        lane = iota((count, sums.shape[1]), 1)
        now = sums / slot_lane(sums, HEAD_DIM)
        for index, (head, first) in enumerate(firsts):
            here, part = pl.ds(first, count), slice(index * count, (index + 1) * count)
            mine = (lane >= head * SLOT) & (lane < head * SLOT + HEAD_DIM)
            new = (now[part] - centre_ref[here, :]).astype(BF16)
            message[here, :] = jnp.where(mine, new, message[here, :])

    merge_sets(level, masks, sets, acc_ref, tops_ref, query_ref, apart_ref, finish)
    share = back_ref.shape[1]
    final = message[...]
    for turn in range(n_tp):
        out_refs[turn][:share] = dot(back_ref[turn], final).astype(BF16)
        out_refs[turn][share:] = gains_ref[...]


def base_kernel(n_tp, codes_ref, *refs):
    shards, bundle_refs, rest_refs = refs[:n_tp], refs[n_tp : 2 * n_tp], refs[2 * n_tp : 3 * n_tp]
    base_ref, weights_ref = refs[-2:]
    share = base_ref.shape[0]
    rows = share * n_tp
    wanted = stored_at(lax.axis_index("tp") * share + iota((share, 1), 0), rows)
    base = None
    for turn in range(n_tp):
        spots = codes_ref[turn]
        moved = dot(one_hot(wanted == spots)[:, : shards[turn].shape[0]], shards[turn][...])
        base = moved if base is None else base + moved
    base_ref[...] = base.astype(BF16)
    wide = weights_ref.shape[1]
    heads = wide // SLOT
    gap = jnp.zeros((SLOT - HEAD_DIM, base_ref.shape[1]), BF16)
    for turn, (ref, rest_ref) in enumerate(zip(bundle_refs, rest_refs)):
        along = heads * HEAD_DIM - rest_ref.shape[0]
        depth = ref.shape[0] - along
        for head in range(heads):
            at, to = head * HEAD_DIM, head * SLOT
            early = min(max(along - at, 0), HEAD_DIM)
            if early:
                weights_ref[turn, to : to + early, :] = ref[depth + at : depth + at + early, :]
            if early < HEAD_DIM:
                weights_ref[turn, to + early : to + HEAD_DIM, :] = rest_ref[
                    at + early - along : at + HEAD_DIM - along, :
                ]
            weights_ref[turn, to + HEAD_DIM : to + SLOT, :] = gap


def mix_kernel(n_tp, base_ref, weights_ref, *refs):
    message_refs, out_ref = refs[:n_tp], refs[-1]
    share, wide = base_ref.shape[0], weights_ref.shape[1]
    features = n_tp * (wide // SLOT) * HEAD_DIM
    inside = (iota((share, wide), 1) & (SLOT - 1)) < HEAD_DIM
    parts, centres, gains = [], [], []
    for ref in message_refs:
        message = ref[:share].astype(F32)
        extra = ref[share:].astype(F32)
        parts.append(jnp.where(inside, message, 0.0))
        centres.append(message[:, HEAD_DIM : HEAD_DIM + 1])
        gains.append(extra[0:1] + extra[1:2] + extra[2:3])
    each = features // n_tp
    sums = [jnp.sum(part, axis=1, keepdims=True) + centre * each for part, centre in zip(parts, centres)]
    mean = sum(sums) * (1.0 / features)
    parts = [jnp.where(inside, part + (centre - mean), 0.0) for part, centre in zip(parts, centres)]
    spread = jnp.sum(sum(part * part for part in parts), axis=1, keepdims=True) * (1.0 / features)
    factor = lax.rsqrt(spread + EPS)
    total = base_ref[...].astype(F32)
    for turn, (part, gain) in enumerate(zip(parts, gains)):
        total = total + dot((part * factor * gain).astype(BF16), weights_ref[turn])
    out_ref[...] = total.astype(BF16)


def swap(block, axis, mask):
    count = lax.axis_size(axis)
    return lax.ppermute(block, axis, [(index, index ^ mask) for index in range(count)])


def gather_tp(block):
    across = swap(block, "tp", 2)
    return [block, swap(block, "tp", 1), across, swap(across, "tp", 1)]


def body(
    tiles,
    tile_target,
    slide_id,
    proj_weight,
    norm_gain,
    query_weight,
    key_weight,
    value_weight,
    sub_gain,
    out_weight,
):
    n_seq = lax.axis_size("seq")
    n_tp = lax.axis_size("tp")
    rows, tile_width = tiles.shape
    features = proj_weight.shape[1]
    width = query_weight.shape[1]
    heads = width // HEAD_DIM
    wide = heads * SLOT
    share = rows // n_tp
    peer = rows // n_seq
    sub_pad = up_to(peer // n_tp, 8)
    arriving = n_seq * sub_pad
    chunks = tile_width // LANES
    block_rows = up_to(chunks * sub_pad + 8, 16)

    first_group = max(1, n_seq // 16)
    sizes = [min(first_group * 2**branch, n_seq) for branch in range(BRANCHES)]
    groups = []
    for level in range(BRANCHES):
        masks = tuple(range(1 if level == 0 else sizes[level - 1], sizes[level]))
        if masks:
            groups.append((level, masks))

    vmem_bytes = VMEM_BYTES if n_seq <= 8 else LARGE_VMEM_BYTES
    blocks, bundle, rest = call(
        functools.partial(route_kernel, n_seq, n_tp, peer),
        "route",
        [((n_seq * n_tp, block_rows, LANES), BF16), ((tile_width + width // 3, features), BF16)]
        + [((width - width // 3, features), BF16)],
        [tile_target.reshape(-1, LANES), slide_id.reshape(-1, LANES), tiles, proj_weight, out_weight],
        scratch=[
            pltpu.VMEM((rows // LANES, LANES), jnp.int32),
            pltpu.VMEM((rows // LANES, LANES), jnp.int32),
            pltpu.VMEM(tiles.shape, BF16),
            pltpu.VMEM((n_seq * n_tp, block_rows, LANES), BF16),
            pltpu.VMEM((tile_width + width // 3, features), BF16),
            pltpu.VMEM((width - width // 3, features), BF16),
            pltpu.SemaphoreType.DMA((8,)),
            pltpu.SemaphoreType.DMA((n_seq,)),
        ],
        cost=3,
        vmem_bytes=ALL_VMEM_BYTES,
        apart=(0, 1, 2, 3, 4),
        out_apart=(0, 1, 2),
    )
    received = lax.all_to_all(blocks, ("seq", "tp"), split_axis=0, concat_axis=0, tiled=True)
    bundles, rests = gather_tp(bundle), gather_tp(rest)

    total, last, codes, ids = call(
        functools.partial(project_kernel, n_seq, n_tp, peer),
        "project",
        [((arriving, features), F32), ((arriving, tile_width), BF16)]
        + [((n_tp, 1, up_to(arriving, LANES)), jnp.int32), ((n_seq, rows), F32)],
        [received] + bundles[:-1],
        scratch=[
            pltpu.VMEM(received.shape, BF16),
            pltpu.VMEM((n_tp, arriving, tile_width), F32),
            pltpu.SemaphoreType.DMA((n_seq,)),
        ],
        vmem_bytes=vmem_bytes,
        apart=(0,),
    )
    (stream,) = call(
        stream_kernel,
        "stream",
        [((arriving, features), BF16)],
        [total, last, bundles[-1]],
        vmem_bytes=vmem_bytes,
    )
    shards = gather_tp(stream)

    gain = norm_gain.reshape(-1, LANES)
    weights = [gain, key_weight.T, value_weight.T, query_weight.T]
    partial, same, apart, back, gains, *far_apart = call(
        functools.partial(first_heads_kernel, groups),
        "heads_1",
        [
            ((rows, 3 * width), BF16),
            ((rows, wide), BF16),
            ((rows, wide), BF16),
            ((n_tp, share, rows), BF16),
            ((16, wide), BF16),
        ]
        + [(((rows >> level) * len(masks), wide), BF16) for level, masks in groups],
        [codes] + weights + [shards[0], ids, sub_gain.reshape(1, width)],
        scratch=[pltpu.VMEM((rows, wide), BF16)],
        vmem_bytes=vmem_bytes,
    )
    for turn in range(1, n_tp - 1):
        (partial,) = call(
            functools.partial(more_heads_kernel, turn),
            "heads_2",
            [((rows, 3 * width), BF16)],
            [codes] + weights + [shards[turn], partial],
            cost=10 if turn == n_tp - 2 else 1,
            vmem_bytes=vmem_bytes,
        )
    packed, *sets = call(
        functools.partial(last_heads_kernel, n_tp - 1, [level for level, _ in groups]),
        "heads_3",
        [((rows, 3 * width), BF16)] + [((rows >> level, 2 * width), BF16) for level, _ in groups],
        [codes] + weights + [shards[n_tp - 1], partial],
        vmem_bytes=vmem_bytes,
    )
    sent = [[swap(one, "seq", mask) for mask in masks] for one, (_, masks) in zip(sets[:-1], groups)]
    direct = {mask: swap(sets[-1], "seq", mask) for mask in groups[-1][1] if mask % 2 == 0}
    sent.append([swap(direct[mask - 1], "seq", 1) if mask % 2 else direct[mask] for mask in groups[-1][1]])

    acc, tops, masked = call(
        own_kernel,
        "own",
        [((rows, wide), F32), ((heads, rows, LANES), F32), ((rows, wide), BF16)],
        [packed, same, apart],
        scratch=[pltpu.VMEM((rows, wide), BF16)] * 2,
        cost=0.1,
        vmem_bytes=vmem_bytes,
    )
    for index in range(len(groups) - 1):
        final = index == len(groups) - 2
        acc, tops, *rest_of = call(
            functools.partial(mid_kernel if final else near_kernel, [groups[index]]),
            "mid" if final else "near",
            [((rows, wide), F32), ((heads, rows, LANES), F32)]
            + ([((rows, wide), BF16), ((rows, wide), F32)] if final else []),
            [acc, tops, masked, far_apart[index]] + sent[index],
            cost=6,
            vmem_bytes=vmem_bytes,
        )
    early, centre = rest_of
    messages = call(
        functools.partial(far_kernel, n_tp, *groups[-1]),
        "far",
        [((share + 16, wide), BF16)] * n_tp,
        [acc, tops, masked, early, centre, back, gains, far_apart[-1]] + sent[-1],
        scratch=[pltpu.VMEM((rows, wide), BF16)],
        vmem_bytes=vmem_bytes,
    )
    arrived = [messages[0]] + [swap(messages[turn], "tp", turn) for turn in range(1, n_tp)]
    base, padded = call(
        functools.partial(base_kernel, n_tp),
        "base",
        [((share, features), BF16), ((n_tp, wide, features), BF16)],
        [codes] + shards + bundles + rests,
        vmem_bytes=vmem_bytes,
    )
    (result,) = call(
        functools.partial(mix_kernel, n_tp),
        "mix",
        [((share, features), BF16)],
        [base, padded] + arrived,
    )
    return result


def solution(mesh):
    return jax.shard_map(
        body,
        mesh=mesh,
        in_specs=(
            P("seq", "tp"),
            P("seq"),
            P("seq"),
            P("tp", None),
            P(),
            P(None, "tp"),
            P(None, "tp"),
            P(None, "tp"),
            P("tp"),
            P("tp", None),
        ),
        out_specs=P(("seq", "tp"), None),
        check_vma=False,
    )
```

time: 103 us -> 81.3 us (0.79)
  waiting for transfers between devices: 43.6 us -> 30.7 us
  local copies, waits for them, and re-layouts: 12.7 us -> 1.14 us
  starting transfers between devices: 23.5 us -> 24.9 us
  Pallas kernels: 22.7 us -> 24 us
    ppermute x19, waiting for transfers between devices: 43.6 us -> 29.9 us  [swap(): lax.ppermute(block, axis, [(index, index ^ mask) for index in range(count)])]
    unnamed x41 -> x16, local copies, waits for them, and re-layouts: 9.26 us -> 1.14 us
    ppermute x19, starting transfers between devices: 16.2 us -> 20 us  [swap(): lax.ppermute(block, axis, [(index, index ^ mask) for index in range(count)])]
    reshape x4 -> x0, local copies, waits for them, and re-layouts: 2.82 us -> none  [the longest x1 1.44 us: body(): ids = ids.transpose(1, 0, 2).reshape(n_seq, rows)]
    all_to_all x1, starting transfers between devices: 7.3 us -> 4.89 us  [body(): lax.all_to_all(blocks, ('seq', 'tp'), split_axis=0, concat_axis=0, tiled=...]
    pallas_call x7 -> x13, Pallas kernels: 22.7 us -> 24 us  [call(): pl.pallas_call(kernel, name=name, out_shape=[jax.ShapeDtypeStruct(shape,...]
  transfers between devices with their start and end apart: 20 -> 20, of which waited for: 7 -> 8; matrix products, arithmetic and copies ran while one was open for 4% -> 0% of each run, Pallas kernels for 18% -> 22%
where the time goes in v1:
time: 81.3 us; the launch traced here: 81 us
  waiting for transfers between devices  30.7 us (38%)
  starting transfers between devices  24.9 us (31%)
  Pallas kernels  24 us (30%)
  local copies, waits for them, and re-layouts  1.14 us (1%)
    ppermute x19, waiting for transfers between devices, swap(): lax.ppermute(block, axis, [(index, index ^ mask) for index in range(count)])  29.9 us
    pallas_call x13, Pallas kernels, call(): pl.pallas_call(kernel, name=name, out_shape=[jax.ShapeDtypeStruct(shape,...  24 us
    ppermute x19, starting transfers between devices, swap(): lax.ppermute(block, axis, [(index, index ^ mask) for index in range(count)])  20 us
    all_to_all x1, starting transfers between devices, body(): lax.all_to_all(blocks, ('seq', 'tp'), split_axis=0, concat_axis=0, tiled=...  4.89 us
  transfers between devices with their start and end apart: 20, of which 8 were waited for; matrix products, arithmetic and copies ran while one was open for 0% of the time, Pallas kernels for 22%

profile of v1, /device:TPU:0, one launch (start us, length us, event | category | flops | bytes accessed | tf_op | source)
XLA Modules:
  0.0 81.0 jit_solution(6952679173462833735)
XLA Ops:
  0.0 3.4 %route.1 = (bf16[32,80,128]{2,1,0:T(8,128)(2,1)}, bf16[448,768]{1,0:T(8,128)(2,1)}, bf16[128,768]{1,0:T(8,128)(2,1)}) custom-call(s32[6,128]{1,0:T(8,128)} %bitcast.24, s32[6,128]{1,0:T(8,128)} %bitcast.25, bf16[768,384]{1,0:T(8,128)(2,1)} %tiles_hbm.1, bf16[384,768]{1,0:T(8,128)(2,1)} %proj_hbm.1, bf16[192,768]{1,0:T(8,128)(2,1)} %out_weight_hbm.1), custom_call_target="tpu_custom_call" | custom-call | flops 3000000000 | tf_op jit(solution)/shard_map/route/pallas_call | solution.py:68
  3.4 3.0 %collective-permute-start.1 = (bf16[448,768]{1,0:T(8,128)(2,1)}, bf16[448,768]{1,0:T(8,128)(2,1)S(1)}, u32[]{:S(2)}, u32[]{:S(2)}) collective-permute-start(bf16[448,768]{1,0:T(8,128)(2,1)} %get-tuple-element.40.refs_0_.refs_4_), channel_id=1, source_target_pairs={{0,2},{1,3},{2,0},{3,1},{4,6},{5,7},{6,4},{7,5},{8,10},{9,11},{10,... | collective-permute-start | bytes 2064392 | tf_op jit(solution)/shard_map/ppermute | solution.py:586
  6.4 4.9 %all-to-all-start = ((bf16[32,80,128]{2,1,0:T(8,128)(2,1)}), bf16[32,80,128]{2,1,0:T(8,128)(2,1)S(1)}, u32[]{:S(2)}, u32[]{:S(2)}) async-start(bf16[32,80,128]{2,1,0:T(8,128)(2,1)} %get-tuple-element.39), calls=%async_computation | async-start | bytes 1310720 | tf_op jit(solution)/shard_map/all_to_all | solution.py:650
  11.6 16.8 %collective-permute-done.1.refs_2_.refs_6_ = bf16[448,768]{1,0:T(8,128)(2,1)S(1)} collective-permute-done((bf16[448,768]{1,0:T(8,128)(2,1)}, bf16[448,768]{1,0:T(8,128)(2,1)S(1)}, u32[]{:S(2)}, u32[]{:S(2)}) %collective-permute-start.1) | collective-permute-done | bytes 688160 | tf_op jit(solution)/shard_map/ppermute | solution.py:586
  30.3 2.1 %project.1 = (f32[192,768]{1,0:T(8,128)S(1)}, bf16[192,384]{1,0:T(8,128)(2,1)S(1)}, s32[4,1,256]{2,1,0:T(1,128)S(1)}, f32[8,768]{1,0:T(8,128)S(1)}) custom-call(bf16[32,80,128]{2,1,0:T(8,128)(2,1)S(1)} %all-to-all-done.recv_hbm, bf16[448,768]{1,0:T(8,128)(2,1)S(1)} %copy-done, bf16[448,768]{1,0:T(8,128)(2,1)S(1)} %collective-permute-done.refs_1_.refs_5_, ...), custom_call_target="tpu_custom_call" | custom-call | flops 1000000000 | tf_op jit(solution)/shard_map/project/pallas_call | solution.py:68
  32.9 1.4 %collective-permute-start.4 = (bf16[192,768]{1,0:T(8,128)(2,1)S(1)}, bf16[192,768]{1,0:T(8,128)(2,1)S(1)}, u32[]{:S(2)}, u32[]{:S(2)}) collective-permute-start(bf16[192,768]{1,0:T(8,128)(2,1)S(1)} %stream.1.refs_0_.stream_ref), channel_id=1, source_target_pairs={{0,2},{1,3},{2,0},{3,1},{4,6},{5,7},{6,4},{7,5},{8,10},{9,11},{10,... | collective-permute-start | bytes 884744 | tf_op jit(solution)/shard_map/ppermute | solution.py:586
  34.3 2.5 %heads_1.1 = (bf16[768,576]{1,0:T(8,128)(2,1)S(1)}, bf16[768,256]{1,0:T(8,128)(2,1)S(1)}, bf16[768,256]{1,0:T(8,128)(2,1)S(1)}, bf16[4,192,768]{2,1,0:T(8,128)(2...) custom-call(s32[4,1,256]{2,1,0:T(1,128)S(1)} %get-tuple-element.41.c, ...), custom_call_target="tpu_custom_call" | custom-call | flops 1000000000 | tf_op jit(solution)/shard_map/heads_1/pallas_call | solution.py:68
  36.8 5.1 %collective-permute-done.4.refs_2_.stream_ref = bf16[192,768]{1,0:T(8,128)(2,1)S(1)} collective-permute-done((bf16[192,768]{1,0:T(8,128)(2,1)S(1)}, bf16[192,768]{1,0:T(8,128)(2,1)S(1)}, u32[]{:S(2)}, u32[]{:S(2)}) %collective-permute-start.4) | collective-permute-done | bytes 294944 | tf_op jit(solution)/shard_map/ppermute | solution.py:586
  45.0 1.5 %collective-permute-start.9 = (bf16[384,384]{1,0:T(8,128)(2,1)S(1)}, bf16[384,384]{1,0:T(8,128)(2,1)S(1)}, u32[]{:S(2)}, u32[]{:S(2)}) collective-permute-start(bf16[384,384]{1,0:T(8,128)(2,1)S(1)} %get-tuple-element.56), channel_id=1, source_target_pairs={{0,4},{4,0},{8,12},{12,8},{16,20},{20,16},{24,28},{28,24},{1,5},{5... | collective-permute-start | bytes 884744 | tf_op jit(solution)/shard_map/ppermute | solution.py:586
  46.5 1.6 %collective-permute-start.7 = (bf16[128,768]{1,0:T(8,128)(2,1)S(1)}, bf16[128,768]{1,0:T(8,128)(2,1)S(1)}, u32[]{:S(2)}, u32[]{:S(2)}) collective-permute-start(bf16[128,768]{1,0:T(8,128)(2,1)S(1)} %copy-done.2), channel_id=1, source_target_pairs={{0,2},{1,3},{2,0},{3,1},{4,6},{5,7},{6,4},{7,5},{8,10},{9,11},{10,... | collective-permute-start | bytes 589832 | tf_op jit(solution)/shard_map/ppermute | solution.py:586
  48.1 1.6 %collective-permute-start.10 = (bf16[192,384]{1,0:T(8,128)(2,1)S(1)}, bf16[192,384]{1,0:T(8,128)(2,1)S(1)}, u32[]{:S(2)}, u32[]{:S(2)}) collective-permute-start(bf16[192,384]{1,0:T(8,128)(2,1)S(1)} %get-tuple-element.60), channel_id=1, source_target_pairs={{0,8},{4,12},{8,0},{12,4},{16,24},{20,28},{24,16},{28,20},{1,9},{5... | collective-permute-start | bytes 442376 | tf_op jit(solution)/shard_map/ppermute | solution.py:586
  50.1 2.6 %collective-permute-start.12 = (bf16[96,384]{1,0:T(8,128)(2,1)S(1)}, bf16[96,384]{1,0:T(8,128)(2,1)S(1)}, u32[]{:S(2)}, u32[]{:S(2)}) collective-permute-start(bf16[96,384]{1,0:T(8,128)(2,1)S(1)} %get-tuple-element.68), channel_id=1, source_target_pairs={{0,16},{4,20},{8,24},{12,28},{16,0},{20,4},{24,8},{28,12},{1,17},{... | collective-permute-start | bytes 221192 | tf_op jit(solution)/shard_map/ppermute | solution.py:586
  52.7 4.3 %own.1 = (f32[768,256]{1,0:T(8,128)S(1)}, f32[4,768,128]{2,1,0:T(8,128)S(1)}, bf16[768,256]{1,0:T(8,128)(2,1)S(1)}) custom-call(bf16[768,576]{1,0:T(8,128)(2,1)S(1)} %get-tuple-element.49.packed_ref, bf16[768,256]{1,0:T(8,128)(2,1)S(1)} %get-tuple-element.50.same_ref, bf16[768,256]{1,0:T(8,128)(2,1)S(1)} %get-tuple-element.51.apart_ref), custom_call_target="tpu_custom_call" | custom-call | flops 100000000 | tf_op jit(solution)/shard_map/own/pallas_call | solution.py:68
  57.0 2.0 %collective-permute-start.14 = (bf16[96,384]{1,0:T(8,128)(2,1)S(1)}, bf16[96,384]{1,0:T(8,128)(2,1)S(1)}, u32[]{:S(2)}, u32[]{:S(2)}) collective-permute-start(bf16[96,384]{1,0:T(8,128)(2,1)S(1)} %get-tuple-element.68), channel_id=1, source_target_pairs={{0,24},{4,28},{8,16},{12,20},{16,8},{20,12},{24,0},{28,4},{1,25},{... | collective-permute-start | bytes 221192 | tf_op jit(solution)/shard_map/ppermute | solution.py:586
  59.1 2.5 %near.1 = (f32[768,256]{1,0:T(8,128)S(1)}, f32[4,768,128]{2,1,0:T(8,128)S(1)}) custom-call(f32[768,256]{1,0:T(8,128)S(1)} %get-tuple-element.52.acc_ref, f32[4,768,128]{2,1,0:T(8,128)S(1)} %get-tuple-element.53.tops_ref, bf16[768,256]{1,0:T(8,128)(2,1)S(1)} %get-tuple-element.54.query_ref, bf16[384,256]{1,0:T(8,128)(2,1)S(1)} %get-tuple-element.55.refs_0_, ...), custom_call_target="tpu_custom_call" | custom-call | flops 6000000000 | tf_op jit(solution)/shard_map/near/pallas_call | solution.py:68
  62.2 1.2 %collective-permute-done.14.refs_3_ = bf16[96,384]{1,0:T(8,128)(2,1)S(1)} collective-permute-done((bf16[96,384]{1,0:T(8,128)(2,1)S(1)}, bf16[96,384]{1,0:T(8,128)(2,1)S(1)}, u32[]{:S(2)}, u32[]{:S(2)}) %collective-permute-start.14) | collective-permute-done | bytes 73760 | tf_op jit(solution)/shard_map/ppermute | solution.py:586
  63.4 1.5 %collective-permute-start.13 = (bf16[96,384]{1,0:T(8,128)(2,1)S(1)}, bf16[96,384]{1,0:T(8,128)(2,1)S(1)}, u32[]{:S(2)}, u32[]{:S(2)}) collective-permute-start(bf16[96,384]{1,0:T(8,128)(2,1)S(1)} %collective-permute-done.12.refs_1_), channel_id=1, source_target_pairs={{0,4},{4,0},{8,12},{12,8},{16,20},{20,16},{24,28},{28,24},{1,5},{5... | collective-permute-start | bytes 221192 | tf_op jit(solution)/shard_map/ppermute | solution.py:586
  65.4 1.9 %mid.1 = (f32[768,256]{1,0:T(8,128)S(1)}, f32[4,768,128]{2,1,0:T(8,128)S(1)}, bf16[768,256]{1,0:T(8,128)(2,1)S(1)}, f32[768,256]{1,0:T(8,128)S(1)}) custom-call(f32[768,256]{1,0:T(8,128)S(1)} %get-tuple-element.57.acc_ref, f32[4,768,128]{2,1,0:T(8,128)S(1)} %get-tuple-element.58.tops_ref, bf16[768,256]{1,0:T(8,128)(2,1)S(1)} %get-tuple-element.54.query_ref, ...), custom_call_target="tpu_custom_call" | custom-call | flops 6000000000 | tf_op jit(solution)/shard_map/mid/pallas_call | solution.py:68
  67.7 1.5 %collective-permute-done.15.refs_4_ = bf16[96,384]{1,0:T(8,128)(2,1)S(1)} collective-permute-done((bf16[96,384]{1,0:T(8,128)(2,1)S(1)}, bf16[96,384]{1,0:T(8,128)(2,1)S(1)}, u32[]{:S(2)}, u32[]{:S(2)}) %collective-permute-start.15) | collective-permute-done | bytes 73760 | tf_op jit(solution)/shard_map/ppermute | solution.py:586
  69.2 1.8 %far.1 = (bf16[208,256]{1,0:T(8,128)(2,1)S(1)}, bf16[208,256]{1,0:T(8,128)(2,1)S(1)}, bf16[208,256]{1,0:T(8,128)(2,1)S(1)}, bf16[208,256]{1,0:T(8,128)(2,1)S(1)}) custom-call(f32[768,256]{1,0:T(8,128)S(1)} %get-tuple-element.61.acc_ref, f32[4,768,128]{2,1,0:T(8,128)S(1)} %get-tuple-element.62.tops_ref, bf16[768,256]{1,0:T(8,128)(2,1)S(1)} %get-tuple-element.54.query_ref, ...), custom_call_target="tpu_custom_call" | custom-call | flops 1000000000 | tf_op jit(solution)/shard_map/far/pallas_call | solution.py:68
  71.1 2.7 %collective-permute-start.17 = (bf16[208,256]{1,0:T(8,128)(2,1)S(1)}, bf16[208,256]{1,0:T(8,128)(2,1)S(1)}, u32[]{:S(2)}, u32[]{:S(2)}) collective-permute-start(bf16[208,256]{1,0:T(8,128)(2,1)S(1)} %get-tuple-element.71), channel_id=1, source_target_pairs={{0,2},{1,3},{2,0},{3,1},{4,6},{5,7},{6,4},{7,5},{8,10},{9,11},{10,... | collective-permute-start | bytes 319496 | tf_op jit(solution)/shard_map/ppermute | solution.py:586
  74.4 3.2 %collective-permute-done.17.refs_2_ = bf16[208,256]{1,0:T(8,128)(2,1)S(1)} collective-permute-done((bf16[208,256]{1,0:T(8,128)(2,1)S(1)}, bf16[208,256]{1,0:T(8,128)(2,1)S(1)}, u32[]{:S(2)}, u32[]{:S(2)}) %collective-permute-start.17) | collective-permute-done | bytes 106528 | tf_op jit(solution)/shard_map/ppermute | solution.py:586
  77.6 1.8 %collective-permute-done.18.refs_3_ = bf16[208,256]{1,0:T(8,128)(2,1)S(1)} collective-permute-done((bf16[208,256]{1,0:T(8,128)(2,1)S(1)}, bf16[208,256]{1,0:T(8,128)(2,1)S(1)}, u32[]{:S(2)}, u32[]{:S(2)}) %collective-permute-start.18) | collective-permute-done | bytes 106528 | tf_op jit(solution)/shard_map/ppermute | solution.py:586
  79.4 1.6 %mix.1 = bf16[192,768]{1,0:T(8,128)(2,1)} custom-call(bf16[192,768]{1,0:T(8,128)(2,1)S(1)} %get-tuple-element.45.base_ref, bf16[4,256,768]{2,1,0:T(8,128)(2,1)S(1)} %get-tuple-element.46.weights_ref, bf16[208,256]{1,0:T(8,128)(2,1)S(1)} %get-tuple-element.69.refs_0_, bf16[208,256]{1,0:T(8,128)(2,1)S(1)} %collective-permute-done.16.refs_1_, ...), custom_call_target="tpu_custom_call" | custom-call | flops 1000000000 | tf_op jit(solution)/shard_map/mix/pallas_call | solution.py:68
  (45 shorter events, 8.2 us)
Async XLA Ops:
  3.4 25.0 %collective-permute-start.1 = (bf16[448,768]{1,0:T(8,128)(2,1)}, bf16[448,768]{1,0:T(8,128)(2,1)S(1)}, u32[]{:S(2)}, u32[]{:S(2)}) collective-permute-start(bf16[448,768]{1,0:T(8,128)(2,1)} %get-tuple-element.40.refs_0_.refs_4_), channel_id=1, source_target_pairs={{0,2},{1,3},{2,0},{3,1},{4,6},{5,7},{6,4},{7,5},{8,10},{9,11},{10,... | collective-permute-start | bytes 2064392 | tf_op jit(solution)/shard_map/ppermute | solution.py:586
  6.4 22.8 %all-to-all-start = ((bf16[32,80,128]{2,1,0:T(8,128)(2,1)}), bf16[32,80,128]{2,1,0:T(8,128)(2,1)S(1)}, u32[]{:S(2)}, u32[]{:S(2)}) async-start(bf16[32,80,128]{2,1,0:T(8,128)(2,1)} %get-tuple-element.39), calls=%async_computation | async-start | bytes 1310720 | tf_op jit(solution)/shard_map/all_to_all | solution.py:650
  11.3 17.1 %collective-permute-start = (bf16[448,768]{1,0:T(8,128)(2,1)}, bf16[448,768]{1,0:T(8,128)(2,1)S(1)}, u32[]{:S(2)}, u32[]{:S(2)}) collective-permute-start(bf16[448,768]{1,0:T(8,128)(2,1)} %get-tuple-element.40.refs_0_.refs_4_), channel_id=1, source_target_pairs={{0,1},{1,0},{2,3},{3,2},{4,5},{5,4},{6,7},{7,6},{8,9},{9,8},{10,11... | collective-permute-start | bytes 2064392 | tf_op jit(solution)/shard_map/ppermute | solution.py:586
  28.4 4.0 %collective-permute-start.2 = (bf16[448,768]{1,0:T(8,128)(2,1)S(1)}, bf16[448,768]{1,0:T(8,128)(2,1)S(1)}, u32[]{:S(2)}, u32[]{:S(2)}) collective-permute-start(bf16[448,768]{1,0:T(8,128)(2,1)S(1)} %collective-permute-done.1.refs_2_.refs_6_), channel_id=1, source_target_pairs={{0,1},{1,0},{2,3},{3,2},{4,5},{5,4},{6,7},{7,6},{8,9},{9,8},{10,11... | collective-permute-start | bytes 2064392 | tf_op jit(solution)/shard_map/ppermute | solution.py:586
  32.5 1.8 %copy-start.3 = (bf16[768,192]{0,1:T(8,128)(2,1)S(1)}, bf16[768,192]{0,1:T(8,128)(2,1)}, u32[]{:S(2)}) copy-start(bf16[768,192]{0,1:T(8,128)(2,1)} %param.16) | copy-start | bytes 884740
  32.5 1.8 %copy-start.4 = (bf16[768,192]{0,1:T(8,128)(2,1)S(1)}, bf16[768,192]{0,1:T(8,128)(2,1)}, u32[]{:S(2)}) copy-start(bf16[768,192]{0,1:T(8,128)(2,1)} %param.17) | copy-start | bytes 884740
  32.9 9.1 %collective-permute-start.4 = (bf16[192,768]{1,0:T(8,128)(2,1)S(1)}, bf16[192,768]{1,0:T(8,128)(2,1)S(1)}, u32[]{:S(2)}, u32[]{:S(2)}) collective-permute-start(bf16[192,768]{1,0:T(8,128)(2,1)S(1)} %stream.1.refs_0_.stream_ref), channel_id=1, source_target_pairs={{0,2},{1,3},{2,0},{3,1},{4,6},{5,7},{6,4},{7,5},{8,10},{9,11},{10,... | collective-permute-start | bytes 884744 | tf_op jit(solution)/shard_map/ppermute | solution.py:586
  34.3 7.6 %collective-permute-start.3 = (bf16[192,768]{1,0:T(8,128)(2,1)S(1)}, bf16[192,768]{1,0:T(8,128)(2,1)S(1)}, u32[]{:S(2)}, u32[]{:S(2)}) collective-permute-start(bf16[192,768]{1,0:T(8,128)(2,1)S(1)} %stream.1.refs_0_.stream_ref), channel_id=1, source_target_pairs={{0,1},{1,0},{2,3},{3,2},{4,5},{5,4},{6,7},{7,6},{8,9},{9,8},{10,11... | collective-permute-start | bytes 884744 | tf_op jit(solution)/shard_map/ppermute | solution.py:586
  41.9 1.9 %collective-permute-start.5 = (bf16[192,768]{1,0:T(8,128)(2,1)S(1)}, bf16[192,768]{1,0:T(8,128)(2,1)S(1)}, u32[]{:S(2)}, u32[]{:S(2)}) collective-permute-start(bf16[192,768]{1,0:T(8,128)(2,1)S(1)} %collective-permute-done.4.refs_2_.stream_ref), channel_id=1, source_target_pairs={{0,1},{1,0},{2,3},{3,2},{4,5},{5,4},{6,7},{7,6},{8,9},{9,8},{10,11... | collective-permute-start | bytes 884744 | tf_op jit(solution)/shard_map/ppermute | solution.py:586
  43.8 2.6 %copy-start.2 = (bf16[128,768]{1,0:T(8,128)(2,1)S(1)}, bf16[128,768]{1,0:T(8,128)(2,1)}, u32[]{:S(2)}) copy-start(bf16[128,768]{1,0:T(8,128)(2,1)} %get-tuple-element.44.refs_8_) | copy-start | bytes 589828
  45.0 12.1 %collective-permute-start.9 = (bf16[384,384]{1,0:T(8,128)(2,1)S(1)}, bf16[384,384]{1,0:T(8,128)(2,1)S(1)}, u32[]{:S(2)}, u32[]{:S(2)}) collective-permute-start(bf16[384,384]{1,0:T(8,128)(2,1)S(1)} %get-tuple-element.56), channel_id=1, source_target_pairs={{0,4},{4,0},{8,12},{12,8},{16,20},{20,16},{24,28},{28,24},{1,5},{5... | collective-permute-start | bytes 884744 | tf_op jit(solution)/shard_map/ppermute | solution.py:586
  46.5 15.1 %collective-permute-start.7 = (bf16[128,768]{1,0:T(8,128)(2,1)S(1)}, bf16[128,768]{1,0:T(8,128)(2,1)S(1)}, u32[]{:S(2)}, u32[]{:S(2)}) collective-permute-start(bf16[128,768]{1,0:T(8,128)(2,1)S(1)} %copy-done.2), channel_id=1, source_target_pairs={{0,2},{1,3},{2,0},{3,1},{4,6},{5,7},{6,4},{7,5},{8,10},{9,11},{10,... | collective-permute-start | bytes 589832 | tf_op jit(solution)/shard_map/ppermute | solution.py:586
  48.1 16.7 %collective-permute-start.10 = (bf16[192,384]{1,0:T(8,128)(2,1)S(1)}, bf16[192,384]{1,0:T(8,128)(2,1)S(1)}, u32[]{:S(2)}, u32[]{:S(2)}) collective-permute-start(bf16[192,384]{1,0:T(8,128)(2,1)S(1)} %get-tuple-element.60), channel_id=1, source_target_pairs={{0,8},{4,12},{8,0},{12,4},{16,24},{20,28},{24,16},{28,20},{1,9},{5... | collective-permute-start | bytes 442376 | tf_op jit(solution)/shard_map/ppermute | solution.py:586
  49.7 15.7 %collective-permute-start.11 = (bf16[192,384]{1,0:T(8,128)(2,1)S(1)}, bf16[192,384]{1,0:T(8,128)(2,1)S(1)}, u32[]{:S(2)}, u32[]{:S(2)}) collective-permute-start(bf16[192,384]{1,0:T(8,128)(2,1)S(1)} %get-tuple-element.60), channel_id=1, source_target_pairs={{0,12},{4,8},{8,4},{12,0},{16,28},{20,24},{24,20},{28,16},{1,13},{... | collective-permute-start | bytes 442376 | tf_op jit(solution)/shard_map/ppermute | solution.py:586
  50.1 11.6 %collective-permute-start.12 = (bf16[96,384]{1,0:T(8,128)(2,1)S(1)}, bf16[96,384]{1,0:T(8,128)(2,1)S(1)}, u32[]{:S(2)}, u32[]{:S(2)}) collective-permute-start(bf16[96,384]{1,0:T(8,128)(2,1)S(1)} %get-tuple-element.68), channel_id=1, source_target_pairs={{0,16},{4,20},{8,24},{12,28},{16,0},{20,4},{24,8},{28,12},{1,17},{... | collective-permute-start | bytes 221192 | tf_op jit(solution)/shard_map/ppermute | solution.py:586
  57.0 6.3 %collective-permute-start.14 = (bf16[96,384]{1,0:T(8,128)(2,1)S(1)}, bf16[96,384]{1,0:T(8,128)(2,1)S(1)}, u32[]{:S(2)}, u32[]{:S(2)}) collective-permute-start(bf16[96,384]{1,0:T(8,128)(2,1)S(1)} %get-tuple-element.68), channel_id=1, source_target_pairs={{0,24},{4,28},{8,16},{12,20},{16,8},{20,12},{24,0},{28,4},{1,25},{... | collective-permute-start | bytes 221192 | tf_op jit(solution)/shard_map/ppermute | solution.py:586
  61.6 12.3 %collective-permute-start.6 = (bf16[128,768]{1,0:T(8,128)(2,1)S(1)}, bf16[128,768]{1,0:T(8,128)(2,1)S(1)}, u32[]{:S(2)}, u32[]{:S(2)}) collective-permute-start(bf16[128,768]{1,0:T(8,128)(2,1)S(1)} %copy-done.2), channel_id=1, source_target_pairs={{0,1},{1,0},{2,3},{3,2},{4,5},{5,4},{6,7},{7,6},{8,9},{9,8},{10,11... | collective-permute-start | bytes 589832 | tf_op jit(solution)/shard_map/ppermute | solution.py:586
  61.7 12.2 %collective-permute-start.8 = (bf16[128,768]{1,0:T(8,128)(2,1)S(1)}, bf16[128,768]{1,0:T(8,128)(2,1)S(1)}, u32[]{:S(2)}, u32[]{:S(2)}) collective-permute-start(bf16[128,768]{1,0:T(8,128)(2,1)S(1)} %collective-permute-done.7.refs_10_), channel_id=1, source_target_pairs={{0,1},{1,0},{2,3},{3,2},{4,5},{5,4},{6,7},{7,6},{8,9},{9,8},{10,11... | collective-permute-start | bytes 589832 | tf_op jit(solution)/shard_map/ppermute | solution.py:586
  63.4 4.4 %collective-permute-start.13 = (bf16[96,384]{1,0:T(8,128)(2,1)S(1)}, bf16[96,384]{1,0:T(8,128)(2,1)S(1)}, u32[]{:S(2)}, u32[]{:S(2)}) collective-permute-start(bf16[96,384]{1,0:T(8,128)(2,1)S(1)} %collective-permute-done.12.refs_1_), channel_id=1, source_target_pairs={{0,4},{4,0},{8,12},{12,8},{16,20},{20,16},{24,28},{28,24},{1,5},{5... | collective-permute-start | bytes 221192 | tf_op jit(solution)/shard_map/ppermute | solution.py:586
  64.8 4.4 %collective-permute-start.15 = (bf16[96,384]{1,0:T(8,128)(2,1)S(1)}, bf16[96,384]{1,0:T(8,128)(2,1)S(1)}, u32[]{:S(2)}, u32[]{:S(2)}) collective-permute-start(bf16[96,384]{1,0:T(8,128)(2,1)S(1)} %collective-permute-done.14.refs_3_), channel_id=1, source_target_pairs={{0,4},{4,0},{8,12},{12,8},{16,20},{20,16},{24,28},{28,24},{1,5},{5... | collective-permute-start | bytes 221192 | tf_op jit(solution)/shard_map/ppermute | solution.py:586
  69.2 4.7 %copy-start.1 = (bf16[448,768]{1,0:T(8,128)(2,1)S(1)}, bf16[448,768]{1,0:T(8,128)(2,1)}, u32[]{:S(2)}) copy-start(bf16[448,768]{1,0:T(8,128)(2,1)} %get-tuple-element.40.refs_0_.refs_4_) | copy-start | bytes 2064388
  71.0 3.4 %collective-permute-start.16 = (bf16[208,256]{1,0:T(8,128)(2,1)S(1)}, bf16[208,256]{1,0:T(8,128)(2,1)S(1)}, u32[]{:S(2)}, u32[]{:S(2)}) collective-permute-start(bf16[208,256]{1,0:T(8,128)(2,1)S(1)} %get-tuple-element.70), channel_id=1, source_target_pairs={{0,1},{1,0},{2,3},{3,2},{4,5},{5,4},{6,7},{7,6},{8,9},{9,8},{10,11... | collective-permute-start | bytes 319496 | tf_op jit(solution)/shard_map/ppermute | solution.py:586
  71.1 6.5 %collective-permute-start.17 = (bf16[208,256]{1,0:T(8,128)(2,1)S(1)}, bf16[208,256]{1,0:T(8,128)(2,1)S(1)}, u32[]{:S(2)}, u32[]{:S(2)}) collective-permute-start(bf16[208,256]{1,0:T(8,128)(2,1)S(1)} %get-tuple-element.71), channel_id=1, source_target_pairs={{0,2},{1,3},{2,0},{3,1},{4,6},{5,7},{6,4},{7,5},{8,10},{9,11},{10,... | collective-permute-start | bytes 319496 | tf_op jit(solution)/shard_map/ppermute | solution.py:586
  73.8 5.6 %collective-permute-start.18 = (bf16[208,256]{1,0:T(8,128)(2,1)S(1)}, bf16[208,256]{1,0:T(8,128)(2,1)S(1)}, u32[]{:S(2)}, u32[]{:S(2)}) collective-permute-start(bf16[208,256]{1,0:T(8,128)(2,1)S(1)} %get-tuple-element.72), channel_id=1, source_target_pairs={{0,3},{1,2},{2,1},{3,0},{4,7},{5,6},{6,5},{7,4},{8,11},{9,10},{10,... | collective-permute-start | bytes 319496 | tf_op jit(solution)/shard_map/ppermute | solution.py:586
  (4 other events, 6.6 us)

commit v2 on v1

--- a/solution.py
+++ b/solution.py
@@ -62,7 +62,7 @@
     return start
 
 
-def call(kernel, name, outs, args, scratch=(), cost=1, vmem_bytes=VMEM_BYTES, apart=(), out_apart=()):
+def call(kernel, name, outs, args, scratch=(), cost=1, vmem_bytes=VMEM_BYTES, apart=(), out_apart=(), aliases=None):
     vmem = pl.BlockSpec(memory_space=pltpu.VMEM)
     anywhere = pl.BlockSpec(memory_space=pltpu.HBM)
     return pl.pallas_call(
@@ -72,6 +72,7 @@
         in_specs=[anywhere if index in apart else vmem for index in range(len(args))],
         out_specs=[anywhere if index in out_apart else vmem for index in range(len(outs))],
         scratch_shapes=list(scratch),
+        input_output_aliases=aliases or {},
         compiler_params=pltpu.CompilerParams(vmem_limit_bytes=vmem_bytes),
         cost_estimate=pl.CostEstimate(flops=int(cost * 1e9), bytes_accessed=0, transcendentals=0),
     )(*args)
@@ -90,6 +91,7 @@
     tiles_hbm,
     proj_hbm,
     out_weight_hbm,
+    gain_hbm,
     out_hbm,
     bundle_hbm,
     rest_hbm,
@@ -99,23 +101,32 @@
     out_ref,
     bundle_ref,
     rest_ref,
+    gain_ref,
     sems,
     out_sems,
 ):
     depth = proj_hbm.shape[0]
-    along = bundle_hbm.shape[0] - depth
+    width = out_weight_hbm.shape[0]
+    along = width - rest_ref.shape[0]
     fetches = [
         pltpu.make_async_copy(target_hbm, target_ref, sems.at[0]),
         pltpu.make_async_copy(slide_hbm, slide_ref, sems.at[1]),
         pltpu.make_async_copy(tiles_hbm, tiles_ref, sems.at[2]),
         pltpu.make_async_copy(proj_hbm, bundle_ref.at[pl.ds(0, depth)], sems.at[3]),
         pltpu.make_async_copy(out_weight_hbm.at[pl.ds(0, along)], bundle_ref.at[pl.ds(depth, along)], sems.at[4]),
-        pltpu.make_async_copy(out_weight_hbm.at[pl.ds(along, rest_hbm.shape[0])], rest_ref, sems.at[5]),
+        pltpu.make_async_copy(out_weight_hbm.at[pl.ds(along, rest_ref.shape[0])], rest_ref, sems.at[5]),
+        pltpu.make_async_copy(gain_hbm, gain_ref, sems.at[6]),
     ]
     for fetch in fetches:
         fetch.start()
+    rows = tiles_ref.shape[0]
+    share = rows // n_tp
+    code_rows = up_to(n_seq * up_to(peer // n_tp, 8), LANES) // LANES
+    kept = stored_at(iota((1, rows), 1), rows) - lax.axis_index("tp") * share
+    held = (kept >= 0) & (kept < share) & ((kept >> 7) + code_rows == (iota((n_seq * 8, rows), 0) & 7))
+    kept_lane = one_hot(iota((LANES, rows), 0) == (kept & 127))
+    before = one_hot(iota((LANES, LANES), 0) <= iota((LANES, LANES), 1))
     fetches[0].wait()
-    rows = tiles_ref.shape[0]
     chunks = tiles_ref.shape[1] // LANES
     sub = peer // n_tp
     sub_pad = up_to(sub, 8)
@@ -124,9 +135,15 @@
     target = one_row(target_ref)
     owner = jnp.floor((target.astype(F32) + 0.5) * (1.0 / rows)).astype(jnp.int32)
     flags = jnp.where(iota((n_seq, rows), 0) == owner, 1.0, 0.0)
-    before = one_hot(iota((rows, rows), 0) <= iota((rows, rows), 1))
-    counts = dot(flags.astype(BF16), before)
-    slot = jnp.sum(flags * counts, axis=0, keepdims=True).astype(jnp.int32) - 1
+    parts = [flags[:, at : at + LANES] for at in range(0, rows, LANES)]
+    counts = dot(jnp.concatenate(parts, axis=0).astype(BF16), before)
+    ahead = jnp.zeros((n_seq, 1), F32)
+    slots = []
+    for index, part in enumerate(parts):
+        count = counts[index * n_seq : (index + 1) * n_seq]
+        slots.append(jnp.sum(part * (count + ahead), axis=0, keepdims=True))
+        ahead = ahead + count[:, LANES - 1 :]
+    slot = jnp.concatenate(slots, axis=1).astype(jnp.int32) - 1
     lane_of = jnp.zeros_like(slot)
     for turn in range(1, n_tp):
         lane_of = lane_of + jnp.where(slot >= turn * sub, 1, 0)
@@ -141,27 +158,28 @@
         code = code * jnp.where((high >> bit) & 1 == 1, 256.0 ** (2**bit), 1.0)
     arrival = place * sub_pad + low
     extra = n_seq * 8
-    code_rows = up_to(n_seq * sub_pad, LANES) // LANES
     line = iota((extra, rows), 0)
     mine = (owner == (line >> 3)) & (lane_of == column) & ((arrival >> 7) == (line & 7))
     coded = dot_nt(
         jnp.where(mine, code, 0.0).astype(BF16),
         one_hot(iota((LANES, rows), 0) == (arrival & 127)),
     )
-    share = rows // n_tp
     fetches[1].wait()
-    kept = stored_at(iota((1, rows), 1), rows) - column * share
-    held = (kept >= 0) & (kept < share) & ((kept >> 7) + code_rows == (line & 7))
-    ids = dot_nt(
-        jnp.where(held, one_row(slide_ref).astype(F32), 0.0).astype(BF16),
-        one_hot(iota((LANES, rows), 0) == (kept & 127)),
-    )
+    ids = dot_nt(jnp.where(held, one_row(slide_ref).astype(F32), 0.0).astype(BF16), kept_lane)
     notes = coded + ids
     for fetch in fetches[3:]:
         fetch.wait()
+    gain = gain_ref[...]
+    high = gain.astype(BF16).astype(F32)
+    mid = (gain - high).astype(BF16).astype(F32)
+    low = (gain - high) - mid
+    line = iota((16, width), 0)
+    parts = jnp.where(line == 0, high, jnp.where(line == 1, mid, jnp.where(line == 2, low, 0.0)))
+    bundle_ref[depth + along :] = jnp.zeros((16, bundle_ref.shape[1]), BF16)
+    bundle_ref[depth + along :, :width] = parts.astype(BF16)
     stores = [
-        pltpu.make_async_copy(bundle_ref, bundle_hbm, sems.at[6]),
-        pltpu.make_async_copy(rest_ref, rest_hbm, sems.at[7]),
+        pltpu.make_async_copy(bundle_ref, bundle_hbm, sems.at[7]),
+        pltpu.make_async_copy(rest_ref, rest_hbm, sems.at[8]),
     ]
     for store in stores:
         store.start()
@@ -194,8 +212,8 @@
 
 
 def project_kernel(n_seq, n_tp, peer, recv_hbm, *refs):
-    weight_refs = refs[: n_tp - 1]
-    total_ref, last_ref, codes_ref, ids_ref, recv_ref, work, sems = refs[n_tp - 1 :]
+    total_ref, later_ref, codes_ref, ids_ref, recv_ref, work, sems = refs[n_tp - 2 :]
+    weight_refs = refs[: n_tp - 2]
     fetches = []
     for source in range(n_seq):
         some = pl.ds(source * n_tp, n_tp)
@@ -226,11 +244,12 @@
                 pieces.append(note[code_rows + piece : code_rows + piece + 1, :length])
         ids_ref[source : source + 1, :] = jnp.concatenate(pieces, axis=1)
     total = None
-    for turn in range(n_tp - 1):
-        part_sum = dot(work[turn].astype(BF16), weight_refs[turn][: work.shape[2]])
+    for turn in range(1, n_tp - 1):
+        part_sum = dot(work[turn].astype(BF16), weight_refs[turn - 1][: work.shape[2]])
         total = part_sum if total is None else total + part_sum
     total_ref[...] = total
-    last_ref[...] = work[n_tp - 1].astype(BF16)
+    later_ref[0] = work[0].astype(BF16)
+    later_ref[1] = work[n_tp - 1].astype(BF16)
     for turn in range(n_tp):
         codes = notes[turn]
         power = jnp.zeros((8, LANES), F32)
@@ -244,9 +263,9 @@
             codes_ref[turn, :, piece * LANES : (piece + 1) * LANES] = spots[piece : piece + 1].astype(jnp.int32)
 
 
-def stream_kernel(total_ref, last_ref, weight_ref, stream_ref):
-    part_sum = dot(last_ref[...], weight_ref[: last_ref.shape[1]])
-    stream_ref[...] = (total_ref[...] + part_sum).astype(BF16)
+def stream_kernel(total_ref, later_ref, first_ref, last_ref, stream_ref):
+    total = total_ref[...] + dot(later_ref[0], first_ref[...])
+    stream_ref[...] = (total + dot(later_ref[1], last_ref[: later_ref.shape[2]])).astype(BF16)
 
 
 def key_value_query(stream, gain, weights):
@@ -277,20 +296,20 @@
     query_ref,
     stream_ref,
     ids_ref,
-    sub_gain_ref,
-    out_ref,
-    same_ref,
-    apart_ref,
-    back_ref,
-    gains_ref,
     *refs,
 ):
+    n_tp = codes_ref.shape[0]
+    bundle_refs, rest_refs, refs = refs[:n_tp], refs[n_tp : 2 * n_tp], refs[2 * n_tp :]
+    out_ref, same_ref, apart_ref, back_ref, weights_ref, gains_ref, spreads_ref = refs[:7]
+    refs = refs[7:]
     rows, wide = same_ref.shape
     heads = wide // SLOT
     width = heads * HEAD_DIM
     place, column = lax.axis_index("seq"), lax.axis_index("tp")
     first = place_heads(0, codes_ref, gain_ref, key_ref, value_ref, query_ref, stream_ref, rows)
     out_ref[...] = first.astype(BF16)
+    for shift in range(2):
+        spreads_ref[shift] = one_hot(spread_mask(2 * width, wide, shift * width))
 
     ids = ids_ref[pl.ds(place, 1), :].astype(jnp.int32)
     same_ref[...] = id_lanes(ids, wide, None).astype(BF16)
@@ -299,13 +318,22 @@
     for turn in range(back_ref.shape[0]):
         wanted = stored_at((column ^ turn) * share + iota((share, 1), 0), rows)
         back_ref[turn] = one_hot(wanted == iota((share, rows), 1))
-    gain = sub_gain_ref[...]
-    high = gain.astype(BF16).astype(F32)
-    mid = (gain - high).astype(BF16).astype(F32)
-    low = (gain - high) - mid
-    line = iota((16, width), 0)
-    parts = jnp.where(line == 0, high, jnp.where(line == 1, mid, jnp.where(line == 2, low, 0.0)))
-    gains_ref[...] = dot(parts.astype(BF16), one_hot(spread_mask(width, wide, 0))).astype(BF16)
+    spread = one_hot(spread_mask(width, wide, 0))
+    gap = jnp.zeros((SLOT - HEAD_DIM, weights_ref.shape[2]), BF16)
+    for turn, (ref, rest_ref) in enumerate(zip(bundle_refs, rest_refs)):
+        along = width - rest_ref.shape[0]
+        depth = ref.shape[0] - 16 - along
+        gains_ref[turn] = dot(ref[depth + along :, :width], spread).astype(BF16)
+        for head in range(heads):
+            at, to = head * HEAD_DIM, head * SLOT
+            early = min(max(along - at, 0), HEAD_DIM)
+            if early:
+                weights_ref[turn, to : to + early, :] = ref[depth + at : depth + at + early, :]
+            if early < HEAD_DIM:
+                weights_ref[turn, to + early : to + HEAD_DIM, :] = rest_ref[
+                    at + early - along : at + HEAD_DIM - along, :
+                ]
+            weights_ref[turn, to + HEAD_DIM : to + SLOT, :] = gap
     apart_refs, apart_all = refs[:-1], refs[-1]
     for ref, (level, masks) in zip(apart_refs, groups):
         count = rows >> level
@@ -360,24 +388,21 @@
     return dot_tn(one_hot(iota((IDS, count), 0) == ids), table.astype(BF16))
 
 
-def agreement(level, firsts, column, rows, total, count):
+def agreement(level, group, column, rows, total, count):
     q_on, k_on = [], []
-    for index, (head, first) in enumerate(firsts):
-        for size, lines in ((count, q_on), (total, k_on)):
+    for index, (head, first) in enumerate(group):
+        for size, on in ((count, q_on), (total, k_on)):
             line, at = iota((8, size), 0), iota((8, size), 1)
-            if size > count:
-                for step in range(1, size // count):
-                    at = at - jnp.where(iota((8, size), 1) >= step * count, count, 0)
+            for step in range(1, size // count):
+                at = at - jnp.where(iota((8, size), 1) >= step * count, count, 0)
             start = jnp.zeros((8, size), jnp.int32)
             length = jnp.zeros((8, size), jnp.int32)
             for branch in range(level, BRANCHES):
                 start = jnp.where(line == branch, head_start(branch, head, column, rows) - first, start)
                 length = jnp.where(line == branch, rows >> branch, length)
-            lines.append(jnp.where((at >= start) & (at < start + length), 1.0, 0.0))
+            on.append(jnp.where((at >= start) & (at < start + length), 1.0, 0.0))
         blank = jnp.zeros((8, count), F32)
-        q_on[index] = jnp.concatenate(
-            [q_on[index] if place == index else blank for place in range(len(firsts))], axis=1
-        )
+        q_on[index] = jnp.concatenate([q_on[index] if place == index else blank for place in range(len(group))], axis=1)
     return jnp.concatenate(q_on, axis=0).astype(BF16), jnp.concatenate(k_on, axis=0).astype(BF16)
 
 
@@ -385,19 +410,18 @@
     return jnp.concatenate([block] * times, axis=1)
 
 
-def own_kernel(packed_ref, same_ref, apart_ref, acc_ref, tops_ref, masked_ref, keys_ref, values_ref):
+def own_kernel(packed_ref, same_ref, apart_ref, spreads_ref, acc_ref, tops_ref, masked_ref, keys_ref, values_ref):
     rows, wide = masked_ref.shape
     heads = wide // SLOT
     width = heads * HEAD_DIM
     column = lax.axis_index("tp")
-    spread = one_hot(spread_mask(width, wide, 0))
     pairs = packed_ref[:, : 2 * width]
-    query = dot(packed_ref[:, 2 * width :], spread)
+    query = dot(packed_ref[:, 2 * width :], spreads_ref[0, :width])
     masked_ref[...] = (query + same_ref[...].astype(F32)).astype(BF16)
-    key = dot(pairs, one_hot(spread_mask(2 * width, wide, 0)))
+    key = dot(pairs, spreads_ref[0])
     keys_ref[...] = (key + apart_ref[...].astype(F32)).astype(BF16)
     ones = jnp.where((iota((rows, wide), 1) & (SLOT - 1)) >= HEAD_DIM, 1.0, 0.0)
-    value = dot(pairs, one_hot(spread_mask(2 * width, wide, width)))
+    value = dot(pairs, spreads_ref[1])
     values_ref[...] = (value + ones).astype(BF16)
     half = rows // 2
     slot_of = iota((half, wide), 1) >> 6
@@ -421,43 +445,60 @@
         acc_ref[start : start + half, :] = acc
 
 
-def merge_sets(level, masks, sets, acc_ref, tops_ref, query_ref, apart_ref, finish):
+def weigh_inner(weights, group, column, rows):
+    count = rows >> 1
+    length = rows >> 2
+    head = group[0][0]
+    start = head_start(2, head, column, rows) - head_start(1, head, column, rows)
+    low, high = start // LANES * LANES, up_to(start + length, LANES)
+    q_on, k_on = agreement(1, group, column, rows, count, count)
+    part = weights[start : start + length]
+    part = [part[:, :low], part[:, low:high] * dot_tn(q_on[:, start : start + length], k_on[:, low:high]), part[:, high:]]
+    part = jnp.concatenate([one for one in part if one.shape[1]], axis=1)
+    return jnp.concatenate([part, weights[length:]] if start == 0 else [weights[:start], part], axis=0)
+
+
+def merge_sets(level, masks, sets, acc_ref, tops_ref, query_ref, spreads_ref, apart_ref):
     rows, wide = query_ref.shape
-    heads = wide // SLOT
-    width = heads * HEAD_DIM
     column = lax.axis_index("tp")
     count = rows >> level
     some = min(max(1, rows // count), len(masks))
     total = some * count
-    spread_key = one_hot(spread_mask(2 * width, wide, 0))
-    spread_value = one_hot(spread_mask(2 * width, wide, width))
     slot_of = iota((count, wide), 1) >> 6
-    together = heads if heads * count * total <= 2**20 else 1
+    ones = jnp.where((iota((total, wide), 1) & (SLOT - 1)) >= HEAD_DIM, 1.0, 0.0)
+    chunks = []
+    for begin in range(0, len(masks), some):
+        pairs = jnp.concatenate([ref[...] for ref in sets[begin : begin + some]], axis=0)
+        keys = dot(pairs, spreads_ref[0]) + apart_ref[begin * count : begin * count + total, :].astype(F32)
+        values = dot(pairs, spreads_ref[1]) + ones
+        chunks.append((keys.astype(BF16), values.astype(BF16)))
+    heads = wide // SLOT
+    together = heads if heads * count * total <= 2**19 else 1
+    states = []
     for low in range(0, heads, together):
-        firsts = [(head, head_start(level, head, column, rows)) for head in range(low, low + together)]
-        q_on, k_on = agreement(level, firsts, column, rows, total, count)
-        times = dot_tn(q_on, k_on)
-        query = jnp.concatenate(
-            [
-                jnp.where(slot_of == head, query_ref[pl.ds(first, count), :], jnp.zeros((), BF16))
-                for head, first in firsts
-            ],
-            axis=0,
-        )
-        sums = jnp.concatenate([acc_ref[pl.ds(first, count), :] for _, first in firsts], axis=0)
-        tops = jnp.concatenate([tops_ref[head, pl.ds(first, count), :] for head, first in firsts], axis=0)
-        for begin in range(0, len(masks), some):
-            pairs = jnp.concatenate([ref[...] for ref in sets[begin : begin + some]], axis=0)
-            keys = dot(pairs, spread_key) + apart_ref[begin * count : begin * count + total, :].astype(F32)
-            ones = jnp.where((iota((total, wide), 1) & (SLOT - 1)) >= HEAD_DIM, 1.0, 0.0)
-            values = (dot(pairs, spread_value) + ones).astype(BF16)
-            scores = dot_nt(query, keys.astype(BF16))
+        group = [(head, head_start(level, head, column, rows)) for head in range(low, low + together)]
+        heres = [(head, pl.ds(first, count)) for head, first in group]
+        query = [jnp.where(slot_of == head, query_ref[here, :], jnp.zeros((), BF16)) for head, here in heres]
+        sums = [acc_ref[here, :] for _, here in heres]
+        tops = [tops_ref[head, here, :] for head, here in heres]
+        states.append((group, heres) + tuple(jnp.concatenate(parts, axis=0) for parts in (query, sums, tops)))
+    merged = []
+    for group, heres, query, sums, tops in states:
+        inner = level == 1 and total == count and together == 1
+        if not inner:
+            times = dot_tn(*agreement(level, group, column, rows, total, count))
+        for keys, values in chunks:
+            scores = dot_nt(query, keys)
             top = jnp.maximum(tops, jnp.max(scores, axis=1, keepdims=True))
-            weights = jnp.exp(scores - repeat(top, total // LANES)) * times
+            weights = jnp.exp(scores - repeat(top, total // LANES))
+            weights = weigh_inner(weights, group, column, rows) if inner else weights * times
             got = dot(weights.astype(BF16), values)
             sums = sums * repeat(jnp.exp(tops - top), wide // LANES) + got
             tops = top
-        finish(firsts, sums, tops)
+        for index, (head, here) in enumerate(heres):
+            part = slice(index * count, (index + 1) * count)
+            merged.append((head, here, sums[part], tops[part]))
+    return merged
 
 
 def slot_lane(values, inner):
@@ -469,29 +510,26 @@
     return dot(high, pick) + dot(low, pick)
 
 
-def near_kernel(groups, acc_ref, tops_ref, query_ref, *refs):
+def near_kernel(groups, acc_ref, tops_ref, query_ref, spreads_ref, *refs):
     apart_refs, refs = refs[: len(groups)], refs[len(groups) :]
     sums_ref, new_tops_ref = refs[-2:]
     wide = query_ref.shape[1]
-    sums_ref[...] = acc_ref[...]
-    new_tops_ref[...] = tops_ref[...]
-
-    def finish(firsts, sums, tops):
-        count = sums.shape[0] // len(firsts)
-        slot_of = iota((count, wide), 1) >> 6
-        for index, (head, first) in enumerate(firsts):
-            here, part = pl.ds(first, count), slice(index * count, (index + 1) * count)
-            sums_ref[here, :] = jnp.where(slot_of == head, sums[part], sums_ref[here, :])
-            new_tops_ref[head, here, :] = tops[part]
+    del acc_ref, tops_ref
 
     for apart_ref, (level, masks) in zip(apart_refs, groups):
-        merge_sets(level, masks, refs[: len(masks)], sums_ref, new_tops_ref, query_ref, apart_ref, finish)
+        merged = merge_sets(
+            level, masks, refs[: len(masks)], sums_ref, new_tops_ref, query_ref, spreads_ref, apart_ref
+        )
         refs = refs[len(masks) :]
-
-
-def mid_kernel(groups, acc_ref, tops_ref, query_ref, *refs):
+        for head, here, sums, tops in merged:
+            slot_of = iota(sums.shape, 1) >> 6
+            sums_ref[here, :] = jnp.where(slot_of == head, sums, sums_ref[here, :])
+            new_tops_ref[head, here, :] = tops
+
+
+def mid_kernel(groups, acc_ref, tops_ref, query_ref, spreads_ref, *refs):
     sums_ref, _, early_ref, centre_ref = refs[-4:]
-    near_kernel(groups, acc_ref, tops_ref, query_ref, *refs[:-2])
+    near_kernel(groups, acc_ref, tops_ref, query_ref, spreads_ref, *refs[:-2])
     rows, wide = query_ref.shape
     heads = wide // SLOT
     every = sums_ref[...]
@@ -503,69 +541,44 @@
     early_ref[...] = jnp.where(inner < HEAD_DIM, attn - centre, centre).astype(BF16)
 
 
-def far_kernel(n_tp, level, masks, acc_ref, tops_ref, query_ref, early_ref, centre_ref, back_ref, gains_ref, *refs):
+def far_kernel(n_tp, level, masks, acc_ref, tops_ref, query_ref, spreads_ref, early_ref, centre_ref, back_ref, *refs):
     apart_ref, refs = refs[0], refs[1:]
     sets, refs = refs[: len(masks)], refs[len(masks) :]
     out_refs, message = refs[:n_tp], refs[-1]
     message[...] = early_ref[...]
 
-    def finish(firsts, sums, tops):
-        count = sums.shape[0] // len(firsts)
-        lane = iota((count, sums.shape[1]), 1)
-        now = sums / slot_lane(sums, HEAD_DIM)
-        for index, (head, first) in enumerate(firsts):
-            here, part = pl.ds(first, count), slice(index * count, (index + 1) * count)
-            mine = (lane >= head * SLOT) & (lane < head * SLOT + HEAD_DIM)
-            new = (now[part] - centre_ref[here, :]).astype(BF16)
-            message[here, :] = jnp.where(mine, new, message[here, :])
-
-    merge_sets(level, masks, sets, acc_ref, tops_ref, query_ref, apart_ref, finish)
-    share = back_ref.shape[1]
+    merged = merge_sets(level, masks, sets, acc_ref, tops_ref, query_ref, spreads_ref, apart_ref)
+    for head, here, sums, _ in merged:
+        lane = iota(sums.shape, 1)
+        mine = (lane >= head * SLOT) & (lane < head * SLOT + HEAD_DIM)
+        new = (sums / slot_lane(sums, HEAD_DIM) - centre_ref[here, :]).astype(BF16)
+        message[here, :] = jnp.where(mine, new, message[here, :])
     final = message[...]
     for turn in range(n_tp):
-        out_refs[turn][:share] = dot(back_ref[turn], final).astype(BF16)
-        out_refs[turn][share:] = gains_ref[...]
+        out_refs[turn][...] = dot(back_ref[turn], final).astype(BF16)
 
 
 def base_kernel(n_tp, codes_ref, *refs):
-    shards, bundle_refs, rest_refs = refs[:n_tp], refs[n_tp : 2 * n_tp], refs[2 * n_tp : 3 * n_tp]
-    base_ref, weights_ref = refs[-2:]
+    shards, base_ref = refs[:n_tp], refs[n_tp]
     share = base_ref.shape[0]
-    rows = share * n_tp
-    wanted = stored_at(lax.axis_index("tp") * share + iota((share, 1), 0), rows)
+    wanted = stored_at(lax.axis_index("tp") * share + iota((share, 1), 0), share * n_tp)
     base = None
     for turn in range(n_tp):
         spots = codes_ref[turn]
         moved = dot(one_hot(wanted == spots)[:, : shards[turn].shape[0]], shards[turn][...])
         base = moved if base is None else base + moved
     base_ref[...] = base.astype(BF16)
-    wide = weights_ref.shape[1]
-    heads = wide // SLOT
-    gap = jnp.zeros((SLOT - HEAD_DIM, base_ref.shape[1]), BF16)
-    for turn, (ref, rest_ref) in enumerate(zip(bundle_refs, rest_refs)):
-        along = heads * HEAD_DIM - rest_ref.shape[0]
-        depth = ref.shape[0] - along
-        for head in range(heads):
-            at, to = head * HEAD_DIM, head * SLOT
-            early = min(max(along - at, 0), HEAD_DIM)
-            if early:
-                weights_ref[turn, to : to + early, :] = ref[depth + at : depth + at + early, :]
-            if early < HEAD_DIM:
-                weights_ref[turn, to + early : to + HEAD_DIM, :] = rest_ref[
-                    at + early - along : at + HEAD_DIM - along, :
-                ]
-            weights_ref[turn, to + HEAD_DIM : to + SLOT, :] = gap
-
-
-def mix_kernel(n_tp, base_ref, weights_ref, *refs):
+
+
+def mix_kernel(n_tp, base_ref, weights_ref, gains_ref, *refs):
     message_refs, out_ref = refs[:n_tp], refs[-1]
     share, wide = base_ref.shape[0], weights_ref.shape[1]
     features = n_tp * (wide // SLOT) * HEAD_DIM
     inside = (iota((share, wide), 1) & (SLOT - 1)) < HEAD_DIM
     parts, centres, gains = [], [], []
-    for ref in message_refs:
-        message = ref[:share].astype(F32)
-        extra = ref[share:].astype(F32)
+    for turn, ref in enumerate(message_refs):
+        message = ref[...].astype(F32)
+        extra = gains_ref[turn].astype(F32)
         parts.append(jnp.where(inside, message, 0.0))
         centres.append(message[:, HEAD_DIM : HEAD_DIM + 1])
         gains.append(extra[0:1] + extra[1:2] + extra[2:3])
@@ -629,33 +642,35 @@
     blocks, bundle, rest = call(
         functools.partial(route_kernel, n_seq, n_tp, peer),
         "route",
-        [((n_seq * n_tp, block_rows, LANES), BF16), ((tile_width + width // 3, features), BF16)]
+        [((n_seq * n_tp, block_rows, LANES), BF16), ((tile_width + width // 3 + 16, features), BF16)]
         + [((width - width // 3, features), BF16)],
-        [tile_target.reshape(-1, LANES), slide_id.reshape(-1, LANES), tiles, proj_weight, out_weight],
+        [tile_target.reshape(-1, LANES), slide_id.reshape(-1, LANES), tiles]
+        + [proj_weight, out_weight, sub_gain.reshape(1, width)],
         scratch=[
             pltpu.VMEM((rows // LANES, LANES), jnp.int32),
             pltpu.VMEM((rows // LANES, LANES), jnp.int32),
             pltpu.VMEM(tiles.shape, BF16),
             pltpu.VMEM((n_seq * n_tp, block_rows, LANES), BF16),
-            pltpu.VMEM((tile_width + width // 3, features), BF16),
+            pltpu.VMEM((tile_width + width // 3 + 16, features), BF16),
             pltpu.VMEM((width - width // 3, features), BF16),
-            pltpu.SemaphoreType.DMA((8,)),
+            pltpu.VMEM((1, width), F32),
+            pltpu.SemaphoreType.DMA((9,)),
             pltpu.SemaphoreType.DMA((n_seq,)),
         ],
         cost=3,
         vmem_bytes=ALL_VMEM_BYTES,
-        apart=(0, 1, 2, 3, 4),
+        apart=(0, 1, 2, 3, 4, 5),
         out_apart=(0, 1, 2),
     )
     received = lax.all_to_all(blocks, ("seq", "tp"), split_axis=0, concat_axis=0, tiled=True)
     bundles, rests = gather_tp(bundle), gather_tp(rest)
 
-    total, last, codes, ids = call(
+    total, later, codes, ids = call(
         functools.partial(project_kernel, n_seq, n_tp, peer),
         "project",
-        [((arriving, features), F32), ((arriving, tile_width), BF16)]
+        [((arriving, features), F32), ((2, arriving, tile_width), BF16)]
         + [((n_tp, 1, up_to(arriving, LANES)), jnp.int32), ((n_seq, rows), F32)],
-        [received] + bundles[:-1],
+        [received] + bundles[1:-1],
         scratch=[
             pltpu.VMEM(received.shape, BF16),
             pltpu.VMEM((n_tp, arriving, tile_width), F32),
@@ -668,14 +683,14 @@
         stream_kernel,
         "stream",
         [((arriving, features), BF16)],
-        [total, last, bundles[-1]],
+        [total, later, proj_weight, bundles[-1]],
         vmem_bytes=vmem_bytes,
     )
     shards = gather_tp(stream)
 
     gain = norm_gain.reshape(-1, LANES)
     weights = [gain, key_weight.T, value_weight.T, query_weight.T]
-    partial, same, apart, back, gains, *far_apart = call(
+    partial, same, apart, back, padded, gains, spreads, *far_apart = call(
         functools.partial(first_heads_kernel, groups),
         "heads_1",
         [
@@ -683,10 +698,12 @@
             ((rows, wide), BF16),
             ((rows, wide), BF16),
             ((n_tp, share, rows), BF16),
-            ((16, wide), BF16),
+            ((n_tp, wide, features), BF16),
+            ((n_tp, 16, wide), BF16),
+            ((2, 2 * width, wide), BF16),
         ]
         + [(((rows >> level) * len(masks), wide), BF16) for level, masks in groups],
-        [codes] + weights + [shards[0], ids, sub_gain.reshape(1, width)],
+        [codes] + weights + [shards[0], ids] + bundles + rests,
         scratch=[pltpu.VMEM((rows, wide), BF16)],
         vmem_bytes=vmem_bytes,
     )
@@ -714,7 +731,7 @@
         own_kernel,
         "own",
         [((rows, wide), F32), ((heads, rows, LANES), F32), ((rows, wide), BF16)],
-        [packed, same, apart],
+        [packed, same, apart, spreads],
         scratch=[pltpu.VMEM((rows, wide), BF16)] * 2,
         cost=0.1,
         vmem_bytes=vmem_bytes,
@@ -726,7 +743,8 @@
             "mid" if final else "near",
             [((rows, wide), F32), ((heads, rows, LANES), F32)]
             + ([((rows, wide), BF16), ((rows, wide), F32)] if final else []),
-            [acc, tops, masked, far_apart[index]] + sent[index],
+            [acc, tops, masked, spreads, far_apart[index]] + sent[index],
+            aliases={0: 0, 1: 1},
             cost=6,
             vmem_bytes=vmem_bytes,
         )
@@ -734,24 +752,24 @@
     messages = call(
         functools.partial(far_kernel, n_tp, *groups[-1]),
         "far",
-        [((share + 16, wide), BF16)] * n_tp,
-        [acc, tops, masked, early, centre, back, gains, far_apart[-1]] + sent[-1],
+        [((share, wide), BF16)] * n_tp,
+        [acc, tops, masked, spreads, early, centre, back, far_apart[-1]] + sent[-1],
         scratch=[pltpu.VMEM((rows, wide), BF16)],
         vmem_bytes=vmem_bytes,
     )
     arrived = [messages[0]] + [swap(messages[turn], "tp", turn) for turn in range(1, n_tp)]
-    base, padded = call(
+    (base,) = call(
         functools.partial(base_kernel, n_tp),
         "base",
-        [((share, features), BF16), ((n_tp, wide, features), BF16)],
-        [codes] + shards + bundles + rests,
+        [((share, features), BF16)],
+        [codes] + shards,
         vmem_bytes=vmem_bytes,
     )
     (result,) = call(
         functools.partial(mix_kernel, n_tp),
         "mix",
         [((share, features), BF16)],
-        [base, padded] + arrived,
+        [base, padded, gains] + arrived,
     )
     return result
 

time: 81.3 us -> 75.9 us (0.934)
  starting transfers between devices: 24.9 us -> 22.6 us
  waiting for transfers between devices: 30.7 us -> 29.5 us
  local copies, waits for them, and re-layouts: 1.14 us -> 0.06 us
    ppermute x19, starting transfers between devices: 20 us -> 17.7 us  [swap(): lax.ppermute(block, axis, [(index, index ^ mask) for index in range(count)])]
    unnamed x16 -> x14, local copies, waits for them, and re-layouts: 1.14 us -> 0.06 us
  transfers between devices with their start and end apart: 20 -> 20, of which waited for: 8 -> 8; matrix products, arithmetic and copies ran while one was open for 0% -> 0% of each run, Pallas kernels for 22% -> 21%
where the time goes in v2:
time: 75.9 us; the launch traced here: 75.7 us
  waiting for transfers between devices  29.5 us (39%)
  Pallas kernels  23.3 us (31%)
  starting transfers between devices  22.6 us (30%)
    ppermute x19, waiting for transfers between devices, swap(): lax.ppermute(block, axis, [(index, index ^ mask) for index in range(count)])  29.5 us
    pallas_call x13, Pallas kernels, call(): pl.pallas_call(kernel, name=name, out_shape=[jax.ShapeDtypeStruct(shape,...  23.3 us
    ppermute x19, starting transfers between devices, swap(): lax.ppermute(block, axis, [(index, index ^ mask) for index in range(count)])  17.7 us
    all_to_all x1, starting transfers between devices, body(): lax.all_to_all(blocks, ('seq', 'tp'), split_axis=0, concat_axis=0, tiled=...  4.89 us
  transfers between devices with their start and end apart: 20, of which 8 were waited for; matrix products, arithmetic and copies ran while one was open for 0% of the time, Pallas kernels for 21%

profile of v2, /device:TPU:0, one launch (start us, length us, event | category | flops | bytes accessed | tf_op | source)
XLA Modules:
  0.0 75.7 jit_solution(8330742282527142245)
XLA Ops:
  0.0 3.4 %route.1 = (bf16[32,80,128]{2,1,0:T(8,128)(2,1)}, bf16[464,768]{1,0:T(8,128)(2,1)}, bf16[128,768]{1,0:T(8,128)(2,1)}) custom-call(s32[6,128]{1,0:T(8,128)} %bitcast.23, s32[6,128]{1,0:T(8,128)} %bitcast.24, bf16[768,384]{1,0:T(8,128)(2,1)} %tiles_hbm.1, bf16[384,768]{1,0:T(8,128)(2,1)} %first_ref.1, bf16[192,768]{1,0:T(8,128)(2,1)} %out_weight_hbm.1, ...), custom_call_target="tpu_custom_call" | custom-call | flops 3000000000 | tf_op jit(solution)/shard_map/route/pallas_call | solution.py:68
  3.4 3.0 %collective-permute-start.1 = (bf16[464,768]{1,0:T(8,128)(2,1)}, bf16[464,768]{1,0:T(8,128)(2,1)S(1)}, u32[]{:S(2)}, u32[]{:S(2)}) collective-permute-start(bf16[464,768]{1,0:T(8,128)(2,1)} %get-tuple-element.40.refs_0_), channel_id=1, source_target_pairs={{0,2},{1,3},{2,0},{3,1},{4,6},{5,7},{6,4},{7,5},{8,10},{9,11},{10,... | collective-permute-start | bytes 2138120 | tf_op jit(solution)/shard_map/ppermute | solution.py:599
  6.4 4.9 %all-to-all-start = ((bf16[32,80,128]{2,1,0:T(8,128)(2,1)}), bf16[32,80,128]{2,1,0:T(8,128)(2,1)S(1)}, u32[]{:S(2)}, u32[]{:S(2)}) async-start(bf16[32,80,128]{2,1,0:T(8,128)(2,1)} %get-tuple-element.39), calls=%async_computation | async-start | bytes 1310720 | tf_op jit(solution)/shard_map/all_to_all | solution.py:665
  11.6 17.5 %collective-permute-done.1.refs_1_.refs_2_ = bf16[464,768]{1,0:T(8,128)(2,1)S(1)} collective-permute-done((bf16[464,768]{1,0:T(8,128)(2,1)}, bf16[464,768]{1,0:T(8,128)(2,1)S(1)}, u32[]{:S(2)}, u32[]{:S(2)}) %collective-permute-start.1) | collective-permute-done | bytes 712736 | tf_op jit(solution)/shard_map/ppermute | solution.py:599
  29.1 1.8 %collective-permute-start.7 = (bf16[128,768]{1,0:T(8,128)(2,1)}, bf16[128,768]{1,0:T(8,128)(2,1)S(1)}, u32[]{:S(2)}, u32[]{:S(2)}) collective-permute-start(bf16[128,768]{1,0:T(8,128)(2,1)} %get-tuple-element.45.refs_4_), channel_id=1, source_target_pairs={{0,2},{1,3},{2,0},{3,1},{4,6},{5,7},{6,4},{7,5},{8,10},{9,11},{10,... | collective-permute-start | bytes 589832 | tf_op jit(solution)/shard_map/ppermute | solution.py:599
  30.9 2.0 %project.1 = (f32[192,768]{1,0:T(8,128)S(1)}, bf16[2,192,384]{2,1,0:T(8,128)(2,1)S(1)}, s32[4,1,256]{2,1,0:T(1,128)S(1)}, f32[8,768]{1,0:T(8,128)S(1)}) custom-call(bf16[32,80,128]{2,1,0:T(8,128)(2,1)S(1)} %all-to-all-done.recv_hbm, bf16[464,768]{1,0:T(8,128)(2,1)S(1)} %collective-permute-done.refs_0_.refs_1_, ...), custom_call_target="tpu_custom_call" | custom-call | flops 1000000000 | tf_op jit(solution)/shard_map/project/pallas_call | solution.py:68
  34.3 2.6 %collective-permute-done.7.refs_6_ = bf16[128,768]{1,0:T(8,128)(2,1)S(1)} collective-permute-done((bf16[128,768]{1,0:T(8,128)(2,1)}, bf16[128,768]{1,0:T(8,128)(2,1)S(1)}, u32[]{:S(2)}, u32[]{:S(2)}) %collective-permute-start.7) | collective-permute-done | bytes 196640 | tf_op jit(solution)/shard_map/ppermute | solution.py:599
  36.9 1.4 %collective-permute-done.8.refs_7_ = bf16[128,768]{1,0:T(8,128)(2,1)S(1)} collective-permute-done((bf16[128,768]{1,0:T(8,128)(2,1)S(1)}, bf16[128,768]{1,0:T(8,128)(2,1)S(1)}, u32[]{:S(2)}, u32[]{:S(2)}) %collective-permute-start.8) | collective-permute-done | bytes 196640 | tf_op jit(solution)/shard_map/ppermute | solution.py:599
  38.4 2.6 %heads_1.1 = (bf16[768,576]{1,0:T(8,128)(2,1)S(1)}, bf16[768,256]{1,0:T(8,128)(2,1)S(1)}, bf16[768,256]{1,0:T(8,128)(2,1)S(1)}, bf16[4,192,768]{2,1,0:T(8,128)(2...) custom-call(s32[4,1,256]{2,1,0:T(1,128)S(1)} %get-tuple-element.41.c, ...), custom_call_target="tpu_custom_call" | custom-call | flops 1000000000 | tf_op jit(solution)/shard_map/heads_1/pallas_call | solution.py:68
  41.0 2.0 %collective-permute-done.4.refs_2_.stream_ref = bf16[192,768]{1,0:T(8,128)(2,1)S(1)} collective-permute-done((bf16[192,768]{1,0:T(8,128)(2,1)S(1)}, bf16[192,768]{1,0:T(8,128)(2,1)S(1)}, u32[]{:S(2)}, u32[]{:S(2)}) %collective-permute-start.4) | collective-permute-done | bytes 294944 | tf_op jit(solution)/shard_map/ppermute | solution.py:599
  46.1 1.8 %collective-permute-start.9 = (bf16[384,384]{1,0:T(8,128)(2,1)S(1)}, bf16[384,384]{1,0:T(8,128)(2,1)S(1)}, u32[]{:S(2)}, u32[]{:S(2)}) collective-permute-start(bf16[384,384]{1,0:T(8,128)(2,1)S(1)} %get-tuple-element.57), channel_id=1, source_target_pairs={{0,4},{4,0},{8,12},{12,8},{16,20},{20,16},{24,28},{28,24},{1,5},{5... | collective-permute-start | bytes 884744 | tf_op jit(solution)/shard_map/ppermute | solution.py:599
  47.8 2.6 %collective-permute-start.12 = (bf16[96,384]{1,0:T(8,128)(2,1)S(1)}, bf16[96,384]{1,0:T(8,128)(2,1)S(1)}, u32[]{:S(2)}, u32[]{:S(2)}) collective-permute-start(bf16[96,384]{1,0:T(8,128)(2,1)S(1)} %get-tuple-element.68), channel_id=1, source_target_pairs={{0,16},{4,20},{8,24},{12,28},{16,0},{20,4},{24,8},{28,12},{1,17},{... | collective-permute-start | bytes 221192 | tf_op jit(solution)/shard_map/ppermute | solution.py:599
  50.4 1.3 %collective-permute-start.14 = (bf16[96,384]{1,0:T(8,128)(2,1)S(1)}, bf16[96,384]{1,0:T(8,128)(2,1)S(1)}, u32[]{:S(2)}, u32[]{:S(2)}) collective-permute-start(bf16[96,384]{1,0:T(8,128)(2,1)S(1)} %get-tuple-element.68), channel_id=1, source_target_pairs={{0,24},{4,28},{8,16},{12,20},{16,8},{20,12},{24,0},{28,4},{1,25},{... | collective-permute-start | bytes 221192 | tf_op jit(solution)/shard_map/ppermute | solution.py:599
  52.0 1.8 %collective-permute-start.11 = (bf16[192,384]{1,0:T(8,128)(2,1)S(1)}, bf16[192,384]{1,0:T(8,128)(2,1)S(1)}, u32[]{:S(2)}, u32[]{:S(2)}) collective-permute-start(bf16[192,384]{1,0:T(8,128)(2,1)S(1)} %get-tuple-element.61), channel_id=1, source_target_pairs={{0,12},{4,8},{8,4},{12,0},{16,28},{20,24},{24,20},{28,16},{1,13},{... | collective-permute-start | bytes 442376 | tf_op jit(solution)/shard_map/ppermute | solution.py:599
  53.8 4.2 %own.1 = (f32[768,256]{1,0:T(8,128)S(1)}, f32[4,768,128]{2,1,0:T(8,128)S(1)}, bf16[768,256]{1,0:T(8,128)(2,1)S(1)}) custom-call(bf16[768,576]{1,0:T(8,128)(2,1)S(1)} %get-tuple-element.49.packed_ref, bf16[768,256]{1,0:T(8,128)(2,1)S(1)} %get-tuple-element.50.same_ref, bf16[768,256]{1,0:T(8,128)(2,1)S(1)} %get-tuple-element.51.apart_ref, ...), custom_call_target="tpu_custom_call" | custom-call | flops 100000000 | tf_op jit(solution)/shard_map/own/pallas_call | solution.py:68
  58.0 1.6 %collective-permute-start.13 = (bf16[96,384]{1,0:T(8,128)(2,1)S(1)}, bf16[96,384]{1,0:T(8,128)(2,1)S(1)}, u32[]{:S(2)}, u32[]{:S(2)}) collective-permute-start(bf16[96,384]{1,0:T(8,128)(2,1)S(1)} %collective-permute-done.12.refs_1_), channel_id=1, source_target_pairs={{0,4},{4,0},{8,12},{12,8},{16,20},{20,16},{24,28},{28,24},{1,5},{5... | collective-permute-start | bytes 221192 | tf_op jit(solution)/shard_map/ppermute | solution.py:599
  60.1 2.0 %near.1 = (f32[768,256]{1,0:T(8,128)S(1)}, f32[4,768,128]{2,1,0:T(8,128)S(1)}) custom-call(f32[768,256]{1,0:T(8,128)S(1)} %get-tuple-element.53.acc_ref, f32[4,768,128]{2,1,0:T(8,128)S(1)} %get-tuple-element.54.tops_ref, bf16[768,256]{1,0:T(8,128)(2,1)S(1)} %get-tuple-element.55.query_ref, ...), custom_call_target="tpu_custom_call", output_to_operand_aliasing={{0}: (0, {}), {1}: (1, {})} | custom-call | flops 6000000000 | tf_op jit(solution)/shard_map/near/pallas_call | solution.py:68
  62.4 1.8 %mid.1 = (f32[768,256]{1,0:T(8,128)S(1)}, f32[4,768,128]{2,1,0:T(8,128)S(1)}, bf16[768,256]{1,0:T(8,128)(2,1)S(1)}, f32[768,256]{1,0:T(8,128)S(1)}) custom-call(f32[768,256]{1,0:T(8,128)S(1)} %get-tuple-element.58.acc_ref, f32[4,768,128]{2,1,0:T(8,128)S(1)} %get-tuple-element.59.tops_ref, ...), custom_call_target="tpu_custom_call", output_to_operand_aliasing={{0}: (0, {}), {1}: (1, {})} | custom-call | flops 6000000000 | tf_op jit(solution)/shard_map/mid/pallas_call | solution.py:68
  64.2 1.3 %collective-permute-done.15.refs_4_ = bf16[96,384]{1,0:T(8,128)(2,1)S(1)} collective-permute-done((bf16[96,384]{1,0:T(8,128)(2,1)S(1)}, bf16[96,384]{1,0:T(8,128)(2,1)S(1)}, u32[]{:S(2)}, u32[]{:S(2)}) %collective-permute-start.15) | collective-permute-done | bytes 73760 | tf_op jit(solution)/shard_map/ppermute | solution.py:599
  65.5 1.6 %far.1 = (bf16[192,256]{1,0:T(8,128)(2,1)S(1)}, bf16[192,256]{1,0:T(8,128)(2,1)S(1)}, bf16[192,256]{1,0:T(8,128)(2,1)S(1)}, bf16[192,256]{1,0:T(8,128)(2,1)S(1)}) custom-call(f32[768,256]{1,0:T(8,128)S(1)} %get-tuple-element.62.acc_ref, f32[4,768,128]{2,1,0:T(8,128)S(1)} %get-tuple-element.63.tops_ref, bf16[768,256]{1,0:T(8,128)(2,1)S(1)} %get-tuple-element.55.query_ref, ...), custom_call_target="tpu_custom_call" | custom-call | flops 1000000000 | tf_op jit(solution)/shard_map/far/pallas_call | solution.py:68
  67.2 1.6 %collective-permute-start.17 = (bf16[192,256]{1,0:T(8,128)(2,1)S(1)}, bf16[192,256]{1,0:T(8,128)(2,1)S(1)}, u32[]{:S(2)}, u32[]{:S(2)}) collective-permute-start(bf16[192,256]{1,0:T(8,128)(2,1)S(1)} %get-tuple-element.71), channel_id=1, source_target_pairs={{0,2},{1,3},{2,0},{3,1},{4,6},{5,7},{6,4},{7,5},{8,10},{9,11},{10,... | collective-permute-start | bytes 294920 | tf_op jit(solution)/shard_map/ppermute | solution.py:599
  69.6 3.3 %collective-permute-done.17.refs_2_ = bf16[192,256]{1,0:T(8,128)(2,1)S(1)} collective-permute-done((bf16[192,256]{1,0:T(8,128)(2,1)S(1)}, bf16[192,256]{1,0:T(8,128)(2,1)S(1)}, u32[]{:S(2)}, u32[]{:S(2)}) %collective-permute-start.17) | collective-permute-done | bytes 98336 | tf_op jit(solution)/shard_map/ppermute | solution.py:599
  72.9 1.2 %collective-permute-done.18.refs_3_ = bf16[192,256]{1,0:T(8,128)(2,1)S(1)} collective-permute-done((bf16[192,256]{1,0:T(8,128)(2,1)S(1)}, bf16[192,256]{1,0:T(8,128)(2,1)S(1)}, u32[]{:S(2)}, u32[]{:S(2)}) %collective-permute-start.18) | collective-permute-done | bytes 98336 | tf_op jit(solution)/shard_map/ppermute | solution.py:599
  74.1 1.6 %mix.1 = bf16[192,768]{1,0:T(8,128)(2,1)} custom-call(bf16[192,768]{1,0:T(8,128)(2,1)S(1)} %base.1.base_ref, bf16[4,256,768]{2,1,0:T(8,128)(2,1)S(1)} %get-tuple-element.46.weights_ref, bf16[4,16,256]{2,1,0:T(8,128)(2,1)S(1)} %get-tuple-element.47.gains_ref, bf16[192,256]{1,0:T(8,128)(2,1)S(1)} %get-tuple-element.69.refs_0_, ...), custom_call_target="tpu_custom_call" | custom-call | flops 1000000000 | tf_op jit(solution)/shard_map/mix/pallas_call | solution.py:68
  (43 shorter events, 6.6 us)
Async XLA Ops:
  3.4 25.7 %collective-permute-start.1 = (bf16[464,768]{1,0:T(8,128)(2,1)}, bf16[464,768]{1,0:T(8,128)(2,1)S(1)}, u32[]{:S(2)}, u32[]{:S(2)}) collective-permute-start(bf16[464,768]{1,0:T(8,128)(2,1)} %get-tuple-element.40.refs_0_), channel_id=1, source_target_pairs={{0,2},{1,3},{2,0},{3,1},{4,6},{5,7},{6,4},{7,5},{8,10},{9,11},{10,... | collective-permute-start | bytes 2138120 | tf_op jit(solution)/shard_map/ppermute | solution.py:599
  6.4 24.5 %all-to-all-start = ((bf16[32,80,128]{2,1,0:T(8,128)(2,1)}), bf16[32,80,128]{2,1,0:T(8,128)(2,1)S(1)}, u32[]{:S(2)}, u32[]{:S(2)}) async-start(bf16[32,80,128]{2,1,0:T(8,128)(2,1)} %get-tuple-element.39), calls=%async_computation | async-start | bytes 1310720 | tf_op jit(solution)/shard_map/all_to_all | solution.py:665
  11.3 19.6 %collective-permute-start = (bf16[464,768]{1,0:T(8,128)(2,1)}, bf16[464,768]{1,0:T(8,128)(2,1)S(1)}, u32[]{:S(2)}, u32[]{:S(2)}) collective-permute-start(bf16[464,768]{1,0:T(8,128)(2,1)} %get-tuple-element.40.refs_0_), channel_id=1, source_target_pairs={{0,1},{1,0},{2,3},{3,2},{4,5},{5,4},{6,7},{7,6},{8,9},{9,8},{10,11... | collective-permute-start | bytes 2138120 | tf_op jit(solution)/shard_map/ppermute | solution.py:599
  29.1 3.9 %collective-permute-start.2 = (bf16[464,768]{1,0:T(8,128)(2,1)S(1)}, bf16[464,768]{1,0:T(8,128)(2,1)S(1)}, u32[]{:S(2)}, u32[]{:S(2)}) collective-permute-start(bf16[464,768]{1,0:T(8,128)(2,1)S(1)} %collective-permute-done.1.refs_1_.refs_2_), channel_id=1, source_target_pairs={{0,1},{1,0},{2,3},{3,2},{4,5},{5,4},{6,7},{7,6},{8,9},{9,8},{10,11... | collective-permute-start | bytes 2138120 | tf_op jit(solution)/shard_map/ppermute | solution.py:599
  29.1 7.8 %collective-permute-start.7 = (bf16[128,768]{1,0:T(8,128)(2,1)}, bf16[128,768]{1,0:T(8,128)(2,1)S(1)}, u32[]{:S(2)}, u32[]{:S(2)}) collective-permute-start(bf16[128,768]{1,0:T(8,128)(2,1)} %get-tuple-element.45.refs_4_), channel_id=1, source_target_pairs={{0,2},{1,3},{2,0},{3,1},{4,6},{5,7},{6,4},{7,5},{8,10},{9,11},{10,... | collective-permute-start | bytes 589832 | tf_op jit(solution)/shard_map/ppermute | solution.py:599
  33.0 5.3 %copy-start = (bf16[464,768]{1,0:T(8,128)(2,1)S(1)}, bf16[464,768]{1,0:T(8,128)(2,1)}, u32[]{:S(2)}) copy-start(bf16[464,768]{1,0:T(8,128)(2,1)} %get-tuple-element.40.refs_0_) | copy-start | bytes 2138116
  33.0 5.3 %copy-start.1 = (bf16[768,192]{0,1:T(8,128)(2,1)S(1)}, bf16[768,192]{0,1:T(8,128)(2,1)}, u32[]{:S(2)}) copy-start(bf16[768,192]{0,1:T(8,128)(2,1)} %param.16) | copy-start | bytes 884740
  33.0 5.3 %copy-start.2 = (bf16[768,192]{0,1:T(8,128)(2,1)S(1)}, bf16[768,192]{0,1:T(8,128)(2,1)}, u32[]{:S(2)}) copy-start(bf16[768,192]{0,1:T(8,128)(2,1)} %param.17) | copy-start | bytes 884740
  33.0 5.3 %copy-start.3 = (bf16[768,192]{0,1:T(8,128)(2,1)S(1)}, bf16[768,192]{0,1:T(8,128)(2,1)}, u32[]{:S(2)}) copy-start(bf16[768,192]{0,1:T(8,128)(2,1)} %param.15) | copy-start | bytes 884740
  33.5 9.5 %collective-permute-start.4 = (bf16[192,768]{1,0:T(8,128)(2,1)S(1)}, bf16[192,768]{1,0:T(8,128)(2,1)S(1)}, u32[]{:S(2)}, u32[]{:S(2)}) collective-permute-start(bf16[192,768]{1,0:T(8,128)(2,1)S(1)} %stream.1.refs_0_.stream_ref), channel_id=1, source_target_pairs={{0,2},{1,3},{2,0},{3,1},{4,6},{5,7},{6,4},{7,5},{8,10},{9,11},{10,... | collective-permute-start | bytes 884744 | tf_op jit(solution)/shard_map/ppermute | solution.py:599
  33.8 9.2 %collective-permute-start.3 = (bf16[192,768]{1,0:T(8,128)(2,1)S(1)}, bf16[192,768]{1,0:T(8,128)(2,1)S(1)}, u32[]{:S(2)}, u32[]{:S(2)}) collective-permute-start(bf16[192,768]{1,0:T(8,128)(2,1)S(1)} %stream.1.refs_0_.stream_ref), channel_id=1, source_target_pairs={{0,1},{1,0},{2,3},{3,2},{4,5},{5,4},{6,7},{7,6},{8,9},{9,8},{10,11... | collective-permute-start | bytes 884744 | tf_op jit(solution)/shard_map/ppermute | solution.py:599
  33.9 3.0 %collective-permute-start.6 = (bf16[128,768]{1,0:T(8,128)(2,1)S(1)}, bf16[128,768]{1,0:T(8,128)(2,1)S(1)}, u32[]{:S(2)}, u32[]{:S(2)}) collective-permute-start(bf16[128,768]{1,0:T(8,128)(2,1)S(1)} %copy-done.4), channel_id=1, source_target_pairs={{0,1},{1,0},{2,3},{3,2},{4,5},{5,4},{6,7},{7,6},{8,9},{9,8},{10,11... | collective-permute-start | bytes 589832 | tf_op jit(solution)/shard_map/ppermute | solution.py:599
  36.9 1.4 %collective-permute-start.8 = (bf16[128,768]{1,0:T(8,128)(2,1)S(1)}, bf16[128,768]{1,0:T(8,128)(2,1)S(1)}, u32[]{:S(2)}, u32[]{:S(2)}) collective-permute-start(bf16[128,768]{1,0:T(8,128)(2,1)S(1)} %collective-permute-done.7.refs_6_), channel_id=1, source_target_pairs={{0,1},{1,0},{2,3},{3,2},{4,5},{5,4},{6,7},{7,6},{8,9},{9,8},{10,11... | collective-permute-start | bytes 589832 | tf_op jit(solution)/shard_map/ppermute | solution.py:599
  43.0 1.9 %collective-permute-start.5 = (bf16[192,768]{1,0:T(8,128)(2,1)S(1)}, bf16[192,768]{1,0:T(8,128)(2,1)S(1)}, u32[]{:S(2)}, u32[]{:S(2)}) collective-permute-start(bf16[192,768]{1,0:T(8,128)(2,1)S(1)} %collective-permute-done.4.refs_2_.stream_ref), channel_id=1, source_target_pairs={{0,1},{1,0},{2,3},{3,2},{4,5},{5,4},{6,7},{7,6},{8,9},{9,8},{10,11... | collective-permute-start | bytes 884744 | tf_op jit(solution)/shard_map/ppermute | solution.py:599
  46.1 14.0 %collective-permute-start.9 = (bf16[384,384]{1,0:T(8,128)(2,1)S(1)}, bf16[384,384]{1,0:T(8,128)(2,1)S(1)}, u32[]{:S(2)}, u32[]{:S(2)}) collective-permute-start(bf16[384,384]{1,0:T(8,128)(2,1)S(1)} %get-tuple-element.57), channel_id=1, source_target_pairs={{0,4},{4,0},{8,12},{12,8},{16,20},{20,16},{24,28},{28,24},{1,5},{5... | collective-permute-start | bytes 884744 | tf_op jit(solution)/shard_map/ppermute | solution.py:599
  47.8 10.1 %collective-permute-start.12 = (bf16[96,384]{1,0:T(8,128)(2,1)S(1)}, bf16[96,384]{1,0:T(8,128)(2,1)S(1)}, u32[]{:S(2)}, u32[]{:S(2)}) collective-permute-start(bf16[96,384]{1,0:T(8,128)(2,1)S(1)} %get-tuple-element.68), channel_id=1, source_target_pairs={{0,16},{4,20},{8,24},{12,28},{16,0},{20,4},{24,8},{28,12},{1,17},{... | collective-permute-start | bytes 221192 | tf_op jit(solution)/shard_map/ppermute | solution.py:599
  50.4 9.1 %collective-permute-start.14 = (bf16[96,384]{1,0:T(8,128)(2,1)S(1)}, bf16[96,384]{1,0:T(8,128)(2,1)S(1)}, u32[]{:S(2)}, u32[]{:S(2)}) collective-permute-start(bf16[96,384]{1,0:T(8,128)(2,1)S(1)} %get-tuple-element.68), channel_id=1, source_target_pairs={{0,24},{4,28},{8,16},{12,20},{16,8},{20,12},{24,0},{28,4},{1,25},{... | collective-permute-start | bytes 221192 | tf_op jit(solution)/shard_map/ppermute | solution.py:599
  51.8 10.3 %collective-permute-start.10 = (bf16[192,384]{1,0:T(8,128)(2,1)S(1)}, bf16[192,384]{1,0:T(8,128)(2,1)S(1)}, u32[]{:S(2)}, u32[]{:S(2)}) collective-permute-start(bf16[192,384]{1,0:T(8,128)(2,1)S(1)} %get-tuple-element.61), channel_id=1, source_target_pairs={{0,8},{4,12},{8,0},{12,4},{16,24},{20,28},{24,16},{28,20},{1,9},{5... | collective-permute-start | bytes 442376 | tf_op jit(solution)/shard_map/ppermute | solution.py:599
  52.0 10.4 %collective-permute-start.11 = (bf16[192,384]{1,0:T(8,128)(2,1)S(1)}, bf16[192,384]{1,0:T(8,128)(2,1)S(1)}, u32[]{:S(2)}, u32[]{:S(2)}) collective-permute-start(bf16[192,384]{1,0:T(8,128)(2,1)S(1)} %get-tuple-element.61), channel_id=1, source_target_pairs={{0,12},{4,8},{8,4},{12,0},{16,28},{20,24},{24,20},{28,16},{1,13},{... | collective-permute-start | bytes 442376 | tf_op jit(solution)/shard_map/ppermute | solution.py:599
  58.0 6.2 %collective-permute-start.13 = (bf16[96,384]{1,0:T(8,128)(2,1)S(1)}, bf16[96,384]{1,0:T(8,128)(2,1)S(1)}, u32[]{:S(2)}, u32[]{:S(2)}) collective-permute-start(bf16[96,384]{1,0:T(8,128)(2,1)S(1)} %collective-permute-done.12.refs_1_), channel_id=1, source_target_pairs={{0,4},{4,0},{8,12},{12,8},{16,20},{20,16},{24,28},{28,24},{1,5},{5... | collective-permute-start | bytes 221192 | tf_op jit(solution)/shard_map/ppermute | solution.py:599
  59.5 5.9 %collective-permute-start.15 = (bf16[96,384]{1,0:T(8,128)(2,1)S(1)}, bf16[96,384]{1,0:T(8,128)(2,1)S(1)}, u32[]{:S(2)}, u32[]{:S(2)}) collective-permute-start(bf16[96,384]{1,0:T(8,128)(2,1)S(1)} %collective-permute-done.14.refs_3_), channel_id=1, source_target_pairs={{0,4},{4,0},{8,12},{12,8},{16,20},{20,16},{24,28},{28,24},{1,5},{5... | collective-permute-start | bytes 221192 | tf_op jit(solution)/shard_map/ppermute | solution.py:599
  67.1 2.5 %collective-permute-start.16 = (bf16[192,256]{1,0:T(8,128)(2,1)S(1)}, bf16[192,256]{1,0:T(8,128)(2,1)S(1)}, u32[]{:S(2)}, u32[]{:S(2)}) collective-permute-start(bf16[192,256]{1,0:T(8,128)(2,1)S(1)} %get-tuple-element.70), channel_id=1, source_target_pairs={{0,1},{1,0},{2,3},{3,2},{4,5},{5,4},{6,7},{7,6},{8,9},{9,8},{10,11... | collective-permute-start | bytes 294920 | tf_op jit(solution)/shard_map/ppermute | solution.py:599
  67.2 5.7 %collective-permute-start.17 = (bf16[192,256]{1,0:T(8,128)(2,1)S(1)}, bf16[192,256]{1,0:T(8,128)(2,1)S(1)}, u32[]{:S(2)}, u32[]{:S(2)}) collective-permute-start(bf16[192,256]{1,0:T(8,128)(2,1)S(1)} %get-tuple-element.71), channel_id=1, source_target_pairs={{0,2},{1,3},{2,0},{3,1},{4,6},{5,7},{6,4},{7,5},{8,10},{9,11},{10,... | collective-permute-start | bytes 294920 | tf_op jit(solution)/shard_map/ppermute | solution.py:599
  68.8 5.3 %collective-permute-start.18 = (bf16[192,256]{1,0:T(8,128)(2,1)S(1)}, bf16[192,256]{1,0:T(8,128)(2,1)S(1)}, u32[]{:S(2)}, u32[]{:S(2)}) collective-permute-start(bf16[192,256]{1,0:T(8,128)(2,1)S(1)} %get-tuple-element.72), channel_id=1, source_target_pairs={{0,3},{1,2},{2,1},{3,0},{4,7},{5,6},{6,5},{7,4},{8,11},{9,10},{10,... | collective-permute-start | bytes 294920 | tf_op jit(solution)/shard_map/ppermute | solution.py:599
  (3 other events, 8.3 us)

commit v3 on v2

--- a/solution.py
+++ b/solution.py
@@ -17,6 +17,7 @@
 EPS = 1e-05
 BF16 = jnp.bfloat16
 F32 = jnp.float32
+HINT_COST = 1
 VMEM_BYTES = 16 * 1024 * 1024
 LARGE_VMEM_BYTES = 48 * 1024 * 1024
 ALL_VMEM_BYTES = 56 * 1024 * 1024
@@ -89,33 +90,18 @@
     target_hbm,
     slide_hbm,
     tiles_hbm,
-    proj_hbm,
-    out_weight_hbm,
-    gain_hbm,
     out_hbm,
-    bundle_hbm,
-    rest_hbm,
     target_ref,
     slide_ref,
     tiles_ref,
     out_ref,
-    bundle_ref,
-    rest_ref,
-    gain_ref,
     sems,
     out_sems,
 ):
-    depth = proj_hbm.shape[0]
-    width = out_weight_hbm.shape[0]
-    along = width - rest_ref.shape[0]
     fetches = [
         pltpu.make_async_copy(target_hbm, target_ref, sems.at[0]),
         pltpu.make_async_copy(slide_hbm, slide_ref, sems.at[1]),
         pltpu.make_async_copy(tiles_hbm, tiles_ref, sems.at[2]),
-        pltpu.make_async_copy(proj_hbm, bundle_ref.at[pl.ds(0, depth)], sems.at[3]),
-        pltpu.make_async_copy(out_weight_hbm.at[pl.ds(0, along)], bundle_ref.at[pl.ds(depth, along)], sems.at[4]),
-        pltpu.make_async_copy(out_weight_hbm.at[pl.ds(along, rest_ref.shape[0])], rest_ref, sems.at[5]),
-        pltpu.make_async_copy(gain_hbm, gain_ref, sems.at[6]),
     ]
     for fetch in fetches:
         fetch.start()
@@ -167,22 +153,7 @@
     fetches[1].wait()
     ids = dot_nt(jnp.where(held, one_row(slide_ref).astype(F32), 0.0).astype(BF16), kept_lane)
     notes = coded + ids
-    for fetch in fetches[3:]:
-        fetch.wait()
-    gain = gain_ref[...]
-    high = gain.astype(BF16).astype(F32)
-    mid = (gain - high).astype(BF16).astype(F32)
-    low = (gain - high) - mid
-    line = iota((16, width), 0)
-    parts = jnp.where(line == 0, high, jnp.where(line == 1, mid, jnp.where(line == 2, low, 0.0)))
-    bundle_ref[depth + along :] = jnp.zeros((16, bundle_ref.shape[1]), BF16)
-    bundle_ref[depth + along :, :width] = parts.astype(BF16)
-    stores = [
-        pltpu.make_async_copy(bundle_ref, bundle_hbm, sems.at[7]),
-        pltpu.make_async_copy(rest_ref, rest_hbm, sems.at[8]),
-    ]
-    for store in stores:
-        store.start()
+    stores = []
     fetches[2].wait()
     picked = dot(chooser, tiles_ref[...])
     pad = out_hbm.shape[1] - chunks * sub_pad - 8
@@ -211,9 +182,21 @@
     return (inner < HEAD_DIM) & (row == (lane >> 6) * HEAD_DIM + inner)
 
 
-def project_kernel(n_seq, n_tp, peer, recv_hbm, *refs):
-    total_ref, later_ref, codes_ref, ids_ref, recv_ref, work, sems = refs[n_tp - 2 :]
-    weight_refs = refs[: n_tp - 2]
+def hint_kernel(weight_ref, out_ref):
+    out_ref[...] = weight_ref[: out_ref.shape[0], : out_ref.shape[1]]
+
+
+def scale_kernel(gain_ref, weight_ref, scaled_ref):
+    width = weight_ref.shape[0]
+    same = iota((width, width), 0) == iota((width, width), 1)
+    gain = jnp.sum(jnp.where(same, gain_ref[...], 0.0), axis=1, keepdims=True)
+    scaled_ref[...] = (weight_ref[...].astype(F32) * gain).astype(BF16)
+
+
+def project_kernel(n_seq, n_tp, peer, recv_hbm, early_ref, beside_ref, *refs):
+    del early_ref, beside_ref
+    weight_refs = refs[: n_tp - 1]
+    total_ref, later_ref, codes_ref, ids_ref, recv_ref, work, sems = refs[n_tp - 1 :]
     fetches = []
     for source in range(n_seq):
         some = pl.ds(source * n_tp, n_tp)
@@ -244,12 +227,11 @@
                 pieces.append(note[code_rows + piece : code_rows + piece + 1, :length])
         ids_ref[source : source + 1, :] = jnp.concatenate(pieces, axis=1)
     total = None
-    for turn in range(1, n_tp - 1):
-        part_sum = dot(work[turn].astype(BF16), weight_refs[turn - 1][: work.shape[2]])
+    for turn in range(1, n_tp):
+        part_sum = dot(work[turn].astype(BF16), weight_refs[turn - 1][...])
         total = part_sum if total is None else total + part_sum
     total_ref[...] = total
-    later_ref[0] = work[0].astype(BF16)
-    later_ref[1] = work[n_tp - 1].astype(BF16)
+    later_ref[...] = work[0].astype(BF16)
     for turn in range(n_tp):
         codes = notes[turn]
         power = jnp.zeros((8, LANES), F32)
@@ -263,9 +245,8 @@
             codes_ref[turn, :, piece * LANES : (piece + 1) * LANES] = spots[piece : piece + 1].astype(jnp.int32)
 
 
-def stream_kernel(total_ref, later_ref, first_ref, last_ref, stream_ref):
-    total = total_ref[...] + dot(later_ref[0], first_ref[...])
-    stream_ref[...] = (total + dot(later_ref[1], last_ref[: later_ref.shape[2]])).astype(BF16)
+def stream_kernel(total_ref, later_ref, weight_ref, stream_ref):
+    stream_ref[...] = (total_ref[...] + dot(later_ref[...], weight_ref[...])).astype(BF16)
 
 
 def key_value_query(stream, gain, weights):
@@ -298,10 +279,8 @@
     ids_ref,
     *refs,
 ):
-    n_tp = codes_ref.shape[0]
-    bundle_refs, rest_refs, refs = refs[:n_tp], refs[n_tp : 2 * n_tp], refs[2 * n_tp :]
-    out_ref, same_ref, apart_ref, back_ref, weights_ref, gains_ref, spreads_ref = refs[:7]
-    refs = refs[7:]
+    out_ref, same_ref, apart_ref, back_ref, spreads_ref = refs[:5]
+    refs = refs[5:]
     rows, wide = same_ref.shape
     heads = wide // SLOT
     width = heads * HEAD_DIM
@@ -318,22 +297,6 @@
     for turn in range(back_ref.shape[0]):
         wanted = stored_at((column ^ turn) * share + iota((share, 1), 0), rows)
         back_ref[turn] = one_hot(wanted == iota((share, rows), 1))
-    spread = one_hot(spread_mask(width, wide, 0))
-    gap = jnp.zeros((SLOT - HEAD_DIM, weights_ref.shape[2]), BF16)
-    for turn, (ref, rest_ref) in enumerate(zip(bundle_refs, rest_refs)):
-        along = width - rest_ref.shape[0]
-        depth = ref.shape[0] - 16 - along
-        gains_ref[turn] = dot(ref[depth + along :, :width], spread).astype(BF16)
-        for head in range(heads):
-            at, to = head * HEAD_DIM, head * SLOT
-            early = min(max(along - at, 0), HEAD_DIM)
-            if early:
-                weights_ref[turn, to : to + early, :] = ref[depth + at : depth + at + early, :]
-            if early < HEAD_DIM:
-                weights_ref[turn, to + early : to + HEAD_DIM, :] = rest_ref[
-                    at + early - along : at + HEAD_DIM - along, :
-                ]
-            weights_ref[turn, to + HEAD_DIM : to + SLOT, :] = gap
     apart_refs, apart_all = refs[:-1], refs[-1]
     for ref, (level, masks) in zip(apart_refs, groups):
         count = rows >> level
@@ -348,11 +311,12 @@
             ref[index * count : (index + 1) * count, :] = chosen
 
 
-def more_heads_kernel(
-    turn, codes_ref, gain_ref, key_ref, value_ref, query_ref, stream_ref, before_ref, out_ref
-):
+def more_heads_kernel(turn, codes_ref, gain_ref, key_ref, value_ref, query_ref, stream_ref, before_ref, *refs):
+    given_ref, out_ref, on_ref = refs if len(refs) == 3 else (None, refs[-1], None)
     more = place_heads(turn, codes_ref, gain_ref, key_ref, value_ref, query_ref, stream_ref, out_ref.shape[0])
     out_ref[...] = (before_ref[...].astype(F32) + more).astype(BF16)
+    if on_ref is not None:
+        on_ref[...] = given_ref[...]
 
 
 def last_heads_kernel(
@@ -559,7 +523,8 @@
 
 
 def base_kernel(n_tp, codes_ref, *refs):
-    shards, base_ref = refs[:n_tp], refs[n_tp]
+    shards, part_refs = refs[:n_tp], refs[n_tp : 2 * n_tp]
+    base_ref, weights_ref = refs[-2:]
     share = base_ref.shape[0]
     wanted = stored_at(lax.axis_index("tp") * share + iota((share, 1), 0), share * n_tp)
     base = None
@@ -568,20 +533,25 @@
         moved = dot(one_hot(wanted == spots)[:, : shards[turn].shape[0]], shards[turn][...])
         base = moved if base is None else base + moved
     base_ref[...] = base.astype(BF16)
-
-
-def mix_kernel(n_tp, base_ref, weights_ref, gains_ref, *refs):
+    heads = weights_ref.shape[1] // SLOT
+    gap = jnp.zeros((SLOT - HEAD_DIM, weights_ref.shape[2]), BF16)
+    for turn, ref in enumerate(part_refs):
+        for head in range(heads):
+            at, to = head * HEAD_DIM, head * SLOT
+            weights_ref[turn, to : to + HEAD_DIM, :] = ref[at : at + HEAD_DIM, :]
+            weights_ref[turn, to + HEAD_DIM : to + SLOT, :] = gap
+
+
+def mix_kernel(n_tp, base_ref, weights_ref, *refs):
     message_refs, out_ref = refs[:n_tp], refs[-1]
     share, wide = base_ref.shape[0], weights_ref.shape[1]
     features = n_tp * (wide // SLOT) * HEAD_DIM
     inside = (iota((share, wide), 1) & (SLOT - 1)) < HEAD_DIM
-    parts, centres, gains = [], [], []
-    for turn, ref in enumerate(message_refs):
+    parts, centres = [], []
+    for ref in message_refs:
         message = ref[...].astype(F32)
-        extra = gains_ref[turn].astype(F32)
         parts.append(jnp.where(inside, message, 0.0))
         centres.append(message[:, HEAD_DIM : HEAD_DIM + 1])
-        gains.append(extra[0:1] + extra[1:2] + extra[2:3])
     each = features // n_tp
     sums = [jnp.sum(part, axis=1, keepdims=True) + centre * each for part, centre in zip(parts, centres)]
     mean = sum(sums) * (1.0 / features)
@@ -589,8 +559,8 @@
     spread = jnp.sum(sum(part * part for part in parts), axis=1, keepdims=True) * (1.0 / features)
     factor = lax.rsqrt(spread + EPS)
     total = base_ref[...].astype(F32)
-    for turn, (part, gain) in enumerate(zip(parts, gains)):
-        total = total + dot((part * factor * gain).astype(BF16), weights_ref[turn])
+    for turn, part in enumerate(parts):
+        total = total + dot((part * factor).astype(BF16), weights_ref[turn])
     out_ref[...] = total.astype(BF16)
 
 
@@ -639,38 +609,38 @@
             groups.append((level, masks))
 
     vmem_bytes = VMEM_BYTES if n_seq <= 8 else LARGE_VMEM_BYTES
-    blocks, bundle, rest = call(
+    (blocks,) = call(
         functools.partial(route_kernel, n_seq, n_tp, peer),
         "route",
-        [((n_seq * n_tp, block_rows, LANES), BF16), ((tile_width + width // 3 + 16, features), BF16)]
-        + [((width - width // 3, features), BF16)],
-        [tile_target.reshape(-1, LANES), slide_id.reshape(-1, LANES), tiles]
-        + [proj_weight, out_weight, sub_gain.reshape(1, width)],
+        [((n_seq * n_tp, block_rows, LANES), BF16)],
+        [tile_target.reshape(-1, LANES), slide_id.reshape(-1, LANES), tiles],
         scratch=[
             pltpu.VMEM((rows // LANES, LANES), jnp.int32),
             pltpu.VMEM((rows // LANES, LANES), jnp.int32),
             pltpu.VMEM(tiles.shape, BF16),
             pltpu.VMEM((n_seq * n_tp, block_rows, LANES), BF16),
-            pltpu.VMEM((tile_width + width // 3 + 16, features), BF16),
-            pltpu.VMEM((width - width // 3, features), BF16),
-            pltpu.VMEM((1, width), F32),
-            pltpu.SemaphoreType.DMA((9,)),
+            pltpu.SemaphoreType.DMA((3,)),
             pltpu.SemaphoreType.DMA((n_seq,)),
         ],
         cost=3,
         vmem_bytes=ALL_VMEM_BYTES,
-        apart=(0, 1, 2, 3, 4, 5),
-        out_apart=(0, 1, 2),
+        apart=(0, 1, 2),
+        out_apart=(0,),
     )
     received = lax.all_to_all(blocks, ("seq", "tp"), split_axis=0, concat_axis=0, tiled=True)
-    bundles, rests = gather_tp(bundle), gather_tp(rest)
-
+    proj_parts = gather_tp(proj_weight)
+    (early,) = call(hint_kernel, "hint", [((16, LANES), BF16)], [proj_parts[-1]], cost=HINT_COST)
+    (scaled,) = call(
+        scale_kernel, "scale", [((width, features), BF16)], [sub_gain.reshape(1, width), out_weight], cost=1
+    )
+
+    beside = swap(scaled, "tp", 1)
     total, later, codes, ids = call(
         functools.partial(project_kernel, n_seq, n_tp, peer),
         "project",
-        [((arriving, features), F32), ((2, arriving, tile_width), BF16)]
+        [((arriving, features), F32), ((arriving, tile_width), BF16)]
         + [((n_tp, 1, up_to(arriving, LANES)), jnp.int32), ((n_seq, rows), F32)],
-        [received] + bundles[1:-1],
+        [received, early, beside] + proj_parts[1:],
         scratch=[
             pltpu.VMEM(received.shape, BF16),
             pltpu.VMEM((n_tp, arriving, tile_width), F32),
@@ -683,14 +653,14 @@
         stream_kernel,
         "stream",
         [((arriving, features), BF16)],
-        [total, later, proj_weight, bundles[-1]],
+        [total, later, proj_weight],
         vmem_bytes=vmem_bytes,
     )
     shards = gather_tp(stream)
 
     gain = norm_gain.reshape(-1, LANES)
     weights = [gain, key_weight.T, value_weight.T, query_weight.T]
-    partial, same, apart, back, padded, gains, spreads, *far_apart = call(
+    partial, same, apart, back, spreads, *far_apart = call(
         functools.partial(first_heads_kernel, groups),
         "heads_1",
         [
@@ -698,24 +668,27 @@
             ((rows, wide), BF16),
             ((rows, wide), BF16),
             ((n_tp, share, rows), BF16),
-            ((n_tp, wide, features), BF16),
-            ((n_tp, 16, wide), BF16),
             ((2, 2 * width, wide), BF16),
         ]
         + [(((rows >> level) * len(masks), wide), BF16) for level, masks in groups],
-        [codes] + weights + [shards[0], ids] + bundles + rests,
+        [codes] + weights + [shards[0], ids],
         scratch=[pltpu.VMEM((rows, wide), BF16)],
         vmem_bytes=vmem_bytes,
     )
+    across = swap(scaled, "tp", 2)
+    out_parts = [scaled, beside]
     for turn in range(1, n_tp - 1):
-        (partial,) = call(
+        given = [across] if turn == 1 else out_parts[3:]
+        partial, *on = call(
             functools.partial(more_heads_kernel, turn),
             "heads_2",
-            [((rows, 3 * width), BF16)],
-            [codes] + weights + [shards[turn], partial],
+            [((rows, 3 * width), BF16)] + [((width, features), BF16)] * (turn == 1),
+            [codes] + weights + [shards[turn], partial] + given,
             cost=10 if turn == n_tp - 2 else 1,
             vmem_bytes=vmem_bytes,
         )
+        if on:
+            out_parts += on + [swap(on[0], "tp", 1)]
     packed, *sets = call(
         functools.partial(last_heads_kernel, n_tp - 1, [level for level, _ in groups]),
         "heads_3",
@@ -758,18 +731,18 @@
         vmem_bytes=vmem_bytes,
     )
     arrived = [messages[0]] + [swap(messages[turn], "tp", turn) for turn in range(1, n_tp)]
-    (base,) = call(
+    base, padded = call(
         functools.partial(base_kernel, n_tp),
         "base",
-        [((share, features), BF16)],
-        [codes] + shards,
+        [((share, features), BF16), ((n_tp, wide, features), BF16)],
+        [codes] + shards + out_parts,
         vmem_bytes=vmem_bytes,
     )
     (result,) = call(
         functools.partial(mix_kernel, n_tp),
         "mix",
         [((share, features), BF16)],
-        [base, padded, gains] + arrived,
+        [base, padded] + arrived,
     )
     return result
 

time: 75.9 us -> 73 us (0.962)
  waiting for transfers between devices: 29.5 us -> 22.5 us
  Pallas kernels: 23.3 us -> 26.1 us
  starting transfers between devices: 22.6 us -> 23.8 us
    ppermute x19, waiting for transfers between devices: 29.5 us -> 17.8 us  [swap(): lax.ppermute(block, axis, [(index, index ^ mask) for index in range(count)])]
    all_to_all x1, waiting for transfers between devices: 0.01 us -> 4.76 us  [body(): lax.all_to_all(blocks, ('seq', 'tp'), split_axis=0, concat_axis=0, tiled=...]
    pallas_call x13 -> x15, Pallas kernels: 23.3 us -> 26.1 us  [call(): pl.pallas_call(kernel, name=name, out_shape=[jax.ShapeDtypeStruct(shape,...]
    ppermute x19, starting transfers between devices: 17.7 us -> 18.9 us  [swap(): lax.ppermute(block, axis, [(index, index ^ mask) for index in range(count)])]
  transfers between devices with their start and end apart: 20 -> 20, of which waited for: 8 -> 7; matrix products, arithmetic and copies ran while one was open for 0% -> 0% of each run, Pallas kernels for 21% -> 30%
where the time goes in v3:
time: 73 us; the launch traced here: 72.7 us
  Pallas kernels  26.1 us (36%)
  starting transfers between devices  23.8 us (33%)
  waiting for transfers between devices  22.5 us (31%)
    pallas_call x15, Pallas kernels, call(): pl.pallas_call(kernel, name=name, out_shape=[jax.ShapeDtypeStruct(shape,...  26.1 us
    ppermute x19, starting transfers between devices, swap(): lax.ppermute(block, axis, [(index, index ^ mask) for index in range(count)])  18.9 us
    ppermute x19, waiting for transfers between devices, swap(): lax.ppermute(block, axis, [(index, index ^ mask) for index in range(count)])  17.8 us
    all_to_all x1, starting transfers between devices, body(): lax.all_to_all(blocks, ('seq', 'tp'), split_axis=0, concat_axis=0, tiled=...  4.9 us
    all_to_all x1, waiting for transfers between devices, body(): lax.all_to_all(blocks, ('seq', 'tp'), split_axis=0, concat_axis=0, tiled=...  4.76 us
  transfers between devices with their start and end apart: 20, of which 7 were waited for; matrix products, arithmetic and copies ran while one was open for 0% of the time, Pallas kernels for 30%

profile of v3, /device:TPU:0, one launch (start us, length us, event | category | flops | bytes accessed | tf_op | source)
XLA Modules:
  0.0 72.7 jit_solution(4759721423783363311)
XLA Ops:
  0.0 3.0 %collective-permute-start = (bf16[384,768]{1,0:T(8,128)(2,1)}, bf16[384,768]{1,0:T(8,128)(2,1)S(1)}, u32[]{:S(2)}, u32[]{:S(2)}) collective-permute-start(bf16[384,768]{1,0:T(8,128)(2,1)} %weight_ref.3), channel_id=1, source_target_pairs={{0,2},{1,3},{2,0},{3,1},{4,6},{5,7},{6,4},{7,5},{8,10},{9,11},{10,... | collective-permute-start | bytes 1769480 | tf_op jit(solution)/shard_map/ppermute | solution.py:569
  3.0 3.4 %route.1 = bf16[32,80,128]{2,1,0:T(8,128)(2,1)} custom-call(s32[6,128]{1,0:T(8,128)} %bitcast.24, s32[6,128]{1,0:T(8,128)} %bitcast.25, bf16[768,384]{1,0:T(8,128)(2,1)} %tiles_hbm.1), custom_call_target="tpu_custom_call" | custom-call | flops 3000000000 | tf_op jit(solution)/shard_map/route/pallas_call | solution.py:69
  6.4 4.9 %all-to-all-start = ((bf16[32,80,128]{2,1,0:T(8,128)(2,1)}), bf16[32,80,128]{2,1,0:T(8,128)(2,1)S(1)}, u32[]{:S(2)}, u32[]{:S(2)}) async-start(bf16[32,80,128]{2,1,0:T(8,128)(2,1)} %route.1), calls=%async_computation | async-start | bytes 1310720 | tf_op jit(solution)/shard_map/all_to_all | solution.py:630
  11.3 9.5 %collective-permute-done.refs_1_ = bf16[384,768]{1,0:T(8,128)(2,1)S(1)} collective-permute-done((bf16[384,768]{1,0:T(8,128)(2,1)}, bf16[384,768]{1,0:T(8,128)(2,1)S(1)}, u32[]{:S(2)}, u32[]{:S(2)}) %collective-permute-start) | collective-permute-done | bytes 589856 | tf_op jit(solution)/shard_map/ppermute | solution.py:569
  22.2 2.3 %collective-permute-start.7 = (bf16[192,768]{1,0:T(8,128)(2,1)}, bf16[192,768]{1,0:T(8,128)(2,1)}, u32[]{:S(2)}, u32[]{:S(2)}) collective-permute-start(bf16[192,768]{1,0:T(8,128)(2,1)} %scale.1.refs_4_), channel_id=1, source_target_pairs={{0,2},{1,3},{2,0},{3,1},{4,6},{5,7},{6,4},{7,5},{8,10},{9,11},{10,... | collective-permute-start | bytes 884744 | tf_op jit(solution)/shard_map/ppermute | solution.py:569
  24.5 4.8 %all-to-all-done.recv_hbm = bf16[32,80,128]{2,1,0:T(8,128)(2,1)S(1)} async-done(((bf16[32,80,128]{2,1,0:T(8,128)(2,1)}), bf16[32,80,128]{2,1,0:T(8,128)(2,1)S(1)}, u32[]{:S(2)}, u32[]{:S(2)}) %all-to-all-start) | async-done | bytes 655392 | tf_op jit(solution)/shard_map/all_to_all | solution.py:630
  29.2 2.1 %project.1 = (f32[192,768]{1,0:T(8,128)S(1)}, bf16[192,384]{1,0:T(8,128)(2,1)S(1)}, s32[4,1,256]{2,1,0:T(1,128)S(1)}, f32[8,768]{1,0:T(8,128)S(1)}) custom-call(bf16[32,80,128]{2,1,0:T(8,128)(2,1)S(1)} %all-to-all-done.recv_hbm, bf16[16,128]{1,0:T(8,128)(2,1)S(1)} %hint.1.early_ref, bf16[192,768]{1,0:T(8,128)(2,1)S(1)} %collective-permute-done.2.beside_ref.refs_5_, ...), custom_call_target="tpu_custom_call" | custom-call | flops 1000000000 | tf_op jit(solution)/shard_map/project/pallas_call | solution.py:69
  31.9 1.6 %collective-permute-start.5 = (bf16[192,768]{1,0:T(8,128)(2,1)S(1)}, bf16[192,768]{1,0:T(8,128)(2,1)S(1)}, u32[]{:S(2)}, u32[]{:S(2)}) collective-permute-start(bf16[192,768]{1,0:T(8,128)(2,1)S(1)} %stream.1.stream_ref.refs_0_), channel_id=1, source_target_pairs={{0,2},{1,3},{2,0},{3,1},{4,6},{5,7},{6,4},{7,5},{8,10},{9,11},{10,... | collective-permute-start | bytes 884744 | tf_op jit(solution)/shard_map/ppermute | solution.py:569
  33.5 2.6 %heads_1.1 = (bf16[768,576]{1,0:T(8,128)(2,1)S(1)}, bf16[768,256]{1,0:T(8,128)(2,1)S(1)}, bf16[768,256]{1,0:T(8,128)(2,1)S(1)}, bf16[4,192,768]{2,1,0:T(8,128)(2...) custom-call(s32[4,1,256]{2,1,0:T(1,128)S(1)} %get-tuple-element.38.c, ...), custom_call_target="tpu_custom_call" | custom-call | flops 1000000000 | tf_op jit(solution)/shard_map/heads_1/pallas_call | solution.py:69
  36.1 1.9 %heads_2.2 = (bf16[768,576]{1,0:T(8,128)(2,1)S(1)}, bf16[192,768]{1,0:T(8,128)(2,1)S(1)}) custom-call(s32[4,1,256]{2,1,0:T(1,128)S(1)} %get-tuple-element.38.codes_ref, f32[6,128]{1,0:T(8,128)S(1)} %bitcast.20, bf16[192,768]{1,0:T(8,128)(2,1)S(1)} %bitcast.8, bf16[192,768]{1,0:T(8,128)(2,1)S(1)} %bitcast.12, bf16[192,768]{1,0:T(8,128)(2,1)S(1)} %bitcast.16, ...), custom_call_target="tpu_custom_call" | custom-call | flops 1000000000 | tf_op jit(solution)/shard_map/heads_2/pallas_call | solution.py:69
  38.1 3.1 %collective-permute-done.5.refs_2_.stream_ref = bf16[192,768]{1,0:T(8,128)(2,1)S(1)} collective-permute-done((bf16[192,768]{1,0:T(8,128)(2,1)S(1)}, bf16[192,768]{1,0:T(8,128)(2,1)S(1)}, u32[]{:S(2)}, u32[]{:S(2)}) %collective-permute-start.5) | collective-permute-done | bytes 294944 | tf_op jit(solution)/shard_map/ppermute | solution.py:569
  42.8 1.1 %heads_3.1 = (bf16[768,576]{1,0:T(8,128)(2,1)S(1)}, bf16[384,384]{1,0:T(8,128)(2,1)S(1)}, bf16[192,384]{1,0:T(8,128)(2,1)S(1)}, bf16[96,384]{1,0:T(8,128)(2,1)S(1)}) custom-call(s32[4,1,256]{2,1,0:T(1,128)S(1)} %get-tuple-element.38.codes_ref, f32[6,128]{1,0:T(8,128)S(1)} %bitcast.22, bf16[192,768]{1,0:T(8,128)(2,1)S(1)} %bitcast.10, ...), custom_call_target="tpu_custom_call" | custom-call | flops 1000000000 | tf_op jit(solution)/shard_map/heads_3/pallas_call | solution.py:69
  43.9 1.5 %collective-permute-start.9 = (bf16[384,384]{1,0:T(8,128)(2,1)S(1)}, bf16[384,384]{1,0:T(8,128)(2,1)S(1)}, u32[]{:S(2)}, u32[]{:S(2)}) collective-permute-start(bf16[384,384]{1,0:T(8,128)(2,1)S(1)} %get-tuple-element.55), channel_id=1, source_target_pairs={{0,4},{4,0},{8,12},{12,8},{16,20},{20,16},{24,28},{28,24},{1,5},{5... | collective-permute-start | bytes 884744 | tf_op jit(solution)/shard_map/ppermute | solution.py:569
  45.6 3.2 %collective-permute-start.14 = (bf16[96,384]{1,0:T(8,128)(2,1)S(1)}, bf16[96,384]{1,0:T(8,128)(2,1)S(1)}, u32[]{:S(2)}, u32[]{:S(2)}) collective-permute-start(bf16[96,384]{1,0:T(8,128)(2,1)S(1)} %get-tuple-element.66), channel_id=1, source_target_pairs={{0,24},{4,28},{8,16},{12,20},{16,8},{20,12},{24,0},{28,4},{1,25},{... | collective-permute-start | bytes 221192 | tf_op jit(solution)/shard_map/ppermute | solution.py:569
  48.9 2.4 %collective-permute-start.11 = (bf16[192,384]{1,0:T(8,128)(2,1)S(1)}, bf16[192,384]{1,0:T(8,128)(2,1)S(1)}, u32[]{:S(2)}, u32[]{:S(2)}) collective-permute-start(bf16[192,384]{1,0:T(8,128)(2,1)S(1)} %get-tuple-element.59), channel_id=1, source_target_pairs={{0,12},{4,8},{8,4},{12,0},{16,28},{20,24},{24,20},{28,16},{1,13},{... | collective-permute-start | bytes 442376 | tf_op jit(solution)/shard_map/ppermute | solution.py:569
  51.3 4.2 %own.1 = (f32[768,256]{1,0:T(8,128)S(1)}, f32[4,768,128]{2,1,0:T(8,128)S(1)}, bf16[768,256]{1,0:T(8,128)(2,1)S(1)}) custom-call(bf16[768,576]{1,0:T(8,128)(2,1)S(1)} %get-tuple-element.47.packed_ref, bf16[768,256]{1,0:T(8,128)(2,1)S(1)} %get-tuple-element.48.same_ref, bf16[768,256]{1,0:T(8,128)(2,1)S(1)} %get-tuple-element.49.apart_ref, ...), custom_call_target="tpu_custom_call" | custom-call | flops 100000000 | tf_op jit(solution)/shard_map/own/pallas_call | solution.py:69
  57.6 2.0 %near.1 = (f32[768,256]{1,0:T(8,128)S(1)}, f32[4,768,128]{2,1,0:T(8,128)S(1)}) custom-call(f32[768,256]{1,0:T(8,128)S(1)} %get-tuple-element.51.acc_ref, f32[4,768,128]{2,1,0:T(8,128)S(1)} %get-tuple-element.52.tops_ref, bf16[768,256]{1,0:T(8,128)(2,1)S(1)} %get-tuple-element.53.query_ref, ...), custom_call_target="tpu_custom_call", output_to_operand_aliasing={{0}: (0, {}), {1}: (1, {})} | custom-call | flops 6000000000 | tf_op jit(solution)/shard_map/near/pallas_call | solution.py:69
  59.6 1.8 %mid.1 = (f32[768,256]{1,0:T(8,128)S(1)}, f32[4,768,128]{2,1,0:T(8,128)S(1)}, bf16[768,256]{1,0:T(8,128)(2,1)S(1)}, f32[768,256]{1,0:T(8,128)S(1)}) custom-call(f32[768,256]{1,0:T(8,128)S(1)} %get-tuple-element.56.acc_ref, f32[4,768,128]{2,1,0:T(8,128)S(1)} %get-tuple-element.57.tops_ref, ...), custom_call_target="tpu_custom_call", output_to_operand_aliasing={{0}: (0, {}), {1}: (1, {})} | custom-call | flops 6000000000 | tf_op jit(solution)/shard_map/mid/pallas_call | solution.py:69
  62.5 1.6 %far.1 = (bf16[192,256]{1,0:T(8,128)(2,1)S(1)}, bf16[192,256]{1,0:T(8,128)(2,1)S(1)}, bf16[192,256]{1,0:T(8,128)(2,1)S(1)}, bf16[192,256]{1,0:T(8,128)(2,1)S(1)}) custom-call(f32[768,256]{1,0:T(8,128)S(1)} %get-tuple-element.60.acc_ref, f32[4,768,128]{2,1,0:T(8,128)S(1)} %get-tuple-element.61.tops_ref, bf16[768,256]{1,0:T(8,128)(2,1)S(1)} %get-tuple-element.53.query_ref, ...), custom_call_target="tpu_custom_call" | custom-call | flops 1000000000 | tf_op jit(solution)/shard_map/far/pallas_call | solution.py:69
  64.2 1.1 %collective-permute-start.17 = (bf16[192,256]{1,0:T(8,128)(2,1)S(1)}, bf16[192,256]{1,0:T(8,128)(2,1)S(1)}, u32[]{:S(2)}, u32[]{:S(2)}) collective-permute-start(bf16[192,256]{1,0:T(8,128)(2,1)S(1)} %get-tuple-element.69), channel_id=1, source_target_pairs={{0,2},{1,3},{2,0},{3,1},{4,6},{5,7},{6,4},{7,5},{8,10},{9,11},{10,... | collective-permute-start | bytes 294920 | tf_op jit(solution)/shard_map/ppermute | solution.py:569
  66.1 1.5 %base.1 = (bf16[192,768]{1,0:T(8,128)(2,1)S(1)}, bf16[4,256,768]{2,1,0:T(8,128)(2,1)S(1)}) custom-call(s32[4,1,256]{2,1,0:T(1,128)S(1)} %get-tuple-element.38.codes_ref, bf16[192,768]{1,0:T(8,128)(2,1)S(1)} %stream.1.stream_ref.refs_0_, bf16[192,768]{1,0:T(8,128)(2,1)S(1)} %collective-permute-done.4.stream_ref.refs_1_, ...), custom_call_target="tpu_custom_call" | custom-call | flops 1000000000 | tf_op jit(solution)/shard_map/base/pallas_call | solution.py:69
  67.6 2.2 %collective-permute-done.17.refs_2_ = bf16[192,256]{1,0:T(8,128)(2,1)S(1)} collective-permute-done((bf16[192,256]{1,0:T(8,128)(2,1)S(1)}, bf16[192,256]{1,0:T(8,128)(2,1)S(1)}, u32[]{:S(2)}, u32[]{:S(2)}) %collective-permute-start.17) | collective-permute-done | bytes 98336 | tf_op jit(solution)/shard_map/ppermute | solution.py:569
  69.9 1.2 %collective-permute-done.18.refs_3_ = bf16[192,256]{1,0:T(8,128)(2,1)S(1)} collective-permute-done((bf16[192,256]{1,0:T(8,128)(2,1)S(1)}, bf16[192,256]{1,0:T(8,128)(2,1)S(1)}, u32[]{:S(2)}, u32[]{:S(2)}) %collective-permute-start.18) | collective-permute-done | bytes 98336 | tf_op jit(solution)/shard_map/ppermute | solution.py:569
  71.1 1.6 %mix.1 = bf16[192,768]{1,0:T(8,128)(2,1)} custom-call(bf16[192,768]{1,0:T(8,128)(2,1)S(1)} %get-tuple-element.44.base_ref, bf16[4,256,768]{2,1,0:T(8,128)(2,1)S(1)} %get-tuple-element.45.weights_ref, bf16[192,256]{1,0:T(8,128)(2,1)S(1)} %get-tuple-element.67.refs_0_, bf16[192,256]{1,0:T(8,128)(2,1)S(1)} %collective-permute-done.16.refs_1_, ...), custom_call_target="tpu_custom_call" | custom-call | flops 1000000000 | tf_op jit(solution)/shard_map/mix/pallas_call | solution.py:69
  (45 shorter events, 7.8 us)
Async XLA Ops:
  0.0 20.8 %collective-permute-start = (bf16[384,768]{1,0:T(8,128)(2,1)}, bf16[384,768]{1,0:T(8,128)(2,1)S(1)}, u32[]{:S(2)}, u32[]{:S(2)}) collective-permute-start(bf16[384,768]{1,0:T(8,128)(2,1)} %weight_ref.3), channel_id=1, source_target_pairs={{0,2},{1,3},{2,0},{3,1},{4,6},{5,7},{6,4},{7,5},{8,10},{9,11},{10,... | collective-permute-start | bytes 1769480 | tf_op jit(solution)/shard_map/ppermute | solution.py:569
  3.0 17.8 %copy-start = (bf16[384,768]{1,0:T(8,128)(2,1)S(1)}, bf16[384,768]{1,0:T(8,128)(2,1)}, u32[]{:S(2)}) copy-start(bf16[384,768]{1,0:T(8,128)(2,1)} %weight_ref.3) | copy-start | bytes 1769476
  3.0 18.4 %copy-start.1 = (bf16[192,768]{1,0:T(8,128)(2,1)S(1)}, bf16[192,768]{1,0:T(8,128)(2,1)}, u32[]{:S(2)}) copy-start(bf16[192,768]{1,0:T(8,128)(2,1)} %weight_ref.2) | copy-start | bytes 884740
  3.0 18.4 %copy-start.6 = (f32[192]{0:T(256)S(1)}, f32[192]{0:T(256)}, u32[]{:S(2)}) copy-start(f32[192]{0:T(256)} %param.18) | copy-start | bytes 2308
  6.4 22.8 %all-to-all-start = ((bf16[32,80,128]{2,1,0:T(8,128)(2,1)}), bf16[32,80,128]{2,1,0:T(8,128)(2,1)S(1)}, u32[]{:S(2)}, u32[]{:S(2)}) async-start(bf16[32,80,128]{2,1,0:T(8,128)(2,1)} %route.1), calls=%async_computation | async-start | bytes 1310720 | tf_op jit(solution)/shard_map/all_to_all | solution.py:630
  20.8 3.6 %collective-permute-start.1 = (bf16[384,768]{1,0:T(8,128)(2,1)S(1)}, bf16[384,768]{1,0:T(8,128)(2,1)S(1)}, u32[]{:S(2)}, u32[]{:S(2)}) collective-permute-start(bf16[384,768]{1,0:T(8,128)(2,1)S(1)} %collective-permute-done.refs_1_), channel_id=1, source_target_pairs={{0,1},{1,0},{2,3},{3,2},{4,5},{5,4},{6,7},{7,6},{8,9},{9,8},{10,11... | collective-permute-start | bytes 1769480 | tf_op jit(solution)/shard_map/ppermute | solution.py:569
  20.8 3.7 %collective-permute-start.3 = (bf16[384,768]{1,0:T(8,128)(2,1)S(1)}, bf16[384,768]{1,0:T(8,128)(2,1)S(1)}, u32[]{:S(2)}, u32[]{:S(2)}) collective-permute-start(bf16[384,768]{1,0:T(8,128)(2,1)S(1)} %copy-done), channel_id=1, source_target_pairs={{0,1},{1,0},{2,3},{3,2},{4,5},{5,4},{6,7},{7,6},{8,9},{9,8},{10,11... | collective-permute-start | bytes 1769480 | tf_op jit(solution)/shard_map/ppermute | solution.py:569
  22.2 2.3 %collective-permute-start.2 = (bf16[192,768]{1,0:T(8,128)(2,1)}, bf16[192,768]{1,0:T(8,128)(2,1)S(1)}, u32[]{:S(2)}, u32[]{:S(2)}) collective-permute-start(bf16[192,768]{1,0:T(8,128)(2,1)} %scale.1.refs_4_), channel_id=1, source_target_pairs={{0,1},{1,0},{2,3},{3,2},{4,5},{5,4},{6,7},{7,6},{8,9},{9,8},{10,11... | collective-permute-start | bytes 884744 | tf_op jit(solution)/shard_map/ppermute | solution.py:569
  22.2 13.9 %collective-permute-start.7 = (bf16[192,768]{1,0:T(8,128)(2,1)}, bf16[192,768]{1,0:T(8,128)(2,1)}, u32[]{:S(2)}, u32[]{:S(2)}) collective-permute-start(bf16[192,768]{1,0:T(8,128)(2,1)} %scale.1.refs_4_), channel_id=1, source_target_pairs={{0,2},{1,3},{2,0},{3,1},{4,6},{5,7},{6,4},{7,5},{8,10},{9,11},{10,... | collective-permute-start | bytes 884744 | tf_op jit(solution)/shard_map/ppermute | solution.py:569
  31.4 2.1 %copy-start.2 = (bf16[768,192]{0,1:T(8,128)(2,1)S(1)}, bf16[768,192]{0,1:T(8,128)(2,1)}, u32[]{:S(2)}) copy-start(bf16[768,192]{0,1:T(8,128)(2,1)} %param.16) | copy-start | bytes 884740
  31.7 4.4 %collective-permute-start.4 = (bf16[192,768]{1,0:T(8,128)(2,1)S(1)}, bf16[192,768]{1,0:T(8,128)(2,1)S(1)}, u32[]{:S(2)}, u32[]{:S(2)}) collective-permute-start(bf16[192,768]{1,0:T(8,128)(2,1)S(1)} %stream.1.stream_ref.refs_0_), channel_id=1, source_target_pairs={{0,1},{1,0},{2,3},{3,2},{4,5},{5,4},{6,7},{7,6},{8,9},{9,8},{10,11... | collective-permute-start | bytes 884744 | tf_op jit(solution)/shard_map/ppermute | solution.py:569
  31.9 9.4 %collective-permute-start.5 = (bf16[192,768]{1,0:T(8,128)(2,1)S(1)}, bf16[192,768]{1,0:T(8,128)(2,1)S(1)}, u32[]{:S(2)}, u32[]{:S(2)}) collective-permute-start(bf16[192,768]{1,0:T(8,128)(2,1)S(1)} %stream.1.stream_ref.refs_0_), channel_id=1, source_target_pairs={{0,2},{1,3},{2,0},{3,1},{4,6},{5,7},{6,4},{7,5},{8,10},{9,11},{10,... | collective-permute-start | bytes 884744 | tf_op jit(solution)/shard_map/ppermute | solution.py:569
  38.1 3.2 %collective-permute-start.8 = (bf16[192,768]{1,0:T(8,128)(2,1)S(1)}, bf16[192,768]{1,0:T(8,128)(2,1)S(1)}, u32[]{:S(2)}, u32[]{:S(2)}) collective-permute-start(bf16[192,768]{1,0:T(8,128)(2,1)S(1)} %get-tuple-element.43.refs_6_), channel_id=1, source_target_pairs={{0,1},{1,0},{2,3},{3,2},{4,5},{5,4},{6,7},{7,6},{8,9},{9,8},{10,11... | collective-permute-start | bytes 884744 | tf_op jit(solution)/shard_map/ppermute | solution.py:569
  41.2 1.6 %collective-permute-start.6 = (bf16[192,768]{1,0:T(8,128)(2,1)S(1)}, bf16[192,768]{1,0:T(8,128)(2,1)S(1)}, u32[]{:S(2)}, u32[]{:S(2)}) collective-permute-start(bf16[192,768]{1,0:T(8,128)(2,1)S(1)} %collective-permute-done.5.refs_2_.stream_ref), channel_id=1, source_target_pairs={{0,1},{1,0},{2,3},{3,2},{4,5},{5,4},{6,7},{7,6},{8,9},{9,8},{10,11... | collective-permute-start | bytes 884744 | tf_op jit(solution)/shard_map/ppermute | solution.py:569
  43.9 13.7 %collective-permute-start.9 = (bf16[384,384]{1,0:T(8,128)(2,1)S(1)}, bf16[384,384]{1,0:T(8,128)(2,1)S(1)}, u32[]{:S(2)}, u32[]{:S(2)}) collective-permute-start(bf16[384,384]{1,0:T(8,128)(2,1)S(1)} %get-tuple-element.55), channel_id=1, source_target_pairs={{0,4},{4,0},{8,12},{12,8},{16,20},{20,16},{24,28},{28,24},{1,5},{5... | collective-permute-start | bytes 884744 | tf_op jit(solution)/shard_map/ppermute | solution.py:569
  45.4 10.1 %collective-permute-start.12 = (bf16[96,384]{1,0:T(8,128)(2,1)S(1)}, bf16[96,384]{1,0:T(8,128)(2,1)S(1)}, u32[]{:S(2)}, u32[]{:S(2)}) collective-permute-start(bf16[96,384]{1,0:T(8,128)(2,1)S(1)} %get-tuple-element.66), channel_id=1, source_target_pairs={{0,16},{4,20},{8,24},{12,28},{16,0},{20,4},{24,8},{28,12},{1,17},{... | collective-permute-start | bytes 221192 | tf_op jit(solution)/shard_map/ppermute | solution.py:569
  45.6 11.0 %collective-permute-start.14 = (bf16[96,384]{1,0:T(8,128)(2,1)S(1)}, bf16[96,384]{1,0:T(8,128)(2,1)S(1)}, u32[]{:S(2)}, u32[]{:S(2)}) collective-permute-start(bf16[96,384]{1,0:T(8,128)(2,1)S(1)} %get-tuple-element.66), channel_id=1, source_target_pairs={{0,24},{4,28},{8,16},{12,20},{16,8},{20,12},{24,0},{28,4},{1,25},{... | collective-permute-start | bytes 221192 | tf_op jit(solution)/shard_map/ppermute | solution.py:569
  48.7 10.9 %collective-permute-start.10 = (bf16[192,384]{1,0:T(8,128)(2,1)S(1)}, bf16[192,384]{1,0:T(8,128)(2,1)S(1)}, u32[]{:S(2)}, u32[]{:S(2)}) collective-permute-start(bf16[192,384]{1,0:T(8,128)(2,1)S(1)} %get-tuple-element.59), channel_id=1, source_target_pairs={{0,8},{4,12},{8,0},{12,4},{16,24},{20,28},{24,16},{28,20},{1,9},{5... | collective-permute-start | bytes 442376 | tf_op jit(solution)/shard_map/ppermute | solution.py:569
  48.9 10.7 %collective-permute-start.11 = (bf16[192,384]{1,0:T(8,128)(2,1)S(1)}, bf16[192,384]{1,0:T(8,128)(2,1)S(1)}, u32[]{:S(2)}, u32[]{:S(2)}) collective-permute-start(bf16[192,384]{1,0:T(8,128)(2,1)S(1)} %get-tuple-element.59), channel_id=1, source_target_pairs={{0,12},{4,8},{8,4},{12,0},{16,28},{20,24},{24,20},{28,16},{1,13},{... | collective-permute-start | bytes 442376 | tf_op jit(solution)/shard_map/ppermute | solution.py:569
  55.5 6.0 %collective-permute-start.13 = (bf16[96,384]{1,0:T(8,128)(2,1)S(1)}, bf16[96,384]{1,0:T(8,128)(2,1)S(1)}, u32[]{:S(2)}, u32[]{:S(2)}) collective-permute-start(bf16[96,384]{1,0:T(8,128)(2,1)S(1)} %collective-permute-done.12.refs_1_), channel_id=1, source_target_pairs={{0,4},{4,0},{8,12},{12,8},{16,20},{20,16},{24,28},{28,24},{1,5},{5... | collective-permute-start | bytes 221192 | tf_op jit(solution)/shard_map/ppermute | solution.py:569
  56.5 6.0 %collective-permute-start.15 = (bf16[96,384]{1,0:T(8,128)(2,1)S(1)}, bf16[96,384]{1,0:T(8,128)(2,1)S(1)}, u32[]{:S(2)}, u32[]{:S(2)}) collective-permute-start(bf16[96,384]{1,0:T(8,128)(2,1)S(1)} %collective-permute-done.14.refs_3_), channel_id=1, source_target_pairs={{0,4},{4,0},{8,12},{12,8},{16,20},{20,16},{24,28},{28,24},{1,5},{5... | collective-permute-start | bytes 221192 | tf_op jit(solution)/shard_map/ppermute | solution.py:569
  64.1 3.5 %collective-permute-start.16 = (bf16[192,256]{1,0:T(8,128)(2,1)S(1)}, bf16[192,256]{1,0:T(8,128)(2,1)S(1)}, u32[]{:S(2)}, u32[]{:S(2)}) collective-permute-start(bf16[192,256]{1,0:T(8,128)(2,1)S(1)} %get-tuple-element.68), channel_id=1, source_target_pairs={{0,1},{1,0},{2,3},{3,2},{4,5},{5,4},{6,7},{7,6},{8,9},{9,8},{10,11... | collective-permute-start | bytes 294920 | tf_op jit(solution)/shard_map/ppermute | solution.py:569
  64.2 5.7 %collective-permute-start.17 = (bf16[192,256]{1,0:T(8,128)(2,1)S(1)}, bf16[192,256]{1,0:T(8,128)(2,1)S(1)}, u32[]{:S(2)}, u32[]{:S(2)}) collective-permute-start(bf16[192,256]{1,0:T(8,128)(2,1)S(1)} %get-tuple-element.69), channel_id=1, source_target_pairs={{0,2},{1,3},{2,0},{3,1},{4,6},{5,7},{6,4},{7,5},{8,10},{9,11},{10,... | collective-permute-start | bytes 294920 | tf_op jit(solution)/shard_map/ppermute | solution.py:569
  65.3 5.8 %collective-permute-start.18 = (bf16[192,256]{1,0:T(8,128)(2,1)S(1)}, bf16[192,256]{1,0:T(8,128)(2,1)S(1)}, u32[]{:S(2)}, u32[]{:S(2)}) collective-permute-start(bf16[192,256]{1,0:T(8,128)(2,1)S(1)} %get-tuple-element.70), channel_id=1, source_target_pairs={{0,3},{1,2},{2,1},{3,0},{4,7},{5,6},{6,5},{7,4},{8,11},{9,10},{10,... | collective-permute-start | bytes 294920 | tf_op jit(solution)/shard_map/ppermute | solution.py:569
  (3 other events, 6.3 us)

commit v4 on v3

--- a/solution.py
+++ b/solution.py
@@ -137,6 +137,10 @@
     target_row = (owner * n_tp + lane_of) * sub_pad + low
     chooser = one_hot(iota((blocks * sub_pad, rows), 0) == target_row)
 
+    stores = []
+    fetches[1].wait()
+    fetches[2].wait()
+    picked = dot(chooser, tiles_ref[...])
     spot = stored_at(target - owner * rows, rows)
     high = spot >> 7
     code = ((spot & 127) + 128).astype(F32)
@@ -150,12 +154,8 @@
         jnp.where(mine, code, 0.0).astype(BF16),
         one_hot(iota((LANES, rows), 0) == (arrival & 127)),
     )
-    fetches[1].wait()
     ids = dot_nt(jnp.where(held, one_row(slide_ref).astype(F32), 0.0).astype(BF16), kept_lane)
     notes = coded + ids
-    stores = []
-    fetches[2].wait()
-    picked = dot(chooser, tiles_ref[...])
     pad = out_hbm.shape[1] - chunks * sub_pad - 8
     for block in range(blocks):
         base = block * sub_pad
@@ -186,39 +186,49 @@
     out_ref[...] = weight_ref[: out_ref.shape[0], : out_ref.shape[1]]
 
 
-def scale_kernel(gain_ref, weight_ref, scaled_ref):
+def scale_kernel(gain_ref, weight_ref, scaled_hbm, scaled_ref, sem):
     width = weight_ref.shape[0]
     same = iota((width, width), 0) == iota((width, width), 1)
     gain = jnp.sum(jnp.where(same, gain_ref[...], 0.0), axis=1, keepdims=True)
     scaled_ref[...] = (weight_ref[...].astype(F32) * gain).astype(BF16)
+    store = pltpu.make_async_copy(scaled_ref, scaled_hbm, sem)
+    store.start()
+    store.wait()
 
 
 def project_kernel(n_seq, n_tp, peer, recv_hbm, early_ref, beside_ref, *refs):
     del early_ref, beside_ref
     weight_refs = refs[: n_tp - 1]
-    total_ref, later_ref, codes_ref, ids_ref, recv_ref, work, sems = refs[n_tp - 1 :]
+    total_ref, later_ref, codes_ref, ids_ref, recv_ref, sems = refs[n_tp - 1 :]
     fetches = []
     for source in range(n_seq):
         some = pl.ds(source * n_tp, n_tp)
         fetches.append(pltpu.make_async_copy(recv_hbm.at[some], recv_ref.at[some], sems.at[source]))
         fetches[-1].start()
     sub_pad = up_to(peer // n_tp, 8)
-    chunks = work.shape[2] // LANES
+    chunks = later_ref.shape[1] // LANES
     column = lax.axis_index("tp")
     code_rows = codes_ref.shape[2] // LANES
     share = ids_ref.shape[1] // n_tp
     at = chunks * sub_pad
     even = at // 16 * 16
-    notes = [jnp.zeros((8, LANES), F32)] * n_tp
+    for fetch in fetches:
+        fetch.wait()
+    notes, laid = [], []
+    for turn in range(n_tp):
+        blocks = [recv_ref[source * n_tp + (column ^ turn)].astype(F32) for source in range(n_seq)]
+        notes.append(sum(block[at : at + 8] for block in blocks))
+        columns = [
+            jnp.concatenate([block[part * sub_pad : (part + 1) * sub_pad] for block in blocks], axis=0).astype(BF16)
+            for part in range(chunks)
+        ]
+        laid.append(jnp.concatenate(columns, axis=1))
+    total = None
+    for turn in range(1, n_tp):
+        part_sum = dot(laid[turn], weight_refs[turn - 1][...])
+        total = part_sum if total is None else total + part_sum
+    total_ref[...] = total
     for source in range(n_seq):
-        fetches[source].wait()
-        for turn in range(n_tp):
-            block = recv_ref[source * n_tp + (column ^ turn)].astype(F32)
-            for part in range(chunks):
-                work[turn, source * sub_pad : (source + 1) * sub_pad, part * LANES : (part + 1) * LANES] = block[
-                    part * sub_pad : (part + 1) * sub_pad
-                ]
-            notes[turn] = notes[turn] + block[at : at + 8]
         pieces = []
         for other in range(n_tp):
             note = recv_ref[source * n_tp + other, even : even + 16, :].astype(F32)[at - even :]
@@ -226,12 +236,7 @@
                 length = min(LANES, share - piece * LANES)
                 pieces.append(note[code_rows + piece : code_rows + piece + 1, :length])
         ids_ref[source : source + 1, :] = jnp.concatenate(pieces, axis=1)
-    total = None
-    for turn in range(1, n_tp):
-        part_sum = dot(work[turn].astype(BF16), weight_refs[turn - 1][...])
-        total = part_sum if total is None else total + part_sum
-    total_ref[...] = total
-    later_ref[...] = work[0].astype(BF16)
+    later_ref[...] = laid[0]
     for turn in range(n_tp):
         codes = notes[turn]
         power = jnp.zeros((8, LANES), F32)
@@ -491,7 +496,9 @@
             new_tops_ref[head, here, :] = tops
 
 
-def mid_kernel(groups, acc_ref, tops_ref, query_ref, spreads_ref, *refs):
+def mid_kernel(groups, acc_ref, tops_ref, query_ref, spreads_ref, back_ref, *refs, n_sent):
+    sent_refs = refs[-n_sent:]
+    refs = refs[:-n_sent]
     sums_ref, _, early_ref, centre_ref = refs[-4:]
     near_kernel(groups, acc_ref, tops_ref, query_ref, spreads_ref, *refs[:-2])
     rows, wide = query_ref.shape
@@ -502,7 +509,10 @@
     average = jnp.full((wide, wide), 1.0, BF16)
     centre = (dot(attn.astype(BF16), average) * (1.0 / (heads * HEAD_DIM))).astype(BF16).astype(F32)
     centre_ref[...] = centre
-    early_ref[...] = jnp.where(inner < HEAD_DIM, attn - centre, centre).astype(BF16)
+    early = jnp.where(inner < HEAD_DIM, attn - centre, centre).astype(BF16)
+    early_ref[...] = early
+    for index, ref in enumerate(sent_refs):
+        ref[...] = dot(back_ref[back_ref.shape[0] - n_sent + index], early).astype(BF16)
 
 
 def far_kernel(n_tp, level, masks, acc_ref, tops_ref, query_ref, spreads_ref, early_ref, centre_ref, back_ref, *refs):
@@ -512,14 +522,28 @@
     message[...] = early_ref[...]
 
     merged = merge_sets(level, masks, sets, acc_ref, tops_ref, query_ref, spreads_ref, apart_ref)
+    changed = None
     for head, here, sums, _ in merged:
         lane = iota(sums.shape, 1)
         mine = (lane >= head * SLOT) & (lane < head * SLOT + HEAD_DIM)
         new = (sums / slot_lane(sums, HEAD_DIM) - centre_ref[here, :]).astype(BF16)
         message[here, :] = jnp.where(mine, new, message[here, :])
+        changed = new if changed is None else jnp.where(lane >= head * SLOT, new, changed)
     final = message[...]
+    rows = message.shape[0]
+    count = rows >> level
     for turn in range(n_tp):
-        out_refs[turn][...] = dot(back_ref[turn], final).astype(BF16)
+        ref = out_refs[turn]
+        if ref.shape[0] == back_ref.shape[1]:
+            ref[...] = dot(back_ref[turn], final).astype(BF16)
+        else:
+            each = rows // CLASSES
+            classes = count // each
+            line = iota((ref.shape[0], count), 0)
+            spot = (lax.axis_index("tp") ^ turn) * (each // n_tp) + line // classes
+            wanted = (line % classes) * each + spot
+            pick = (iota((ref.shape[0], count), 1) == wanted) & (line < count // n_tp)
+            ref[...] = dot(one_hot(pick), changed).astype(BF16)
 
 
 def base_kernel(n_tp, codes_ref, *refs):
@@ -542,16 +566,24 @@
             weights_ref[turn, to + HEAD_DIM : to + SLOT, :] = gap
 
 
-def mix_kernel(n_tp, base_ref, weights_ref, *refs):
-    message_refs, out_ref = refs[:n_tp], refs[-1]
+def mix_kernel(n_tp, level, base_ref, weights_ref, *refs):
+    message_refs, change_refs, out_ref = refs[:n_tp], refs[n_tp:-1], refs[-1]
     share, wide = base_ref.shape[0], weights_ref.shape[1]
     features = n_tp * (wide // SLOT) * HEAD_DIM
-    inside = (iota((share, wide), 1) & (SLOT - 1)) < HEAD_DIM
+    lane = iota((share, wide), 1)
+    inside = (lane & (SLOT - 1)) < HEAD_DIM
     parts, centres = [], []
-    for ref in message_refs:
+    for turn, ref in enumerate(message_refs):
         message = ref[...].astype(F32)
+        centres.append(message[:, HEAD_DIM : HEAD_DIM + 1])
+        if turn >= n_tp - len(change_refs):
+            change = change_refs[turn - n_tp + len(change_refs)][...]
+            count = change.shape[0]
+            moved = dot(one_hot(iota((share, count), 1) == iota((share, count), 0) >> level), change)
+            head = (lax.axis_index("tp") ^ turn) * (wide // SLOT) + (lane >> 6)
+            late = ((iota((share, wide), 0) ^ head) & (2**level - 1)) == 0
+            message = jnp.where(late, moved, message)
         parts.append(jnp.where(inside, message, 0.0))
-        centres.append(message[:, HEAD_DIM : HEAD_DIM + 1])
     each = features // n_tp
     sums = [jnp.sum(part, axis=1, keepdims=True) + centre * each for part, centre in zip(parts, centres)]
     mean = sum(sums) * (1.0 / features)
@@ -631,7 +663,13 @@
     proj_parts = gather_tp(proj_weight)
     (early,) = call(hint_kernel, "hint", [((16, LANES), BF16)], [proj_parts[-1]], cost=HINT_COST)
     (scaled,) = call(
-        scale_kernel, "scale", [((width, features), BF16)], [sub_gain.reshape(1, width), out_weight], cost=1
+        scale_kernel,
+        "scale",
+        [((width, features), BF16)],
+        [sub_gain.reshape(1, width), out_weight],
+        scratch=[pltpu.VMEM((width, features), BF16), pltpu.SemaphoreType.DMA],
+        cost=1,
+        out_apart=(0,),
     )
 
     beside = swap(scaled, "tp", 1)
@@ -641,9 +679,9 @@
         [((arriving, features), F32), ((arriving, tile_width), BF16)]
         + [((n_tp, 1, up_to(arriving, LANES)), jnp.int32), ((n_seq, rows), F32)],
         [received, early, beside] + proj_parts[1:],
+        cost=0.5,
         scratch=[
             pltpu.VMEM(received.shape, BF16),
-            pltpu.VMEM((n_tp, arriving, tile_width), F32),
             pltpu.SemaphoreType.DMA((n_seq,)),
         ],
         vmem_bytes=vmem_bytes,
@@ -654,6 +692,7 @@
         "stream",
         [((arriving, features), BF16)],
         [total, later, proj_weight],
+        cost=0.1,
         vmem_bytes=vmem_bytes,
     )
     shards = gather_tp(stream)
@@ -709,37 +748,44 @@
         cost=0.1,
         vmem_bytes=vmem_bytes,
     )
+    n_sent = n_tp - 1
     for index in range(len(groups) - 1):
-        final = index == len(groups) - 2
-        acc, tops, *rest_of = call(
-            functools.partial(mid_kernel if final else near_kernel, [groups[index]]),
-            "mid" if final else "near",
-            [((rows, wide), F32), ((heads, rows, LANES), F32)]
-            + ([((rows, wide), BF16), ((rows, wide), F32)] if final else []),
-            [acc, tops, masked, spreads, far_apart[index]] + sent[index],
+        kernel, outs, given = near_kernel, [], []
+        if index == len(groups) - 2:
+            kernel, given = functools.partial(mid_kernel, n_sent=n_sent), [back]
+            outs = [((rows, wide), BF16), ((rows, wide), F32)] + [((share, wide), BF16)] * n_sent
+        acc, tops, *more = call(
+            functools.partial(kernel, [groups[index]]),
+            "mid" if outs else "near",
+            [((rows, wide), F32), ((heads, rows, LANES), F32)] + outs,
+            [acc, tops, masked, spreads] + given + [far_apart[index]] + sent[index],
             aliases={0: 0, 1: 1},
             cost=6,
             vmem_bytes=vmem_bytes,
         )
-    early, centre = rest_of
+    early, centre, *ahead = more
     messages = call(
         functools.partial(far_kernel, n_tp, *groups[-1]),
         "far",
-        [((share, wide), BF16)] * n_tp,
+        [((share, wide), BF16)] * (n_tp - n_sent)
+        + [((up_to((rows >> groups[-1][0]) // n_tp, 16), wide), BF16)] * n_sent,
         [acc, tops, masked, spreads, early, centre, back, far_apart[-1]] + sent[-1],
         scratch=[pltpu.VMEM((rows, wide), BF16)],
         vmem_bytes=vmem_bytes,
     )
+    ahead = [swap(one, "tp", n_tp - n_sent + index) for index, one in enumerate(ahead)]
     arrived = [messages[0]] + [swap(messages[turn], "tp", turn) for turn in range(1, n_tp)]
+    arrived = arrived[: n_tp - n_sent] + ahead + arrived[n_tp - n_sent :]
     base, padded = call(
         functools.partial(base_kernel, n_tp),
         "base",
         [((share, features), BF16), ((n_tp, wide, features), BF16)],
         [codes] + shards + out_parts,
+        cost=0.3,
         vmem_bytes=vmem_bytes,
     )
     (result,) = call(
-        functools.partial(mix_kernel, n_tp),
+        functools.partial(mix_kernel, n_tp, groups[-1][0]),
         "mix",
         [((share, features), BF16)],
         [base, padded] + arrived,

time: 73 us -> 71.2 us (0.975)
  waiting for transfers between devices: 22.5 us -> 19 us
  starting transfers between devices: 23.8 us -> 26.3 us
    ppermute x19 -> x22, waiting for transfers between devices: 17.8 us -> 14.7 us  [swap(): lax.ppermute(block, axis, [(index, index ^ mask) for index in range(count)])]
    ppermute x19 -> x22, starting transfers between devices: 18.9 us -> 21.4 us  [swap(): lax.ppermute(block, axis, [(index, index ^ mask) for index in range(count)])]
  transfers between devices with their start and end apart: 20 -> 23, of which waited for: 7 -> 6; matrix products, arithmetic and copies ran while one was open for 0% -> 0% of each run, Pallas kernels for 30% -> 32%
where the time goes in v4:
time: 71.2 us; the launch traced here: 70.9 us
  starting transfers between devices  26.3 us (37%)
  Pallas kernels  25.4 us (36%)
  waiting for transfers between devices  19 us (27%)
    pallas_call x15, Pallas kernels, call(): pl.pallas_call(kernel, name=name, out_shape=[jax.ShapeDtypeStruct(shape,...  25.4 us
    ppermute x22, starting transfers between devices, swap(): lax.ppermute(block, axis, [(index, index ^ mask) for index in range(count)])  21.4 us
    ppermute x22, waiting for transfers between devices, swap(): lax.ppermute(block, axis, [(index, index ^ mask) for index in range(count)])  14.7 us
    all_to_all x1, starting transfers between devices, body(): lax.all_to_all(blocks, ('seq', 'tp'), split_axis=0, concat_axis=0, tiled=...  4.9 us
    all_to_all x1, waiting for transfers between devices, body(): lax.all_to_all(blocks, ('seq', 'tp'), split_axis=0, concat_axis=0, tiled=...  4.27 us
  transfers between devices with their start and end apart: 23, of which 6 were waited for; matrix products, arithmetic and copies ran while one was open for 0% of the time, Pallas kernels for 32%

profile of v4, /device:TPU:0, one launch (start us, length us, event | category | flops | bytes accessed | tf_op | source)
XLA Modules:
  0.0 70.9 jit_solution(5420159699345811460)
XLA Ops:
  0.0 3.0 %collective-permute-start = (bf16[384,768]{1,0:T(8,128)(2,1)}, bf16[384,768]{1,0:T(8,128)(2,1)S(1)}, u32[]{:S(2)}, u32[]{:S(2)}) collective-permute-start(bf16[384,768]{1,0:T(8,128)(2,1)} %weight_ref.3), channel_id=1, source_target_pairs={{0,2},{1,3},{2,0},{3,1},{4,6},{5,7},{6,4},{7,5},{8,10},{9,11},{10,... | collective-permute-start | bytes 1769480 | tf_op jit(solution)/shard_map/ppermute | solution.py:601
  3.0 3.1 %route.1 = bf16[32,80,128]{2,1,0:T(8,128)(2,1)} custom-call(s32[6,128]{1,0:T(8,128)} %bitcast.24, s32[6,128]{1,0:T(8,128)} %bitcast.25, bf16[768,384]{1,0:T(8,128)(2,1)} %tiles_hbm.1), custom_call_target="tpu_custom_call" | custom-call | flops 3000000000 | tf_op jit(solution)/shard_map/route/pallas_call | solution.py:69
  6.1 4.9 %all-to-all-start = ((bf16[32,80,128]{2,1,0:T(8,128)(2,1)}), bf16[32,80,128]{2,1,0:T(8,128)(2,1)S(1)}, u32[]{:S(2)}, u32[]{:S(2)}) async-start(bf16[32,80,128]{2,1,0:T(8,128)(2,1)} %route.1), calls=%async_computation | async-start | bytes 1310720 | tf_op jit(solution)/shard_map/all_to_all | solution.py:662
  11.0 10.0 %collective-permute-done.refs_1_ = bf16[384,768]{1,0:T(8,128)(2,1)S(1)} collective-permute-done((bf16[384,768]{1,0:T(8,128)(2,1)}, bf16[384,768]{1,0:T(8,128)(2,1)S(1)}, u32[]{:S(2)}, u32[]{:S(2)}) %collective-permute-start) | collective-permute-done | bytes 589856 | tf_op jit(solution)/shard_map/ppermute | solution.py:601
  22.4 2.1 %collective-permute-start.7 = (bf16[192,768]{1,0:T(8,128)(2,1)}, bf16[192,768]{1,0:T(8,128)(2,1)}, u32[]{:S(2)}, u32[]{:S(2)}) collective-permute-start(bf16[192,768]{1,0:T(8,128)(2,1)} %scale.1.refs_4_), channel_id=1, source_target_pairs={{0,2},{1,3},{2,0},{3,1},{4,6},{5,7},{6,4},{7,5},{8,10},{9,11},{10,... | collective-permute-start | bytes 884744 | tf_op jit(solution)/shard_map/ppermute | solution.py:601
  24.6 4.3 %all-to-all-done.recv_hbm = bf16[32,80,128]{2,1,0:T(8,128)(2,1)S(1)} async-done(((bf16[32,80,128]{2,1,0:T(8,128)(2,1)}), bf16[32,80,128]{2,1,0:T(8,128)(2,1)S(1)}, u32[]{:S(2)}, u32[]{:S(2)}) %all-to-all-start) | async-done | bytes 655392 | tf_op jit(solution)/shard_map/all_to_all | solution.py:662
  28.9 1.6 %project.1 = (f32[192,768]{1,0:T(8,128)S(1)}, bf16[192,384]{1,0:T(8,128)(2,1)S(1)}, s32[4,1,256]{2,1,0:T(1,128)S(1)}, f32[8,768]{1,0:T(8,128)S(1)}) custom-call(bf16[32,80,128]{2,1,0:T(8,128)(2,1)S(1)} %all-to-all-done.recv_hbm, bf16[16,128]{1,0:T(8,128)(2,1)S(1)} %hint.1.early_ref, bf16[192,768]{1,0:T(8,128)(2,1)S(1)} %collective-permute-done.2.beside_ref.refs_5_, ...), custom_call_target="tpu_custom_call" | custom-call | flops 500000000 | tf_op jit(solution)/shard_map/project/pallas_call | solution.py:69
  30.9 1.6 %collective-permute-start.5 = (bf16[192,768]{1,0:T(8,128)(2,1)S(1)}, bf16[192,768]{1,0:T(8,128)(2,1)S(1)}, u32[]{:S(2)}, u32[]{:S(2)}) collective-permute-start(bf16[192,768]{1,0:T(8,128)(2,1)S(1)} %stream.1.stream_ref.refs_0_), channel_id=1, source_target_pairs={{0,2},{1,3},{2,0},{3,1},{4,6},{5,7},{6,4},{7,5},{8,10},{9,11},{10,... | collective-permute-start | bytes 884744 | tf_op jit(solution)/shard_map/ppermute | solution.py:601
  32.5 2.6 %heads_1.1 = (bf16[768,576]{1,0:T(8,128)(2,1)S(1)}, bf16[768,256]{1,0:T(8,128)(2,1)S(1)}, bf16[768,256]{1,0:T(8,128)(2,1)S(1)}, bf16[4,192,768]{2,1,0:T(8,128)(2...) custom-call(s32[4,1,256]{2,1,0:T(1,128)S(1)} %get-tuple-element.41.c, ...), custom_call_target="tpu_custom_call" | custom-call | flops 1000000000 | tf_op jit(solution)/shard_map/heads_1/pallas_call | solution.py:69
  35.1 1.9 %heads_2.2 = (bf16[768,576]{1,0:T(8,128)(2,1)S(1)}, bf16[192,768]{1,0:T(8,128)(2,1)S(1)}) custom-call(s32[4,1,256]{2,1,0:T(1,128)S(1)} %get-tuple-element.41.codes_ref, f32[6,128]{1,0:T(8,128)S(1)} %bitcast.20, bf16[192,768]{1,0:T(8,128)(2,1)S(1)} %bitcast.8, bf16[192,768]{1,0:T(8,128)(2,1)S(1)} %bitcast.12, bf16[192,768]{1,0:T(8,128)(2,1)S(1)} %bitcast.16, ...), custom_call_target="tpu_custom_call" | custom-call | flops 1000000000 | tf_op jit(solution)/shard_map/heads_2/pallas_call | solution.py:69
  37.2 3.1 %collective-permute-done.5.refs_2_.stream_ref = bf16[192,768]{1,0:T(8,128)(2,1)S(1)} collective-permute-done((bf16[192,768]{1,0:T(8,128)(2,1)S(1)}, bf16[192,768]{1,0:T(8,128)(2,1)S(1)}, u32[]{:S(2)}, u32[]{:S(2)}) %collective-permute-start.5) | collective-permute-done | bytes 294944 | tf_op jit(solution)/shard_map/ppermute | solution.py:601
  43.0 1.5 %collective-permute-start.9 = (bf16[384,384]{1,0:T(8,128)(2,1)S(1)}, bf16[384,384]{1,0:T(8,128)(2,1)S(1)}, u32[]{:S(2)}, u32[]{:S(2)}) collective-permute-start(bf16[384,384]{1,0:T(8,128)(2,1)S(1)} %get-tuple-element.58), channel_id=1, source_target_pairs={{0,4},{4,0},{8,12},{12,8},{16,20},{20,16},{24,28},{28,24},{1,5},{5... | collective-permute-start | bytes 884744 | tf_op jit(solution)/shard_map/ppermute | solution.py:601
  44.4 1.2 %collective-permute-start.12 = (bf16[96,384]{1,0:T(8,128)(2,1)S(1)}, bf16[96,384]{1,0:T(8,128)(2,1)S(1)}, u32[]{:S(2)}, u32[]{:S(2)}) collective-permute-start(bf16[96,384]{1,0:T(8,128)(2,1)S(1)} %get-tuple-element.69), channel_id=1, source_target_pairs={{0,16},{4,20},{8,24},{12,28},{16,0},{20,4},{24,8},{28,12},{1,17},{... | collective-permute-start | bytes 221192 | tf_op jit(solution)/shard_map/ppermute | solution.py:601
  45.6 2.5 %collective-permute-start.14 = (bf16[96,384]{1,0:T(8,128)(2,1)S(1)}, bf16[96,384]{1,0:T(8,128)(2,1)S(1)}, u32[]{:S(2)}, u32[]{:S(2)}) collective-permute-start(bf16[96,384]{1,0:T(8,128)(2,1)S(1)} %get-tuple-element.69), channel_id=1, source_target_pairs={{0,24},{4,28},{8,16},{12,20},{16,8},{20,12},{24,0},{28,4},{1,25},{... | collective-permute-start | bytes 221192 | tf_op jit(solution)/shard_map/ppermute | solution.py:601
  48.1 2.1 %collective-permute-start.11 = (bf16[192,384]{1,0:T(8,128)(2,1)S(1)}, bf16[192,384]{1,0:T(8,128)(2,1)S(1)}, u32[]{:S(2)}, u32[]{:S(2)}) collective-permute-start(bf16[192,384]{1,0:T(8,128)(2,1)S(1)} %get-tuple-element.63), channel_id=1, source_target_pairs={{0,12},{4,8},{8,4},{12,0},{16,28},{20,24},{24,20},{28,16},{1,13},{... | collective-permute-start | bytes 442376 | tf_op jit(solution)/shard_map/ppermute | solution.py:601
  50.3 4.2 %own.1 = (f32[768,256]{1,0:T(8,128)S(1)}, f32[4,768,128]{2,1,0:T(8,128)S(1)}, bf16[768,256]{1,0:T(8,128)(2,1)S(1)}) custom-call(bf16[768,576]{1,0:T(8,128)(2,1)S(1)} %get-tuple-element.50.packed_ref, bf16[768,256]{1,0:T(8,128)(2,1)S(1)} %get-tuple-element.51.same_ref, bf16[768,256]{1,0:T(8,128)(2,1)S(1)} %get-tuple-element.52.apart_ref, ...), custom_call_target="tpu_custom_call" | custom-call | flops 100000000 | tf_op jit(solution)/shard_map/own/pallas_call | solution.py:69
  54.5 1.4 %collective-permute-start.13 = (bf16[96,384]{1,0:T(8,128)(2,1)S(1)}, bf16[96,384]{1,0:T(8,128)(2,1)S(1)}, u32[]{:S(2)}, u32[]{:S(2)}) collective-permute-start(bf16[96,384]{1,0:T(8,128)(2,1)S(1)} %collective-permute-done.12.refs_1_), channel_id=1, source_target_pairs={{0,4},{4,0},{8,12},{12,8},{16,20},{20,16},{24,28},{28,24},{1,5},{5... | collective-permute-start | bytes 221192 | tf_op jit(solution)/shard_map/ppermute | solution.py:601
  56.6 2.0 %near.1 = (f32[768,256]{1,0:T(8,128)S(1)}, f32[4,768,128]{2,1,0:T(8,128)S(1)}) custom-call(f32[768,256]{1,0:T(8,128)S(1)} %get-tuple-element.54.acc_ref, f32[4,768,128]{2,1,0:T(8,128)S(1)} %get-tuple-element.55.tops_ref, bf16[768,256]{1,0:T(8,128)(2,1)S(1)} %get-tuple-element.56.query_ref, ...), custom_call_target="tpu_custom_call", output_to_operand_aliasing={{0}: (0, {}), {1}: (1, {})} | custom-call | flops 6000000000 | tf_op jit(solution)/shard_map/near/pallas_call | solution.py:69
  58.6 2.0 %mid.1 = (f32[768,256]{1,0:T(8,128)S(1)}, f32[4,768,128]{2,1,0:T(8,128)S(1)}, bf16[768,256]{1,0:T(8,128)(2,1)S(1)}, f32[768,256]{1,0:T(8,128)S(1)}, bf16[192,256...) custom-call(f32[768,256]{1,0:T(8,128)S(1)} %get-tuple-element.59.acc, ...), custom_call_target="tpu_custom_call", output_to_operand_aliasing={{0}: (0, {}), {1}: (1, {})} | custom-call | flops 6000000000 | tf_op jit(solution)/shard_map/mid/pallas_call | solution.py:69
  60.8 1.4 %collective-permute-start.17 = (bf16[192,256]{1,0:T(8,128)(2,1)S(1)}, bf16[192,256]{1,0:T(8,128)(2,1)S(1)}, u32[]{:S(2)}, u32[]{:S(2)}) collective-permute-start(bf16[192,256]{1,0:T(8,128)(2,1)S(1)} %get-tuple-element.72), channel_id=1, source_target_pairs={{0,2},{1,3},{2,0},{3,1},{4,6},{5,7},{6,4},{7,5},{8,10},{9,11},{10,... | collective-permute-start | bytes 294920 | tf_op jit(solution)/shard_map/ppermute | solution.py:601
  62.6 1.4 %far.1 = (bf16[192,256]{1,0:T(8,128)(2,1)S(1)}, bf16[32,256]{1,0:T(8,128)(2,1)S(1)}, bf16[32,256]{1,0:T(8,128)(2,1)S(1)}, bf16[32,256]{1,0:T(8,128)(2,1)S(1)}) custom-call(f32[768,256]{1,0:T(8,128)S(1)} %get-tuple-element.64.acc_ref, f32[4,768,128]{2,1,0:T(8,128)S(1)} %get-tuple-element.65.tops_ref, bf16[768,256]{1,0:T(8,128)(2,1)S(1)} %get-tuple-element.56.query_ref, ...), custom_call_target="tpu_custom_call" | custom-call | flops 1000000000 | tf_op jit(solution)/shard_map/far/pallas_call | solution.py:69
  64.5 1.3 %collective-permute-start.20 = (bf16[32,256]{1,0:T(8,128)(2,1)S(1)}, bf16[32,256]{1,0:T(8,128)(2,1)S(1)}, u32[]{:S(2)}, u32[]{:S(2)}) collective-permute-start(bf16[32,256]{1,0:T(8,128)(2,1)S(1)} %get-tuple-element.75), channel_id=1, source_target_pairs={{0,2},{1,3},{2,0},{3,1},{4,6},{5,7},{6,4},{7,5},{8,10},{9,11},{10,... | collective-permute-start | bytes 49160 | tf_op jit(solution)/shard_map/ppermute | solution.py:601
  66.6 1.5 %base.1 = (bf16[192,768]{1,0:T(8,128)(2,1)S(1)}, bf16[4,256,768]{2,1,0:T(8,128)(2,1)S(1)}) custom-call(s32[4,1,256]{2,1,0:T(1,128)S(1)} %get-tuple-element.41.codes_ref, bf16[192,768]{1,0:T(8,128)(2,1)S(1)} %stream.1.stream_ref.refs_0_, bf16[192,768]{1,0:T(8,128)(2,1)S(1)} %collective-permute-done.4.stream_ref.refs_1_, ...), custom_call_target="tpu_custom_call" | custom-call | flops 300000000 | tf_op jit(solution)/shard_map/base/pallas_call | solution.py:69
  69.1 1.8 %mix.1 = bf16[192,768]{1,0:T(8,128)(2,1)} custom-call(bf16[192,768]{1,0:T(8,128)(2,1)S(1)} %get-tuple-element.47.base_ref, bf16[4,256,768]{2,1,0:T(8,128)(2,1)S(1)} %get-tuple-element.48.weights_ref, bf16[192,256]{1,0:T(8,128)(2,1)S(1)} %get-tuple-element.70.refs_0_, bf16[192,256]{1,0:T(8,128)(2,1)S(1)} %collective-permute-done.16.refs_1_, ...), custom_call_target="tpu_custom_call" | custom-call | flops 1000000000 | tf_op jit(solution)/shard_map/mix/pallas_call | solution.py:69
  (51 shorter events, 8.1 us)
Async XLA Ops:
  0.0 21.0 %collective-permute-start = (bf16[384,768]{1,0:T(8,128)(2,1)}, bf16[384,768]{1,0:T(8,128)(2,1)S(1)}, u32[]{:S(2)}, u32[]{:S(2)}) collective-permute-start(bf16[384,768]{1,0:T(8,128)(2,1)} %weight_ref.3), channel_id=1, source_target_pairs={{0,2},{1,3},{2,0},{3,1},{4,6},{5,7},{6,4},{7,5},{8,10},{9,11},{10,... | collective-permute-start | bytes 1769480 | tf_op jit(solution)/shard_map/ppermute | solution.py:601
  3.0 18.5 %copy-start.6 = (f32[192]{0:T(256)S(1)}, f32[192]{0:T(256)}, u32[]{:S(2)}) copy-start(f32[192]{0:T(256)} %param.18) | copy-start | bytes 2308
  6.1 22.8 %all-to-all-start = ((bf16[32,80,128]{2,1,0:T(8,128)(2,1)}), bf16[32,80,128]{2,1,0:T(8,128)(2,1)S(1)}, u32[]{:S(2)}, u32[]{:S(2)}) async-start(bf16[32,80,128]{2,1,0:T(8,128)(2,1)} %route.1), calls=%async_computation | async-start | bytes 1310720 | tf_op jit(solution)/shard_map/all_to_all | solution.py:662
  21.0 3.6 %collective-permute-start.1 = (bf16[384,768]{1,0:T(8,128)(2,1)S(1)}, bf16[384,768]{1,0:T(8,128)(2,1)S(1)}, u32[]{:S(2)}, u32[]{:S(2)}) collective-permute-start(bf16[384,768]{1,0:T(8,128)(2,1)S(1)} %collective-permute-done.refs_1_), channel_id=1, source_target_pairs={{0,1},{1,0},{2,3},{3,2},{4,5},{5,4},{6,7},{7,6},{8,9},{9,8},{10,11... | collective-permute-start | bytes 1769480 | tf_op jit(solution)/shard_map/ppermute | solution.py:601
  21.0 3.6 %collective-permute-start.3 = (bf16[384,768]{1,0:T(8,128)(2,1)S(1)}, bf16[384,768]{1,0:T(8,128)(2,1)S(1)}, u32[]{:S(2)}, u32[]{:S(2)}) collective-permute-start(bf16[384,768]{1,0:T(8,128)(2,1)S(1)} %copy-done), channel_id=1, source_target_pairs={{0,1},{1,0},{2,3},{3,2},{4,5},{5,4},{6,7},{7,6},{8,9},{9,8},{10,11... | collective-permute-start | bytes 1769480 | tf_op jit(solution)/shard_map/ppermute | solution.py:601
  22.4 2.2 %collective-permute-start.2 = (bf16[192,768]{1,0:T(8,128)(2,1)}, bf16[192,768]{1,0:T(8,128)(2,1)S(1)}, u32[]{:S(2)}, u32[]{:S(2)}) collective-permute-start(bf16[192,768]{1,0:T(8,128)(2,1)} %scale.1.refs_4_), channel_id=1, source_target_pairs={{0,1},{1,0},{2,3},{3,2},{4,5},{5,4},{6,7},{7,6},{8,9},{9,8},{10,11... | collective-permute-start | bytes 884744 | tf_op jit(solution)/shard_map/ppermute | solution.py:601
  22.4 12.7 %collective-permute-start.7 = (bf16[192,768]{1,0:T(8,128)(2,1)}, bf16[192,768]{1,0:T(8,128)(2,1)}, u32[]{:S(2)}, u32[]{:S(2)}) collective-permute-start(bf16[192,768]{1,0:T(8,128)(2,1)} %scale.1.refs_4_), channel_id=1, source_target_pairs={{0,2},{1,3},{2,0},{3,1},{4,6},{5,7},{6,4},{7,5},{8,10},{9,11},{10,... | collective-permute-start | bytes 884744 | tf_op jit(solution)/shard_map/ppermute | solution.py:601
  30.8 4.4 %collective-permute-start.4 = (bf16[192,768]{1,0:T(8,128)(2,1)S(1)}, bf16[192,768]{1,0:T(8,128)(2,1)S(1)}, u32[]{:S(2)}, u32[]{:S(2)}) collective-permute-start(bf16[192,768]{1,0:T(8,128)(2,1)S(1)} %stream.1.stream_ref.refs_0_), channel_id=1, source_target_pairs={{0,1},{1,0},{2,3},{3,2},{4,5},{5,4},{6,7},{7,6},{8,9},{9,8},{10,11... | collective-permute-start | bytes 884744 | tf_op jit(solution)/shard_map/ppermute | solution.py:601
  30.9 9.4 %collective-permute-start.5 = (bf16[192,768]{1,0:T(8,128)(2,1)S(1)}, bf16[192,768]{1,0:T(8,128)(2,1)S(1)}, u32[]{:S(2)}, u32[]{:S(2)}) collective-permute-start(bf16[192,768]{1,0:T(8,128)(2,1)S(1)} %stream.1.stream_ref.refs_0_), channel_id=1, source_target_pairs={{0,2},{1,3},{2,0},{3,1},{4,6},{5,7},{6,4},{7,5},{8,10},{9,11},{10,... | collective-permute-start | bytes 884744 | tf_op jit(solution)/shard_map/ppermute | solution.py:601
  37.1 3.2 %collective-permute-start.8 = (bf16[192,768]{1,0:T(8,128)(2,1)S(1)}, bf16[192,768]{1,0:T(8,128)(2,1)S(1)}, u32[]{:S(2)}, u32[]{:S(2)}) collective-permute-start(bf16[192,768]{1,0:T(8,128)(2,1)S(1)} %get-tuple-element.46.refs_6_), channel_id=1, source_target_pairs={{0,1},{1,0},{2,3},{3,2},{4,5},{5,4},{6,7},{7,6},{8,9},{9,8},{10,11... | collective-permute-start | bytes 884744 | tf_op jit(solution)/shard_map/ppermute | solution.py:601
  40.3 1.6 %collective-permute-start.6 = (bf16[192,768]{1,0:T(8,128)(2,1)S(1)}, bf16[192,768]{1,0:T(8,128)(2,1)S(1)}, u32[]{:S(2)}, u32[]{:S(2)}) collective-permute-start(bf16[192,768]{1,0:T(8,128)(2,1)S(1)} %collective-permute-done.5.refs_2_.stream_ref), channel_id=1, source_target_pairs={{0,1},{1,0},{2,3},{3,2},{4,5},{5,4},{6,7},{7,6},{8,9},{9,8},{10,11... | collective-permute-start | bytes 884744 | tf_op jit(solution)/shard_map/ppermute | solution.py:601
  43.0 13.7 %collective-permute-start.9 = (bf16[384,384]{1,0:T(8,128)(2,1)S(1)}, bf16[384,384]{1,0:T(8,128)(2,1)S(1)}, u32[]{:S(2)}, u32[]{:S(2)}) collective-permute-start(bf16[384,384]{1,0:T(8,128)(2,1)S(1)} %get-tuple-element.58), channel_id=1, source_target_pairs={{0,4},{4,0},{8,12},{12,8},{16,20},{20,16},{24,28},{28,24},{1,5},{5... | collective-permute-start | bytes 884744 | tf_op jit(solution)/shard_map/ppermute | solution.py:601
  44.4 10.1 %collective-permute-start.12 = (bf16[96,384]{1,0:T(8,128)(2,1)S(1)}, bf16[96,384]{1,0:T(8,128)(2,1)S(1)}, u32[]{:S(2)}, u32[]{:S(2)}) collective-permute-start(bf16[96,384]{1,0:T(8,128)(2,1)S(1)} %get-tuple-element.69), channel_id=1, source_target_pairs={{0,16},{4,20},{8,24},{12,28},{16,0},{20,4},{24,8},{28,12},{1,17},{... | collective-permute-start | bytes 221192 | tf_op jit(solution)/shard_map/ppermute | solution.py:601
  45.6 10.3 %collective-permute-start.14 = (bf16[96,384]{1,0:T(8,128)(2,1)S(1)}, bf16[96,384]{1,0:T(8,128)(2,1)S(1)}, u32[]{:S(2)}, u32[]{:S(2)}) collective-permute-start(bf16[96,384]{1,0:T(8,128)(2,1)S(1)} %get-tuple-element.69), channel_id=1, source_target_pairs={{0,24},{4,28},{8,16},{12,20},{16,8},{20,12},{24,0},{28,4},{1,25},{... | collective-permute-start | bytes 221192 | tf_op jit(solution)/shard_map/ppermute | solution.py:601
  48.1 10.5 %collective-permute-start.10 = (bf16[192,384]{1,0:T(8,128)(2,1)S(1)}, bf16[192,384]{1,0:T(8,128)(2,1)S(1)}, u32[]{:S(2)}, u32[]{:S(2)}) collective-permute-start(bf16[192,384]{1,0:T(8,128)(2,1)S(1)} %get-tuple-element.63), channel_id=1, source_target_pairs={{0,8},{4,12},{8,0},{12,4},{16,24},{20,28},{24,16},{28,20},{1,9},{5... | collective-permute-start | bytes 442376 | tf_op jit(solution)/shard_map/ppermute | solution.py:601
  48.1 10.5 %collective-permute-start.11 = (bf16[192,384]{1,0:T(8,128)(2,1)S(1)}, bf16[192,384]{1,0:T(8,128)(2,1)S(1)}, u32[]{:S(2)}, u32[]{:S(2)}) collective-permute-start(bf16[192,384]{1,0:T(8,128)(2,1)S(1)} %get-tuple-element.63), channel_id=1, source_target_pairs={{0,12},{4,8},{8,4},{12,0},{16,28},{20,24},{24,20},{28,16},{1,13},{... | collective-permute-start | bytes 442376 | tf_op jit(solution)/shard_map/ppermute | solution.py:601
  54.5 8.1 %collective-permute-start.13 = (bf16[96,384]{1,0:T(8,128)(2,1)S(1)}, bf16[96,384]{1,0:T(8,128)(2,1)S(1)}, u32[]{:S(2)}, u32[]{:S(2)}) collective-permute-start(bf16[96,384]{1,0:T(8,128)(2,1)S(1)} %collective-permute-done.12.refs_1_), channel_id=1, source_target_pairs={{0,4},{4,0},{8,12},{12,8},{16,20},{20,16},{24,28},{28,24},{1,5},{5... | collective-permute-start | bytes 221192 | tf_op jit(solution)/shard_map/ppermute | solution.py:601
  55.9 6.7 %collective-permute-start.15 = (bf16[96,384]{1,0:T(8,128)(2,1)S(1)}, bf16[96,384]{1,0:T(8,128)(2,1)S(1)}, u32[]{:S(2)}, u32[]{:S(2)}) collective-permute-start(bf16[96,384]{1,0:T(8,128)(2,1)S(1)} %collective-permute-done.14.refs_3_), channel_id=1, source_target_pairs={{0,4},{4,0},{8,12},{12,8},{16,20},{20,16},{24,28},{28,24},{1,5},{5... | collective-permute-start | bytes 221192 | tf_op jit(solution)/shard_map/ppermute | solution.py:601
  60.7 8.4 %collective-permute-start.16 = (bf16[192,256]{1,0:T(8,128)(2,1)S(1)}, bf16[192,256]{1,0:T(8,128)(2,1)S(1)}, u32[]{:S(2)}, u32[]{:S(2)}) collective-permute-start(bf16[192,256]{1,0:T(8,128)(2,1)S(1)} %get-tuple-element.71), channel_id=1, source_target_pairs={{0,1},{1,0},{2,3},{3,2},{4,5},{5,4},{6,7},{7,6},{8,9},{9,8},{10,11... | collective-permute-start | bytes 294920 | tf_op jit(solution)/shard_map/ppermute | solution.py:601
  60.8 8.3 %collective-permute-start.17 = (bf16[192,256]{1,0:T(8,128)(2,1)S(1)}, bf16[192,256]{1,0:T(8,128)(2,1)S(1)}, u32[]{:S(2)}, u32[]{:S(2)}) collective-permute-start(bf16[192,256]{1,0:T(8,128)(2,1)S(1)} %get-tuple-element.72), channel_id=1, source_target_pairs={{0,2},{1,3},{2,0},{3,1},{4,6},{5,7},{6,4},{7,5},{8,10},{9,11},{10,... | collective-permute-start | bytes 294920 | tf_op jit(solution)/shard_map/ppermute | solution.py:601
  62.1 6.9 %collective-permute-start.18 = (bf16[192,256]{1,0:T(8,128)(2,1)S(1)}, bf16[192,256]{1,0:T(8,128)(2,1)S(1)}, u32[]{:S(2)}, u32[]{:S(2)}) collective-permute-start(bf16[192,256]{1,0:T(8,128)(2,1)S(1)} %get-tuple-element.73), channel_id=1, source_target_pairs={{0,3},{1,2},{2,1},{3,0},{4,7},{5,6},{6,5},{7,4},{8,11},{9,10},{10,... | collective-permute-start | bytes 294920 | tf_op jit(solution)/shard_map/ppermute | solution.py:601
  64.1 1.7 %collective-permute-start.19 = (bf16[32,256]{1,0:T(8,128)(2,1)S(1)}, bf16[32,256]{1,0:T(8,128)(2,1)S(1)}, u32[]{:S(2)}, u32[]{:S(2)}) collective-permute-start(bf16[32,256]{1,0:T(8,128)(2,1)S(1)} %get-tuple-element.74), channel_id=1, source_target_pairs={{0,1},{1,0},{2,3},{3,2},{4,5},{5,4},{6,7},{7,6},{8,9},{9,8},{10,11... | collective-permute-start | bytes 49160 | tf_op jit(solution)/shard_map/ppermute | solution.py:601
  64.5 3.9 %collective-permute-start.20 = (bf16[32,256]{1,0:T(8,128)(2,1)S(1)}, bf16[32,256]{1,0:T(8,128)(2,1)S(1)}, u32[]{:S(2)}, u32[]{:S(2)}) collective-permute-start(bf16[32,256]{1,0:T(8,128)(2,1)S(1)} %get-tuple-element.75), channel_id=1, source_target_pairs={{0,2},{1,3},{2,0},{3,1},{4,6},{5,7},{6,4},{7,5},{8,10},{9,11},{10,... | collective-permute-start | bytes 49160 | tf_op jit(solution)/shard_map/ppermute | solution.py:601
  65.8 3.3 %collective-permute-start.21 = (bf16[32,256]{1,0:T(8,128)(2,1)S(1)}, bf16[32,256]{1,0:T(8,128)(2,1)S(1)}, u32[]{:S(2)}, u32[]{:S(2)}) collective-permute-start(bf16[32,256]{1,0:T(8,128)(2,1)S(1)} %get-tuple-element.76), channel_id=1, source_target_pairs={{0,3},{1,2},{2,1},{3,0},{4,7},{5,6},{6,5},{7,4},{8,11},{9,10},{10,... | collective-permute-start | bytes 49160 | tf_op jit(solution)/shard_map/ppermute | solution.py:601
  (6 other events, 55.4 us)

commit v5 on v4

--- a/solution.py
+++ b/solution.py
@@ -198,15 +198,15 @@
 
 def project_kernel(n_seq, n_tp, peer, recv_hbm, early_ref, beside_ref, *refs):
     del early_ref, beside_ref
-    weight_refs = refs[: n_tp - 1]
-    total_ref, later_ref, codes_ref, ids_ref, recv_ref, sems = refs[n_tp - 1 :]
+    weight_refs = refs[:n_tp]
+    stream_ref, codes_ref, ids_ref, recv_ref, sems = refs[n_tp:]
     fetches = []
     for source in range(n_seq):
         some = pl.ds(source * n_tp, n_tp)
         fetches.append(pltpu.make_async_copy(recv_hbm.at[some], recv_ref.at[some], sems.at[source]))
         fetches[-1].start()
     sub_pad = up_to(peer // n_tp, 8)
-    chunks = later_ref.shape[1] // LANES
+    chunks = weight_refs[0].shape[0] // LANES
     column = lax.axis_index("tp")
     code_rows = codes_ref.shape[2] // LANES
     share = ids_ref.shape[1] // n_tp
@@ -224,10 +224,10 @@
         ]
         laid.append(jnp.concatenate(columns, axis=1))
     total = None
-    for turn in range(1, n_tp):
-        part_sum = dot(laid[turn], weight_refs[turn - 1][...])
+    for turn in reversed(range(n_tp)):
+        part_sum = dot(laid[turn], weight_refs[turn][...])
         total = part_sum if total is None else total + part_sum
-    total_ref[...] = total
+    stream_ref[...] = total.astype(BF16)
     for source in range(n_seq):
         pieces = []
         for other in range(n_tp):
@@ -236,7 +236,6 @@
                 length = min(LANES, share - piece * LANES)
                 pieces.append(note[code_rows + piece : code_rows + piece + 1, :length])
         ids_ref[source : source + 1, :] = jnp.concatenate(pieces, axis=1)
-    later_ref[...] = laid[0]
     for turn in range(n_tp):
         codes = notes[turn]
         power = jnp.zeros((8, LANES), F32)
@@ -248,10 +247,6 @@
         spots = jnp.where(codes > 0.0, codes * scale - 128.0 + power, -1.0)
         for piece in range(code_rows):
             codes_ref[turn, :, piece * LANES : (piece + 1) * LANES] = spots[piece : piece + 1].astype(jnp.int32)
-
-
-def stream_kernel(total_ref, later_ref, weight_ref, stream_ref):
-    stream_ref[...] = (total_ref[...] + dot(later_ref[...], weight_ref[...])).astype(BF16)
 
 
 def key_value_query(stream, gain, weights):
@@ -393,25 +388,25 @@
     value = dot(pairs, spreads_ref[1])
     values_ref[...] = (value + ones).astype(BF16)
     half = rows // 2
-    slot_of = iota((half, wide), 1) >> 6
-    for part in range(2):
-        start = part * half
-        query = masked_ref[start : start + half, :]
-        acc = None
-        for head in range(heads):
-            one = jnp.where(slot_of == head, query, jnp.zeros((), BF16))
-            scores = dot_nt(one, keys_ref[...])
-            top = jnp.max(scores, axis=1, keepdims=True)
-            tops_ref[head, start : start + half, :] = jnp.broadcast_to(top, (half, LANES))
-            weights = jnp.exp(scores - top)
-            if part == (head & 1):
-                times = dot_tn(*agreement(0, [(head, start)], column, rows, half, half))
-                scaled = weights[:, start : start + half] * times
-                others = weights[:, half - start : rows - start]
-                weights = jnp.concatenate([scaled, others] if part == 0 else [others, scaled], axis=1)
-            got = dot(weights.astype(BF16), values_ref[...])
-            acc = got if acc is None else jnp.where(slot_of == head, got, acc)
-        acc_ref[start : start + half, :] = acc
+    slot_of = iota((rows, wide), 1) >> 6
+    query = masked_ref[...]
+    acc = None
+    for head in range(heads):
+        one = jnp.where(slot_of == head, query, jnp.zeros((), BF16))
+        scores = dot_nt(one, keys_ref[...])
+        top = jnp.max(scores, axis=1, keepdims=True)
+        tops_ref[head] = jnp.broadcast_to(top, (rows, LANES))
+        weights = jnp.exp(scores - top)
+        start = (head & 1) * half
+        times = dot_tn(*agreement(0, [(head, start)], column, rows, half, half))
+        scaled = weights[start : start + half, start : start + half] * times
+        others = weights[start : start + half, half - start : rows - start]
+        part = jnp.concatenate([others, scaled] if start else [scaled, others], axis=1)
+        rest = weights[half - start : rows - start]
+        weights = jnp.concatenate([rest, part] if start else [part, rest], axis=0)
+        got = dot(weights.astype(BF16), values_ref[...])
+        acc = got if acc is None else jnp.where(slot_of == head, got, acc)
+    acc_ref[...] = acc
 
 
 def weigh_inner(weights, group, column, rows):
@@ -673,12 +668,12 @@
     )
 
     beside = swap(scaled, "tp", 1)
-    total, later, codes, ids = call(
+    stream, codes, ids = call(
         functools.partial(project_kernel, n_seq, n_tp, peer),
         "project",
-        [((arriving, features), F32), ((arriving, tile_width), BF16)]
+        [((arriving, features), BF16)]
         + [((n_tp, 1, up_to(arriving, LANES)), jnp.int32), ((n_seq, rows), F32)],
-        [received, early, beside] + proj_parts[1:],
+        [received, early, beside] + proj_parts,
         cost=0.5,
         scratch=[
             pltpu.VMEM(received.shape, BF16),
@@ -686,14 +681,6 @@
         ],
         vmem_bytes=vmem_bytes,
         apart=(0,),
-    )
-    (stream,) = call(
-        stream_kernel,
-        "stream",
-        [((arriving, features), BF16)],
-        [total, later, proj_weight],
-        cost=0.1,
-        vmem_bytes=vmem_bytes,
     )
     shards = gather_tp(stream)
 

time: 71.2 us -> 71 us (level)
    pallas_call x15 -> x14, Pallas kernels: 25.4 us -> 25 us  [call(): pl.pallas_call(kernel, name=name, out_shape=[jax.ShapeDtypeStruct(shape,...]
  transfers between devices with their start and end apart: 23 -> 23, of which waited for: 6 -> 7; matrix products, arithmetic and copies ran while one was open for 0% -> 0% of each run, Pallas kernels for 32% -> 31%
where the time goes in v5:
time: 71 us; the launch traced here: 70.7 us
  starting transfers between devices  26.3 us (37%)
  Pallas kernels  25 us (35%)
  waiting for transfers between devices  19.2 us (27%)
    pallas_call x14, Pallas kernels, call(): pl.pallas_call(kernel, name=name, out_shape=[jax.ShapeDtypeStruct(shape,...  25 us
    ppermute x22, starting transfers between devices, swap(): lax.ppermute(block, axis, [(index, index ^ mask) for index in range(count)])  21.4 us
    ppermute x22, waiting for transfers between devices, swap(): lax.ppermute(block, axis, [(index, index ^ mask) for index in range(count)])  14.9 us
    all_to_all x1, starting transfers between devices, body(): lax.all_to_all(blocks, ('seq', 'tp'), split_axis=0, concat_axis=0, tiled=...  4.9 us
    all_to_all x1, waiting for transfers between devices, body(): lax.all_to_all(blocks, ('seq', 'tp'), split_axis=0, concat_axis=0, tiled=...  4.27 us
  transfers between devices with their start and end apart: 23, of which 7 were waited for; matrix products, arithmetic and copies ran while one was open for 0% of the time, Pallas kernels for 31%

profile of v5, /device:TPU:0, one launch (start us, length us, event | category | flops | bytes accessed | tf_op | source)
XLA Modules:
  0.0 70.7 jit_solution(12140453759676508758)
XLA Ops:
  0.0 3.0 %collective-permute-start = (bf16[384,768]{1,0:T(8,128)(2,1)}, bf16[384,768]{1,0:T(8,128)(2,1)S(1)}, u32[]{:S(2)}, u32[]{:S(2)}) collective-permute-start(bf16[384,768]{1,0:T(8,128)(2,1)} %refs_0_.1), channel_id=1, source_target_pairs={{0,2},{1,3},{2,0},{3,1},{4,6},{5,7},{6,4},{7,5},{8,10},{9,11},{10,... | collective-permute-start | bytes 1769480 | tf_op jit(solution)/shard_map/ppermute | solution.py:596
  3.0 3.1 %route.1 = bf16[32,80,128]{2,1,0:T(8,128)(2,1)} custom-call(s32[6,128]{1,0:T(8,128)} %bitcast.24, s32[6,128]{1,0:T(8,128)} %bitcast.25, bf16[768,384]{1,0:T(8,128)(2,1)} %tiles_hbm.1), custom_call_target="tpu_custom_call" | custom-call | flops 3000000000 | tf_op jit(solution)/shard_map/route/pallas_call | solution.py:69
  6.1 4.9 %all-to-all-start = ((bf16[32,80,128]{2,1,0:T(8,128)(2,1)}), bf16[32,80,128]{2,1,0:T(8,128)(2,1)S(1)}, u32[]{:S(2)}, u32[]{:S(2)}) async-start(bf16[32,80,128]{2,1,0:T(8,128)(2,1)} %route.1), calls=%async_computation | async-start | bytes 1310720 | tf_op jit(solution)/shard_map/all_to_all | solution.py:657
  11.0 10.0 %collective-permute-done.refs_2_ = bf16[384,768]{1,0:T(8,128)(2,1)S(1)} collective-permute-done((bf16[384,768]{1,0:T(8,128)(2,1)}, bf16[384,768]{1,0:T(8,128)(2,1)S(1)}, u32[]{:S(2)}, u32[]{:S(2)}) %collective-permute-start) | collective-permute-done | bytes 589856 | tf_op jit(solution)/shard_map/ppermute | solution.py:596
  22.4 2.1 %collective-permute-start.7 = (bf16[192,768]{1,0:T(8,128)(2,1)}, bf16[192,768]{1,0:T(8,128)(2,1)}, u32[]{:S(2)}, u32[]{:S(2)}) collective-permute-start(bf16[192,768]{1,0:T(8,128)(2,1)} %scale.1.refs_4_), channel_id=1, source_target_pairs={{0,2},{1,3},{2,0},{3,1},{4,6},{5,7},{6,4},{7,5},{8,10},{9,11},{10,... | collective-permute-start | bytes 884744 | tf_op jit(solution)/shard_map/ppermute | solution.py:596
  24.6 4.3 %all-to-all-done.recv_hbm = bf16[32,80,128]{2,1,0:T(8,128)(2,1)S(1)} async-done(((bf16[32,80,128]{2,1,0:T(8,128)(2,1)}), bf16[32,80,128]{2,1,0:T(8,128)(2,1)S(1)}, u32[]{:S(2)}, u32[]{:S(2)}) %all-to-all-start) | async-done | bytes 655392 | tf_op jit(solution)/shard_map/all_to_all | solution.py:657
  28.9 1.7 %project.1 = (bf16[192,768]{1,0:T(8,128)(2,1)S(1)}, s32[4,1,256]{2,1,0:T(1,128)S(1)}, f32[8,768]{1,0:T(8,128)S(1)}) custom-call(bf16[32,80,128]{2,1,0:T(8,128)(2,1)S(1)} %all-to-all-done.recv_hbm, bf16[16,128]{1,0:T(8,128)(2,1)S(1)} %hint.1.early_ref, bf16[192,768]{1,0:T(8,128)(2,1)S(1)} %collective-permute-done.2.beside_ref.refs_5_, ...), custom_call_target="tpu_custom_call" | custom-call | flops 500000000 | tf_op jit(solution)/shard_map/project/pallas_call | solution.py:69
  30.7 1.6 %collective-permute-start.5 = (bf16[192,768]{1,0:T(8,128)(2,1)S(1)}, bf16[192,768]{1,0:T(8,128)(2,1)S(1)}, u32[]{:S(2)}, u32[]{:S(2)}) collective-permute-start(bf16[192,768]{1,0:T(8,128)(2,1)S(1)} %get-tuple-element.41.stream_ref.refs_0_), channel_id=1, source_target_pairs={{0,2},{1,3},{2,0},{3,1},{4,6},{5,7},{6,4},{7,5},{8,10},{9,11},{10,... | collective-permute-start | bytes 884744 | tf_op jit(solution)/shard_map/ppermute | solution.py:596
  32.3 2.6 %heads_1.1 = (bf16[768,576]{1,0:T(8,128)(2,1)S(1)}, bf16[768,256]{1,0:T(8,128)(2,1)S(1)}, bf16[768,256]{1,0:T(8,128)(2,1)S(1)}, bf16[4,192,768]{2,1,0:T(8,128)(2...) custom-call(s32[4,1,256]{2,1,0:T(1,128)S(1)} %get-tuple-element.40.c, ...), custom_call_target="tpu_custom_call" | custom-call | flops 1000000000 | tf_op jit(solution)/shard_map/heads_1/pallas_call | solution.py:69
  35.0 1.9 %heads_2.2 = (bf16[768,576]{1,0:T(8,128)(2,1)S(1)}, bf16[192,768]{1,0:T(8,128)(2,1)S(1)}) custom-call(s32[4,1,256]{2,1,0:T(1,128)S(1)} %get-tuple-element.40.codes_ref, f32[6,128]{1,0:T(8,128)S(1)} %bitcast.20, bf16[192,768]{1,0:T(8,128)(2,1)S(1)} %bitcast.8, bf16[192,768]{1,0:T(8,128)(2,1)S(1)} %bitcast.12, bf16[192,768]{1,0:T(8,128)(2,1)S(1)} %bitcast.16, ...), custom_call_target="tpu_custom_call" | custom-call | flops 1000000000 | tf_op jit(solution)/shard_map/heads_2/pallas_call | solution.py:69
  37.0 3.1 %collective-permute-done.5.refs_2_.stream_ref = bf16[192,768]{1,0:T(8,128)(2,1)S(1)} collective-permute-done((bf16[192,768]{1,0:T(8,128)(2,1)S(1)}, bf16[192,768]{1,0:T(8,128)(2,1)S(1)}, u32[]{:S(2)}, u32[]{:S(2)}) %collective-permute-start.5) | collective-permute-done | bytes 294944 | tf_op jit(solution)/shard_map/ppermute | solution.py:596
  42.8 1.5 %collective-permute-start.9 = (bf16[384,384]{1,0:T(8,128)(2,1)S(1)}, bf16[384,384]{1,0:T(8,128)(2,1)S(1)}, u32[]{:S(2)}, u32[]{:S(2)}) collective-permute-start(bf16[384,384]{1,0:T(8,128)(2,1)S(1)} %get-tuple-element.56), channel_id=1, source_target_pairs={{0,4},{4,0},{8,12},{12,8},{16,20},{20,16},{24,28},{28,24},{1,5},{5... | collective-permute-start | bytes 884744 | tf_op jit(solution)/shard_map/ppermute | solution.py:596
  44.3 1.4 %collective-permute-start.12 = (bf16[96,384]{1,0:T(8,128)(2,1)S(1)}, bf16[96,384]{1,0:T(8,128)(2,1)S(1)}, u32[]{:S(2)}, u32[]{:S(2)}) collective-permute-start(bf16[96,384]{1,0:T(8,128)(2,1)S(1)} %get-tuple-element.67), channel_id=1, source_target_pairs={{0,16},{4,20},{8,24},{12,28},{16,0},{20,4},{24,8},{28,12},{1,17},{... | collective-permute-start | bytes 221192 | tf_op jit(solution)/shard_map/ppermute | solution.py:596
  45.6 2.5 %collective-permute-start.14 = (bf16[96,384]{1,0:T(8,128)(2,1)S(1)}, bf16[96,384]{1,0:T(8,128)(2,1)S(1)}, u32[]{:S(2)}, u32[]{:S(2)}) collective-permute-start(bf16[96,384]{1,0:T(8,128)(2,1)S(1)} %get-tuple-element.67), channel_id=1, source_target_pairs={{0,24},{4,28},{8,16},{12,20},{16,8},{20,12},{24,0},{28,4},{1,25},{... | collective-permute-start | bytes 221192 | tf_op jit(solution)/shard_map/ppermute | solution.py:596
  48.1 2.0 %collective-permute-start.11 = (bf16[192,384]{1,0:T(8,128)(2,1)S(1)}, bf16[192,384]{1,0:T(8,128)(2,1)S(1)}, u32[]{:S(2)}, u32[]{:S(2)}) collective-permute-start(bf16[192,384]{1,0:T(8,128)(2,1)S(1)} %get-tuple-element.61), channel_id=1, source_target_pairs={{0,12},{4,8},{8,4},{12,0},{16,28},{20,24},{24,20},{28,16},{1,13},{... | collective-permute-start | bytes 442376 | tf_op jit(solution)/shard_map/ppermute | solution.py:596
  50.1 4.0 %own.1 = (f32[768,256]{1,0:T(8,128)S(1)}, f32[4,768,128]{2,1,0:T(8,128)S(1)}, bf16[768,256]{1,0:T(8,128)(2,1)S(1)}) custom-call(bf16[768,576]{1,0:T(8,128)(2,1)S(1)} %get-tuple-element.48.packed_ref, bf16[768,256]{1,0:T(8,128)(2,1)S(1)} %get-tuple-element.49.same_ref, bf16[768,256]{1,0:T(8,128)(2,1)S(1)} %get-tuple-element.50.apart_ref, ...), custom_call_target="tpu_custom_call" | custom-call | flops 100000000 | tf_op jit(solution)/shard_map/own/pallas_call | solution.py:69
  54.1 1.6 %collective-permute-start.13 = (bf16[96,384]{1,0:T(8,128)(2,1)S(1)}, bf16[96,384]{1,0:T(8,128)(2,1)S(1)}, u32[]{:S(2)}, u32[]{:S(2)}) collective-permute-start(bf16[96,384]{1,0:T(8,128)(2,1)S(1)} %collective-permute-done.12.refs_1_), channel_id=1, source_target_pairs={{0,4},{4,0},{8,12},{12,8},{16,20},{20,16},{24,28},{28,24},{1,5},{5... | collective-permute-start | bytes 221192 | tf_op jit(solution)/shard_map/ppermute | solution.py:596
  56.2 2.0 %near.1 = (f32[768,256]{1,0:T(8,128)S(1)}, f32[4,768,128]{2,1,0:T(8,128)S(1)}) custom-call(f32[768,256]{1,0:T(8,128)S(1)} %get-tuple-element.52.acc_ref, f32[4,768,128]{2,1,0:T(8,128)S(1)} %get-tuple-element.53.tops_ref, bf16[768,256]{1,0:T(8,128)(2,1)S(1)} %get-tuple-element.54.query_ref, ...), custom_call_target="tpu_custom_call", output_to_operand_aliasing={{0}: (0, {}), {1}: (1, {})} | custom-call | flops 6000000000 | tf_op jit(solution)/shard_map/near/pallas_call | solution.py:69
  58.4 2.0 %mid.1 = (f32[768,256]{1,0:T(8,128)S(1)}, f32[4,768,128]{2,1,0:T(8,128)S(1)}, bf16[768,256]{1,0:T(8,128)(2,1)S(1)}, f32[768,256]{1,0:T(8,128)S(1)}, bf16[192,256...) custom-call(f32[768,256]{1,0:T(8,128)S(1)} %get-tuple-element.57.acc, ...), custom_call_target="tpu_custom_call", output_to_operand_aliasing={{0}: (0, {}), {1}: (1, {})} | custom-call | flops 6000000000 | tf_op jit(solution)/shard_map/mid/pallas_call | solution.py:69
  60.6 1.4 %collective-permute-start.17 = (bf16[192,256]{1,0:T(8,128)(2,1)S(1)}, bf16[192,256]{1,0:T(8,128)(2,1)S(1)}, u32[]{:S(2)}, u32[]{:S(2)}) collective-permute-start(bf16[192,256]{1,0:T(8,128)(2,1)S(1)} %get-tuple-element.70), channel_id=1, source_target_pairs={{0,2},{1,3},{2,0},{3,1},{4,6},{5,7},{6,4},{7,5},{8,10},{9,11},{10,... | collective-permute-start | bytes 294920 | tf_op jit(solution)/shard_map/ppermute | solution.py:596
  62.4 1.4 %far.1 = (bf16[192,256]{1,0:T(8,128)(2,1)S(1)}, bf16[32,256]{1,0:T(8,128)(2,1)S(1)}, bf16[32,256]{1,0:T(8,128)(2,1)S(1)}, bf16[32,256]{1,0:T(8,128)(2,1)S(1)}) custom-call(f32[768,256]{1,0:T(8,128)S(1)} %get-tuple-element.62.acc_ref, f32[4,768,128]{2,1,0:T(8,128)S(1)} %get-tuple-element.63.tops_ref, bf16[768,256]{1,0:T(8,128)(2,1)S(1)} %get-tuple-element.54.query_ref, ...), custom_call_target="tpu_custom_call" | custom-call | flops 1000000000 | tf_op jit(solution)/shard_map/far/pallas_call | solution.py:69
  64.3 1.3 %collective-permute-start.20 = (bf16[32,256]{1,0:T(8,128)(2,1)S(1)}, bf16[32,256]{1,0:T(8,128)(2,1)S(1)}, u32[]{:S(2)}, u32[]{:S(2)}) collective-permute-start(bf16[32,256]{1,0:T(8,128)(2,1)S(1)} %get-tuple-element.73), channel_id=1, source_target_pairs={{0,2},{1,3},{2,0},{3,1},{4,6},{5,7},{6,4},{7,5},{8,10},{9,11},{10,... | collective-permute-start | bytes 49160 | tf_op jit(solution)/shard_map/ppermute | solution.py:596
  66.4 1.5 %base.1 = (bf16[192,768]{1,0:T(8,128)(2,1)S(1)}, bf16[4,256,768]{2,1,0:T(8,128)(2,1)S(1)}) custom-call(s32[4,1,256]{2,1,0:T(1,128)S(1)} %get-tuple-element.40.codes_ref, bf16[192,768]{1,0:T(8,128)(2,1)S(1)} %get-tuple-element.41.stream_ref.refs_0_, bf16[192,768]{1,0:T(8,128)(2,1)S(1)} %collective-permute-done.4.stream_ref.refs_1_, ...), custom_call_target="tpu_custom_call" | custom-call | flops 300000000 | tf_op jit(solution)/shard_map/base/pallas_call | solution.py:69
  68.9 1.8 %mix.1 = bf16[192,768]{1,0:T(8,128)(2,1)} custom-call(bf16[192,768]{1,0:T(8,128)(2,1)S(1)} %get-tuple-element.45.base_ref, bf16[4,256,768]{2,1,0:T(8,128)(2,1)S(1)} %get-tuple-element.46.weights_ref, bf16[192,256]{1,0:T(8,128)(2,1)S(1)} %get-tuple-element.68.refs_0_, bf16[192,256]{1,0:T(8,128)(2,1)S(1)} %collective-permute-done.16.refs_1_, ...), custom_call_target="tpu_custom_call" | custom-call | flops 1000000000 | tf_op jit(solution)/shard_map/mix/pallas_call | solution.py:69
  (50 shorter events, 7.7 us)
Async XLA Ops:
  0.0 21.0 %collective-permute-start = (bf16[384,768]{1,0:T(8,128)(2,1)}, bf16[384,768]{1,0:T(8,128)(2,1)S(1)}, u32[]{:S(2)}, u32[]{:S(2)}) collective-permute-start(bf16[384,768]{1,0:T(8,128)(2,1)} %refs_0_.1), channel_id=1, source_target_pairs={{0,2},{1,3},{2,0},{3,1},{4,6},{5,7},{6,4},{7,5},{8,10},{9,11},{10,... | collective-permute-start | bytes 1769480 | tf_op jit(solution)/shard_map/ppermute | solution.py:596
  3.0 18.5 %copy-start.6 = (f32[192]{0:T(256)S(1)}, f32[192]{0:T(256)}, u32[]{:S(2)}) copy-start(f32[192]{0:T(256)} %param.18) | copy-start | bytes 2308
  6.1 22.8 %all-to-all-start = ((bf16[32,80,128]{2,1,0:T(8,128)(2,1)}), bf16[32,80,128]{2,1,0:T(8,128)(2,1)S(1)}, u32[]{:S(2)}, u32[]{:S(2)}) async-start(bf16[32,80,128]{2,1,0:T(8,128)(2,1)} %route.1), calls=%async_computation | async-start | bytes 1310720 | tf_op jit(solution)/shard_map/all_to_all | solution.py:657
  21.0 3.6 %collective-permute-start.1 = (bf16[384,768]{1,0:T(8,128)(2,1)S(1)}, bf16[384,768]{1,0:T(8,128)(2,1)S(1)}, u32[]{:S(2)}, u32[]{:S(2)}) collective-permute-start(bf16[384,768]{1,0:T(8,128)(2,1)S(1)} %collective-permute-done.refs_2_), channel_id=1, source_target_pairs={{0,1},{1,0},{2,3},{3,2},{4,5},{5,4},{6,7},{7,6},{8,9},{9,8},{10,11... | collective-permute-start | bytes 1769480 | tf_op jit(solution)/shard_map/ppermute | solution.py:596
  21.0 3.6 %collective-permute-start.3 = (bf16[384,768]{1,0:T(8,128)(2,1)S(1)}, bf16[384,768]{1,0:T(8,128)(2,1)S(1)}, u32[]{:S(2)}, u32[]{:S(2)}) collective-permute-start(bf16[384,768]{1,0:T(8,128)(2,1)S(1)} %copy-done), channel_id=1, source_target_pairs={{0,1},{1,0},{2,3},{3,2},{4,5},{5,4},{6,7},{7,6},{8,9},{9,8},{10,11... | collective-permute-start | bytes 1769480 | tf_op jit(solution)/shard_map/ppermute | solution.py:596
  22.4 2.2 %collective-permute-start.2 = (bf16[192,768]{1,0:T(8,128)(2,1)}, bf16[192,768]{1,0:T(8,128)(2,1)S(1)}, u32[]{:S(2)}, u32[]{:S(2)}) collective-permute-start(bf16[192,768]{1,0:T(8,128)(2,1)} %scale.1.refs_4_), channel_id=1, source_target_pairs={{0,1},{1,0},{2,3},{3,2},{4,5},{5,4},{6,7},{7,6},{8,9},{9,8},{10,11... | collective-permute-start | bytes 884744 | tf_op jit(solution)/shard_map/ppermute | solution.py:596
  22.4 12.5 %collective-permute-start.7 = (bf16[192,768]{1,0:T(8,128)(2,1)}, bf16[192,768]{1,0:T(8,128)(2,1)}, u32[]{:S(2)}, u32[]{:S(2)}) collective-permute-start(bf16[192,768]{1,0:T(8,128)(2,1)} %scale.1.refs_4_), channel_id=1, source_target_pairs={{0,2},{1,3},{2,0},{3,1},{4,6},{5,7},{6,4},{7,5},{8,10},{9,11},{10,... | collective-permute-start | bytes 884744 | tf_op jit(solution)/shard_map/ppermute | solution.py:596
  30.6 4.3 %collective-permute-start.4 = (bf16[192,768]{1,0:T(8,128)(2,1)S(1)}, bf16[192,768]{1,0:T(8,128)(2,1)S(1)}, u32[]{:S(2)}, u32[]{:S(2)}) collective-permute-start(bf16[192,768]{1,0:T(8,128)(2,1)S(1)} %get-tuple-element.41.stream_ref.refs_0_), channel_id=1, source_target_pairs={{0,1},{1,0},{2,3},{3,2},{4,5},{5,4},{6,7},{7,6},{8,9},{9,8},{10,11... | collective-permute-start | bytes 884744 | tf_op jit(solution)/shard_map/ppermute | solution.py:596
  30.7 9.4 %collective-permute-start.5 = (bf16[192,768]{1,0:T(8,128)(2,1)S(1)}, bf16[192,768]{1,0:T(8,128)(2,1)S(1)}, u32[]{:S(2)}, u32[]{:S(2)}) collective-permute-start(bf16[192,768]{1,0:T(8,128)(2,1)S(1)} %get-tuple-element.41.stream_ref.refs_0_), channel_id=1, source_target_pairs={{0,2},{1,3},{2,0},{3,1},{4,6},{5,7},{6,4},{7,5},{8,10},{9,11},{10,... | collective-permute-start | bytes 884744 | tf_op jit(solution)/shard_map/ppermute | solution.py:596
  36.9 3.2 %collective-permute-start.8 = (bf16[192,768]{1,0:T(8,128)(2,1)S(1)}, bf16[192,768]{1,0:T(8,128)(2,1)S(1)}, u32[]{:S(2)}, u32[]{:S(2)}) collective-permute-start(bf16[192,768]{1,0:T(8,128)(2,1)S(1)} %get-tuple-element.44.refs_6_), channel_id=1, source_target_pairs={{0,1},{1,0},{2,3},{3,2},{4,5},{5,4},{6,7},{7,6},{8,9},{9,8},{10,11... | collective-permute-start | bytes 884744 | tf_op jit(solution)/shard_map/ppermute | solution.py:596
  40.1 1.6 %collective-permute-start.6 = (bf16[192,768]{1,0:T(8,128)(2,1)S(1)}, bf16[192,768]{1,0:T(8,128)(2,1)S(1)}, u32[]{:S(2)}, u32[]{:S(2)}) collective-permute-start(bf16[192,768]{1,0:T(8,128)(2,1)S(1)} %collective-permute-done.5.refs_2_.stream_ref), channel_id=1, source_target_pairs={{0,1},{1,0},{2,3},{3,2},{4,5},{5,4},{6,7},{7,6},{8,9},{9,8},{10,11... | collective-permute-start | bytes 884744 | tf_op jit(solution)/shard_map/ppermute | solution.py:596
  42.8 13.4 %collective-permute-start.9 = (bf16[384,384]{1,0:T(8,128)(2,1)S(1)}, bf16[384,384]{1,0:T(8,128)(2,1)S(1)}, u32[]{:S(2)}, u32[]{:S(2)}) collective-permute-start(bf16[384,384]{1,0:T(8,128)(2,1)S(1)} %get-tuple-element.56), channel_id=1, source_target_pairs={{0,4},{4,0},{8,12},{12,8},{16,20},{20,16},{24,28},{28,24},{1,5},{5... | collective-permute-start | bytes 884744 | tf_op jit(solution)/shard_map/ppermute | solution.py:596
  44.3 9.8 %collective-permute-start.12 = (bf16[96,384]{1,0:T(8,128)(2,1)S(1)}, bf16[96,384]{1,0:T(8,128)(2,1)S(1)}, u32[]{:S(2)}, u32[]{:S(2)}) collective-permute-start(bf16[96,384]{1,0:T(8,128)(2,1)S(1)} %get-tuple-element.67), channel_id=1, source_target_pairs={{0,16},{4,20},{8,24},{12,28},{16,0},{20,4},{24,8},{28,12},{1,17},{... | collective-permute-start | bytes 221192 | tf_op jit(solution)/shard_map/ppermute | solution.py:596
  45.6 10.1 %collective-permute-start.14 = (bf16[96,384]{1,0:T(8,128)(2,1)S(1)}, bf16[96,384]{1,0:T(8,128)(2,1)S(1)}, u32[]{:S(2)}, u32[]{:S(2)}) collective-permute-start(bf16[96,384]{1,0:T(8,128)(2,1)S(1)} %get-tuple-element.67), channel_id=1, source_target_pairs={{0,24},{4,28},{8,16},{12,20},{16,8},{20,12},{24,0},{28,4},{1,25},{... | collective-permute-start | bytes 221192 | tf_op jit(solution)/shard_map/ppermute | solution.py:596
  48.1 10.1 %collective-permute-start.10 = (bf16[192,384]{1,0:T(8,128)(2,1)S(1)}, bf16[192,384]{1,0:T(8,128)(2,1)S(1)}, u32[]{:S(2)}, u32[]{:S(2)}) collective-permute-start(bf16[192,384]{1,0:T(8,128)(2,1)S(1)} %get-tuple-element.61), channel_id=1, source_target_pairs={{0,8},{4,12},{8,0},{12,4},{16,24},{20,28},{24,16},{28,20},{1,9},{5... | collective-permute-start | bytes 442376 | tf_op jit(solution)/shard_map/ppermute | solution.py:596
  48.1 10.3 %collective-permute-start.11 = (bf16[192,384]{1,0:T(8,128)(2,1)S(1)}, bf16[192,384]{1,0:T(8,128)(2,1)S(1)}, u32[]{:S(2)}, u32[]{:S(2)}) collective-permute-start(bf16[192,384]{1,0:T(8,128)(2,1)S(1)} %get-tuple-element.61), channel_id=1, source_target_pairs={{0,12},{4,8},{8,4},{12,0},{16,28},{20,24},{24,20},{28,16},{1,13},{... | collective-permute-start | bytes 442376 | tf_op jit(solution)/shard_map/ppermute | solution.py:596
  54.1 8.3 %collective-permute-start.13 = (bf16[96,384]{1,0:T(8,128)(2,1)S(1)}, bf16[96,384]{1,0:T(8,128)(2,1)S(1)}, u32[]{:S(2)}, u32[]{:S(2)}) collective-permute-start(bf16[96,384]{1,0:T(8,128)(2,1)S(1)} %collective-permute-done.12.refs_1_), channel_id=1, source_target_pairs={{0,4},{4,0},{8,12},{12,8},{16,20},{20,16},{24,28},{28,24},{1,5},{5... | collective-permute-start | bytes 221192 | tf_op jit(solution)/shard_map/ppermute | solution.py:596
  55.7 6.7 %collective-permute-start.15 = (bf16[96,384]{1,0:T(8,128)(2,1)S(1)}, bf16[96,384]{1,0:T(8,128)(2,1)S(1)}, u32[]{:S(2)}, u32[]{:S(2)}) collective-permute-start(bf16[96,384]{1,0:T(8,128)(2,1)S(1)} %collective-permute-done.14.refs_3_), channel_id=1, source_target_pairs={{0,4},{4,0},{8,12},{12,8},{16,20},{20,16},{24,28},{28,24},{1,5},{5... | collective-permute-start | bytes 221192 | tf_op jit(solution)/shard_map/ppermute | solution.py:596
  60.5 8.4 %collective-permute-start.16 = (bf16[192,256]{1,0:T(8,128)(2,1)S(1)}, bf16[192,256]{1,0:T(8,128)(2,1)S(1)}, u32[]{:S(2)}, u32[]{:S(2)}) collective-permute-start(bf16[192,256]{1,0:T(8,128)(2,1)S(1)} %get-tuple-element.69), channel_id=1, source_target_pairs={{0,1},{1,0},{2,3},{3,2},{4,5},{5,4},{6,7},{7,6},{8,9},{9,8},{10,11... | collective-permute-start | bytes 294920 | tf_op jit(solution)/shard_map/ppermute | solution.py:596
  60.6 8.3 %collective-permute-start.17 = (bf16[192,256]{1,0:T(8,128)(2,1)S(1)}, bf16[192,256]{1,0:T(8,128)(2,1)S(1)}, u32[]{:S(2)}, u32[]{:S(2)}) collective-permute-start(bf16[192,256]{1,0:T(8,128)(2,1)S(1)} %get-tuple-element.70), channel_id=1, source_target_pairs={{0,2},{1,3},{2,0},{3,1},{4,6},{5,7},{6,4},{7,5},{8,10},{9,11},{10,... | collective-permute-start | bytes 294920 | tf_op jit(solution)/shard_map/ppermute | solution.py:596
  62.0 6.9 %collective-permute-start.18 = (bf16[192,256]{1,0:T(8,128)(2,1)S(1)}, bf16[192,256]{1,0:T(8,128)(2,1)S(1)}, u32[]{:S(2)}, u32[]{:S(2)}) collective-permute-start(bf16[192,256]{1,0:T(8,128)(2,1)S(1)} %get-tuple-element.71), channel_id=1, source_target_pairs={{0,3},{1,2},{2,1},{3,0},{4,7},{5,6},{6,5},{7,4},{8,11},{9,10},{10,... | collective-permute-start | bytes 294920 | tf_op jit(solution)/shard_map/ppermute | solution.py:596
  63.9 1.7 %collective-permute-start.19 = (bf16[32,256]{1,0:T(8,128)(2,1)S(1)}, bf16[32,256]{1,0:T(8,128)(2,1)S(1)}, u32[]{:S(2)}, u32[]{:S(2)}) collective-permute-start(bf16[32,256]{1,0:T(8,128)(2,1)S(1)} %get-tuple-element.72), channel_id=1, source_target_pairs={{0,1},{1,0},{2,3},{3,2},{4,5},{5,4},{6,7},{7,6},{8,9},{9,8},{10,11... | collective-permute-start | bytes 49160 | tf_op jit(solution)/shard_map/ppermute | solution.py:596
  64.3 3.9 %collective-permute-start.20 = (bf16[32,256]{1,0:T(8,128)(2,1)S(1)}, bf16[32,256]{1,0:T(8,128)(2,1)S(1)}, u32[]{:S(2)}, u32[]{:S(2)}) collective-permute-start(bf16[32,256]{1,0:T(8,128)(2,1)S(1)} %get-tuple-element.73), channel_id=1, source_target_pairs={{0,2},{1,3},{2,0},{3,1},{4,6},{5,7},{6,4},{7,5},{8,10},{9,11},{10,... | collective-permute-start | bytes 49160 | tf_op jit(solution)/shard_map/ppermute | solution.py:596
  65.6 3.3 %collective-permute-start.21 = (bf16[32,256]{1,0:T(8,128)(2,1)S(1)}, bf16[32,256]{1,0:T(8,128)(2,1)S(1)}, u32[]{:S(2)}, u32[]{:S(2)}) collective-permute-start(bf16[32,256]{1,0:T(8,128)(2,1)S(1)} %get-tuple-element.74), channel_id=1, source_target_pairs={{0,3},{1,2},{2,1},{3,0},{4,7},{5,6},{6,5},{7,4},{8,11},{9,10},{10,... | collective-permute-start | bytes 49160 | tf_op jit(solution)/shard_map/ppermute | solution.py:596
  (6 other events, 54.6 us)

commit v6 on v5

--- a/solution.py
+++ b/solution.py
@@ -507,7 +507,9 @@
     early = jnp.where(inner < HEAD_DIM, attn - centre, centre).astype(BF16)
     early_ref[...] = early
     for index, ref in enumerate(sent_refs):
-        ref[...] = dot(back_ref[back_ref.shape[0] - n_sent + index], early).astype(BF16)
+        share = back_ref.shape[1]
+        ref[:share] = dot(back_ref[back_ref.shape[0] - n_sent + index], early).astype(BF16)
+        ref[share:] = jnp.zeros((ref.shape[0] - share, ref.shape[1]), BF16)
 
 
 def far_kernel(n_tp, level, masks, acc_ref, tops_ref, query_ref, spreads_ref, early_ref, centre_ref, back_ref, *refs):
@@ -569,7 +571,7 @@
     inside = (lane & (SLOT - 1)) < HEAD_DIM
     parts, centres = [], []
     for turn, ref in enumerate(message_refs):
-        message = ref[...].astype(F32)
+        message = ref[:share].astype(F32)
         centres.append(message[:, HEAD_DIM : HEAD_DIM + 1])
         if turn >= n_tp - len(change_refs):
             change = change_refs[turn - n_tp + len(change_refs)][...]
@@ -735,12 +737,12 @@
         cost=0.1,
         vmem_bytes=vmem_bytes,
     )
-    n_sent = n_tp - 1
+    n_sent = n_tp // 2
     for index in range(len(groups) - 1):
         kernel, outs, given = near_kernel, [], []
         if index == len(groups) - 2:
             kernel, given = functools.partial(mid_kernel, n_sent=n_sent), [back]
-            outs = [((rows, wide), BF16), ((rows, wide), F32)] + [((share, wide), BF16)] * n_sent
+            outs = [((rows, wide), BF16), ((rows, wide), F32)] + [((share + 16, wide), BF16)] * n_sent
         acc, tops, *more = call(
             functools.partial(kernel, [groups[index]]),
             "mid" if outs else "near",

time: 71 us -> 70.9 us (level)
  starting transfers between devices: 26.3 us -> 25.5 us
    ppermute x22 -> x21, starting transfers between devices: 21.4 us -> 20.6 us  [swap(): lax.ppermute(block, axis, [(index, index ^ mask) for index in range(count)])]
    ppermute x22 -> x21, waiting for transfers between devices: 14.9 us -> 15.4 us  [swap(): lax.ppermute(block, axis, [(index, index ^ mask) for index in range(count)])]
  transfers between devices with their start and end apart: 23 -> 22, of which waited for: 7 -> 6; matrix products, arithmetic and copies ran while one was open for 0% -> 0% of each run, Pallas kernels for 31% -> 32%
where the time goes in v6:
time: 70.9 us; the launch traced here: 70.6 us
  starting transfers between devices  25.5 us (36%)
  Pallas kernels  25.2 us (36%)
  waiting for transfers between devices  19.7 us (28%)
    pallas_call x14, Pallas kernels, call(): pl.pallas_call(kernel, name=name, out_shape=[jax.ShapeDtypeStruct(shape,...  25.2 us
    ppermute x21, starting transfers between devices, swap(): lax.ppermute(block, axis, [(index, index ^ mask) for index in range(count)])  20.6 us
    ppermute x21, waiting for transfers between devices, swap(): lax.ppermute(block, axis, [(index, index ^ mask) for index in range(count)])  15.4 us
    all_to_all x1, starting transfers between devices, body(): lax.all_to_all(blocks, ('seq', 'tp'), split_axis=0, concat_axis=0, tiled=...  4.9 us
    all_to_all x1, waiting for transfers between devices, body(): lax.all_to_all(blocks, ('seq', 'tp'), split_axis=0, concat_axis=0, tiled=...  4.28 us
  transfers between devices with their start and end apart: 22, of which 6 were waited for; matrix products, arithmetic and copies ran while one was open for 0% of the time, Pallas kernels for 32%

profile of v6, /device:TPU:0, one launch (start us, length us, event | category | flops | bytes accessed | tf_op | source)
XLA Modules:
  0.0 70.6 jit_solution(6259294454156731161)
XLA Ops:
  0.0 3.0 %collective-permute-start = (bf16[384,768]{1,0:T(8,128)(2,1)}, bf16[384,768]{1,0:T(8,128)(2,1)S(1)}, u32[]{:S(2)}, u32[]{:S(2)}) collective-permute-start(bf16[384,768]{1,0:T(8,128)(2,1)} %refs_0_.1), channel_id=1, source_target_pairs={{0,2},{1,3},{2,0},{3,1},{4,6},{5,7},{6,4},{7,5},{8,10},{9,11},{10,... | collective-permute-start | bytes 1769480 | tf_op jit(solution)/shard_map/ppermute | solution.py:598
  3.0 3.1 %route.1 = bf16[32,80,128]{2,1,0:T(8,128)(2,1)} custom-call(s32[6,128]{1,0:T(8,128)} %bitcast.24, s32[6,128]{1,0:T(8,128)} %bitcast.25, bf16[768,384]{1,0:T(8,128)(2,1)} %tiles_hbm.1), custom_call_target="tpu_custom_call" | custom-call | flops 3000000000 | tf_op jit(solution)/shard_map/route/pallas_call | solution.py:69
  6.1 4.9 %all-to-all-start = ((bf16[32,80,128]{2,1,0:T(8,128)(2,1)}), bf16[32,80,128]{2,1,0:T(8,128)(2,1)S(1)}, u32[]{:S(2)}, u32[]{:S(2)}) async-start(bf16[32,80,128]{2,1,0:T(8,128)(2,1)} %route.1), calls=%async_computation | async-start | bytes 1310720 | tf_op jit(solution)/shard_map/all_to_all | solution.py:659
  11.0 10.0 %collective-permute-done.refs_2_ = bf16[384,768]{1,0:T(8,128)(2,1)S(1)} collective-permute-done((bf16[384,768]{1,0:T(8,128)(2,1)}, bf16[384,768]{1,0:T(8,128)(2,1)S(1)}, u32[]{:S(2)}, u32[]{:S(2)}) %collective-permute-start) | collective-permute-done | bytes 589856 | tf_op jit(solution)/shard_map/ppermute | solution.py:598
  22.4 2.2 %collective-permute-start.7 = (bf16[192,768]{1,0:T(8,128)(2,1)}, bf16[192,768]{1,0:T(8,128)(2,1)}, u32[]{:S(2)}, u32[]{:S(2)}) collective-permute-start(bf16[192,768]{1,0:T(8,128)(2,1)} %scale.1.refs_4_), channel_id=1, source_target_pairs={{0,2},{1,3},{2,0},{3,1},{4,6},{5,7},{6,4},{7,5},{8,10},{9,11},{10,... | collective-permute-start | bytes 884744 | tf_op jit(solution)/shard_map/ppermute | solution.py:598
  24.6 4.3 %all-to-all-done.recv_hbm = bf16[32,80,128]{2,1,0:T(8,128)(2,1)S(1)} async-done(((bf16[32,80,128]{2,1,0:T(8,128)(2,1)}), bf16[32,80,128]{2,1,0:T(8,128)(2,1)S(1)}, u32[]{:S(2)}, u32[]{:S(2)}) %all-to-all-start) | async-done | bytes 655392 | tf_op jit(solution)/shard_map/all_to_all | solution.py:659
  28.9 1.7 %project.1 = (bf16[192,768]{1,0:T(8,128)(2,1)S(1)}, s32[4,1,256]{2,1,0:T(1,128)S(1)}, f32[8,768]{1,0:T(8,128)S(1)}) custom-call(bf16[32,80,128]{2,1,0:T(8,128)(2,1)S(1)} %all-to-all-done.recv_hbm, bf16[16,128]{1,0:T(8,128)(2,1)S(1)} %hint.1.early_ref, bf16[192,768]{1,0:T(8,128)(2,1)S(1)} %collective-permute-done.2.beside_ref.refs_5_, ...), custom_call_target="tpu_custom_call" | custom-call | flops 500000000 | tf_op jit(solution)/shard_map/project/pallas_call | solution.py:69
  30.7 1.6 %collective-permute-start.5 = (bf16[192,768]{1,0:T(8,128)(2,1)S(1)}, bf16[192,768]{1,0:T(8,128)(2,1)S(1)}, u32[]{:S(2)}, u32[]{:S(2)}) collective-permute-start(bf16[192,768]{1,0:T(8,128)(2,1)S(1)} %get-tuple-element.40.stream_ref.refs_0_), channel_id=1, source_target_pairs={{0,2},{1,3},{2,0},{3,1},{4,6},{5,7},{6,4},{7,5},{8,10},{9,11},{10,... | collective-permute-start | bytes 884744 | tf_op jit(solution)/shard_map/ppermute | solution.py:598
  32.3 2.6 %heads_1.1 = (bf16[768,576]{1,0:T(8,128)(2,1)S(1)}, bf16[768,256]{1,0:T(8,128)(2,1)S(1)}, bf16[768,256]{1,0:T(8,128)(2,1)S(1)}, bf16[4,192,768]{2,1,0:T(8,128)(2...) custom-call(s32[4,1,256]{2,1,0:T(1,128)S(1)} %get-tuple-element.39.c, ...), custom_call_target="tpu_custom_call" | custom-call | flops 1000000000 | tf_op jit(solution)/shard_map/heads_1/pallas_call | solution.py:69
  35.0 1.9 %heads_2.2 = (bf16[768,576]{1,0:T(8,128)(2,1)S(1)}, bf16[192,768]{1,0:T(8,128)(2,1)S(1)}) custom-call(s32[4,1,256]{2,1,0:T(1,128)S(1)} %get-tuple-element.39.codes_ref, f32[6,128]{1,0:T(8,128)S(1)} %bitcast.20, bf16[192,768]{1,0:T(8,128)(2,1)S(1)} %bitcast.8, bf16[192,768]{1,0:T(8,128)(2,1)S(1)} %bitcast.12, bf16[192,768]{1,0:T(8,128)(2,1)S(1)} %bitcast.16, ...), custom_call_target="tpu_custom_call" | custom-call | flops 1000000000 | tf_op jit(solution)/shard_map/heads_2/pallas_call | solution.py:69
  37.0 3.1 %collective-permute-done.5.refs_2_.stream_ref = bf16[192,768]{1,0:T(8,128)(2,1)S(1)} collective-permute-done((bf16[192,768]{1,0:T(8,128)(2,1)S(1)}, bf16[192,768]{1,0:T(8,128)(2,1)S(1)}, u32[]{:S(2)}, u32[]{:S(2)}) %collective-permute-start.5) | collective-permute-done | bytes 294944 | tf_op jit(solution)/shard_map/ppermute | solution.py:598
  42.8 1.5 %collective-permute-start.9 = (bf16[384,384]{1,0:T(8,128)(2,1)S(1)}, bf16[384,384]{1,0:T(8,128)(2,1)S(1)}, u32[]{:S(2)}, u32[]{:S(2)}) collective-permute-start(bf16[384,384]{1,0:T(8,128)(2,1)S(1)} %get-tuple-element.55), channel_id=1, source_target_pairs={{0,4},{4,0},{8,12},{12,8},{16,20},{20,16},{24,28},{28,24},{1,5},{5... | collective-permute-start | bytes 884744 | tf_op jit(solution)/shard_map/ppermute | solution.py:598
  44.3 1.4 %collective-permute-start.12 = (bf16[96,384]{1,0:T(8,128)(2,1)S(1)}, bf16[96,384]{1,0:T(8,128)(2,1)S(1)}, u32[]{:S(2)}, u32[]{:S(2)}) collective-permute-start(bf16[96,384]{1,0:T(8,128)(2,1)S(1)} %get-tuple-element.66), channel_id=1, source_target_pairs={{0,16},{4,20},{8,24},{12,28},{16,0},{20,4},{24,8},{28,12},{1,17},{... | collective-permute-start | bytes 221192 | tf_op jit(solution)/shard_map/ppermute | solution.py:598
  45.6 2.5 %collective-permute-start.14 = (bf16[96,384]{1,0:T(8,128)(2,1)S(1)}, bf16[96,384]{1,0:T(8,128)(2,1)S(1)}, u32[]{:S(2)}, u32[]{:S(2)}) collective-permute-start(bf16[96,384]{1,0:T(8,128)(2,1)S(1)} %get-tuple-element.66), channel_id=1, source_target_pairs={{0,24},{4,28},{8,16},{12,20},{16,8},{20,12},{24,0},{28,4},{1,25},{... | collective-permute-start | bytes 221192 | tf_op jit(solution)/shard_map/ppermute | solution.py:598
  48.1 2.0 %collective-permute-start.11 = (bf16[192,384]{1,0:T(8,128)(2,1)S(1)}, bf16[192,384]{1,0:T(8,128)(2,1)S(1)}, u32[]{:S(2)}, u32[]{:S(2)}) collective-permute-start(bf16[192,384]{1,0:T(8,128)(2,1)S(1)} %get-tuple-element.60), channel_id=1, source_target_pairs={{0,12},{4,8},{8,4},{12,0},{16,28},{20,24},{24,20},{28,16},{1,13},{... | collective-permute-start | bytes 442376 | tf_op jit(solution)/shard_map/ppermute | solution.py:598
  50.1 4.2 %own.1 = (f32[768,256]{1,0:T(8,128)S(1)}, f32[4,768,128]{2,1,0:T(8,128)S(1)}, bf16[768,256]{1,0:T(8,128)(2,1)S(1)}) custom-call(bf16[768,576]{1,0:T(8,128)(2,1)S(1)} %get-tuple-element.47.packed_ref, bf16[768,256]{1,0:T(8,128)(2,1)S(1)} %get-tuple-element.48.same_ref, bf16[768,256]{1,0:T(8,128)(2,1)S(1)} %get-tuple-element.49.apart_ref, ...), custom_call_target="tpu_custom_call" | custom-call | flops 100000000 | tf_op jit(solution)/shard_map/own/pallas_call | solution.py:69
  54.3 1.6 %collective-permute-start.13 = (bf16[96,384]{1,0:T(8,128)(2,1)S(1)}, bf16[96,384]{1,0:T(8,128)(2,1)S(1)}, u32[]{:S(2)}, u32[]{:S(2)}) collective-permute-start(bf16[96,384]{1,0:T(8,128)(2,1)S(1)} %collective-permute-done.12.refs_1_), channel_id=1, source_target_pairs={{0,4},{4,0},{8,12},{12,8},{16,20},{20,16},{24,28},{28,24},{1,5},{5... | collective-permute-start | bytes 221192 | tf_op jit(solution)/shard_map/ppermute | solution.py:598
  56.4 2.1 %near.1 = (f32[768,256]{1,0:T(8,128)S(1)}, f32[4,768,128]{2,1,0:T(8,128)S(1)}) custom-call(f32[768,256]{1,0:T(8,128)S(1)} %get-tuple-element.51.acc_ref, f32[4,768,128]{2,1,0:T(8,128)S(1)} %get-tuple-element.52.tops_ref, bf16[768,256]{1,0:T(8,128)(2,1)S(1)} %get-tuple-element.53.query_ref, ...), custom_call_target="tpu_custom_call", output_to_operand_aliasing={{0}: (0, {}), {1}: (1, {})} | custom-call | flops 6000000000 | tf_op jit(solution)/shard_map/near/pallas_call | solution.py:69
  58.5 2.0 %mid.1 = (f32[768,256]{1,0:T(8,128)S(1)}, f32[4,768,128]{2,1,0:T(8,128)S(1)}, bf16[768,256]{1,0:T(8,128)(2,1)S(1)}, f32[768,256]{1,0:T(8,128)S(1)}, bf16[208,256...) custom-call(f32[768,256]{1,0:T(8,128)S(1)} %get-tuple-element.56.acc_ref, ...), custom_call_target="tpu_custom_call", output_to_operand_aliasing={{0}: (0, {}), {1}: (1, {})} | custom-call | flops 6000000000 | tf_op jit(solution)/shard_map/mid/pallas_call | solution.py:69
  60.5 1.3 %collective-permute-start.17 = (bf16[208,256]{1,0:T(8,128)(2,1)S(1)}, bf16[208,256]{1,0:T(8,128)(2,1)S(1)}, u32[]{:S(2)}, u32[]{:S(2)}) collective-permute-start(bf16[208,256]{1,0:T(8,128)(2,1)S(1)} %get-tuple-element.69), channel_id=1, source_target_pairs={{0,2},{1,3},{2,0},{3,1},{4,6},{5,7},{6,4},{7,5},{8,10},{9,11},{10,... | collective-permute-start | bytes 319496 | tf_op jit(solution)/shard_map/ppermute | solution.py:598
  61.9 1.5 %far.1 = (bf16[192,256]{1,0:T(8,128)(2,1)S(1)}, bf16[192,256]{1,0:T(8,128)(2,1)S(1)}, bf16[32,256]{1,0:T(8,128)(2,1)S(1)}, bf16[32,256]{1,0:T(8,128)(2,1)S(1)}) custom-call(f32[768,256]{1,0:T(8,128)S(1)} %get-tuple-element.61.acc_ref, f32[4,768,128]{2,1,0:T(8,128)S(1)} %get-tuple-element.62.tops_ref, bf16[768,256]{1,0:T(8,128)(2,1)S(1)} %get-tuple-element.53.query_ref, ...), custom_call_target="tpu_custom_call" | custom-call | flops 1000000000 | tf_op jit(solution)/shard_map/far/pallas_call | solution.py:69
  64.3 1.3 %collective-permute-start.19 = (bf16[32,256]{1,0:T(8,128)(2,1)S(1)}, bf16[32,256]{1,0:T(8,128)(2,1)S(1)}, u32[]{:S(2)}, u32[]{:S(2)}) collective-permute-start(bf16[32,256]{1,0:T(8,128)(2,1)S(1)} %get-tuple-element.71), channel_id=1, source_target_pairs={{0,2},{1,3},{2,0},{3,1},{4,6},{5,7},{6,4},{7,5},{8,10},{9,11},{10,... | collective-permute-start | bytes 49160 | tf_op jit(solution)/shard_map/ppermute | solution.py:598
  65.7 1.5 %base.1 = (bf16[192,768]{1,0:T(8,128)(2,1)S(1)}, bf16[4,256,768]{2,1,0:T(8,128)(2,1)S(1)}) custom-call(s32[4,1,256]{2,1,0:T(1,128)S(1)} %get-tuple-element.39.codes_ref, bf16[192,768]{1,0:T(8,128)(2,1)S(1)} %get-tuple-element.40.stream_ref.refs_0_, bf16[192,768]{1,0:T(8,128)(2,1)S(1)} %collective-permute-done.4.stream_ref.refs_1_, ...), custom_call_target="tpu_custom_call" | custom-call | flops 300000000 | tf_op jit(solution)/shard_map/base/pallas_call | solution.py:69
  68.9 1.7 %mix.1 = bf16[192,768]{1,0:T(8,128)(2,1)} custom-call(bf16[192,768]{1,0:T(8,128)(2,1)S(1)} %get-tuple-element.44.base_ref, bf16[4,256,768]{2,1,0:T(8,128)(2,1)S(1)} %get-tuple-element.45.weights_ref, bf16[192,256]{1,0:T(8,128)(2,1)S(1)} %get-tuple-element.67.refs_0_, bf16[192,256]{1,0:T(8,128)(2,1)S(1)} %collective-permute-done.16.refs_1_, ...), custom_call_target="tpu_custom_call" | custom-call | flops 1000000000 | tf_op jit(solution)/shard_map/mix/pallas_call | solution.py:69
  (48 shorter events, 7.6 us)
Async XLA Ops:
  0.0 21.0 %collective-permute-start = (bf16[384,768]{1,0:T(8,128)(2,1)}, bf16[384,768]{1,0:T(8,128)(2,1)S(1)}, u32[]{:S(2)}, u32[]{:S(2)}) collective-permute-start(bf16[384,768]{1,0:T(8,128)(2,1)} %refs_0_.1), channel_id=1, source_target_pairs={{0,2},{1,3},{2,0},{3,1},{4,6},{5,7},{6,4},{7,5},{8,10},{9,11},{10,... | collective-permute-start | bytes 1769480 | tf_op jit(solution)/shard_map/ppermute | solution.py:598
  3.0 18.5 %copy-start.1 = (bf16[192,768]{1,0:T(8,128)(2,1)S(1)}, bf16[192,768]{1,0:T(8,128)(2,1)}, u32[]{:S(2)}) copy-start(bf16[192,768]{1,0:T(8,128)(2,1)} %weight_ref.1) | copy-start | bytes 884740
  3.0 18.5 %copy-start.6 = (f32[192]{0:T(256)S(1)}, f32[192]{0:T(256)}, u32[]{:S(2)}) copy-start(f32[192]{0:T(256)} %param.18) | copy-start | bytes 2308
  6.1 22.8 %all-to-all-start = ((bf16[32,80,128]{2,1,0:T(8,128)(2,1)}), bf16[32,80,128]{2,1,0:T(8,128)(2,1)S(1)}, u32[]{:S(2)}, u32[]{:S(2)}) async-start(bf16[32,80,128]{2,1,0:T(8,128)(2,1)} %route.1), calls=%async_computation | async-start | bytes 1310720 | tf_op jit(solution)/shard_map/all_to_all | solution.py:659
  21.0 3.6 %collective-permute-start.1 = (bf16[384,768]{1,0:T(8,128)(2,1)S(1)}, bf16[384,768]{1,0:T(8,128)(2,1)S(1)}, u32[]{:S(2)}, u32[]{:S(2)}) collective-permute-start(bf16[384,768]{1,0:T(8,128)(2,1)S(1)} %collective-permute-done.refs_2_), channel_id=1, source_target_pairs={{0,1},{1,0},{2,3},{3,2},{4,5},{5,4},{6,7},{7,6},{8,9},{9,8},{10,11... | collective-permute-start | bytes 1769480 | tf_op jit(solution)/shard_map/ppermute | solution.py:598
  21.0 3.6 %collective-permute-start.3 = (bf16[384,768]{1,0:T(8,128)(2,1)S(1)}, bf16[384,768]{1,0:T(8,128)(2,1)S(1)}, u32[]{:S(2)}, u32[]{:S(2)}) collective-permute-start(bf16[384,768]{1,0:T(8,128)(2,1)S(1)} %copy-done), channel_id=1, source_target_pairs={{0,1},{1,0},{2,3},{3,2},{4,5},{5,4},{6,7},{7,6},{8,9},{9,8},{10,11... | collective-permute-start | bytes 1769480 | tf_op jit(solution)/shard_map/ppermute | solution.py:598
  22.4 2.2 %collective-permute-start.2 = (bf16[192,768]{1,0:T(8,128)(2,1)}, bf16[192,768]{1,0:T(8,128)(2,1)S(1)}, u32[]{:S(2)}, u32[]{:S(2)}) collective-permute-start(bf16[192,768]{1,0:T(8,128)(2,1)} %scale.1.refs_4_), channel_id=1, source_target_pairs={{0,1},{1,0},{2,3},{3,2},{4,5},{5,4},{6,7},{7,6},{8,9},{9,8},{10,11... | collective-permute-start | bytes 884744 | tf_op jit(solution)/shard_map/ppermute | solution.py:598
  22.4 12.5 %collective-permute-start.7 = (bf16[192,768]{1,0:T(8,128)(2,1)}, bf16[192,768]{1,0:T(8,128)(2,1)}, u32[]{:S(2)}, u32[]{:S(2)}) collective-permute-start(bf16[192,768]{1,0:T(8,128)(2,1)} %scale.1.refs_4_), channel_id=1, source_target_pairs={{0,2},{1,3},{2,0},{3,1},{4,6},{5,7},{6,4},{7,5},{8,10},{9,11},{10,... | collective-permute-start | bytes 884744 | tf_op jit(solution)/shard_map/ppermute | solution.py:598
  30.6 4.3 %collective-permute-start.4 = (bf16[192,768]{1,0:T(8,128)(2,1)S(1)}, bf16[192,768]{1,0:T(8,128)(2,1)S(1)}, u32[]{:S(2)}, u32[]{:S(2)}) collective-permute-start(bf16[192,768]{1,0:T(8,128)(2,1)S(1)} %get-tuple-element.40.stream_ref.refs_0_), channel_id=1, source_target_pairs={{0,1},{1,0},{2,3},{3,2},{4,5},{5,4},{6,7},{7,6},{8,9},{9,8},{10,11... | collective-permute-start | bytes 884744 | tf_op jit(solution)/shard_map/ppermute | solution.py:598
  30.7 9.4 %collective-permute-start.5 = (bf16[192,768]{1,0:T(8,128)(2,1)S(1)}, bf16[192,768]{1,0:T(8,128)(2,1)S(1)}, u32[]{:S(2)}, u32[]{:S(2)}) collective-permute-start(bf16[192,768]{1,0:T(8,128)(2,1)S(1)} %get-tuple-element.40.stream_ref.refs_0_), channel_id=1, source_target_pairs={{0,2},{1,3},{2,0},{3,1},{4,6},{5,7},{6,4},{7,5},{8,10},{9,11},{10,... | collective-permute-start | bytes 884744 | tf_op jit(solution)/shard_map/ppermute | solution.py:598
  36.9 3.2 %collective-permute-start.8 = (bf16[192,768]{1,0:T(8,128)(2,1)S(1)}, bf16[192,768]{1,0:T(8,128)(2,1)S(1)}, u32[]{:S(2)}, u32[]{:S(2)}) collective-permute-start(bf16[192,768]{1,0:T(8,128)(2,1)S(1)} %get-tuple-element.43.refs_6_), channel_id=1, source_target_pairs={{0,1},{1,0},{2,3},{3,2},{4,5},{5,4},{6,7},{7,6},{8,9},{9,8},{10,11... | collective-permute-start | bytes 884744 | tf_op jit(solution)/shard_map/ppermute | solution.py:598
  40.1 1.6 %collective-permute-start.6 = (bf16[192,768]{1,0:T(8,128)(2,1)S(1)}, bf16[192,768]{1,0:T(8,128)(2,1)S(1)}, u32[]{:S(2)}, u32[]{:S(2)}) collective-permute-start(bf16[192,768]{1,0:T(8,128)(2,1)S(1)} %collective-permute-done.5.refs_2_.stream_ref), channel_id=1, source_target_pairs={{0,1},{1,0},{2,3},{3,2},{4,5},{5,4},{6,7},{7,6},{8,9},{9,8},{10,11... | collective-permute-start | bytes 884744 | tf_op jit(solution)/shard_map/ppermute | solution.py:598
  42.8 13.6 %collective-permute-start.9 = (bf16[384,384]{1,0:T(8,128)(2,1)S(1)}, bf16[384,384]{1,0:T(8,128)(2,1)S(1)}, u32[]{:S(2)}, u32[]{:S(2)}) collective-permute-start(bf16[384,384]{1,0:T(8,128)(2,1)S(1)} %get-tuple-element.55), channel_id=1, source_target_pairs={{0,4},{4,0},{8,12},{12,8},{16,20},{20,16},{24,28},{28,24},{1,5},{5... | collective-permute-start | bytes 884744 | tf_op jit(solution)/shard_map/ppermute | solution.py:598
  44.3 10.0 %collective-permute-start.12 = (bf16[96,384]{1,0:T(8,128)(2,1)S(1)}, bf16[96,384]{1,0:T(8,128)(2,1)S(1)}, u32[]{:S(2)}, u32[]{:S(2)}) collective-permute-start(bf16[96,384]{1,0:T(8,128)(2,1)S(1)} %get-tuple-element.66), channel_id=1, source_target_pairs={{0,16},{4,20},{8,24},{12,28},{16,0},{20,4},{24,8},{28,12},{1,17},{... | collective-permute-start | bytes 221192 | tf_op jit(solution)/shard_map/ppermute | solution.py:598
  45.6 10.3 %collective-permute-start.14 = (bf16[96,384]{1,0:T(8,128)(2,1)S(1)}, bf16[96,384]{1,0:T(8,128)(2,1)S(1)}, u32[]{:S(2)}, u32[]{:S(2)}) collective-permute-start(bf16[96,384]{1,0:T(8,128)(2,1)S(1)} %get-tuple-element.66), channel_id=1, source_target_pairs={{0,24},{4,28},{8,16},{12,20},{16,8},{20,12},{24,0},{28,4},{1,25},{... | collective-permute-start | bytes 221192 | tf_op jit(solution)/shard_map/ppermute | solution.py:598
  48.1 10.4 %collective-permute-start.10 = (bf16[192,384]{1,0:T(8,128)(2,1)S(1)}, bf16[192,384]{1,0:T(8,128)(2,1)S(1)}, u32[]{:S(2)}, u32[]{:S(2)}) collective-permute-start(bf16[192,384]{1,0:T(8,128)(2,1)S(1)} %get-tuple-element.60), channel_id=1, source_target_pairs={{0,8},{4,12},{8,0},{12,4},{16,24},{20,28},{24,16},{28,20},{1,9},{5... | collective-permute-start | bytes 442376 | tf_op jit(solution)/shard_map/ppermute | solution.py:598
  48.1 10.4 %collective-permute-start.11 = (bf16[192,384]{1,0:T(8,128)(2,1)S(1)}, bf16[192,384]{1,0:T(8,128)(2,1)S(1)}, u32[]{:S(2)}, u32[]{:S(2)}) collective-permute-start(bf16[192,384]{1,0:T(8,128)(2,1)S(1)} %get-tuple-element.60), channel_id=1, source_target_pairs={{0,12},{4,8},{8,4},{12,0},{16,28},{20,24},{24,20},{28,16},{1,13},{... | collective-permute-start | bytes 442376 | tf_op jit(solution)/shard_map/ppermute | solution.py:598
  54.3 7.5 %collective-permute-start.13 = (bf16[96,384]{1,0:T(8,128)(2,1)S(1)}, bf16[96,384]{1,0:T(8,128)(2,1)S(1)}, u32[]{:S(2)}, u32[]{:S(2)}) collective-permute-start(bf16[96,384]{1,0:T(8,128)(2,1)S(1)} %collective-permute-done.12.refs_1_), channel_id=1, source_target_pairs={{0,4},{4,0},{8,12},{12,8},{16,20},{20,16},{24,28},{28,24},{1,5},{5... | collective-permute-start | bytes 221192 | tf_op jit(solution)/shard_map/ppermute | solution.py:598
  55.9 6.0 %collective-permute-start.15 = (bf16[96,384]{1,0:T(8,128)(2,1)S(1)}, bf16[96,384]{1,0:T(8,128)(2,1)S(1)}, u32[]{:S(2)}, u32[]{:S(2)}) collective-permute-start(bf16[96,384]{1,0:T(8,128)(2,1)S(1)} %collective-permute-done.14.refs_3_), channel_id=1, source_target_pairs={{0,4},{4,0},{8,12},{12,8},{16,20},{20,16},{24,28},{28,24},{1,5},{5... | collective-permute-start | bytes 221192 | tf_op jit(solution)/shard_map/ppermute | solution.py:598
  60.5 8.4 %collective-permute-start.17 = (bf16[208,256]{1,0:T(8,128)(2,1)S(1)}, bf16[208,256]{1,0:T(8,128)(2,1)S(1)}, u32[]{:S(2)}, u32[]{:S(2)}) collective-permute-start(bf16[208,256]{1,0:T(8,128)(2,1)S(1)} %get-tuple-element.69), channel_id=1, source_target_pairs={{0,2},{1,3},{2,0},{3,1},{4,6},{5,7},{6,4},{7,5},{8,10},{9,11},{10,... | collective-permute-start | bytes 319496 | tf_op jit(solution)/shard_map/ppermute | solution.py:598
  61.8 7.0 %collective-permute-start.18 = (bf16[208,256]{1,0:T(8,128)(2,1)S(1)}, bf16[208,256]{1,0:T(8,128)(2,1)S(1)}, u32[]{:S(2)}, u32[]{:S(2)}) collective-permute-start(bf16[208,256]{1,0:T(8,128)(2,1)S(1)} %get-tuple-element.70), channel_id=1, source_target_pairs={{0,3},{1,2},{2,1},{3,0},{4,7},{5,6},{6,5},{7,4},{8,11},{9,10},{10,... | collective-permute-start | bytes 319496 | tf_op jit(solution)/shard_map/ppermute | solution.py:598
  63.4 5.5 %collective-permute-start.16 = (bf16[192,256]{1,0:T(8,128)(2,1)S(1)}, bf16[192,256]{1,0:T(8,128)(2,1)S(1)}, u32[]{:S(2)}, u32[]{:S(2)}) collective-permute-start(bf16[192,256]{1,0:T(8,128)(2,1)S(1)} %get-tuple-element.68), channel_id=1, source_target_pairs={{0,1},{1,0},{2,3},{3,2},{4,5},{5,4},{6,7},{7,6},{8,9},{9,8},{10,11... | collective-permute-start | bytes 294920 | tf_op jit(solution)/shard_map/ppermute | solution.py:598
  64.3 3.7 %collective-permute-start.19 = (bf16[32,256]{1,0:T(8,128)(2,1)S(1)}, bf16[32,256]{1,0:T(8,128)(2,1)S(1)}, u32[]{:S(2)}, u32[]{:S(2)}) collective-permute-start(bf16[32,256]{1,0:T(8,128)(2,1)S(1)} %get-tuple-element.71), channel_id=1, source_target_pairs={{0,2},{1,3},{2,0},{3,1},{4,6},{5,7},{6,4},{7,5},{8,10},{9,11},{10,... | collective-permute-start | bytes 49160 | tf_op jit(solution)/shard_map/ppermute | solution.py:598
  65.6 3.3 %collective-permute-start.20 = (bf16[32,256]{1,0:T(8,128)(2,1)S(1)}, bf16[32,256]{1,0:T(8,128)(2,1)S(1)}, u32[]{:S(2)}, u32[]{:S(2)}) collective-permute-start(bf16[32,256]{1,0:T(8,128)(2,1)S(1)} %get-tuple-element.72), channel_id=1, source_target_pairs={{0,3},{1,2},{2,1},{3,0},{4,7},{5,6},{6,5},{7,4},{8,11},{9,10},{10,... | collective-permute-start | bytes 49160 | tf_op jit(solution)/shard_map/ppermute | solution.py:598
  (5 other events, 36.1 us)

commit v7 on v6

--- a/solution.py
+++ b/solution.py
@@ -520,10 +520,13 @@
 
     merged = merge_sets(level, masks, sets, acc_ref, tops_ref, query_ref, spreads_ref, apart_ref)
     changed = None
-    for head, here, sums, _ in merged:
+    stacked = jnp.concatenate([sums for _, _, sums, _ in merged], axis=0)
+    stacked = stacked / slot_lane(stacked, HEAD_DIM)
+    for index, (head, here, sums, _) in enumerate(merged):
         lane = iota(sums.shape, 1)
+        length = sums.shape[0]
         mine = (lane >= head * SLOT) & (lane < head * SLOT + HEAD_DIM)
-        new = (sums / slot_lane(sums, HEAD_DIM) - centre_ref[here, :]).astype(BF16)
+        new = (stacked[index * length : (index + 1) * length] - centre_ref[here, :]).astype(BF16)
         message[here, :] = jnp.where(mine, new, message[here, :])
         changed = new if changed is None else jnp.where(lane >= head * SLOT, new, changed)
     final = message[...]
@@ -582,8 +585,7 @@
             message = jnp.where(late, moved, message)
         parts.append(jnp.where(inside, message, 0.0))
     each = features // n_tp
-    sums = [jnp.sum(part, axis=1, keepdims=True) + centre * each for part, centre in zip(parts, centres)]
-    mean = sum(sums) * (1.0 / features)
+    mean = (jnp.sum(sum(parts), axis=1, keepdims=True) + sum(centres) * each) * (1.0 / features)
     parts = [jnp.where(inside, part + (centre - mean), 0.0) for part, centre in zip(parts, centres)]
     spread = jnp.sum(sum(part * part for part in parts), axis=1, keepdims=True) * (1.0 / features)
     factor = lax.rsqrt(spread + EPS)

time: 70.9 us -> 70.8 us (level)
  no operation moved by 1% of the time
where the time goes in v7:
time: 70.8 us; the launch traced here: 70.6 us
  starting transfers between devices  25.5 us (36%)
  Pallas kernels  25.2 us (36%)
  waiting for transfers between devices  19.7 us (28%)
    pallas_call x14, Pallas kernels, call(): pl.pallas_call(kernel, name=name, out_shape=[jax.ShapeDtypeStruct(shape,...  25.2 us
    ppermute x21, starting transfers between devices, swap(): lax.ppermute(block, axis, [(index, index ^ mask) for index in range(count)])  20.6 us
    ppermute x21, waiting for transfers between devices, swap(): lax.ppermute(block, axis, [(index, index ^ mask) for index in range(count)])  15.4 us
    all_to_all x1, starting transfers between devices, body(): lax.all_to_all(blocks, ('seq', 'tp'), split_axis=0, concat_axis=0, tiled=...  4.9 us
    all_to_all x1, waiting for transfers between devices, body(): lax.all_to_all(blocks, ('seq', 'tp'), split_axis=0, concat_axis=0, tiled=...  4.28 us
  transfers between devices with their start and end apart: 22, of which 6 were waited for; matrix products, arithmetic and copies ran while one was open for 0% of the time, Pallas kernels for 32%

profile of v7, /device:TPU:0, one launch (start us, length us, event | category | flops | bytes accessed | tf_op | source)
XLA Modules:
  0.0 70.6 jit_solution(2963231983843145152)
XLA Ops:
  0.0 3.0 %collective-permute-start = (bf16[384,768]{1,0:T(8,128)(2,1)}, bf16[384,768]{1,0:T(8,128)(2,1)S(1)}, u32[]{:S(2)}, u32[]{:S(2)}) collective-permute-start(bf16[384,768]{1,0:T(8,128)(2,1)} %refs_0_.1), channel_id=1, source_target_pairs={{0,2},{1,3},{2,0},{3,1},{4,6},{5,7},{6,4},{7,5},{8,10},{9,11},{10,... | collective-permute-start | bytes 1769480 | tf_op jit(solution)/shard_map/ppermute | solution.py:600
  3.0 3.1 %route.1 = bf16[32,80,128]{2,1,0:T(8,128)(2,1)} custom-call(s32[6,128]{1,0:T(8,128)} %bitcast.24, s32[6,128]{1,0:T(8,128)} %bitcast.25, bf16[768,384]{1,0:T(8,128)(2,1)} %tiles_hbm.1), custom_call_target="tpu_custom_call" | custom-call | flops 3000000000 | tf_op jit(solution)/shard_map/route/pallas_call | solution.py:69
  6.1 4.9 %all-to-all-start = ((bf16[32,80,128]{2,1,0:T(8,128)(2,1)}), bf16[32,80,128]{2,1,0:T(8,128)(2,1)S(1)}, u32[]{:S(2)}, u32[]{:S(2)}) async-start(bf16[32,80,128]{2,1,0:T(8,128)(2,1)} %route.1), calls=%async_computation | async-start | bytes 1310720 | tf_op jit(solution)/shard_map/all_to_all | solution.py:661
  11.0 10.0 %collective-permute-done.refs_2_ = bf16[384,768]{1,0:T(8,128)(2,1)S(1)} collective-permute-done((bf16[384,768]{1,0:T(8,128)(2,1)}, bf16[384,768]{1,0:T(8,128)(2,1)S(1)}, u32[]{:S(2)}, u32[]{:S(2)}) %collective-permute-start) | collective-permute-done | bytes 589856 | tf_op jit(solution)/shard_map/ppermute | solution.py:600
  22.4 2.2 %collective-permute-start.7 = (bf16[192,768]{1,0:T(8,128)(2,1)}, bf16[192,768]{1,0:T(8,128)(2,1)}, u32[]{:S(2)}, u32[]{:S(2)}) collective-permute-start(bf16[192,768]{1,0:T(8,128)(2,1)} %scale.1.refs_4_), channel_id=1, source_target_pairs={{0,2},{1,3},{2,0},{3,1},{4,6},{5,7},{6,4},{7,5},{8,10},{9,11},{10,... | collective-permute-start | bytes 884744 | tf_op jit(solution)/shard_map/ppermute | solution.py:600
  24.6 4.3 %all-to-all-done.recv_hbm = bf16[32,80,128]{2,1,0:T(8,128)(2,1)S(1)} async-done(((bf16[32,80,128]{2,1,0:T(8,128)(2,1)}), bf16[32,80,128]{2,1,0:T(8,128)(2,1)S(1)}, u32[]{:S(2)}, u32[]{:S(2)}) %all-to-all-start) | async-done | bytes 655392 | tf_op jit(solution)/shard_map/all_to_all | solution.py:661
  28.9 1.7 %project.1 = (bf16[192,768]{1,0:T(8,128)(2,1)S(1)}, s32[4,1,256]{2,1,0:T(1,128)S(1)}, f32[8,768]{1,0:T(8,128)S(1)}) custom-call(bf16[32,80,128]{2,1,0:T(8,128)(2,1)S(1)} %all-to-all-done.recv_hbm, bf16[16,128]{1,0:T(8,128)(2,1)S(1)} %hint.1.early_ref, bf16[192,768]{1,0:T(8,128)(2,1)S(1)} %collective-permute-done.2.beside_ref.refs_5_, ...), custom_call_target="tpu_custom_call" | custom-call | flops 500000000 | tf_op jit(solution)/shard_map/project/pallas_call | solution.py:69
  30.7 1.6 %collective-permute-start.5 = (bf16[192,768]{1,0:T(8,128)(2,1)S(1)}, bf16[192,768]{1,0:T(8,128)(2,1)S(1)}, u32[]{:S(2)}, u32[]{:S(2)}) collective-permute-start(bf16[192,768]{1,0:T(8,128)(2,1)S(1)} %get-tuple-element.40.stream_ref.refs_0_), channel_id=1, source_target_pairs={{0,2},{1,3},{2,0},{3,1},{4,6},{5,7},{6,4},{7,5},{8,10},{9,11},{10,... | collective-permute-start | bytes 884744 | tf_op jit(solution)/shard_map/ppermute | solution.py:600
  32.3 2.6 %heads_1.1 = (bf16[768,576]{1,0:T(8,128)(2,1)S(1)}, bf16[768,256]{1,0:T(8,128)(2,1)S(1)}, bf16[768,256]{1,0:T(8,128)(2,1)S(1)}, bf16[4,192,768]{2,1,0:T(8,128)(2...) custom-call(s32[4,1,256]{2,1,0:T(1,128)S(1)} %get-tuple-element.39.c, ...), custom_call_target="tpu_custom_call" | custom-call | flops 1000000000 | tf_op jit(solution)/shard_map/heads_1/pallas_call | solution.py:69
  35.0 1.9 %heads_2.2 = (bf16[768,576]{1,0:T(8,128)(2,1)S(1)}, bf16[192,768]{1,0:T(8,128)(2,1)S(1)}) custom-call(s32[4,1,256]{2,1,0:T(1,128)S(1)} %get-tuple-element.39.codes_ref, f32[6,128]{1,0:T(8,128)S(1)} %bitcast.20, bf16[192,768]{1,0:T(8,128)(2,1)S(1)} %bitcast.8, bf16[192,768]{1,0:T(8,128)(2,1)S(1)} %bitcast.12, bf16[192,768]{1,0:T(8,128)(2,1)S(1)} %bitcast.16, ...), custom_call_target="tpu_custom_call" | custom-call | flops 1000000000 | tf_op jit(solution)/shard_map/heads_2/pallas_call | solution.py:69
  37.0 3.1 %collective-permute-done.5.refs_2_.stream_ref = bf16[192,768]{1,0:T(8,128)(2,1)S(1)} collective-permute-done((bf16[192,768]{1,0:T(8,128)(2,1)S(1)}, bf16[192,768]{1,0:T(8,128)(2,1)S(1)}, u32[]{:S(2)}, u32[]{:S(2)}) %collective-permute-start.5) | collective-permute-done | bytes 294944 | tf_op jit(solution)/shard_map/ppermute | solution.py:600
  42.8 1.5 %collective-permute-start.9 = (bf16[384,384]{1,0:T(8,128)(2,1)S(1)}, bf16[384,384]{1,0:T(8,128)(2,1)S(1)}, u32[]{:S(2)}, u32[]{:S(2)}) collective-permute-start(bf16[384,384]{1,0:T(8,128)(2,1)S(1)} %get-tuple-element.55), channel_id=1, source_target_pairs={{0,4},{4,0},{8,12},{12,8},{16,20},{20,16},{24,28},{28,24},{1,5},{5... | collective-permute-start | bytes 884744 | tf_op jit(solution)/shard_map/ppermute | solution.py:600
  44.3 1.4 %collective-permute-start.12 = (bf16[96,384]{1,0:T(8,128)(2,1)S(1)}, bf16[96,384]{1,0:T(8,128)(2,1)S(1)}, u32[]{:S(2)}, u32[]{:S(2)}) collective-permute-start(bf16[96,384]{1,0:T(8,128)(2,1)S(1)} %get-tuple-element.66), channel_id=1, source_target_pairs={{0,16},{4,20},{8,24},{12,28},{16,0},{20,4},{24,8},{28,12},{1,17},{... | collective-permute-start | bytes 221192 | tf_op jit(solution)/shard_map/ppermute | solution.py:600
  45.6 2.5 %collective-permute-start.14 = (bf16[96,384]{1,0:T(8,128)(2,1)S(1)}, bf16[96,384]{1,0:T(8,128)(2,1)S(1)}, u32[]{:S(2)}, u32[]{:S(2)}) collective-permute-start(bf16[96,384]{1,0:T(8,128)(2,1)S(1)} %get-tuple-element.66), channel_id=1, source_target_pairs={{0,24},{4,28},{8,16},{12,20},{16,8},{20,12},{24,0},{28,4},{1,25},{... | collective-permute-start | bytes 221192 | tf_op jit(solution)/shard_map/ppermute | solution.py:600
  48.1 2.0 %collective-permute-start.11 = (bf16[192,384]{1,0:T(8,128)(2,1)S(1)}, bf16[192,384]{1,0:T(8,128)(2,1)S(1)}, u32[]{:S(2)}, u32[]{:S(2)}) collective-permute-start(bf16[192,384]{1,0:T(8,128)(2,1)S(1)} %get-tuple-element.60), channel_id=1, source_target_pairs={{0,12},{4,8},{8,4},{12,0},{16,28},{20,24},{24,20},{28,16},{1,13},{... | collective-permute-start | bytes 442376 | tf_op jit(solution)/shard_map/ppermute | solution.py:600
  50.1 4.2 %own.1 = (f32[768,256]{1,0:T(8,128)S(1)}, f32[4,768,128]{2,1,0:T(8,128)S(1)}, bf16[768,256]{1,0:T(8,128)(2,1)S(1)}) custom-call(bf16[768,576]{1,0:T(8,128)(2,1)S(1)} %get-tuple-element.47.packed_ref, bf16[768,256]{1,0:T(8,128)(2,1)S(1)} %get-tuple-element.48.same_ref, bf16[768,256]{1,0:T(8,128)(2,1)S(1)} %get-tuple-element.49.apart_ref, ...), custom_call_target="tpu_custom_call" | custom-call | flops 100000000 | tf_op jit(solution)/shard_map/own/pallas_call | solution.py:69
  54.3 1.6 %collective-permute-start.13 = (bf16[96,384]{1,0:T(8,128)(2,1)S(1)}, bf16[96,384]{1,0:T(8,128)(2,1)S(1)}, u32[]{:S(2)}, u32[]{:S(2)}) collective-permute-start(bf16[96,384]{1,0:T(8,128)(2,1)S(1)} %collective-permute-done.12.refs_1_), channel_id=1, source_target_pairs={{0,4},{4,0},{8,12},{12,8},{16,20},{20,16},{24,28},{28,24},{1,5},{5... | collective-permute-start | bytes 221192 | tf_op jit(solution)/shard_map/ppermute | solution.py:600
  56.4 2.1 %near.1 = (f32[768,256]{1,0:T(8,128)S(1)}, f32[4,768,128]{2,1,0:T(8,128)S(1)}) custom-call(f32[768,256]{1,0:T(8,128)S(1)} %get-tuple-element.51.acc_ref, f32[4,768,128]{2,1,0:T(8,128)S(1)} %get-tuple-element.52.tops_ref, bf16[768,256]{1,0:T(8,128)(2,1)S(1)} %get-tuple-element.53.query_ref, ...), custom_call_target="tpu_custom_call", output_to_operand_aliasing={{0}: (0, {}), {1}: (1, {})} | custom-call | flops 6000000000 | tf_op jit(solution)/shard_map/near/pallas_call | solution.py:69
  58.5 2.0 %mid.1 = (f32[768,256]{1,0:T(8,128)S(1)}, f32[4,768,128]{2,1,0:T(8,128)S(1)}, bf16[768,256]{1,0:T(8,128)(2,1)S(1)}, f32[768,256]{1,0:T(8,128)S(1)}, bf16[208,256...) custom-call(f32[768,256]{1,0:T(8,128)S(1)} %get-tuple-element.56.acc_ref, ...), custom_call_target="tpu_custom_call", output_to_operand_aliasing={{0}: (0, {}), {1}: (1, {})} | custom-call | flops 6000000000 | tf_op jit(solution)/shard_map/mid/pallas_call | solution.py:69
  60.5 1.3 %collective-permute-start.17 = (bf16[208,256]{1,0:T(8,128)(2,1)S(1)}, bf16[208,256]{1,0:T(8,128)(2,1)S(1)}, u32[]{:S(2)}, u32[]{:S(2)}) collective-permute-start(bf16[208,256]{1,0:T(8,128)(2,1)S(1)} %get-tuple-element.69), channel_id=1, source_target_pairs={{0,2},{1,3},{2,0},{3,1},{4,6},{5,7},{6,4},{7,5},{8,10},{9,11},{10,... | collective-permute-start | bytes 319496 | tf_op jit(solution)/shard_map/ppermute | solution.py:600
  61.9 1.5 %far.1 = (bf16[192,256]{1,0:T(8,128)(2,1)S(1)}, bf16[192,256]{1,0:T(8,128)(2,1)S(1)}, bf16[32,256]{1,0:T(8,128)(2,1)S(1)}, bf16[32,256]{1,0:T(8,128)(2,1)S(1)}) custom-call(f32[768,256]{1,0:T(8,128)S(1)} %get-tuple-element.61.acc_ref, f32[4,768,128]{2,1,0:T(8,128)S(1)} %get-tuple-element.62.tops_ref, bf16[768,256]{1,0:T(8,128)(2,1)S(1)} %get-tuple-element.53.query_ref, ...), custom_call_target="tpu_custom_call" | custom-call | flops 1000000000 | tf_op jit(solution)/shard_map/far/pallas_call | solution.py:69
  64.3 1.3 %collective-permute-start.19 = (bf16[32,256]{1,0:T(8,128)(2,1)S(1)}, bf16[32,256]{1,0:T(8,128)(2,1)S(1)}, u32[]{:S(2)}, u32[]{:S(2)}) collective-permute-start(bf16[32,256]{1,0:T(8,128)(2,1)S(1)} %get-tuple-element.71), channel_id=1, source_target_pairs={{0,2},{1,3},{2,0},{3,1},{4,6},{5,7},{6,4},{7,5},{8,10},{9,11},{10,... | collective-permute-start | bytes 49160 | tf_op jit(solution)/shard_map/ppermute | solution.py:600
  65.7 1.5 %base.1 = (bf16[192,768]{1,0:T(8,128)(2,1)S(1)}, bf16[4,256,768]{2,1,0:T(8,128)(2,1)S(1)}) custom-call(s32[4,1,256]{2,1,0:T(1,128)S(1)} %get-tuple-element.39.codes_ref, bf16[192,768]{1,0:T(8,128)(2,1)S(1)} %get-tuple-element.40.stream_ref.refs_0_, bf16[192,768]{1,0:T(8,128)(2,1)S(1)} %collective-permute-done.4.stream_ref.refs_1_, ...), custom_call_target="tpu_custom_call" | custom-call | flops 300000000 | tf_op jit(solution)/shard_map/base/pallas_call | solution.py:69
  68.9 1.7 %mix.1 = bf16[192,768]{1,0:T(8,128)(2,1)} custom-call(bf16[192,768]{1,0:T(8,128)(2,1)S(1)} %get-tuple-element.44.base_ref, bf16[4,256,768]{2,1,0:T(8,128)(2,1)S(1)} %get-tuple-element.45.weights_ref, bf16[192,256]{1,0:T(8,128)(2,1)S(1)} %get-tuple-element.67.refs_0_, bf16[192,256]{1,0:T(8,128)(2,1)S(1)} %collective-permute-done.16.refs_1_, ...), custom_call_target="tpu_custom_call" | custom-call | flops 1000000000 | tf_op jit(solution)/shard_map/mix/pallas_call | solution.py:69
  (48 shorter events, 7.6 us)
Async XLA Ops:
  0.0 21.0 %collective-permute-start = (bf16[384,768]{1,0:T(8,128)(2,1)}, bf16[384,768]{1,0:T(8,128)(2,1)S(1)}, u32[]{:S(2)}, u32[]{:S(2)}) collective-permute-start(bf16[384,768]{1,0:T(8,128)(2,1)} %refs_0_.1), channel_id=1, source_target_pairs={{0,2},{1,3},{2,0},{3,1},{4,6},{5,7},{6,4},{7,5},{8,10},{9,11},{10,... | collective-permute-start | bytes 1769480 | tf_op jit(solution)/shard_map/ppermute | solution.py:600
  3.0 18.5 %copy-start.1 = (bf16[192,768]{1,0:T(8,128)(2,1)S(1)}, bf16[192,768]{1,0:T(8,128)(2,1)}, u32[]{:S(2)}) copy-start(bf16[192,768]{1,0:T(8,128)(2,1)} %weight_ref.1) | copy-start | bytes 884740
  3.0 18.5 %copy-start.6 = (f32[192]{0:T(256)S(1)}, f32[192]{0:T(256)}, u32[]{:S(2)}) copy-start(f32[192]{0:T(256)} %param.18) | copy-start | bytes 2308
  6.1 22.8 %all-to-all-start = ((bf16[32,80,128]{2,1,0:T(8,128)(2,1)}), bf16[32,80,128]{2,1,0:T(8,128)(2,1)S(1)}, u32[]{:S(2)}, u32[]{:S(2)}) async-start(bf16[32,80,128]{2,1,0:T(8,128)(2,1)} %route.1), calls=%async_computation | async-start | bytes 1310720 | tf_op jit(solution)/shard_map/all_to_all | solution.py:661
  21.0 3.6 %collective-permute-start.1 = (bf16[384,768]{1,0:T(8,128)(2,1)S(1)}, bf16[384,768]{1,0:T(8,128)(2,1)S(1)}, u32[]{:S(2)}, u32[]{:S(2)}) collective-permute-start(bf16[384,768]{1,0:T(8,128)(2,1)S(1)} %collective-permute-done.refs_2_), channel_id=1, source_target_pairs={{0,1},{1,0},{2,3},{3,2},{4,5},{5,4},{6,7},{7,6},{8,9},{9,8},{10,11... | collective-permute-start | bytes 1769480 | tf_op jit(solution)/shard_map/ppermute | solution.py:600
  21.0 3.6 %collective-permute-start.3 = (bf16[384,768]{1,0:T(8,128)(2,1)S(1)}, bf16[384,768]{1,0:T(8,128)(2,1)S(1)}, u32[]{:S(2)}, u32[]{:S(2)}) collective-permute-start(bf16[384,768]{1,0:T(8,128)(2,1)S(1)} %copy-done), channel_id=1, source_target_pairs={{0,1},{1,0},{2,3},{3,2},{4,5},{5,4},{6,7},{7,6},{8,9},{9,8},{10,11... | collective-permute-start | bytes 1769480 | tf_op jit(solution)/shard_map/ppermute | solution.py:600
  22.4 2.2 %collective-permute-start.2 = (bf16[192,768]{1,0:T(8,128)(2,1)}, bf16[192,768]{1,0:T(8,128)(2,1)S(1)}, u32[]{:S(2)}, u32[]{:S(2)}) collective-permute-start(bf16[192,768]{1,0:T(8,128)(2,1)} %scale.1.refs_4_), channel_id=1, source_target_pairs={{0,1},{1,0},{2,3},{3,2},{4,5},{5,4},{6,7},{7,6},{8,9},{9,8},{10,11... | collective-permute-start | bytes 884744 | tf_op jit(solution)/shard_map/ppermute | solution.py:600
  22.4 12.5 %collective-permute-start.7 = (bf16[192,768]{1,0:T(8,128)(2,1)}, bf16[192,768]{1,0:T(8,128)(2,1)}, u32[]{:S(2)}, u32[]{:S(2)}) collective-permute-start(bf16[192,768]{1,0:T(8,128)(2,1)} %scale.1.refs_4_), channel_id=1, source_target_pairs={{0,2},{1,3},{2,0},{3,1},{4,6},{5,7},{6,4},{7,5},{8,10},{9,11},{10,... | collective-permute-start | bytes 884744 | tf_op jit(solution)/shard_map/ppermute | solution.py:600
  30.6 4.3 %collective-permute-start.4 = (bf16[192,768]{1,0:T(8,128)(2,1)S(1)}, bf16[192,768]{1,0:T(8,128)(2,1)S(1)}, u32[]{:S(2)}, u32[]{:S(2)}) collective-permute-start(bf16[192,768]{1,0:T(8,128)(2,1)S(1)} %get-tuple-element.40.stream_ref.refs_0_), channel_id=1, source_target_pairs={{0,1},{1,0},{2,3},{3,2},{4,5},{5,4},{6,7},{7,6},{8,9},{9,8},{10,11... | collective-permute-start | bytes 884744 | tf_op jit(solution)/shard_map/ppermute | solution.py:600
  30.7 9.4 %collective-permute-start.5 = (bf16[192,768]{1,0:T(8,128)(2,1)S(1)}, bf16[192,768]{1,0:T(8,128)(2,1)S(1)}, u32[]{:S(2)}, u32[]{:S(2)}) collective-permute-start(bf16[192,768]{1,0:T(8,128)(2,1)S(1)} %get-tuple-element.40.stream_ref.refs_0_), channel_id=1, source_target_pairs={{0,2},{1,3},{2,0},{3,1},{4,6},{5,7},{6,4},{7,5},{8,10},{9,11},{10,... | collective-permute-start | bytes 884744 | tf_op jit(solution)/shard_map/ppermute | solution.py:600
  36.9 3.2 %collective-permute-start.8 = (bf16[192,768]{1,0:T(8,128)(2,1)S(1)}, bf16[192,768]{1,0:T(8,128)(2,1)S(1)}, u32[]{:S(2)}, u32[]{:S(2)}) collective-permute-start(bf16[192,768]{1,0:T(8,128)(2,1)S(1)} %get-tuple-element.43.refs_6_), channel_id=1, source_target_pairs={{0,1},{1,0},{2,3},{3,2},{4,5},{5,4},{6,7},{7,6},{8,9},{9,8},{10,11... | collective-permute-start | bytes 884744 | tf_op jit(solution)/shard_map/ppermute | solution.py:600
  40.1 1.6 %collective-permute-start.6 = (bf16[192,768]{1,0:T(8,128)(2,1)S(1)}, bf16[192,768]{1,0:T(8,128)(2,1)S(1)}, u32[]{:S(2)}, u32[]{:S(2)}) collective-permute-start(bf16[192,768]{1,0:T(8,128)(2,1)S(1)} %collective-permute-done.5.refs_2_.stream_ref), channel_id=1, source_target_pairs={{0,1},{1,0},{2,3},{3,2},{4,5},{5,4},{6,7},{7,6},{8,9},{9,8},{10,11... | collective-permute-start | bytes 884744 | tf_op jit(solution)/shard_map/ppermute | solution.py:600
  42.8 13.6 %collective-permute-start.9 = (bf16[384,384]{1,0:T(8,128)(2,1)S(1)}, bf16[384,384]{1,0:T(8,128)(2,1)S(1)}, u32[]{:S(2)}, u32[]{:S(2)}) collective-permute-start(bf16[384,384]{1,0:T(8,128)(2,1)S(1)} %get-tuple-element.55), channel_id=1, source_target_pairs={{0,4},{4,0},{8,12},{12,8},{16,20},{20,16},{24,28},{28,24},{1,5},{5... | collective-permute-start | bytes 884744 | tf_op jit(solution)/shard_map/ppermute | solution.py:600
  44.3 10.0 %collective-permute-start.12 = (bf16[96,384]{1,0:T(8,128)(2,1)S(1)}, bf16[96,384]{1,0:T(8,128)(2,1)S(1)}, u32[]{:S(2)}, u32[]{:S(2)}) collective-permute-start(bf16[96,384]{1,0:T(8,128)(2,1)S(1)} %get-tuple-element.66), channel_id=1, source_target_pairs={{0,16},{4,20},{8,24},{12,28},{16,0},{20,4},{24,8},{28,12},{1,17},{... | collective-permute-start | bytes 221192 | tf_op jit(solution)/shard_map/ppermute | solution.py:600
  45.6 10.3 %collective-permute-start.14 = (bf16[96,384]{1,0:T(8,128)(2,1)S(1)}, bf16[96,384]{1,0:T(8,128)(2,1)S(1)}, u32[]{:S(2)}, u32[]{:S(2)}) collective-permute-start(bf16[96,384]{1,0:T(8,128)(2,1)S(1)} %get-tuple-element.66), channel_id=1, source_target_pairs={{0,24},{4,28},{8,16},{12,20},{16,8},{20,12},{24,0},{28,4},{1,25},{... | collective-permute-start | bytes 221192 | tf_op jit(solution)/shard_map/ppermute | solution.py:600
  48.1 10.4 %collective-permute-start.10 = (bf16[192,384]{1,0:T(8,128)(2,1)S(1)}, bf16[192,384]{1,0:T(8,128)(2,1)S(1)}, u32[]{:S(2)}, u32[]{:S(2)}) collective-permute-start(bf16[192,384]{1,0:T(8,128)(2,1)S(1)} %get-tuple-element.60), channel_id=1, source_target_pairs={{0,8},{4,12},{8,0},{12,4},{16,24},{20,28},{24,16},{28,20},{1,9},{5... | collective-permute-start | bytes 442376 | tf_op jit(solution)/shard_map/ppermute | solution.py:600
  48.1 10.4 %collective-permute-start.11 = (bf16[192,384]{1,0:T(8,128)(2,1)S(1)}, bf16[192,384]{1,0:T(8,128)(2,1)S(1)}, u32[]{:S(2)}, u32[]{:S(2)}) collective-permute-start(bf16[192,384]{1,0:T(8,128)(2,1)S(1)} %get-tuple-element.60), channel_id=1, source_target_pairs={{0,12},{4,8},{8,4},{12,0},{16,28},{20,24},{24,20},{28,16},{1,13},{... | collective-permute-start | bytes 442376 | tf_op jit(solution)/shard_map/ppermute | solution.py:600
  54.3 7.5 %collective-permute-start.13 = (bf16[96,384]{1,0:T(8,128)(2,1)S(1)}, bf16[96,384]{1,0:T(8,128)(2,1)S(1)}, u32[]{:S(2)}, u32[]{:S(2)}) collective-permute-start(bf16[96,384]{1,0:T(8,128)(2,1)S(1)} %collective-permute-done.12.refs_1_), channel_id=1, source_target_pairs={{0,4},{4,0},{8,12},{12,8},{16,20},{20,16},{24,28},{28,24},{1,5},{5... | collective-permute-start | bytes 221192 | tf_op jit(solution)/shard_map/ppermute | solution.py:600
  55.9 6.0 %collective-permute-start.15 = (bf16[96,384]{1,0:T(8,128)(2,1)S(1)}, bf16[96,384]{1,0:T(8,128)(2,1)S(1)}, u32[]{:S(2)}, u32[]{:S(2)}) collective-permute-start(bf16[96,384]{1,0:T(8,128)(2,1)S(1)} %collective-permute-done.14.refs_3_), channel_id=1, source_target_pairs={{0,4},{4,0},{8,12},{12,8},{16,20},{20,16},{24,28},{28,24},{1,5},{5... | collective-permute-start | bytes 221192 | tf_op jit(solution)/shard_map/ppermute | solution.py:600
  60.5 8.4 %collective-permute-start.17 = (bf16[208,256]{1,0:T(8,128)(2,1)S(1)}, bf16[208,256]{1,0:T(8,128)(2,1)S(1)}, u32[]{:S(2)}, u32[]{:S(2)}) collective-permute-start(bf16[208,256]{1,0:T(8,128)(2,1)S(1)} %get-tuple-element.69), channel_id=1, source_target_pairs={{0,2},{1,3},{2,0},{3,1},{4,6},{5,7},{6,4},{7,5},{8,10},{9,11},{10,... | collective-permute-start | bytes 319496 | tf_op jit(solution)/shard_map/ppermute | solution.py:600
  61.8 7.0 %collective-permute-start.18 = (bf16[208,256]{1,0:T(8,128)(2,1)S(1)}, bf16[208,256]{1,0:T(8,128)(2,1)S(1)}, u32[]{:S(2)}, u32[]{:S(2)}) collective-permute-start(bf16[208,256]{1,0:T(8,128)(2,1)S(1)} %get-tuple-element.70), channel_id=1, source_target_pairs={{0,3},{1,2},{2,1},{3,0},{4,7},{5,6},{6,5},{7,4},{8,11},{9,10},{10,... | collective-permute-start | bytes 319496 | tf_op jit(solution)/shard_map/ppermute | solution.py:600
  63.4 5.5 %collective-permute-start.16 = (bf16[192,256]{1,0:T(8,128)(2,1)S(1)}, bf16[192,256]{1,0:T(8,128)(2,1)S(1)}, u32[]{:S(2)}, u32[]{:S(2)}) collective-permute-start(bf16[192,256]{1,0:T(8,128)(2,1)S(1)} %get-tuple-element.68), channel_id=1, source_target_pairs={{0,1},{1,0},{2,3},{3,2},{4,5},{5,4},{6,7},{7,6},{8,9},{9,8},{10,11... | collective-permute-start | bytes 294920 | tf_op jit(solution)/shard_map/ppermute | solution.py:600
  64.3 3.7 %collective-permute-start.19 = (bf16[32,256]{1,0:T(8,128)(2,1)S(1)}, bf16[32,256]{1,0:T(8,128)(2,1)S(1)}, u32[]{:S(2)}, u32[]{:S(2)}) collective-permute-start(bf16[32,256]{1,0:T(8,128)(2,1)S(1)} %get-tuple-element.71), channel_id=1, source_target_pairs={{0,2},{1,3},{2,0},{3,1},{4,6},{5,7},{6,4},{7,5},{8,10},{9,11},{10,... | collective-permute-start | bytes 49160 | tf_op jit(solution)/shard_map/ppermute | solution.py:600
  65.6 3.3 %collective-permute-start.20 = (bf16[32,256]{1,0:T(8,128)(2,1)S(1)}, bf16[32,256]{1,0:T(8,128)(2,1)S(1)}, u32[]{:S(2)}, u32[]{:S(2)}) collective-permute-start(bf16[32,256]{1,0:T(8,128)(2,1)S(1)} %get-tuple-element.72), channel_id=1, source_target_pairs={{0,3},{1,2},{2,1},{3,0},{4,7},{5,6},{6,5},{7,4},{8,11},{9,10},{10,... | collective-permute-start | bytes 49160 | tf_op jit(solution)/shard_map/ppermute | solution.py:600
  (5 other events, 36.1 us)

commit v8 on v7

--- a/solution.py
+++ b/solution.py
@@ -532,18 +532,22 @@
     final = message[...]
     rows = message.shape[0]
     count = rows >> level
+    late = [turn for turn in range(n_tp) if out_refs[turn].shape[0] != back_ref.shape[1]]
+    each = rows // CLASSES
+    classes = count // each
+    picks = []
+    for turn in late:
+        line = iota((out_refs[turn].shape[0], count), 0)
+        spot = (lax.axis_index("tp") ^ turn) * (each // n_tp) + line // classes
+        wanted = (line % classes) * each + spot
+        picks.append((iota(line.shape, 1) == wanted) & (line < count // n_tp))
+    picked = dot(jnp.concatenate([one_hot(pick) for pick in picks], axis=0), changed).astype(BF16)
+    for index, turn in enumerate(late):
+        length = out_refs[turn].shape[0]
+        out_refs[turn][...] = picked[index * length : (index + 1) * length]
     for turn in range(n_tp):
-        ref = out_refs[turn]
-        if ref.shape[0] == back_ref.shape[1]:
-            ref[...] = dot(back_ref[turn], final).astype(BF16)
-        else:
-            each = rows // CLASSES
-            classes = count // each
-            line = iota((ref.shape[0], count), 0)
-            spot = (lax.axis_index("tp") ^ turn) * (each // n_tp) + line // classes
-            wanted = (line % classes) * each + spot
-            pick = (iota((ref.shape[0], count), 1) == wanted) & (line < count // n_tp)
-            ref[...] = dot(one_hot(pick), changed).astype(BF16)
+        if turn not in late:
+            out_refs[turn][...] = dot(back_ref[turn], final).astype(BF16)
 
 
 def base_kernel(n_tp, codes_ref, *refs):

time: 70.8 us -> 70.9 us (level)
  no operation moved by 1% of the time
where the time goes in v8:
time: 70.9 us; the launch traced here: 70.6 us
  starting transfers between devices  25.5 us (36%)
  Pallas kernels  25.2 us (36%)
  waiting for transfers between devices  19.7 us (28%)
    pallas_call x14, Pallas kernels, call(): pl.pallas_call(kernel, name=name, out_shape=[jax.ShapeDtypeStruct(shape,...  25.2 us
    ppermute x21, starting transfers between devices, swap(): lax.ppermute(block, axis, [(index, index ^ mask) for index in range(count)])  20.6 us
    ppermute x21, waiting for transfers between devices, swap(): lax.ppermute(block, axis, [(index, index ^ mask) for index in range(count)])  15.4 us
    all_to_all x1, starting transfers between devices, body(): lax.all_to_all(blocks, ('seq', 'tp'), split_axis=0, concat_axis=0, tiled=...  4.9 us
    all_to_all x1, waiting for transfers between devices, body(): lax.all_to_all(blocks, ('seq', 'tp'), split_axis=0, concat_axis=0, tiled=...  4.28 us
  transfers between devices with their start and end apart: 22, of which 6 were waited for; matrix products, arithmetic and copies ran while one was open for 0% of the time, Pallas kernels for 32%

profile of v8, /device:TPU:0, one launch (start us, length us, event | category | flops | bytes accessed | tf_op | source)
XLA Modules:
  0.0 70.6 jit_solution(16126381897633591742)
XLA Ops:
  0.0 3.0 %collective-permute-start = (bf16[384,768]{1,0:T(8,128)(2,1)}, bf16[384,768]{1,0:T(8,128)(2,1)S(1)}, u32[]{:S(2)}, u32[]{:S(2)}) collective-permute-start(bf16[384,768]{1,0:T(8,128)(2,1)} %refs_0_.1), channel_id=1, source_target_pairs={{0,2},{1,3},{2,0},{3,1},{4,6},{5,7},{6,4},{7,5},{8,10},{9,11},{10,... | collective-permute-start | bytes 1769480 | tf_op jit(solution)/shard_map/ppermute | solution.py:604
  3.0 3.1 %route.1 = bf16[32,80,128]{2,1,0:T(8,128)(2,1)} custom-call(s32[6,128]{1,0:T(8,128)} %bitcast.24, s32[6,128]{1,0:T(8,128)} %bitcast.25, bf16[768,384]{1,0:T(8,128)(2,1)} %tiles_hbm.1), custom_call_target="tpu_custom_call" | custom-call | flops 3000000000 | tf_op jit(solution)/shard_map/route/pallas_call | solution.py:69
  6.1 4.9 %all-to-all-start = ((bf16[32,80,128]{2,1,0:T(8,128)(2,1)}), bf16[32,80,128]{2,1,0:T(8,128)(2,1)S(1)}, u32[]{:S(2)}, u32[]{:S(2)}) async-start(bf16[32,80,128]{2,1,0:T(8,128)(2,1)} %route.1), calls=%async_computation | async-start | bytes 1310720 | tf_op jit(solution)/shard_map/all_to_all | solution.py:665
  11.0 10.0 %collective-permute-done.refs_2_ = bf16[384,768]{1,0:T(8,128)(2,1)S(1)} collective-permute-done((bf16[384,768]{1,0:T(8,128)(2,1)}, bf16[384,768]{1,0:T(8,128)(2,1)S(1)}, u32[]{:S(2)}, u32[]{:S(2)}) %collective-permute-start) | collective-permute-done | bytes 589856 | tf_op jit(solution)/shard_map/ppermute | solution.py:604
  22.4 2.2 %collective-permute-start.7 = (bf16[192,768]{1,0:T(8,128)(2,1)}, bf16[192,768]{1,0:T(8,128)(2,1)}, u32[]{:S(2)}, u32[]{:S(2)}) collective-permute-start(bf16[192,768]{1,0:T(8,128)(2,1)} %scale.1.refs_4_), channel_id=1, source_target_pairs={{0,2},{1,3},{2,0},{3,1},{4,6},{5,7},{6,4},{7,5},{8,10},{9,11},{10,... | collective-permute-start | bytes 884744 | tf_op jit(solution)/shard_map/ppermute | solution.py:604
  24.6 4.3 %all-to-all-done.recv_hbm = bf16[32,80,128]{2,1,0:T(8,128)(2,1)S(1)} async-done(((bf16[32,80,128]{2,1,0:T(8,128)(2,1)}), bf16[32,80,128]{2,1,0:T(8,128)(2,1)S(1)}, u32[]{:S(2)}, u32[]{:S(2)}) %all-to-all-start) | async-done | bytes 655392 | tf_op jit(solution)/shard_map/all_to_all | solution.py:665
  28.9 1.7 %project.1 = (bf16[192,768]{1,0:T(8,128)(2,1)S(1)}, s32[4,1,256]{2,1,0:T(1,128)S(1)}, f32[8,768]{1,0:T(8,128)S(1)}) custom-call(bf16[32,80,128]{2,1,0:T(8,128)(2,1)S(1)} %all-to-all-done.recv_hbm, bf16[16,128]{1,0:T(8,128)(2,1)S(1)} %hint.1.early_ref, bf16[192,768]{1,0:T(8,128)(2,1)S(1)} %collective-permute-done.2.beside_ref.refs_5_, ...), custom_call_target="tpu_custom_call" | custom-call | flops 500000000 | tf_op jit(solution)/shard_map/project/pallas_call | solution.py:69
  30.7 1.6 %collective-permute-start.5 = (bf16[192,768]{1,0:T(8,128)(2,1)S(1)}, bf16[192,768]{1,0:T(8,128)(2,1)S(1)}, u32[]{:S(2)}, u32[]{:S(2)}) collective-permute-start(bf16[192,768]{1,0:T(8,128)(2,1)S(1)} %get-tuple-element.40.stream_ref.refs_0_), channel_id=1, source_target_pairs={{0,2},{1,3},{2,0},{3,1},{4,6},{5,7},{6,4},{7,5},{8,10},{9,11},{10,... | collective-permute-start | bytes 884744 | tf_op jit(solution)/shard_map/ppermute | solution.py:604
  32.3 2.6 %heads_1.1 = (bf16[768,576]{1,0:T(8,128)(2,1)S(1)}, bf16[768,256]{1,0:T(8,128)(2,1)S(1)}, bf16[768,256]{1,0:T(8,128)(2,1)S(1)}, bf16[4,192,768]{2,1,0:T(8,128)(2...) custom-call(s32[4,1,256]{2,1,0:T(1,128)S(1)} %get-tuple-element.39.c, ...), custom_call_target="tpu_custom_call" | custom-call | flops 1000000000 | tf_op jit(solution)/shard_map/heads_1/pallas_call | solution.py:69
  35.0 1.9 %heads_2.2 = (bf16[768,576]{1,0:T(8,128)(2,1)S(1)}, bf16[192,768]{1,0:T(8,128)(2,1)S(1)}) custom-call(s32[4,1,256]{2,1,0:T(1,128)S(1)} %get-tuple-element.39.codes_ref, f32[6,128]{1,0:T(8,128)S(1)} %bitcast.20, bf16[192,768]{1,0:T(8,128)(2,1)S(1)} %bitcast.8, bf16[192,768]{1,0:T(8,128)(2,1)S(1)} %bitcast.12, bf16[192,768]{1,0:T(8,128)(2,1)S(1)} %bitcast.16, ...), custom_call_target="tpu_custom_call" | custom-call | flops 1000000000 | tf_op jit(solution)/shard_map/heads_2/pallas_call | solution.py:69
  37.0 3.1 %collective-permute-done.5.refs_2_.stream_ref = bf16[192,768]{1,0:T(8,128)(2,1)S(1)} collective-permute-done((bf16[192,768]{1,0:T(8,128)(2,1)S(1)}, bf16[192,768]{1,0:T(8,128)(2,1)S(1)}, u32[]{:S(2)}, u32[]{:S(2)}) %collective-permute-start.5) | collective-permute-done | bytes 294944 | tf_op jit(solution)/shard_map/ppermute | solution.py:604
  42.8 1.5 %collective-permute-start.9 = (bf16[384,384]{1,0:T(8,128)(2,1)S(1)}, bf16[384,384]{1,0:T(8,128)(2,1)S(1)}, u32[]{:S(2)}, u32[]{:S(2)}) collective-permute-start(bf16[384,384]{1,0:T(8,128)(2,1)S(1)} %get-tuple-element.55), channel_id=1, source_target_pairs={{0,4},{4,0},{8,12},{12,8},{16,20},{20,16},{24,28},{28,24},{1,5},{5... | collective-permute-start | bytes 884744 | tf_op jit(solution)/shard_map/ppermute | solution.py:604
  44.3 1.4 %collective-permute-start.12 = (bf16[96,384]{1,0:T(8,128)(2,1)S(1)}, bf16[96,384]{1,0:T(8,128)(2,1)S(1)}, u32[]{:S(2)}, u32[]{:S(2)}) collective-permute-start(bf16[96,384]{1,0:T(8,128)(2,1)S(1)} %get-tuple-element.66), channel_id=1, source_target_pairs={{0,16},{4,20},{8,24},{12,28},{16,0},{20,4},{24,8},{28,12},{1,17},{... | collective-permute-start | bytes 221192 | tf_op jit(solution)/shard_map/ppermute | solution.py:604
  45.6 2.5 %collective-permute-start.14 = (bf16[96,384]{1,0:T(8,128)(2,1)S(1)}, bf16[96,384]{1,0:T(8,128)(2,1)S(1)}, u32[]{:S(2)}, u32[]{:S(2)}) collective-permute-start(bf16[96,384]{1,0:T(8,128)(2,1)S(1)} %get-tuple-element.66), channel_id=1, source_target_pairs={{0,24},{4,28},{8,16},{12,20},{16,8},{20,12},{24,0},{28,4},{1,25},{... | collective-permute-start | bytes 221192 | tf_op jit(solution)/shard_map/ppermute | solution.py:604
  48.1 2.0 %collective-permute-start.11 = (bf16[192,384]{1,0:T(8,128)(2,1)S(1)}, bf16[192,384]{1,0:T(8,128)(2,1)S(1)}, u32[]{:S(2)}, u32[]{:S(2)}) collective-permute-start(bf16[192,384]{1,0:T(8,128)(2,1)S(1)} %get-tuple-element.60), channel_id=1, source_target_pairs={{0,12},{4,8},{8,4},{12,0},{16,28},{20,24},{24,20},{28,16},{1,13},{... | collective-permute-start | bytes 442376 | tf_op jit(solution)/shard_map/ppermute | solution.py:604
  50.1 4.2 %own.1 = (f32[768,256]{1,0:T(8,128)S(1)}, f32[4,768,128]{2,1,0:T(8,128)S(1)}, bf16[768,256]{1,0:T(8,128)(2,1)S(1)}) custom-call(bf16[768,576]{1,0:T(8,128)(2,1)S(1)} %get-tuple-element.47.packed_ref, bf16[768,256]{1,0:T(8,128)(2,1)S(1)} %get-tuple-element.48.same_ref, bf16[768,256]{1,0:T(8,128)(2,1)S(1)} %get-tuple-element.49.apart_ref, ...), custom_call_target="tpu_custom_call" | custom-call | flops 100000000 | tf_op jit(solution)/shard_map/own/pallas_call | solution.py:69
  54.3 1.6 %collective-permute-start.13 = (bf16[96,384]{1,0:T(8,128)(2,1)S(1)}, bf16[96,384]{1,0:T(8,128)(2,1)S(1)}, u32[]{:S(2)}, u32[]{:S(2)}) collective-permute-start(bf16[96,384]{1,0:T(8,128)(2,1)S(1)} %collective-permute-done.12.refs_1_), channel_id=1, source_target_pairs={{0,4},{4,0},{8,12},{12,8},{16,20},{20,16},{24,28},{28,24},{1,5},{5... | collective-permute-start | bytes 221192 | tf_op jit(solution)/shard_map/ppermute | solution.py:604
  56.4 2.1 %near.1 = (f32[768,256]{1,0:T(8,128)S(1)}, f32[4,768,128]{2,1,0:T(8,128)S(1)}) custom-call(f32[768,256]{1,0:T(8,128)S(1)} %get-tuple-element.51.acc_ref, f32[4,768,128]{2,1,0:T(8,128)S(1)} %get-tuple-element.52.tops_ref, bf16[768,256]{1,0:T(8,128)(2,1)S(1)} %get-tuple-element.53.query_ref, ...), custom_call_target="tpu_custom_call", output_to_operand_aliasing={{0}: (0, {}), {1}: (1, {})} | custom-call | flops 6000000000 | tf_op jit(solution)/shard_map/near/pallas_call | solution.py:69
  58.5 2.0 %mid.1 = (f32[768,256]{1,0:T(8,128)S(1)}, f32[4,768,128]{2,1,0:T(8,128)S(1)}, bf16[768,256]{1,0:T(8,128)(2,1)S(1)}, f32[768,256]{1,0:T(8,128)S(1)}, bf16[208,256...) custom-call(f32[768,256]{1,0:T(8,128)S(1)} %get-tuple-element.56.acc_ref, ...), custom_call_target="tpu_custom_call", output_to_operand_aliasing={{0}: (0, {}), {1}: (1, {})} | custom-call | flops 6000000000 | tf_op jit(solution)/shard_map/mid/pallas_call | solution.py:69
  60.5 1.3 %collective-permute-start.17 = (bf16[208,256]{1,0:T(8,128)(2,1)S(1)}, bf16[208,256]{1,0:T(8,128)(2,1)S(1)}, u32[]{:S(2)}, u32[]{:S(2)}) collective-permute-start(bf16[208,256]{1,0:T(8,128)(2,1)S(1)} %get-tuple-element.69), channel_id=1, source_target_pairs={{0,2},{1,3},{2,0},{3,1},{4,6},{5,7},{6,4},{7,5},{8,10},{9,11},{10,... | collective-permute-start | bytes 319496 | tf_op jit(solution)/shard_map/ppermute | solution.py:604
  61.9 1.5 %far.1 = (bf16[192,256]{1,0:T(8,128)(2,1)S(1)}, bf16[192,256]{1,0:T(8,128)(2,1)S(1)}, bf16[32,256]{1,0:T(8,128)(2,1)S(1)}, bf16[32,256]{1,0:T(8,128)(2,1)S(1)}) custom-call(f32[768,256]{1,0:T(8,128)S(1)} %get-tuple-element.61.acc_ref, f32[4,768,128]{2,1,0:T(8,128)S(1)} %get-tuple-element.62.tops_ref, bf16[768,256]{1,0:T(8,128)(2,1)S(1)} %get-tuple-element.53.query_ref, ...), custom_call_target="tpu_custom_call" | custom-call | flops 1000000000 | tf_op jit(solution)/shard_map/far/pallas_call | solution.py:69
  64.3 1.3 %collective-permute-start.19 = (bf16[32,256]{1,0:T(8,128)(2,1)S(1)}, bf16[32,256]{1,0:T(8,128)(2,1)S(1)}, u32[]{:S(2)}, u32[]{:S(2)}) collective-permute-start(bf16[32,256]{1,0:T(8,128)(2,1)S(1)} %get-tuple-element.71), channel_id=1, source_target_pairs={{0,2},{1,3},{2,0},{3,1},{4,6},{5,7},{6,4},{7,5},{8,10},{9,11},{10,... | collective-permute-start | bytes 49160 | tf_op jit(solution)/shard_map/ppermute | solution.py:604
  65.8 1.5 %base.1 = (bf16[192,768]{1,0:T(8,128)(2,1)S(1)}, bf16[4,256,768]{2,1,0:T(8,128)(2,1)S(1)}) custom-call(s32[4,1,256]{2,1,0:T(1,128)S(1)} %get-tuple-element.39.codes_ref, bf16[192,768]{1,0:T(8,128)(2,1)S(1)} %get-tuple-element.40.stream_ref.refs_0_, bf16[192,768]{1,0:T(8,128)(2,1)S(1)} %collective-permute-done.4.stream_ref.refs_1_, ...), custom_call_target="tpu_custom_call" | custom-call | flops 300000000 | tf_op jit(solution)/shard_map/base/pallas_call | solution.py:69
  68.9 1.7 %mix.1 = bf16[192,768]{1,0:T(8,128)(2,1)} custom-call(bf16[192,768]{1,0:T(8,128)(2,1)S(1)} %get-tuple-element.44.base_ref, bf16[4,256,768]{2,1,0:T(8,128)(2,1)S(1)} %get-tuple-element.45.weights_ref, bf16[192,256]{1,0:T(8,128)(2,1)S(1)} %get-tuple-element.67.refs_0_, bf16[192,256]{1,0:T(8,128)(2,1)S(1)} %collective-permute-done.16.refs_1_, ...), custom_call_target="tpu_custom_call" | custom-call | flops 1000000000 | tf_op jit(solution)/shard_map/mix/pallas_call | solution.py:69
  (48 shorter events, 7.6 us)
Async XLA Ops:
  0.0 21.0 %collective-permute-start = (bf16[384,768]{1,0:T(8,128)(2,1)}, bf16[384,768]{1,0:T(8,128)(2,1)S(1)}, u32[]{:S(2)}, u32[]{:S(2)}) collective-permute-start(bf16[384,768]{1,0:T(8,128)(2,1)} %refs_0_.1), channel_id=1, source_target_pairs={{0,2},{1,3},{2,0},{3,1},{4,6},{5,7},{6,4},{7,5},{8,10},{9,11},{10,... | collective-permute-start | bytes 1769480 | tf_op jit(solution)/shard_map/ppermute | solution.py:604
  3.0 18.5 %copy-start.1 = (bf16[192,768]{1,0:T(8,128)(2,1)S(1)}, bf16[192,768]{1,0:T(8,128)(2,1)}, u32[]{:S(2)}) copy-start(bf16[192,768]{1,0:T(8,128)(2,1)} %weight_ref.1) | copy-start | bytes 884740
  3.0 18.5 %copy-start.6 = (f32[192]{0:T(256)S(1)}, f32[192]{0:T(256)}, u32[]{:S(2)}) copy-start(f32[192]{0:T(256)} %param.18) | copy-start | bytes 2308
  6.1 22.8 %all-to-all-start = ((bf16[32,80,128]{2,1,0:T(8,128)(2,1)}), bf16[32,80,128]{2,1,0:T(8,128)(2,1)S(1)}, u32[]{:S(2)}, u32[]{:S(2)}) async-start(bf16[32,80,128]{2,1,0:T(8,128)(2,1)} %route.1), calls=%async_computation | async-start | bytes 1310720 | tf_op jit(solution)/shard_map/all_to_all | solution.py:665
  21.0 3.6 %collective-permute-start.1 = (bf16[384,768]{1,0:T(8,128)(2,1)S(1)}, bf16[384,768]{1,0:T(8,128)(2,1)S(1)}, u32[]{:S(2)}, u32[]{:S(2)}) collective-permute-start(bf16[384,768]{1,0:T(8,128)(2,1)S(1)} %collective-permute-done.refs_2_), channel_id=1, source_target_pairs={{0,1},{1,0},{2,3},{3,2},{4,5},{5,4},{6,7},{7,6},{8,9},{9,8},{10,11... | collective-permute-start | bytes 1769480 | tf_op jit(solution)/shard_map/ppermute | solution.py:604
  21.0 3.6 %collective-permute-start.3 = (bf16[384,768]{1,0:T(8,128)(2,1)S(1)}, bf16[384,768]{1,0:T(8,128)(2,1)S(1)}, u32[]{:S(2)}, u32[]{:S(2)}) collective-permute-start(bf16[384,768]{1,0:T(8,128)(2,1)S(1)} %copy-done), channel_id=1, source_target_pairs={{0,1},{1,0},{2,3},{3,2},{4,5},{5,4},{6,7},{7,6},{8,9},{9,8},{10,11... | collective-permute-start | bytes 1769480 | tf_op jit(solution)/shard_map/ppermute | solution.py:604
  22.4 2.2 %collective-permute-start.2 = (bf16[192,768]{1,0:T(8,128)(2,1)}, bf16[192,768]{1,0:T(8,128)(2,1)S(1)}, u32[]{:S(2)}, u32[]{:S(2)}) collective-permute-start(bf16[192,768]{1,0:T(8,128)(2,1)} %scale.1.refs_4_), channel_id=1, source_target_pairs={{0,1},{1,0},{2,3},{3,2},{4,5},{5,4},{6,7},{7,6},{8,9},{9,8},{10,11... | collective-permute-start | bytes 884744 | tf_op jit(solution)/shard_map/ppermute | solution.py:604
  22.4 12.5 %collective-permute-start.7 = (bf16[192,768]{1,0:T(8,128)(2,1)}, bf16[192,768]{1,0:T(8,128)(2,1)}, u32[]{:S(2)}, u32[]{:S(2)}) collective-permute-start(bf16[192,768]{1,0:T(8,128)(2,1)} %scale.1.refs_4_), channel_id=1, source_target_pairs={{0,2},{1,3},{2,0},{3,1},{4,6},{5,7},{6,4},{7,5},{8,10},{9,11},{10,... | collective-permute-start | bytes 884744 | tf_op jit(solution)/shard_map/ppermute | solution.py:604
  30.6 4.3 %collective-permute-start.4 = (bf16[192,768]{1,0:T(8,128)(2,1)S(1)}, bf16[192,768]{1,0:T(8,128)(2,1)S(1)}, u32[]{:S(2)}, u32[]{:S(2)}) collective-permute-start(bf16[192,768]{1,0:T(8,128)(2,1)S(1)} %get-tuple-element.40.stream_ref.refs_0_), channel_id=1, source_target_pairs={{0,1},{1,0},{2,3},{3,2},{4,5},{5,4},{6,7},{7,6},{8,9},{9,8},{10,11... | collective-permute-start | bytes 884744 | tf_op jit(solution)/shard_map/ppermute | solution.py:604
  30.7 9.4 %collective-permute-start.5 = (bf16[192,768]{1,0:T(8,128)(2,1)S(1)}, bf16[192,768]{1,0:T(8,128)(2,1)S(1)}, u32[]{:S(2)}, u32[]{:S(2)}) collective-permute-start(bf16[192,768]{1,0:T(8,128)(2,1)S(1)} %get-tuple-element.40.stream_ref.refs_0_), channel_id=1, source_target_pairs={{0,2},{1,3},{2,0},{3,1},{4,6},{5,7},{6,4},{7,5},{8,10},{9,11},{10,... | collective-permute-start | bytes 884744 | tf_op jit(solution)/shard_map/ppermute | solution.py:604
  36.9 3.2 %collective-permute-start.8 = (bf16[192,768]{1,0:T(8,128)(2,1)S(1)}, bf16[192,768]{1,0:T(8,128)(2,1)S(1)}, u32[]{:S(2)}, u32[]{:S(2)}) collective-permute-start(bf16[192,768]{1,0:T(8,128)(2,1)S(1)} %get-tuple-element.43.refs_6_), channel_id=1, source_target_pairs={{0,1},{1,0},{2,3},{3,2},{4,5},{5,4},{6,7},{7,6},{8,9},{9,8},{10,11... | collective-permute-start | bytes 884744 | tf_op jit(solution)/shard_map/ppermute | solution.py:604
  40.1 1.6 %collective-permute-start.6 = (bf16[192,768]{1,0:T(8,128)(2,1)S(1)}, bf16[192,768]{1,0:T(8,128)(2,1)S(1)}, u32[]{:S(2)}, u32[]{:S(2)}) collective-permute-start(bf16[192,768]{1,0:T(8,128)(2,1)S(1)} %collective-permute-done.5.refs_2_.stream_ref), channel_id=1, source_target_pairs={{0,1},{1,0},{2,3},{3,2},{4,5},{5,4},{6,7},{7,6},{8,9},{9,8},{10,11... | collective-permute-start | bytes 884744 | tf_op jit(solution)/shard_map/ppermute | solution.py:604
  42.8 13.6 %collective-permute-start.9 = (bf16[384,384]{1,0:T(8,128)(2,1)S(1)}, bf16[384,384]{1,0:T(8,128)(2,1)S(1)}, u32[]{:S(2)}, u32[]{:S(2)}) collective-permute-start(bf16[384,384]{1,0:T(8,128)(2,1)S(1)} %get-tuple-element.55), channel_id=1, source_target_pairs={{0,4},{4,0},{8,12},{12,8},{16,20},{20,16},{24,28},{28,24},{1,5},{5... | collective-permute-start | bytes 884744 | tf_op jit(solution)/shard_map/ppermute | solution.py:604
  44.3 10.0 %collective-permute-start.12 = (bf16[96,384]{1,0:T(8,128)(2,1)S(1)}, bf16[96,384]{1,0:T(8,128)(2,1)S(1)}, u32[]{:S(2)}, u32[]{:S(2)}) collective-permute-start(bf16[96,384]{1,0:T(8,128)(2,1)S(1)} %get-tuple-element.66), channel_id=1, source_target_pairs={{0,16},{4,20},{8,24},{12,28},{16,0},{20,4},{24,8},{28,12},{1,17},{... | collective-permute-start | bytes 221192 | tf_op jit(solution)/shard_map/ppermute | solution.py:604
  45.6 10.3 %collective-permute-start.14 = (bf16[96,384]{1,0:T(8,128)(2,1)S(1)}, bf16[96,384]{1,0:T(8,128)(2,1)S(1)}, u32[]{:S(2)}, u32[]{:S(2)}) collective-permute-start(bf16[96,384]{1,0:T(8,128)(2,1)S(1)} %get-tuple-element.66), channel_id=1, source_target_pairs={{0,24},{4,28},{8,16},{12,20},{16,8},{20,12},{24,0},{28,4},{1,25},{... | collective-permute-start | bytes 221192 | tf_op jit(solution)/shard_map/ppermute | solution.py:604
  48.1 10.4 %collective-permute-start.10 = (bf16[192,384]{1,0:T(8,128)(2,1)S(1)}, bf16[192,384]{1,0:T(8,128)(2,1)S(1)}, u32[]{:S(2)}, u32[]{:S(2)}) collective-permute-start(bf16[192,384]{1,0:T(8,128)(2,1)S(1)} %get-tuple-element.60), channel_id=1, source_target_pairs={{0,8},{4,12},{8,0},{12,4},{16,24},{20,28},{24,16},{28,20},{1,9},{5... | collective-permute-start | bytes 442376 | tf_op jit(solution)/shard_map/ppermute | solution.py:604
  48.1 10.4 %collective-permute-start.11 = (bf16[192,384]{1,0:T(8,128)(2,1)S(1)}, bf16[192,384]{1,0:T(8,128)(2,1)S(1)}, u32[]{:S(2)}, u32[]{:S(2)}) collective-permute-start(bf16[192,384]{1,0:T(8,128)(2,1)S(1)} %get-tuple-element.60), channel_id=1, source_target_pairs={{0,12},{4,8},{8,4},{12,0},{16,28},{20,24},{24,20},{28,16},{1,13},{... | collective-permute-start | bytes 442376 | tf_op jit(solution)/shard_map/ppermute | solution.py:604
  54.3 7.5 %collective-permute-start.13 = (bf16[96,384]{1,0:T(8,128)(2,1)S(1)}, bf16[96,384]{1,0:T(8,128)(2,1)S(1)}, u32[]{:S(2)}, u32[]{:S(2)}) collective-permute-start(bf16[96,384]{1,0:T(8,128)(2,1)S(1)} %collective-permute-done.12.refs_1_), channel_id=1, source_target_pairs={{0,4},{4,0},{8,12},{12,8},{16,20},{20,16},{24,28},{28,24},{1,5},{5... | collective-permute-start | bytes 221192 | tf_op jit(solution)/shard_map/ppermute | solution.py:604
  55.9 6.0 %collective-permute-start.15 = (bf16[96,384]{1,0:T(8,128)(2,1)S(1)}, bf16[96,384]{1,0:T(8,128)(2,1)S(1)}, u32[]{:S(2)}, u32[]{:S(2)}) collective-permute-start(bf16[96,384]{1,0:T(8,128)(2,1)S(1)} %collective-permute-done.14.refs_3_), channel_id=1, source_target_pairs={{0,4},{4,0},{8,12},{12,8},{16,20},{20,16},{24,28},{28,24},{1,5},{5... | collective-permute-start | bytes 221192 | tf_op jit(solution)/shard_map/ppermute | solution.py:604
  60.5 8.4 %collective-permute-start.17 = (bf16[208,256]{1,0:T(8,128)(2,1)S(1)}, bf16[208,256]{1,0:T(8,128)(2,1)S(1)}, u32[]{:S(2)}, u32[]{:S(2)}) collective-permute-start(bf16[208,256]{1,0:T(8,128)(2,1)S(1)} %get-tuple-element.69), channel_id=1, source_target_pairs={{0,2},{1,3},{2,0},{3,1},{4,6},{5,7},{6,4},{7,5},{8,10},{9,11},{10,... | collective-permute-start | bytes 319496 | tf_op jit(solution)/shard_map/ppermute | solution.py:604
  61.8 7.1 %collective-permute-start.18 = (bf16[208,256]{1,0:T(8,128)(2,1)S(1)}, bf16[208,256]{1,0:T(8,128)(2,1)S(1)}, u32[]{:S(2)}, u32[]{:S(2)}) collective-permute-start(bf16[208,256]{1,0:T(8,128)(2,1)S(1)} %get-tuple-element.70), channel_id=1, source_target_pairs={{0,3},{1,2},{2,1},{3,0},{4,7},{5,6},{6,5},{7,4},{8,11},{9,10},{10,... | collective-permute-start | bytes 319496 | tf_op jit(solution)/shard_map/ppermute | solution.py:604
  63.4 5.5 %collective-permute-start.16 = (bf16[192,256]{1,0:T(8,128)(2,1)S(1)}, bf16[192,256]{1,0:T(8,128)(2,1)S(1)}, u32[]{:S(2)}, u32[]{:S(2)}) collective-permute-start(bf16[192,256]{1,0:T(8,128)(2,1)S(1)} %get-tuple-element.68), channel_id=1, source_target_pairs={{0,1},{1,0},{2,3},{3,2},{4,5},{5,4},{6,7},{7,6},{8,9},{9,8},{10,11... | collective-permute-start | bytes 294920 | tf_op jit(solution)/shard_map/ppermute | solution.py:604
  64.3 3.7 %collective-permute-start.19 = (bf16[32,256]{1,0:T(8,128)(2,1)S(1)}, bf16[32,256]{1,0:T(8,128)(2,1)S(1)}, u32[]{:S(2)}, u32[]{:S(2)}) collective-permute-start(bf16[32,256]{1,0:T(8,128)(2,1)S(1)} %get-tuple-element.71), channel_id=1, source_target_pairs={{0,2},{1,3},{2,0},{3,1},{4,6},{5,7},{6,4},{7,5},{8,10},{9,11},{10,... | collective-permute-start | bytes 49160 | tf_op jit(solution)/shard_map/ppermute | solution.py:604
  65.6 3.3 %collective-permute-start.20 = (bf16[32,256]{1,0:T(8,128)(2,1)S(1)}, bf16[32,256]{1,0:T(8,128)(2,1)S(1)}, u32[]{:S(2)}, u32[]{:S(2)}) collective-permute-start(bf16[32,256]{1,0:T(8,128)(2,1)S(1)} %get-tuple-element.72), channel_id=1, source_target_pairs={{0,3},{1,2},{2,1},{3,0},{4,7},{5,6},{6,5},{7,4},{8,11},{9,10},{10,... | collective-permute-start | bytes 49160 | tf_op jit(solution)/shard_map/ppermute | solution.py:604
  (5 other events, 36.1 us)
